TPU v7x, 256 devices: a whole 4x4x8 slice. The times are simulated.
256 devices in a mesh: grp: 2 (over core), ctx: 64 (over x, z_lo, y), hd: 2 (over z_hi).
Axes of the slice: x: 4, y: 4, z: 8 (z_hi: 2, z_lo: 4; z = z_hi * 4 + z_lo), core: 2. Of those that a mesh axis runs over, the one named last changes fastest.
Arguments:
- video_q: bfloat16 [8192, 24, 128], P(('ctx', 'hd'), 'grp'), may hold values from -6 to 6
- video_k: bfloat16 [8192, 24, 128], P(('ctx', 'hd'), 'grp'), may hold values from -6 to 6
- video_v: bfloat16 [8192, 24, 128], P(('ctx', 'hd'), 'grp'), may hold values from -6 to 6
- positions: int32 [3, 8192], P(None, ('ctx', 'hd')), may hold values from 0 to 31, as said below
- text_q: bfloat16 [256, 24, 128], P(None, ('grp', 'hd')), may hold values from -16 to 16
- text_k: bfloat16 [256, 24, 128], P(None, ('grp', 'hd')), may hold values from -16 to 16
- text_v: bfloat16 [256, 24, 128], P(None, ('grp', 'hd')), may hold values from -6 to 6
- text_count: int32 [1], replicated, may hold values from 64 to 256
Outputs:
- video_out: bfloat16 [8192, 24, 128], P(('ctx', 'hd'), 'grp')
- text_out: bfloat16 [256, 24, 128], P('ctx', ('grp', 'hd'))
Inputs may be any that keep to these rules, and one draw needn't show every extreme that they name: `positions`: column n holds the frame, row and column of video token n; the columns are distinct cells of a grid of 32 frames of 16 by 16 cells.
All inputs are finite; a program needn't handle non-finite values.
Results may differ from a plain program's by a relative error of at most 0.0073.
Values may be sent and summed in bfloat16 or wider, within the bound.
No kernel may reach another device: no remote copies, remote signals or barrier semaphores. Data moves between devices by JAX's collectives and lax.ppermute only.
A program may use at most 128 MiB of HBM per device.

v0:
```python
import math

import jax
import jax.numpy as jnp
from jax import lax
from jax.sharding import PartitionSpec as P

THETA = 256.0


def rotate(tokens_in, positions):
    head_dim = tokens_in.shape[-1]
    band_t = head_dim // 8
    band_h = (head_dim - band_t) // 2
    band_w = head_dim - band_t - band_h
    values = tokens_in.astype(jnp.float32)
    pieces = []
    offset = 0
    for axis_index, band_size in ((0, band_t), (1, band_h), (2, band_w)):
        half_size = band_size // 2
        frequency = THETA ** (-2.0 * jnp.arange(half_size, dtype=jnp.float32) / band_size)
        angles = positions[axis_index].astype(jnp.float32)[:, None] * frequency[None, :]
        cos_table = jnp.cos(angles)[:, None, :]
        sin_table = jnp.sin(angles)[:, None, :]
        lower_half = values[:, :, offset : offset + half_size]
        upper_half = values[:, :, offset + half_size : offset + band_size]
        pieces.append(lower_half * cos_table - upper_half * sin_table)
        pieces.append(upper_half * cos_table + lower_half * sin_table)
        offset += band_size
    return jnp.concatenate(pieces, axis=-1).astype(jnp.bfloat16)


def local(video_q, video_k, video_v, positions, text_q, text_k, text_v, text_count):
    rotated_q = rotate(video_q, positions)
    rotated_k = rotate(video_k, positions)
    queries_video, keys_video, values_video = (
        lax.all_to_all(rotated_q, "hd", split_axis=1, concat_axis=0, tiled=True),
        lax.all_to_all(rotated_k, "hd", split_axis=1, concat_axis=0, tiled=True),
        lax.all_to_all(video_v, "hd", split_axis=1, concat_axis=0, tiled=True),
    )
    cycle_size = lax.axis_size("ctx")
    text_share = text_q.shape[0] // cycle_size
    own_text = lax.dynamic_slice_in_dim(text_q, lax.axis_index("ctx") * text_share, text_share, 0)
    queries = jnp.concatenate([queries_video, own_text], axis=0)
    scale = 1.0 / math.sqrt(queries.shape[-1])
    text_live = jnp.arange(text_k.shape[0], dtype=jnp.int32) < text_count[0]
    scores = jnp.einsum("qhd,khd->qhk", queries, text_k, preferred_element_type=jnp.float32) * scale
    scores = jnp.where(text_live[None, None, :], scores, -jnp.inf)
    peak = jnp.max(scores, axis=2)
    probs = jnp.exp(scores - peak[..., None])
    total = jnp.sum(probs, axis=2)
    mixed = jnp.einsum(
        "qhk,khd->qhd", probs.astype(jnp.bfloat16), text_v, preferred_element_type=jnp.float32
    )
    keys_all, values_all = (
        lax.all_gather(keys_video, "ctx", axis=0, tiled=True),
        lax.all_gather(values_video, "ctx", axis=0, tiled=True),
    )
    piece_scores = (
        jnp.einsum("qhd,khd->qhk", queries, keys_all, preferred_element_type=jnp.float32) * scale
    )
    new_peak = jnp.maximum(peak, jnp.max(piece_scores, axis=2))
    factor = jnp.exp(peak - new_peak)
    piece_probs = jnp.exp(piece_scores - new_peak[..., None])
    new_total = total * factor + jnp.sum(piece_probs, axis=2)
    new_mixed = mixed * factor[..., None] + jnp.einsum(
        "qhk,khd->qhd",
        piece_probs.astype(jnp.bfloat16),
        values_all,
        preferred_element_type=jnp.float32,
    )
    attended = (new_mixed / new_total[..., None]).astype(jnp.bfloat16)
    video_rows = queries_video.shape[0]
    video_heads = attended[:video_rows]
    text_out = attended[video_rows:]
    video_out = lax.all_to_all(video_heads, "hd", split_axis=0, concat_axis=1, tiled=True)
    return (video_out, text_out)


def solution(mesh):
    return jax.shard_map(
        local,
        mesh=mesh,
        in_specs=(
            P(("ctx", "hd"), "grp", None),
            P(("ctx", "hd"), "grp", None),
            P(("ctx", "hd"), "grp", None),
            P(None, ("ctx", "hd")),
            P(None, ("grp", "hd"), None),
            P(None, ("grp", "hd"), None),
            P(None, ("grp", "hd"), None),
            P(),
        ),
        out_specs=(P(("ctx", "hd"), "grp", None), P("ctx", ("grp", "hd"), None)),
        check_vma=False,
    )
```

profile of v0, /device:TPU:32, one launch (start us, length us, event | category | flops | bytes accessed | tf_op | source)
XLA Modules:
  0.0 806.4 jit_solution(17973969847977759047)
XLA Ops:
  7.2 0.0 copy-start
  7.2 0.0 all-gather.3.cloned.1.call-start
  7.3 0.8 convert_bitcast_fusion
  8.1 1.0 convert_element_type.50
  9.0 0.1 multiply_cosine_fusion.2
  9.1 0.1 copy.19
  9.2 0.1 copy.20
  9.3 1.0 convert_element_type.58
  10.3 0.3 multiply_cosine_fusion
  10.6 0.4 add_convert_fusion.5
  10.9 0.5 add_convert_fusion
  11.4 0.6 concatenate.13
  12.0 17.4 %all_to_all.72 = bf16[64,12,128]{2,0,1:T(8,128)(2,1)S(1)} all-to-all(bf16[64,12,128]{2,0,1:T(8,128)(2,1)S(1)} %concatenate.13), channel_id=1, replica_groups=mesh['grp'=2,'ctx'=64,'hd'=2] {'hd'}, dimensions={1} | all-to-all | bytes 393216 | tf_op jit(solution)/shard_map/all_to_all | solution.py:38
  29.4 0.7 copy.22
  30.1 0.0 all-gather.3.cloned.1.call-update
  30.1 0.0 all-gather.5.cloned.1.call-start
  30.2 13.2 %all_to_all.73 = bf16[64,12,128]{2,0,1:T(8,128)(2,1)S(1)} all-to-all(bf16[64,12,128]{2,0,1:T(8,128)(2,1)} %param.10), channel_id=1, replica_groups=mesh['grp'=2,'ctx'=64,'hd'=2] {'hd'}, dimensions={1} | all-to-all | bytes 393216 | tf_op jit(solution)/shard_map/all_to_all | solution.py:39
  43.4 0.7 copy.23
  44.1 0.0 all-gather.5.cloned.1.call-update
  44.1 0.5 add_convert_fusion.3
  44.6 1.2 concatenate.11
  45.8 3.4 all-to-all-start
  49.9 0.7 constant_dynamic-slice_fusion
  50.6 9.5 %all-to-all-done = bf16[64,12,128]{2,0,1:T(8,128)(2,1)S(1)} async-done(((bf16[64,12,128]{2,0,1:T(8,128)(2,1)}), bf16[64,12,128]{2,0,1:T(8,128)(2,1)S(1)}, u32[]{:S(2)}, u32[]{:S(2)}) %all-to-all-start) | async-done | bytes 196640 | tf_op jit(solution)/shard_map/all_to_all | solution.py:37
  60.2 0.0 copy-done
  60.2 0.5 fusion.24
  60.7 0.5 fusion.16
  61.2 333.5 %all-gather.3.cloned.1.call-done = bf16[8192,6,128]{2,0,1:T(8,128)(2,1)} async-done(((bf16[128,6,128]{2,0,1:T(8,128)(2,1)}), bf16[8192,6,128]{2,0,1:T(8,128)(2,1)}) %all-gather.3.cloned.1.call-update) | async-done | bytes 12582928 | tf_op jit(solution)/shard_map/all_gather | solution.py:56
  394.6 16.2 %bitcast_reduce_fusion = (f32[132,6]{0,1:T(8,128)S(1)}, f32[6,8192,132]{1,2,0:T(8,128)}) fusion(bf16[8192,6,128]{2,0,1:T(8,128)(2,1)} %all-gather.3.cloned.1.call-done, bf16[4,6,128]{2,0,1:T(4,128)(2,1)S(1)} %constant_dynamic-slice_fusion, bf16[128,6,128]{2,0,1:T(8,128)(2,1)S(1)} %bitcast.55), kind=kOutput, calls=%fused_computation.1 | convolution fusion | flops 1674325248 | bytes 38741088 | tf_op jit(solution)/shard_map/qhd,khd->qhk/dot_general | solution.py:60
  410.9 0.0 copy-start.1
  410.9 11.4 %fusion.1 = f32[132,6]{0,1:T(8,128)S(1)} fusion(f32[6,8192,132]{1,2,0:T(8,128)} %get-tuple-element.36, f32[132,6]{0,1:T(8,128)S(1)} %max.13), kind=kLoop, calls=%fused_computation.3 | loop fusion | flops 19463400 | bytes 25958592 | tf_op jit(solution)/shard_map/reduce_sum | solution.py:65
  422.3 347.6 %all-gather.5.cloned.1.call-done = bf16[8192,6,128]{2,0,1:T(8,128)(2,1)} async-done(((bf16[128,6,128]{2,0,1:T(8,128)(2,1)}), bf16[8192,6,128]{2,0,1:T(8,128)(2,1)}) %all-gather.5.cloned.1.call-update) | async-done | bytes 12582928 | tf_op jit(solution)/shard_map/all_gather | solution.py:57
  769.9 15.2 %fusion.12 = f32[132,6,128]{2,0,1:T(8,128)S(1)} fusion(bf16[8192,6,128]{2,0,1:T(8,128)(2,1)} %all-gather.5.cloned.1.call-done, f32[6,8192,132]{1,2,0:T(8,128)} %get-tuple-element.36, f32[132,6]{0,1:T(8,128)S(1)} %max.13), kind=kOutput, calls=%fused_computation.15 | convolution fusion | flops 1680408576 | bytes 38943840 | tf_op jit(solution)/shard_map/qhk,khd->qhd/dot_general | solution.py:66
  785.1 0.0 copy-done.1
  785.1 0.4 fusion.15
  785.5 0.8 copy.24
  786.4 3.4 all-to-all-start.3
  789.8 0.6 slice.84
  790.4 8.5 %all-to-all-done.3 = bf16[128,6,128]{2,1,0:T(8,128)(2,1)S(1)} async-done(((bf16[128,6,128]{2,1,0:T(8,128)(2,1)}), bf16[128,6,128]{2,1,0:T(8,128)(2,1)S(1)}, u32[]{:S(2)}, u32[]{:S(2)}) %all-to-all-start.3) | async-done | bytes 196640 | tf_op jit(solution)/shard_map/all_to_all | solution.py:76
  798.9 0.7 copy.25
  (7 shorter events, 0.1 us)
Async XLA Ops:
  7.2 53.0 %copy-start = (bf16[256,6,128]{2,0,1:T(8,128)(2,1)S(1)}, bf16[256,6,128]{2,0,1:T(8,128)(2,1)}, u32[]{:S(2)}) copy-start(bf16[256,6,128]{2,0,1:T(8,128)(2,1)} %param.13) | copy-start | bytes 1179652
  7.2 387.5 %all-gather.3.cloned.1.call-start = ((), (), s32[]{:S(2)}) async-start(), calls=%async_computation.4 | async-start | bytes 12779520 | tf_op jit(solution)/shard_map/all_gather | solution.py:56
  30.1 739.8 %all-gather.5.cloned.1.call-start = ((), (), s32[]{:S(2)}) async-start(), calls=%async_computation.5 | async-start | bytes 12779520 | tf_op jit(solution)/shard_map/all_gather | solution.py:57
  45.8 14.4 %all-to-all-start = ((bf16[64,12,128]{2,0,1:T(8,128)(2,1)}), bf16[64,12,128]{2,0,1:T(8,128)(2,1)S(1)}, u32[]{:S(2)}, u32[]{:S(2)}) async-start(bf16[64,12,128]{2,0,1:T(8,128)(2,1)} %concatenate.11), calls=%async_computation | async-start | bytes 393216 | tf_op jit(solution)/shard_map/all_to_all | solution.py:37
  410.9 374.2 %copy-start.1 = (bf16[256,6,128]{2,0,1:T(8,128)(2,1)S(1)}, bf16[256,6,128]{2,0,1:T(8,128)(2,1)}, u32[]{:S(2)}) copy-start(bf16[256,6,128]{2,0,1:T(8,128)(2,1)} %param.14) | copy-start | bytes 1179652
  786.4 12.5 %all-to-all-start.3 = ((bf16[128,6,128]{2,1,0:T(8,128)(2,1)}), bf16[128,6,128]{2,1,0:T(8,128)(2,1)S(1)}, u32[]{:S(2)}, u32[]{:S(2)}) async-start(bf16[128,6,128]{2,1,0:T(8,128)(2,1)} %copy.24), calls=%async_computation.3 | async-start | bytes 524288 | tf_op jit(solution)/shard_map/all_to_all | solution.py:76
Sparse Core Ops, SparseCore 0:
  30.2 364.3 all-gather.2
  397.0 372.8 all-gather.4
where the time goes:
time: 812 us; the launch traced here: 806 us
  waiting for transfers between devices  699 us (86%)
  matrix products  32.3 us (4%)
  blocking collectives  30.6 us (4%)
  other arithmetic  16.4 us (2%)
  between operations  14.8 us (2%)
    all_gather x1, waiting for transfers between devices, local(): lax.all_gather(values_video, 'ctx', axis=0, tiled=True)  348 us
    all_gather x1, waiting for transfers between devices, local(): lax.all_gather(keys_video, 'ctx', axis=0, tiled=True)  333 us
    all_to_all x1, blocking collectives, local(): lax.all_to_all(rotated_k, 'hd', split_axis=1, concat_axis=0, tiled=True)  17.4 us
  transfers between devices with their start and end apart: 4, of which 4 were waited for; matrix products, arithmetic and copies ran while one was open for 4% of the time, Pallas kernels for 0%

commit v1 on v0

v1 whole, which is shorter than its diff:
```python
import functools
import math

import jax
import jax.numpy as jnp
import numpy as np
from jax import lax
from jax.experimental import pallas as pl
from jax.experimental.pallas import tpu as pltpu
from jax.sharding import Mesh
from jax.sharding import PartitionSpec as P

THETA = 256.0
HD = 128
SCALE2 = math.log2(math.e) / math.sqrt(HD)

EVEN = (0, 2, -2, 4)
ODD = (1, -1, 3, -3)
ZAXES = ("grp", "za", "zp", "zb")


def z_index(c, z):
    return ((c * 2 + (z // 2) % 2) * 2 + z % 2) * 2 + z // 4


def moves(z, c):
    return EVEN if z % 2 == c else ODD


def z_perm(m, back):
    pairs = []
    for c in range(2):
        for z in range(8):
            there = z_index(z % 2, (z + moves(z, c)[m]) % 8)
            here = z_index(c, z)
            pairs.append((there, here) if back else (here, there))
    return pairs


GROUP_OF = np.array([[[((z + d) % 8) // 2 for d in moves(z, c)] for c in range(2)] for z in range(8)], np.int32)
MESSAGE_OF = np.argsort(GROUP_OF, axis=-1).astype(np.int32)


def rotary_constants():
    freq = np.zeros((3, HD), np.float32)
    swap = np.zeros((HD, HD), np.float32)
    band_t = HD // 8
    band_h = (HD - band_t) // 2
    offset = 0
    for axis, band in enumerate((band_t, band_h, HD - band_t - band_h)):
        half = band // 2
        f = THETA ** (-2.0 * np.arange(half) / band)
        freq[axis, offset : offset + half] = f
        freq[axis, offset + half : offset + band] = f
        for i in range(half):
            swap[offset + half + i, offset + i] = -1.0
            swap[offset + i, offset + half + i] = 1.0
        offset += band
    return freq, swap


FREQ, SWAP = rotary_constants()


def shift(v, axis, step):
    return lax.ppermute(v, axis, [(i, (i + step) % 4) for i in range(4)])


def other_core(v):
    return lax.ppermute(v, "grp", [(0, 1), (1, 0)])


def z_send(v, m):
    return lax.ppermute(v, ZAXES, z_perm(m, False))


def z_return(v, m):
    return lax.ppermute(v, ZAXES, z_perm(m, True))


QROWS = 272
OWN_TEXT = 256


def attend_body(n_parts, has_text, has_carry, keys_step, *refs):
    refs = list(refs)
    count_ref = refs.pop(0) if has_text else None
    q_own, q_other = refs[:2]
    parts = refs[2 : 2 + n_parts]
    refs = refs[2 + n_parts :]
    text = refs.pop(0) if has_text else None
    carry = refs.pop(0) if has_carry else None
    out = refs.pop(0)
    nt = (((1,), (1,)), ((), ()))
    blocks = []
    for part in parts:
        pieces = part.shape[0]
        for i in range(0, pieces, keys_step):
            blocks.append((part, i, min(keys_step, pieces - i)))
    for tile, q_ref in enumerate((q_own, q_other)):
        q = q_ref[0]
        if has_carry:
            acc, top, total = carry[tile, 0, 0], carry[tile, 1, 0][:, :1], carry[tile, 1, 0][:, 64:65]
        else:
            acc = top = total = None

        def update(s, v, acc, top, total):
            peak = jnp.max(s, axis=1, keepdims=True)
            if top is None:
                new = peak
            else:
                new = jnp.maximum(top, peak)
            p = jnp.exp2(s - new)
            add = jnp.sum(p, axis=1, keepdims=True)
            mixed = jnp.dot(p.astype(jnp.bfloat16), v, preferred_element_type=jnp.float32)
            if top is None:
                return mixed, new, add
            alpha = jnp.exp2(top - new)
            return acc * alpha + mixed, new, total * alpha + add

        for part, i, n in blocks:
            k = part[i : i + n, 0, 0].reshape(n * part.shape[3], HD)
            v = part[i : i + n, 1, 0].reshape(n * part.shape[3], HD)
            s = lax.dot_general(q, k, nt, preferred_element_type=jnp.float32) * SCALE2
            acc, top, total = update(s, v, acc, top, total)
        if has_text:
            k, v = text[0, :128], text[0, 128:256]
            s = lax.dot_general(q, k, nt, preferred_element_type=jnp.float32) * SCALE2
            live = lax.broadcasted_iota(jnp.int32, s.shape, 1) < count_ref[0]
            s = jnp.where(live, s, -jnp.inf)
            acc, top, total = update(s, v, acc, top, total)
        out[tile, 0, 0] = acc
        lane = lax.broadcasted_iota(jnp.int32, acc.shape, 1)
        out[tile, 1, 0] = jnp.where(lane < 64, top, total)


def attend(q_own, q_other, parts, text=None, count=None, carry=None, keys_step=4):
    has_text, has_carry = text is not None, carry is not None
    q_spec = pl.BlockSpec((1, QROWS, HD), lambda h, *_: (h, 0, 0))
    state_spec = pl.BlockSpec((2, 2, 1, QROWS, HD), lambda h, *_: (0, 0, h, 0, 0))
    in_specs, args = [q_spec, q_spec], [q_own, q_other]
    keys = 0
    for part in parts:
        in_specs.append(pl.BlockSpec((part.shape[0], 2, 1) + part.shape[3:], lambda h, *_: (0, 0, h, 0, 0)))
        args.append(part)
        keys += part.shape[0] * part.shape[3]
    if has_text:
        in_specs.append(pl.BlockSpec((1, text.shape[1], HD), lambda h, *_: (h, 0, 0)))
        args.append(text)
        keys += 128
    if has_carry:
        in_specs.append(state_spec)
        args.append(carry)
    flops = 4 * 3 * 2 * QROWS * keys * HD
    return pl.pallas_call(
        functools.partial(attend_body, len(parts), has_text, has_carry, keys_step),
        out_shape=jax.ShapeDtypeStruct((2, 2, 3, QROWS, HD), jnp.float32),
        grid_spec=pltpu.PrefetchScalarGridSpec(
            num_scalar_prefetch=1 if has_text else 0,
            grid=(3,),
            in_specs=in_specs,
            out_specs=state_spec,
        ),
        compiler_params=pltpu.CompilerParams(vmem_limit_bytes=40 * 1024 * 1024),
        cost_estimate=pl.CostEstimate(
            flops=flops, bytes_accessed=keys * 3 * 512 + 3400000, transcendentals=3 * 2 * QROWS * keys
        ),
        name="attend",
    )(*(([count] if has_text else []) + args))


def merge_body(mine, theirs, out):
    top1, top2 = mine[0, 1, 0][:, :1], theirs[1, 0][:, :1]
    total1, total2 = mine[0, 1, 0][:, 64:65], theirs[1, 0][:, 64:65]
    top = jnp.maximum(top1, top2)
    w1, w2 = jnp.exp2(top1 - top), jnp.exp2(top2 - top)
    inv = 1.0 / (total1 * w1 + total2 * w2)
    o = (mine[0, 0, 0] * (w1 * inv) + theirs[0, 0] * (w2 * inv)).astype(jnp.bfloat16)
    for m in range(4):
        out[m, 0, :64] = o[m * 64 : (m + 1) * 64]
        out[m, 0, 64:80] = o[OWN_TEXT : OWN_TEXT + 16]


def merge(mine, theirs):
    return pl.pallas_call(
        merge_body,
        out_shape=jax.ShapeDtypeStruct((4, 3, 80, HD), jnp.bfloat16),
        grid=(3,),
        in_specs=[
            pl.BlockSpec((1, 2, 1, QROWS, HD), lambda h: (0, 0, h, 0, 0)),
            pl.BlockSpec((2, 1, QROWS, HD), lambda h: (0, h, 0, 0)),
        ],
        out_specs=pl.BlockSpec((4, 1, 80, HD), lambda h: (0, h, 0, 0)),
        name="merge",
    )(mine, theirs)


def spread(block, first, second):
    right = shift(block, first, 1)
    left = shift(block, first, -1)
    far = jnp.stack([shift(right[0], first, 1), shift(left[1], first, -1)])
    line = jnp.stack([block, right, left, far])
    right2 = shift(line, second, 1)
    left2 = shift(line, second, -1)
    far_a = shift(right2[:2], second, 1)
    far_b = shift(left2[2:], second, -1)
    return line, right2, left2, far_a, far_b


def local(video_q, video_k, video_v, positions, text_q, text_k, text_v, text_count):
    core = lax.axis_index("grp")
    zb, za, zp = lax.axis_index("zb"), lax.axis_index("za"), lax.axis_index("zp")
    z = zb * 4 + za * 2 + zp
    group_of = jnp.asarray(GROUP_OF)[z, core]
    message_of = jnp.asarray(MESSAGE_OF)[z, core]

    angles = jnp.sum(positions.astype(jnp.float32)[:, :, None] * FREQ[:, None, :], axis=0)
    cos, sin = jnp.cos(angles), jnp.sin(angles)

    def rotate(x):
        x = jnp.transpose(x, (1, 0, 2))
        swapped = jnp.einsum("htd,de->hte", x, jnp.asarray(SWAP, jnp.bfloat16), preferred_element_type=jnp.float32)
        return (x.astype(jnp.float32) * cos + swapped * sin).astype(jnp.bfloat16)

    k = rotate(video_k).reshape(4, 3, 64, HD)
    v = jnp.transpose(video_v, (1, 0, 2)).reshape(4, 3, 64, HD)
    q = rotate(video_q).reshape(4, 3, 64, HD)
    kv = jnp.stack([k, v], axis=1)
    pick = lambda a, m: lax.dynamic_index_in_dim(a, group_of[m], 0, keepdims=False)
    kv_in = [z_send(pick(kv, m), m) for m in range(4)]
    q_in = [z_send(pick(q, m), m) for m in range(4)]

    half = zp
    heads = lambda a: lax.dynamic_slice_in_dim(a, za * 3, 3, 1)
    x, y = lax.axis_index("x"), lax.axis_index("y")

    def text_for(c):
        tk = lax.dynamic_slice_in_dim(heads(text_k), c * 128, 128, 0)
        tv = lax.dynamic_slice_in_dim(heads(text_v), c * 128, 128, 0)
        rows = [
            lax.dynamic_slice_in_dim(heads(text_q), (x * 16 + (c + 2 * t) * 4 + y) * 4, 4, 0) for t in range(2)
        ]
        block = jnp.concatenate([tk, tv] + rows + [jnp.zeros((8, 3, HD), jnp.bfloat16)], axis=0)
        return jnp.transpose(block, (1, 0, 2))

    text = jnp.where(core == half, text_for(core), other_core(text_for(1 - core)))
    count = jnp.clip(text_count - core * 128, 0, 128)

    q_own = jnp.concatenate(q_in + [text[:, 256:272]], axis=1)
    q_other = other_core(q_own)

    first = jnp.concatenate(kv_in[:2], axis=2)
    second = jnp.concatenate(kv_in[2:], axis=2)
    line_a, right_a, left_a, far_a0, far_a1 = spread(first, "x", "y")
    line_b, right_b, left_b, far_b0, far_b1 = spread(second, "y", "x")
    state = attend(q_own, q_other, [line_a, line_b], text=text, count=count)
    state = attend(q_own, q_other, [right_a, left_a, right_b, left_b], carry=state)
    state = attend(q_own, q_other, [far_a0, far_a1, far_b0, far_b1], carry=state)

    theirs = other_core(state[1])
    done = merge(state, theirs)
    back = jnp.stack([z_return(done[m], m) for m in range(4)])
    ordered = jnp.stack([lax.dynamic_index_in_dim(back, message_of[j], 0, keepdims=False) for j in range(4)])
    video_out = jnp.transpose(ordered[:, :, :64].reshape(12, 64, HD), (1, 0, 2))
    texts = lax.dynamic_slice(ordered, (zb * 2, 0, 64 + za * 4, 0), (2, 3, 4, HD))
    text_out = jnp.transpose(texts.reshape(6, 4, HD), (1, 0, 2))
    return video_out, text_out


def solution(mesh):
    fine = Mesh(mesh.devices.reshape(2, 4, 2, 2, 4, 2), ("grp", "x", "za", "zp", "y", "zb"))
    ctx = ("x", "za", "zp", "y")
    tokens = P(ctx + ("zb",), "grp", None)
    text = P(None, ("grp", "zb"), None)
    return jax.shard_map(
        local,
        mesh=fine,
        in_specs=(tokens, tokens, tokens, P(None, ctx + ("zb",)), text, text, text, P()),
        out_specs=(tokens, P(ctx, ("grp", "zb"), None)),
        check_vma=False,
    )
```

time: 812 us -> 142 us (0.17)
  waiting for transfers between devices: 699 us -> 22.6 us
  starting transfers between devices: 6.95 us -> 59.2 us
  blocking collectives: 30.6 us -> 0 us
  matrix products: 32.3 us -> 2.47 us
  Pallas kernels: 0 us -> 29.4 us
  other arithmetic: 16.4 us -> 2.72 us
    all_gather x2 -> x0, waiting for transfers between devices: 681 us -> none  [the longest x1 348 us: local(): lax.all_gather(values_video, 'ctx', axis=0, tiled=True)]
    ppermute x0 -> x31, starting transfers between devices: none -> 59.2 us  [the longest x16 29.5 us: shift(): return lax.ppermute(v, axis, [(i, (i + step) % 4) for i in range(4)])]
    all_to_all x2 -> x0, blocking collectives: 30.6 us -> none  [the longest x1 17.4 us: local(): lax.all_to_all(rotated_k, 'hd', split_axis=1, concat_axis=0, tiled=True)]
    dot_general x4 -> x2, matrix products: 32.3 us -> 2.47 us  [rotate(): jnp.einsum('htd,de->hte', x, jnp.asarray(SWAP, jnp.bfloat16), preferred_e...]
    pallas_call x0 -> x4, Pallas kernels: none -> 29.4 us  [the longest x3 25.9 us: attend(): pl.pallas_call(functools.partial(attend_body, len(parts), has_text, has_c...]
    ppermute x0 -> x31, waiting for transfers between devices: none -> 22.6 us  [the longest x16 17.7 us: shift(): return lax.ppermute(v, axis, [(i, (i + step) % 4) for i in range(4)])]
    all_to_all x2 -> x0, waiting for transfers between devices: 18 us -> none  [the longest x1 9.55 us: local(): lax.all_to_all(rotated_q, 'hd', split_axis=1, concat_axis=0, tiled=True)]
    reduce_sum x2 -> x1, other arithmetic: 11.9 us -> 0.77 us  [local(): jnp.sum(positions.astype(jnp.float32)[:, :, None] * FREQ[:, None, :], axi...]
  transfers between devices with their start and end apart: 4 -> 31, of which waited for: 4 -> 10; matrix products, arithmetic and copies ran while one was open for 4% -> 3% of each run, Pallas kernels for 0% -> 11%
where the time goes in v1:
time: 142 us; the launch traced here: 141 us
  starting transfers between devices  59.2 us (42%)
  Pallas kernels  29.4 us (21%)
  waiting for transfers between devices  22.6 us (16%)
  between operations  16.8 us (12%)
  local copies, waits for them, and re-layouts  7.44 us (5%)
  other arithmetic  2.72 us (2%)
  matrix products  2.47 us (2%)
    ppermute x16, starting transfers between devices, shift(): return lax.ppermute(v, axis, [(i, (i + step) % 4) for i in range(4)])  29.5 us
    pallas_call x3, Pallas kernels, attend(): pl.pallas_call(functools.partial(attend_body, len(parts), has_text, has_c...  25.9 us
    ppermute x8, starting transfers between devices, z_send(): return lax.ppermute(v, ZAXES, z_perm(m, False))  20.8 us
    ppermute x16, waiting for transfers between devices, shift(): return lax.ppermute(v, axis, [(i, (i + step) % 4) for i in range(4)])  17.7 us
    ppermute x4, starting transfers between devices, z_return(): return lax.ppermute(v, ZAXES, z_perm(m, True))  8.49 us
    pallas_call x1, Pallas kernels, merge(): pl.pallas_call(merge_body, out_shape=jax.ShapeDtypeStruct((4, 3, 80, HD),...  3.43 us
    ppermute x3, waiting for transfers between devices, other_core(): return lax.ppermute(v, 'grp', [(0, 1), (1, 0)])  3.03 us
  transfers between devices with their start and end apart: 31, of which 10 were waited for; matrix products, arithmetic and copies ran while one was open for 3% of the time, Pallas kernels for 11%

profile of v1, /device:TPU:32, one launch (start us, length us, event | category | flops | bytes accessed | tf_op | source)
XLA Modules:
  0.0 140.6 jit_solution(6643959189334108588)
XLA Ops:
  0.7 0.8 constant_dynamic-slice_fusion.14
  7.1 0.7 convert_element_type.16
  7.7 0.8 multiply_reduce_fusion
  11.2 1.2 fusion.4
  12.4 0.9 fusion.9
  13.3 5.4 %collective-permute-start.16 = (bf16[2,3,64,128]{3,2,1,0:T(8,128)(2,1)S(1)}, bf16[2,3,64,128]{3,2,1,0:T(8,128)(2,1)S(1)}, u32[]{:S(2)}, u32[]{:S(2)}) collective-permute-start(bf16[2,3,64,128]{3,2,1,0:T(8,128)(2,1)S(1)} %get-tuple-element.5), channel_id=1, source_target_pairs={{0,17},{8,129},{16,0},{24,145},{1,16},{9,128},{17,1},{25,144},{128... | collective-permute-start | bytes 294920 | tf_op jit(solution)/shard_map/ppermute | solution.py:74
  18.8 3.2 %collective-permute-start.6 = (bf16[2,3,64,128]{3,2,1,0:T(8,128)(2,1)S(1)}, bf16[2,3,64,128]{3,2,1,0:T(8,128)(2,1)S(1)}, u32[]{:S(2)}, u32[]{:S(2)}) collective-permute-start(bf16[2,3,64,128]{3,2,1,0:T(8,128)(2,1)S(1)} %get-tuple-element.3), channel_id=1, source_target_pairs={{0,0},{8,144},{16,16},{24,129},{1,1},{9,145},{17,17},{25,128},{128... | collective-permute-start | bytes 294920 | tf_op jit(solution)/shard_map/ppermute | solution.py:74
  22.5 1.2 fusion.5
  23.8 3.2 %collective-permute-start = (bf16[3,64,128]{2,1,0:T(8,128)(2,1)S(1)}, bf16[3,64,128]{2,1,0:T(8,128)(2,1)S(1)}, u32[]{:S(2)}, u32[]{:S(2)}) collective-permute-start(bf16[3,64,128]{2,1,0:T(8,128)(2,1)S(1)} %get-tuple-element.25), channel_id=1, source_target_pairs={{0,0},{8,144},{16,16},{24,129},{1,1},{9,145},{17,17},{25,128},{128... | collective-permute-start | bytes 147464 | tf_op jit(solution)/shard_map/ppermute | solution.py:74
  27.2 0.8 constant_dynamic-slice_fusion.10
  28.2 1.8 %collective-permute-done = bf16[3,64,128]{2,1,0:T(8,128)(2,1)S(1)} collective-permute-done((bf16[3,64,128]{2,1,0:T(8,128)(2,1)S(1)}, bf16[3,64,128]{2,1,0:T(8,128)(2,1)S(1)}, u32[]{:S(2)}, u32[]{:S(2)}) %collective-permute-start) | collective-permute-done | bytes 49184 | tf_op jit(solution)/shard_map/ppermute | solution.py:74
  30.0 3.5 %collective-permute-start.1 = (bf16[3,64,128]{2,1,0:T(8,128)(2,1)S(1)}, bf16[3,64,128]{2,1,0:T(8,128)(2,1)S(1)}, u32[]{:S(2)}, u32[]{:S(2)}) collective-permute-start(bf16[3,64,128]{2,1,0:T(8,128)(2,1)S(1)} %get-tuple-element.24), channel_id=1, source_target_pairs={{0,16},{8,128},{16,1},{24,144},{1,17},{9,129},{17,0},{25,145},{128... | collective-permute-start | bytes 147464 | tf_op jit(solution)/shard_map/ppermute | solution.py:74
  33.5 2.9 %collective-permute-start.2 = (bf16[3,64,128]{2,1,0:T(8,128)(2,1)S(1)}, bf16[3,64,128]{2,1,0:T(8,128)(2,1)S(1)}, u32[]{:S(2)}, u32[]{:S(2)}) collective-permute-start(bf16[3,64,128]{2,1,0:T(8,128)(2,1)S(1)} %get-tuple-element.23), channel_id=1, source_target_pairs={{0,17},{8,129},{16,0},{24,145},{1,16},{9,128},{17,1},{25,144},{128... | collective-permute-start | bytes 147464 | tf_op jit(solution)/shard_map/ppermute | solution.py:74
  36.4 2.0 %collective-permute-start.3 = (bf16[3,64,128]{2,1,0:T(8,128)(2,1)S(1)}, bf16[3,64,128]{2,1,0:T(8,128)(2,1)S(1)}, u32[]{:S(2)}, u32[]{:S(2)}) collective-permute-start(bf16[3,64,128]{2,1,0:T(8,128)(2,1)S(1)} %get-tuple-element.22), channel_id=1, source_target_pairs={{0,1},{8,145},{16,17},{24,128},{1,0},{9,144},{17,16},{25,129},{128... | collective-permute-start | bytes 147464 | tf_op jit(solution)/shard_map/ppermute | solution.py:74
  38.5 1.7 %collective-permute-start.18 = (bf16[2,3,128,128]{3,2,1,0:T(8,128)(2,1)S(1)}, bf16[2,3,128,128]{3,2,1,0:T(8,128)(2,1)S(1)}, u32[]{:S(2)}, u32[]{:S(2)}) collective-permute-start(bf16[2,3,128,128]{3,2,1,0:T(8,128)(2,1)S(1)} %constant_dynamic-update-slice_fusion.7), channel_id=1, source_target_pairs={{0,2},{2,4},{4,6},{6,0},{1,3},{3,5},{5,7},{7,1},{8,10},{10,12},{12... | collective-permute-start | bytes 589832 | tf_op jit(solution)/shard_map/ppermute | solution.py:66
  40.1 1.7 %collective-permute-start.19 = (bf16[2,3,128,128]{3,2,1,0:T(8,128)(2,1)S(1)}, bf16[2,3,128,128]{3,2,1,0:T(8,128)(2,1)S(1)}, u32[]{:S(2)}, u32[]{:S(2)}) collective-permute-start(bf16[2,3,128,128]{3,2,1,0:T(8,128)(2,1)S(1)} %constant_dynamic-update-slice_fusion.7), channel_id=1, source_target_pairs={{0,6},{2,0},{4,2},{6,4},{1,7},{3,1},{5,3},{7,5},{8,14},{10,8},{12,... | collective-permute-start | bytes 589832 | tf_op jit(solution)/shard_map/ppermute | solution.py:66
  41.9 3.5 %collective-permute-done.18 = bf16[2,3,128,128]{3,2,1,0:T(8,128)(2,1)S(1)} collective-permute-done((bf16[2,3,128,128]{3,2,1,0:T(8,128)(2,1)S(1)}, bf16[2,3,128,128]{3,2,1,0:T(8,128)(2,1)S(1)}, u32[]{:S(2)}, u32[]{:S(2)}) %collective-permute-start.18) | collective-permute-done | bytes 196640 | tf_op jit(solution)/shard_map/ppermute | solution.py:66
  45.4 1.5 %collective-permute-start.8 = (bf16[2,3,128,128]{3,2,1,0:T(8,128)(2,1)S(1)}, bf16[2,3,128,128]{3,2,1,0:T(8,128)(2,1)S(1)}, u32[]{:S(2)}, u32[]{:S(2)}) collective-permute-start(bf16[2,3,128,128]{3,2,1,0:T(8,128)(2,1)S(1)} %constant_dynamic-update-slice_fusion.5), channel_id=1, source_target_pairs={{0,32},{32,64},{64,96},{96,0},{1,33},{33,65},{65,97},{97,1},{2,34}... | collective-permute-start | bytes 589832 | tf_op jit(solution)/shard_map/ppermute | solution.py:66
  46.9 1.8 %collective-permute-start.9 = (bf16[2,3,128,128]{3,2,1,0:T(8,128)(2,1)S(1)}, bf16[2,3,128,128]{3,2,1,0:T(8,128)(2,1)S(1)}, u32[]{:S(2)}, u32[]{:S(2)}) collective-permute-start(bf16[2,3,128,128]{3,2,1,0:T(8,128)(2,1)S(1)} %constant_dynamic-update-slice_fusion.5), channel_id=1, source_target_pairs={{0,96},{32,0},{64,32},{96,64},{1,97},{33,1},{65,33},{97,65},{2,98}... | collective-permute-start | bytes 589832 | tf_op jit(solution)/shard_map/ppermute | solution.py:66
  48.7 3.9 %collective-permute-done.8 = bf16[2,3,128,128]{3,2,1,0:T(8,128)(2,1)S(1)} collective-permute-done((bf16[2,3,128,128]{3,2,1,0:T(8,128)(2,1)S(1)}, bf16[2,3,128,128]{3,2,1,0:T(8,128)(2,1)S(1)}, u32[]{:S(2)}, u32[]{:S(2)}) %collective-permute-start.8) | collective-permute-done | bytes 196640 | tf_op jit(solution)/shard_map/ppermute | solution.py:66
  52.6 1.2 collective-permute-start.20
  53.9 2.3 %collective-permute-start.21 = (bf16[3,128,128]{2,1,0:T(8,128)(2,1)S(1)}, bf16[3,128,128]{2,1,0:T(8,128)(2,1)S(1)}, u32[]{:S(2)}, u32[]{:S(2)}) collective-permute-start(bf16[3,128,128]{2,1,0:T(8,128)(2,1)S(1)} %slice_bitcast_fusion.1), channel_id=1, source_target_pairs={{0,6},{2,0},{4,2},{6,4},{1,7},{3,1},{5,3},{7,5},{8,14},{10,8},{12,... | collective-permute-start | bytes 294920 | tf_op jit(solution)/shard_map/ppermute | solution.py:66
  56.2 2.3 %collective-permute-done.20 = bf16[3,128,128]{2,1,0:T(8,128)(2,1)S(1)} collective-permute-done((bf16[3,128,128]{2,1,0:T(8,128)(2,1)S(1)}, bf16[3,128,128]{2,1,0:T(8,128)(2,1)S(1)}, u32[]{:S(2)}, u32[]{:S(2)}) %collective-permute-start.20) | collective-permute-done | bytes 98336 | tf_op jit(solution)/shard_map/ppermute | solution.py:66
  58.5 1.6 %collective-permute-start.10 = (bf16[3,128,128]{2,1,0:T(8,128)(2,1)S(1)}, bf16[3,128,128]{2,1,0:T(8,128)(2,1)S(1)}, u32[]{:S(2)}, u32[]{:S(2)}) collective-permute-start(bf16[3,128,128]{2,1,0:T(8,128)(2,1)S(1)} %slice_bitcast_fusion.4), channel_id=1, source_target_pairs={{0,32},{32,64},{64,96},{96,0},{1,33},{33,65},{65,97},{97,1},{2,34}... | collective-permute-start | bytes 294920 | tf_op jit(solution)/shard_map/ppermute | solution.py:66
  60.0 2.2 %collective-permute-start.11 = (bf16[3,128,128]{2,1,0:T(8,128)(2,1)S(1)}, bf16[3,128,128]{2,1,0:T(8,128)(2,1)S(1)}, u32[]{:S(2)}, u32[]{:S(2)}) collective-permute-start(bf16[3,128,128]{2,1,0:T(8,128)(2,1)S(1)} %slice_bitcast_fusion.3), channel_id=1, source_target_pairs={{0,96},{32,0},{64,32},{96,64},{1,97},{33,1},{65,33},{97,65},{2,98}... | collective-permute-start | bytes 294920 | tf_op jit(solution)/shard_map/ppermute | solution.py:66
  62.3 3.1 %collective-permute-done.10 = bf16[3,128,128]{2,1,0:T(8,128)(2,1)S(1)} collective-permute-done((bf16[3,128,128]{2,1,0:T(8,128)(2,1)S(1)}, bf16[3,128,128]{2,1,0:T(8,128)(2,1)S(1)}, u32[]{:S(2)}, u32[]{:S(2)}) %collective-permute-start.10) | collective-permute-done | bytes 98336 | tf_op jit(solution)/shard_map/ppermute | solution.py:66
  65.5 3.6 %collective-permute-start.24 = (bf16[4,2,3,128,128]{4,3,2,1,0:T(8,128)(2,1)S(1)}, bf16[4,2,3,128,128]{4,3,2,1,0:T(8,128)(2,1)S(1)}, u32[]{:S(2)}, u32[]{:S(2)}) collective-permute-start(bf16[4,2,3,128,128]{4,3,2,1,0:T(8,128)(2,1)S(1)} %pad_maximum_fusion.1.refs_4_), channel_id=1, source_target_pairs={{0,96},{32,0},{64,32},{96,64},{1,97},{33,1},{65,33},{97,65},{2,98}... | collective-permute-start | bytes 2359304 | tf_op jit(solution)/shard_map/ppermute | solution.py:66
  69.3 1.6 %collective-permute-start.12 = (bf16[4,2,3,128,128]{4,3,2,1,0:T(8,128)(2,1)S(1)}, bf16[4,2,3,128,128]{4,3,2,1,0:T(8,128)(2,1)S(1)}, u32[]{:S(2)}, u32[]{:S(2)}) collective-permute-start(bf16[4,2,3,128,128]{4,3,2,1,0:T(8,128)(2,1)S(1)} %pad_maximum_fusion.refs_3_), channel_id=1, source_target_pairs={{0,2},{2,4},{4,6},{6,0},{1,3},{3,5},{5,7},{7,1},{8,10},{10,12},{12... | collective-permute-start | bytes 2359304 | tf_op jit(solution)/shard_map/ppermute | solution.py:66
  70.8 2.0 %collective-permute-start.14 = (bf16[4,2,3,128,128]{4,3,2,1,0:T(8,128)(2,1)S(1)}, bf16[4,2,3,128,128]{4,3,2,1,0:T(8,128)(2,1)S(1)}, u32[]{:S(2)}, u32[]{:S(2)}) collective-permute-start(bf16[4,2,3,128,128]{4,3,2,1,0:T(8,128)(2,1)S(1)} %pad_maximum_fusion.refs_3_), channel_id=1, source_target_pairs={{0,6},{2,0},{4,2},{6,4},{1,7},{3,1},{5,3},{7,5},{8,14},{10,8},{12,... | collective-permute-start | bytes 2359304 | tf_op jit(solution)/shard_map/ppermute | solution.py:66
  73.0 1.4 %collective-permute-done.4 = bf16[3,272,128]{2,1,0:T(8,128)(2,1)S(1)} collective-permute-done((bf16[3,272,128]{2,1,0:T(8,128)(2,1)S(1)}, bf16[3,272,128]{2,1,0:T(8,128)(2,1)S(1)}, u32[]{:S(2)}, u32[]{:S(2)}) %collective-permute-start.4) | collective-permute-done | bytes 208928 | tf_op jit(solution)/shard_map/ppermute | solution.py:70
  74.7 3.9 %collective-permute-done.22.refs_4_ = bf16[4,2,3,128,128]{4,3,2,1,0:T(8,128)(2,1)S(1)} collective-permute-done((bf16[4,2,3,128,128]{4,3,2,1,0:T(8,128)(2,1)S(1)}, bf16[4,2,3,128,128]{4,3,2,1,0:T(8,128)(2,1)S(1)}, u32[]{:S(2)}, u32[]{:S(2)}) %collective-permute-start.22) | collective-permute-done | bytes 786464 | tf_op jit(solution)/shard_map/ppermute | solution.py:66
  78.9 3.8 %collective-permute-start.25 = (bf16[2,2,3,128,128]{4,3,2,1,0:T(8,128)(2,1)S(1)}, bf16[2,2,3,128,128]{4,3,2,1,0:T(8,128)(2,1)S(1)}, u32[]{:S(2)}, u32[]{:S(2)}) collective-permute-start(bf16[2,2,3,128,128]{4,3,2,1,0:T(8,128)(2,1)S(1)} %slice.112), channel_id=1, source_target_pairs={{0,96},{32,0},{64,32},{96,64},{1,97},{33,1},{65,33},{97,65},{2,98}... | collective-permute-start | bytes 1179656 | tf_op jit(solution)/shard_map/ppermute | solution.py:66
  82.7 0.9 collective-permute-done.12.refs_2_
  83.5 2.2 %collective-permute-start.13 = (bf16[2,2,3,128,128]{4,3,2,1,0:T(8,128)(2,1)S(1)}, bf16[2,2,3,128,128]{4,3,2,1,0:T(8,128)(2,1)S(1)}, u32[]{:S(2)}, u32[]{:S(2)}) collective-permute-start(bf16[2,2,3,128,128]{4,3,2,1,0:T(8,128)(2,1)S(1)} %slice.107), channel_id=1, source_target_pairs={{0,2},{2,4},{4,6},{6,0},{1,3},{3,5},{5,7},{7,1},{8,10},{10,12},{12... | collective-permute-start | bytes 1179656 | tf_op jit(solution)/shard_map/ppermute | solution.py:66
  85.8 2.2 %collective-permute-start.15 = (bf16[2,2,3,128,128]{4,3,2,1,0:T(8,128)(2,1)S(1)}, bf16[2,2,3,128,128]{4,3,2,1,0:T(8,128)(2,1)S(1)}, u32[]{:S(2)}, u32[]{:S(2)}) collective-permute-start(bf16[2,2,3,128,128]{4,3,2,1,0:T(8,128)(2,1)S(1)} %slice.108), channel_id=1, source_target_pairs={{0,6},{2,0},{4,2},{6,4},{1,7},{3,1},{5,3},{7,5},{8,14},{10,8},{12,... | collective-permute-start | bytes 1179656 | tf_op jit(solution)/shard_map/ppermute | solution.py:66
  88.7 5.1 %attend.3.refs_6_ = f32[2,2,3,272,128]{4,3,2,1,0:T(8,128)S(1)} custom-call(s32[1]{0:T(128)S(6)} %min.6.refs_0_, bf16[3,272,128]{2,1,0:T(8,128)(2,1)S(1)} %constant_dynamic-update-slice_fusion.refs_1_.refs_0_, bf16[3,272,128]{2,1,0:T(8,128)(2,1)S(1)} %collective-permute-done.5.refs_2_.refs_1_, bf16[4,2,3,128,128]{4,3,2,1,0:T(8,128)(2,1)S(1)} %pad_maximum_fusion.refs_3_, ...), custom_call_target="tpu_custom_call" | custom-call | flops 962592768 | bytes 5169472 | tf_op jit(solution)/shard_map/attend/pallas_call | solution.py:155
  93.8 10.3 %attend.4.refs_6_ = f32[2,2,3,272,128]{4,3,2,1,0:T(8,128)S(1)} custom-call(bf16[3,272,128]{2,1,0:T(8,128)(2,1)S(1)} %constant_dynamic-update-slice_fusion.refs_1_.refs_0_, bf16[3,272,128]{2,1,0:T(8,128)(2,1)S(1)} %collective-permute-done.5.refs_2_.refs_1_, bf16[4,2,3,128,128]{4,3,2,1,0:T(8,128)(2,1)S(1)} %collective-permute-done.12.refs_2_, ...), custom_call_target="tpu_custom_call" | custom-call | flops 1711276032 | bytes 6545728 | tf_op jit(solution)/shard_map/attend/pallas_call | solution.py:155
  104.2 10.5 %attend.5.mine = f32[2,2,3,272,128]{4,3,2,1,0:T(8,128)S(1)} custom-call(bf16[3,272,128]{2,1,0:T(8,128)(2,1)S(1)} %constant_dynamic-update-slice_fusion.refs_1_.refs_0_, bf16[3,272,128]{2,1,0:T(8,128)(2,1)S(1)} %collective-permute-done.5.refs_2_.refs_1_, bf16[2,2,3,128,128]{4,3,2,1,0:T(8,128)(2,1)S(1)} %collective-permute-done.13.refs_2_, ...), custom_call_target="tpu_custom_call" | custom-call | flops 855638016 | bytes 4972864 | tf_op jit(solution)/shard_map/attend/pallas_call | solution.py:155
  114.8 0.7 constant_dynamic-slice_fusion.5
  115.6 1.6 %collective-permute-done.26.theirs = f32[2,3,272,128]{3,2,1,0:T(8,128)S(1)} collective-permute-done((f32[2,3,272,128]{3,2,1,0:T(8,128)S(1)}, f32[2,3,272,128]{3,2,1,0:T(8,128)S(1)}, u32[]{:S(2)}, u32[]{:S(2)}) %collective-permute-start.26) | collective-permute-done | bytes 835616 | tf_op jit(solution)/shard_map/ppermute | solution.py:70
  117.2 0.9 copy-done.1
  118.1 3.4 %merge.1 = bf16[4,3,80,128]{3,2,1,0:T(8,128)(2,1)} custom-call(f32[2,2,3,272,128]{4,3,2,1,0:T(8,128)} %copy-done, f32[2,3,272,128]{3,2,1,0:T(8,128)} %copy-done.1), custom_call_target="tpu_custom_call" | custom-call | tf_op jit(solution)/shard_map/merge/pallas_call | solution.py:185
  121.5 0.9 slice_bitcast_fusion.8
  122.5 1.9 %collective-permute-start.27 = (bf16[3,80,128]{2,1,0:T(8,128)(2,1)S(1)}, bf16[3,80,128]{2,1,0:T(8,128)(2,1)S(1)}, u32[]{:S(2)}, u32[]{:S(2)}) collective-permute-start(bf16[3,80,128]{2,1,0:T(8,128)(2,1)S(1)} %get-tuple-element.18), channel_id=1, source_target_pairs={{0,0},{144,8},{16,16},{129,24},{1,1},{145,9},{17,17},{128,25},{8,1... | collective-permute-start | bytes 184328 | tf_op jit(solution)/shard_map/ppermute | solution.py:78
  124.4 1.8 %collective-permute-start.28 = (bf16[3,80,128]{2,1,0:T(8,128)(2,1)S(1)}, bf16[3,80,128]{2,1,0:T(8,128)(2,1)S(1)}, u32[]{:S(2)}, u32[]{:S(2)}) collective-permute-start(bf16[3,80,128]{2,1,0:T(8,128)(2,1)S(1)} %get-tuple-element.21), channel_id=1, source_target_pairs={{16,0},{128,8},{1,16},{144,24},{17,1},{129,9},{0,17},{145,25},{25,... | collective-permute-start | bytes 184328 | tf_op jit(solution)/shard_map/ppermute | solution.py:78
  126.2 2.7 %collective-permute-start.29 = (bf16[3,80,128]{2,1,0:T(8,128)(2,1)S(1)}, bf16[3,80,128]{2,1,0:T(8,128)(2,1)S(1)}, u32[]{:S(2)}, u32[]{:S(2)}) collective-permute-start(bf16[3,80,128]{2,1,0:T(8,128)(2,1)S(1)} %get-tuple-element.20), channel_id=1, source_target_pairs={{17,0},{129,8},{0,16},{145,24},{16,1},{128,9},{1,17},{144,25},{24,... | collective-permute-start | bytes 184328 | tf_op jit(solution)/shard_map/ppermute | solution.py:78
  128.9 2.0 %collective-permute-start.30 = (bf16[3,80,128]{2,1,0:T(8,128)(2,1)S(1)}, bf16[3,80,128]{2,1,0:T(8,128)(2,1)S(1)}, u32[]{:S(2)}, u32[]{:S(2)}) collective-permute-start(bf16[3,80,128]{2,1,0:T(8,128)(2,1)S(1)} %get-tuple-element.19), channel_id=1, source_target_pairs={{1,0},{145,8},{17,16},{128,24},{0,1},{144,9},{16,17},{129,25},{9,1... | collective-permute-start | bytes 184328 | tf_op jit(solution)/shard_map/ppermute | solution.py:78
  139.3 0.7 slice.118
  (71 shorter events, 4.3 us)
Async XLA Ops:
  0.6 26.4 %copy-start.3 = (bf16[256,6,128]{2,0,1:T(8,128)(2,1)S(1)}, bf16[256,6,128]{2,0,1:T(8,128)(2,1)}, u32[]{:S(2)}) copy-start(bf16[256,6,128]{2,0,1:T(8,128)(2,1)} %param.18) | copy-start | bytes 1179652
  0.6 26.4 %copy-start.2 = (bf16[256,6,128]{2,0,1:T(8,128)(2,1)S(1)}, bf16[256,6,128]{2,0,1:T(8,128)(2,1)}, u32[]{:S(2)}) copy-start(bf16[256,6,128]{2,0,1:T(8,128)(2,1)} %param.19) | copy-start | bytes 1179652
  13.3 20.2 %collective-permute-start.16 = (bf16[2,3,64,128]{3,2,1,0:T(8,128)(2,1)S(1)}, bf16[2,3,64,128]{3,2,1,0:T(8,128)(2,1)S(1)}, u32[]{:S(2)}, u32[]{:S(2)}) collective-permute-start(bf16[2,3,64,128]{3,2,1,0:T(8,128)(2,1)S(1)} %get-tuple-element.5), channel_id=1, source_target_pairs={{0,17},{8,129},{16,0},{24,145},{1,16},{9,128},{17,1},{25,144},{128... | collective-permute-start | bytes 294920 | tf_op jit(solution)/shard_map/ppermute | solution.py:74
  18.7 17.7 %collective-permute-start.17 = (bf16[2,3,64,128]{3,2,1,0:T(8,128)(2,1)S(1)}, bf16[2,3,64,128]{3,2,1,0:T(8,128)(2,1)S(1)}, u32[]{:S(2)}, u32[]{:S(2)}) collective-permute-start(bf16[2,3,64,128]{3,2,1,0:T(8,128)(2,1)S(1)} %get-tuple-element.2), channel_id=1, source_target_pairs={{0,1},{8,145},{16,17},{24,128},{1,0},{9,144},{17,16},{25,129},{128... | collective-permute-start | bytes 294920 | tf_op jit(solution)/shard_map/ppermute | solution.py:74
  18.8 19.7 %collective-permute-start.6 = (bf16[2,3,64,128]{3,2,1,0:T(8,128)(2,1)S(1)}, bf16[2,3,64,128]{3,2,1,0:T(8,128)(2,1)S(1)}, u32[]{:S(2)}, u32[]{:S(2)}) collective-permute-start(bf16[2,3,64,128]{3,2,1,0:T(8,128)(2,1)S(1)} %get-tuple-element.3), channel_id=1, source_target_pairs={{0,0},{8,144},{16,16},{24,129},{1,1},{9,145},{17,17},{25,128},{128... | collective-permute-start | bytes 294920 | tf_op jit(solution)/shard_map/ppermute | solution.py:74
  22.0 18.1 %collective-permute-start.7 = (bf16[2,3,64,128]{3,2,1,0:T(8,128)(2,1)S(1)}, bf16[2,3,64,128]{3,2,1,0:T(8,128)(2,1)S(1)}, u32[]{:S(2)}, u32[]{:S(2)}) collective-permute-start(bf16[2,3,64,128]{3,2,1,0:T(8,128)(2,1)S(1)} %get-tuple-element.4), channel_id=1, source_target_pairs={{0,16},{8,128},{16,1},{24,144},{1,17},{9,129},{17,0},{25,145},{128... | collective-permute-start | bytes 294920 | tf_op jit(solution)/shard_map/ppermute | solution.py:74
  23.8 6.2 %collective-permute-start = (bf16[3,64,128]{2,1,0:T(8,128)(2,1)S(1)}, bf16[3,64,128]{2,1,0:T(8,128)(2,1)S(1)}, u32[]{:S(2)}, u32[]{:S(2)}) collective-permute-start(bf16[3,64,128]{2,1,0:T(8,128)(2,1)S(1)} %get-tuple-element.25), channel_id=1, source_target_pairs={{0,0},{8,144},{16,16},{24,129},{1,1},{9,145},{17,17},{25,128},{128... | collective-permute-start | bytes 147464 | tf_op jit(solution)/shard_map/ppermute | solution.py:74
  30.0 39.3 %collective-permute-start.1 = (bf16[3,64,128]{2,1,0:T(8,128)(2,1)S(1)}, bf16[3,64,128]{2,1,0:T(8,128)(2,1)S(1)}, u32[]{:S(2)}, u32[]{:S(2)}) collective-permute-start(bf16[3,64,128]{2,1,0:T(8,128)(2,1)S(1)} %get-tuple-element.24), channel_id=1, source_target_pairs={{0,16},{8,128},{16,1},{24,144},{1,17},{9,129},{17,0},{25,145},{128... | collective-permute-start | bytes 147464 | tf_op jit(solution)/shard_map/ppermute | solution.py:74
  33.5 37.3 %collective-permute-start.2 = (bf16[3,64,128]{2,1,0:T(8,128)(2,1)S(1)}, bf16[3,64,128]{2,1,0:T(8,128)(2,1)S(1)}, u32[]{:S(2)}, u32[]{:S(2)}) collective-permute-start(bf16[3,64,128]{2,1,0:T(8,128)(2,1)S(1)} %get-tuple-element.23), channel_id=1, source_target_pairs={{0,17},{8,129},{16,0},{24,145},{1,16},{9,128},{17,1},{25,144},{128... | collective-permute-start | bytes 147464 | tf_op jit(solution)/shard_map/ppermute | solution.py:74
  36.4 36.5 %collective-permute-start.3 = (bf16[3,64,128]{2,1,0:T(8,128)(2,1)S(1)}, bf16[3,64,128]{2,1,0:T(8,128)(2,1)S(1)}, u32[]{:S(2)}, u32[]{:S(2)}) collective-permute-start(bf16[3,64,128]{2,1,0:T(8,128)(2,1)S(1)} %get-tuple-element.22), channel_id=1, source_target_pairs={{0,1},{8,145},{16,17},{24,128},{1,0},{9,144},{17,16},{25,129},{128... | collective-permute-start | bytes 147464 | tf_op jit(solution)/shard_map/ppermute | solution.py:74
  38.5 7.0 %collective-permute-start.18 = (bf16[2,3,128,128]{3,2,1,0:T(8,128)(2,1)S(1)}, bf16[2,3,128,128]{3,2,1,0:T(8,128)(2,1)S(1)}, u32[]{:S(2)}, u32[]{:S(2)}) collective-permute-start(bf16[2,3,128,128]{3,2,1,0:T(8,128)(2,1)S(1)} %constant_dynamic-update-slice_fusion.7), channel_id=1, source_target_pairs={{0,2},{2,4},{4,6},{6,0},{1,3},{3,5},{5,7},{7,1},{8,10},{10,12},{12... | collective-permute-start | bytes 589832 | tf_op jit(solution)/shard_map/ppermute | solution.py:66
  40.1 6.8 %collective-permute-start.19 = (bf16[2,3,128,128]{3,2,1,0:T(8,128)(2,1)S(1)}, bf16[2,3,128,128]{3,2,1,0:T(8,128)(2,1)S(1)}, u32[]{:S(2)}, u32[]{:S(2)}) collective-permute-start(bf16[2,3,128,128]{3,2,1,0:T(8,128)(2,1)S(1)} %constant_dynamic-update-slice_fusion.7), channel_id=1, source_target_pairs={{0,6},{2,0},{4,2},{6,4},{1,7},{3,1},{5,3},{7,5},{8,14},{10,8},{12,... | collective-permute-start | bytes 589832 | tf_op jit(solution)/shard_map/ppermute | solution.py:66
  45.4 7.2 %collective-permute-start.8 = (bf16[2,3,128,128]{3,2,1,0:T(8,128)(2,1)S(1)}, bf16[2,3,128,128]{3,2,1,0:T(8,128)(2,1)S(1)}, u32[]{:S(2)}, u32[]{:S(2)}) collective-permute-start(bf16[2,3,128,128]{3,2,1,0:T(8,128)(2,1)S(1)} %constant_dynamic-update-slice_fusion.5), channel_id=1, source_target_pairs={{0,32},{32,64},{64,96},{96,0},{1,33},{33,65},{65,97},{97,1},{2,34}... | collective-permute-start | bytes 589832 | tf_op jit(solution)/shard_map/ppermute | solution.py:66
  46.9 7.0 %collective-permute-start.9 = (bf16[2,3,128,128]{3,2,1,0:T(8,128)(2,1)S(1)}, bf16[2,3,128,128]{3,2,1,0:T(8,128)(2,1)S(1)}, u32[]{:S(2)}, u32[]{:S(2)}) collective-permute-start(bf16[2,3,128,128]{3,2,1,0:T(8,128)(2,1)S(1)} %constant_dynamic-update-slice_fusion.5), channel_id=1, source_target_pairs={{0,96},{32,0},{64,32},{96,64},{1,97},{33,1},{65,33},{97,65},{2,98}... | collective-permute-start | bytes 589832 | tf_op jit(solution)/shard_map/ppermute | solution.py:66
  52.6 5.8 %collective-permute-start.20 = (bf16[3,128,128]{2,1,0:T(8,128)(2,1)S(1)}, bf16[3,128,128]{2,1,0:T(8,128)(2,1)S(1)}, u32[]{:S(2)}, u32[]{:S(2)}) collective-permute-start(bf16[3,128,128]{2,1,0:T(8,128)(2,1)S(1)} %slice_bitcast_fusion.2), channel_id=1, source_target_pairs={{0,2},{2,4},{4,6},{6,0},{1,3},{3,5},{5,7},{7,1},{8,10},{10,12},{12... | collective-permute-start | bytes 294920 | tf_op jit(solution)/shard_map/ppermute | solution.py:66
  53.9 6.1 %collective-permute-start.21 = (bf16[3,128,128]{2,1,0:T(8,128)(2,1)S(1)}, bf16[3,128,128]{2,1,0:T(8,128)(2,1)S(1)}, u32[]{:S(2)}, u32[]{:S(2)}) collective-permute-start(bf16[3,128,128]{2,1,0:T(8,128)(2,1)S(1)} %slice_bitcast_fusion.1), channel_id=1, source_target_pairs={{0,6},{2,0},{4,2},{6,4},{1,7},{3,1},{5,3},{7,5},{8,14},{10,8},{12,... | collective-permute-start | bytes 294920 | tf_op jit(solution)/shard_map/ppermute | solution.py:66
  58.5 6.9 %collective-permute-start.10 = (bf16[3,128,128]{2,1,0:T(8,128)(2,1)S(1)}, bf16[3,128,128]{2,1,0:T(8,128)(2,1)S(1)}, u32[]{:S(2)}, u32[]{:S(2)}) collective-permute-start(bf16[3,128,128]{2,1,0:T(8,128)(2,1)S(1)} %slice_bitcast_fusion.4), channel_id=1, source_target_pairs={{0,32},{32,64},{64,96},{96,0},{1,33},{33,65},{65,97},{97,1},{2,34}... | collective-permute-start | bytes 294920 | tf_op jit(solution)/shard_map/ppermute | solution.py:66
  60.0 5.5 %collective-permute-start.11 = (bf16[3,128,128]{2,1,0:T(8,128)(2,1)S(1)}, bf16[3,128,128]{2,1,0:T(8,128)(2,1)S(1)}, u32[]{:S(2)}, u32[]{:S(2)}) collective-permute-start(bf16[3,128,128]{2,1,0:T(8,128)(2,1)S(1)} %slice_bitcast_fusion.3), channel_id=1, source_target_pairs={{0,96},{32,0},{64,32},{96,64},{1,97},{33,1},{65,33},{97,65},{2,98}... | collective-permute-start | bytes 294920 | tf_op jit(solution)/shard_map/ppermute | solution.py:66
  65.4 13.2 %collective-permute-start.22 = (bf16[4,2,3,128,128]{4,3,2,1,0:T(8,128)(2,1)S(1)}, bf16[4,2,3,128,128]{4,3,2,1,0:T(8,128)(2,1)S(1)}, u32[]{:S(2)}, u32[]{:S(2)}) collective-permute-start(bf16[4,2,3,128,128]{4,3,2,1,0:T(8,128)(2,1)S(1)} %pad_maximum_fusion.1.refs_4_), channel_id=1, source_target_pairs={{0,32},{32,64},{64,96},{96,0},{1,33},{33,65},{65,97},{97,1},{2,34}... | collective-permute-start | bytes 2359304 | tf_op jit(solution)/shard_map/ppermute | solution.py:66
  65.5 13.3 %collective-permute-start.24 = (bf16[4,2,3,128,128]{4,3,2,1,0:T(8,128)(2,1)S(1)}, bf16[4,2,3,128,128]{4,3,2,1,0:T(8,128)(2,1)S(1)}, u32[]{:S(2)}, u32[]{:S(2)}) collective-permute-start(bf16[4,2,3,128,128]{4,3,2,1,0:T(8,128)(2,1)S(1)} %pad_maximum_fusion.1.refs_4_), channel_id=1, source_target_pairs={{0,96},{32,0},{64,32},{96,64},{1,97},{33,1},{65,33},{97,65},{2,98}... | collective-permute-start | bytes 2359304 | tf_op jit(solution)/shard_map/ppermute | solution.py:66
  69.3 14.2 %collective-permute-start.12 = (bf16[4,2,3,128,128]{4,3,2,1,0:T(8,128)(2,1)S(1)}, bf16[4,2,3,128,128]{4,3,2,1,0:T(8,128)(2,1)S(1)}, u32[]{:S(2)}, u32[]{:S(2)}) collective-permute-start(bf16[4,2,3,128,128]{4,3,2,1,0:T(8,128)(2,1)S(1)} %pad_maximum_fusion.refs_3_), channel_id=1, source_target_pairs={{0,2},{2,4},{4,6},{6,0},{1,3},{3,5},{5,7},{7,1},{8,10},{10,12},{12... | collective-permute-start | bytes 2359304 | tf_op jit(solution)/shard_map/ppermute | solution.py:66
  70.8 14.9 %collective-permute-start.14 = (bf16[4,2,3,128,128]{4,3,2,1,0:T(8,128)(2,1)S(1)}, bf16[4,2,3,128,128]{4,3,2,1,0:T(8,128)(2,1)S(1)}, u32[]{:S(2)}, u32[]{:S(2)}) collective-permute-start(bf16[4,2,3,128,128]{4,3,2,1,0:T(8,128)(2,1)S(1)} %pad_maximum_fusion.refs_3_), channel_id=1, source_target_pairs={{0,6},{2,0},{4,2},{6,4},{1,7},{3,1},{5,3},{7,5},{8,14},{10,8},{12,... | collective-permute-start | bytes 2359304 | tf_op jit(solution)/shard_map/ppermute | solution.py:66
  72.9 1.5 %collective-permute-start.4 = (bf16[3,272,128]{2,1,0:T(8,128)(2,1)S(1)}, bf16[3,272,128]{2,1,0:T(8,128)(2,1)S(1)}, u32[]{:S(2)}, u32[]{:S(2)}) collective-permute-start(bf16[3,272,128]{2,1,0:T(8,128)(2,1)S(1)} %bitcast.112), channel_id=1, source_target_pairs={{0,128},{128,0},{1,129},{129,1},{2,130},{130,2},{3,131},{131,3},{4... | collective-permute-start | bytes 626696 | tf_op jit(solution)/shard_map/ppermute | solution.py:70
  74.5 14.2 %collective-permute-start.5 = (bf16[3,272,128]{2,1,0:T(8,128)(2,1)S(1)}, bf16[3,272,128]{2,1,0:T(8,128)(2,1)S(1)}, u32[]{:S(2)}, u32[]{:S(2)}) collective-permute-start(bf16[3,272,128]{2,1,0:T(8,128)(2,1)S(1)} %constant_dynamic-update-slice_fusion.refs_1_.refs_0_), channel_id=1, source_target_pairs={{0,128},{128,0},{1,129},{129,1},{2,130},{130,2},{3,131},{131,3},{4... | collective-permute-start | bytes 626696 | tf_op jit(solution)/shard_map/ppermute | solution.py:70
  78.6 25.5 %collective-permute-start.23 = (bf16[2,2,3,128,128]{4,3,2,1,0:T(8,128)(2,1)S(1)}, bf16[2,2,3,128,128]{4,3,2,1,0:T(8,128)(2,1)S(1)}, u32[]{:S(2)}, u32[]{:S(2)}) collective-permute-start(bf16[2,2,3,128,128]{4,3,2,1,0:T(8,128)(2,1)S(1)} %slice.111), channel_id=1, source_target_pairs={{0,32},{32,64},{64,96},{96,0},{1,33},{33,65},{65,97},{97,1},{2,34}... | collective-permute-start | bytes 1179656 | tf_op jit(solution)/shard_map/ppermute | solution.py:66
  78.9 25.3 %collective-permute-start.25 = (bf16[2,2,3,128,128]{4,3,2,1,0:T(8,128)(2,1)S(1)}, bf16[2,2,3,128,128]{4,3,2,1,0:T(8,128)(2,1)S(1)}, u32[]{:S(2)}, u32[]{:S(2)}) collective-permute-start(bf16[2,2,3,128,128]{4,3,2,1,0:T(8,128)(2,1)S(1)} %slice.112), channel_id=1, source_target_pairs={{0,96},{32,0},{64,32},{96,64},{1,97},{33,1},{65,33},{97,65},{2,98}... | collective-permute-start | bytes 1179656 | tf_op jit(solution)/shard_map/ppermute | solution.py:66
  83.5 20.7 %collective-permute-start.13 = (bf16[2,2,3,128,128]{4,3,2,1,0:T(8,128)(2,1)S(1)}, bf16[2,2,3,128,128]{4,3,2,1,0:T(8,128)(2,1)S(1)}, u32[]{:S(2)}, u32[]{:S(2)}) collective-permute-start(bf16[2,2,3,128,128]{4,3,2,1,0:T(8,128)(2,1)S(1)} %slice.107), channel_id=1, source_target_pairs={{0,2},{2,4},{4,6},{6,0},{1,3},{3,5},{5,7},{7,1},{8,10},{10,12},{12... | collective-permute-start | bytes 1179656 | tf_op jit(solution)/shard_map/ppermute | solution.py:66
  85.8 18.4 %collective-permute-start.15 = (bf16[2,2,3,128,128]{4,3,2,1,0:T(8,128)(2,1)S(1)}, bf16[2,2,3,128,128]{4,3,2,1,0:T(8,128)(2,1)S(1)}, u32[]{:S(2)}, u32[]{:S(2)}) collective-permute-start(bf16[2,2,3,128,128]{4,3,2,1,0:T(8,128)(2,1)S(1)} %slice.108), channel_id=1, source_target_pairs={{0,6},{2,0},{4,2},{6,4},{1,7},{3,1},{5,3},{7,5},{8,14},{10,8},{12,... | collective-permute-start | bytes 1179656 | tf_op jit(solution)/shard_map/ppermute | solution.py:66
  114.7 2.5 %copy-start = (f32[2,2,3,272,128]{4,3,2,1,0:T(8,128)}, f32[2,2,3,272,128]{4,3,2,1,0:T(8,128)S(1)}, u32[]{:S(2)}) copy-start(f32[2,2,3,272,128]{4,3,2,1,0:T(8,128)S(1)} %attend.5.mine) | copy-start | bytes 5013508
  114.7 2.4 %collective-permute-start.26 = (f32[2,3,272,128]{3,2,1,0:T(8,128)S(1)}, f32[2,3,272,128]{3,2,1,0:T(8,128)S(1)}, u32[]{:S(2)}, u32[]{:S(2)}) collective-permute-start(f32[2,3,272,128]{3,2,1,0:T(8,128)S(1)} %slice_bitcast_fusion), channel_id=1, source_target_pairs={{0,128},{128,0},{1,129},{129,1},{2,130},{130,2},{3,131},{131,3},{4... | collective-permute-start | bytes 2506760 | tf_op jit(solution)/shard_map/ppermute | solution.py:70
  117.2 0.9 copy-start.1
  122.5 16.6 %collective-permute-start.27 = (bf16[3,80,128]{2,1,0:T(8,128)(2,1)S(1)}, bf16[3,80,128]{2,1,0:T(8,128)(2,1)S(1)}, u32[]{:S(2)}, u32[]{:S(2)}) collective-permute-start(bf16[3,80,128]{2,1,0:T(8,128)(2,1)S(1)} %get-tuple-element.18), channel_id=1, source_target_pairs={{0,0},{144,8},{16,16},{129,24},{1,1},{145,9},{17,17},{128,25},{8,1... | collective-permute-start | bytes 184328 | tf_op jit(solution)/shard_map/ppermute | solution.py:78
  124.4 14.7 %collective-permute-start.28 = (bf16[3,80,128]{2,1,0:T(8,128)(2,1)S(1)}, bf16[3,80,128]{2,1,0:T(8,128)(2,1)S(1)}, u32[]{:S(2)}, u32[]{:S(2)}) collective-permute-start(bf16[3,80,128]{2,1,0:T(8,128)(2,1)S(1)} %get-tuple-element.21), channel_id=1, source_target_pairs={{16,0},{128,8},{1,16},{144,24},{17,1},{129,9},{0,17},{145,25},{25,... | collective-permute-start | bytes 184328 | tf_op jit(solution)/shard_map/ppermute | solution.py:78
  126.2 12.9 %collective-permute-start.29 = (bf16[3,80,128]{2,1,0:T(8,128)(2,1)S(1)}, bf16[3,80,128]{2,1,0:T(8,128)(2,1)S(1)}, u32[]{:S(2)}, u32[]{:S(2)}) collective-permute-start(bf16[3,80,128]{2,1,0:T(8,128)(2,1)S(1)} %get-tuple-element.20), channel_id=1, source_target_pairs={{17,0},{129,8},{0,16},{145,24},{16,1},{128,9},{1,17},{144,25},{24,... | collective-permute-start | bytes 184328 | tf_op jit(solution)/shard_map/ppermute | solution.py:78
  128.9 10.2 %collective-permute-start.30 = (bf16[3,80,128]{2,1,0:T(8,128)(2,1)S(1)}, bf16[3,80,128]{2,1,0:T(8,128)(2,1)S(1)}, u32[]{:S(2)}, u32[]{:S(2)}) collective-permute-start(bf16[3,80,128]{2,1,0:T(8,128)(2,1)S(1)} %get-tuple-element.19), channel_id=1, source_target_pairs={{1,0},{145,8},{17,16},{128,24},{0,1},{144,9},{16,17},{129,25},{9,1... | collective-permute-start | bytes 184328 | tf_op jit(solution)/shard_map/ppermute | solution.py:78

commit v2 on v0

v2 whole, which is shorter than its diff:
```python
import functools
import math

import jax
import jax.numpy as jnp
import numpy as np
from jax import lax
from jax.experimental import pallas as pl
from jax.experimental.pallas import tpu as pltpu
from jax.sharding import Mesh
from jax.sharding import PartitionSpec as P

THETA = 256.0
HD = 128
SCALE2 = math.log2(math.e) / math.sqrt(HD)
NT = (((1,), (1,)), ((), ()))
TN = (((0,), (0,)), ((), ()))

EVEN = (0, 2, -2, 4)
ODD = (1, -1, 3, -3)
ZAXES = ("grp", "za", "zp", "zb")
OWN, TEXT, OTHER = 256, 16, 256
HALF = OWN + TEXT
QROWS = OWN + TEXT + OTHER
PACK = 128 + 128 + TEXT


def z_index(c, z):
    return ((c * 2 + (z // 2) % 2) * 2 + z % 2) * 2 + z // 4


def z_perm(m, back):
    pairs = []
    for c in range(2):
        for z in range(8):
            d = EVEN[m] if z % 2 == c else ODD[m]
            there = z_index(z % 2, (z + d) % 8)
            here = z_index(c, z)
            pairs.append((there, here) if back else (here, there))
    return pairs


def rotary_constants():
    freq = np.zeros((3, HD), np.float32)
    swap = np.zeros((HD, HD), np.float32)
    band_t = HD // 8
    band_h = (HD - band_t) // 2
    offset = 0
    for axis, band in enumerate((band_t, band_h, HD - band_t - band_h)):
        half = band // 2
        f = THETA ** (-2.0 * np.arange(half) / band)
        freq[axis, offset : offset + half] = f
        freq[axis, offset + half : offset + band] = f
        for i in range(half):
            swap[offset + half + i, offset + i] = -1.0
            swap[offset + i, offset + half + i] = 1.0
        offset += band
    return freq, swap


FREQ, SWAP = rotary_constants()


def shift(v, axis, step):
    return lax.ppermute(v, axis, [(i, (i + step) % 4) for i in range(4)])


def other_core(v):
    return lax.ppermute(v, "grp", [(0, 1), (1, 0)])


def z_send(v, m):
    return lax.ppermute(v, ZAXES, z_perm(m, False))


def z_return(v, m):
    return lax.ppermute(v, ZAXES, z_perm(m, True))


def place():
    core = lax.axis_index("grp")
    za, zp, zb = lax.axis_index("za"), lax.axis_index("zp"), lax.axis_index("zb")
    return core, zb * 4 + za * 2 + zp, za, zp, zb


def group_of(m, core, z, zp):
    d = jnp.where(zp == core, EVEN[m] + 8, ODD[m] + 8)
    return lax.rem(z + d, 8) // 2


def prepare_body(q_ref, k_ref, v_ref, pos_ref, tq_ref, tk_ref, tv_ref, freq_ref, swap_ref, *outs):
    core, z, za, zp, zb = place()
    y = lax.axis_index("y")
    x = lax.axis_index("x")
    messages, own_text, send_text = outs[:4], outs[4], outs[5]
    angles = lax.dot_general(
        pos_ref[...].astype(jnp.float32),
        freq_ref[...],
        TN,
        precision=lax.Precision.HIGHEST,
        preferred_element_type=jnp.float32,
    )
    cos, sin = jnp.cos(angles), jnp.sin(angles)
    swap = swap_ref[...]

    def rotate(block):
        swapped = jnp.dot(block.reshape(3 * 64, HD), swap, preferred_element_type=jnp.float32)
        return (block.astype(jnp.float32) * cos + swapped.reshape(3, 64, HD) * sin).astype(jnp.bfloat16)

    for m in range(4):
        heads = pl.ds(group_of(m, core, z, zp) * 3, 3)
        messages[m][0] = rotate(k_ref[heads])
        messages[m][1] = v_ref[heads]
        messages[m][2] = rotate(q_ref[heads])

    heads = pl.ds(za * 3, 3)
    rows = lax.broadcasted_iota(jnp.int32, (TEXT, 256), 0)
    source = lax.broadcasted_iota(jnp.int32, (TEXT, 256), 1)
    pick = (source == x * 64 + (rows // 4) * 16 + y * 4 + rows % 4).astype(jnp.float32).astype(jnp.bfloat16)
    tq = tq_ref[heads]
    for out, c in ((own_text, core), (send_text, 1 - core)):
        half = pl.ds(pl.multiple_of(c * 128, 128), 128)
        out[:, :128] = tk_ref[heads, half]
        out[:, 128:256] = tv_ref[heads, half]
        for h in range(3):
            out[h, 256:] = jnp.dot(pick, tq[h], preferred_element_type=jnp.float32).astype(jnp.bfloat16)


def prepare(q, k, v, positions, tq, tk, tv):
    message = jax.ShapeDtypeStruct((3, 3, 64, HD), jnp.bfloat16)
    text = jax.ShapeDtypeStruct((3, PACK, HD), jnp.bfloat16)
    return pl.pallas_call(
        prepare_body,
        out_shape=[message] * 4 + [text] * 2,
        cost_estimate=pl.CostEstimate(flops=50000000, bytes_accessed=3000000, transcendentals=20000),
        compiler_params=pltpu.CompilerParams(vmem_limit_bytes=32 * 1024 * 1024),
        name="prepare",
    )(q, k, v, positions, tq, tk, tv, jnp.asarray(FREQ), jnp.asarray(SWAP, jnp.bfloat16))


def softmax_step(q, k, v, state, live=None):
    s = lax.dot_general(q, k, NT, preferred_element_type=jnp.float32)
    if live is not None:
        s = jnp.where(live(s.shape), s, -jnp.inf)
    peak = jnp.max(s, axis=1, keepdims=True)
    if state is not None:
        acc, top, total = state
        peak = jnp.maximum(top, peak)
    p = jnp.exp2(s * SCALE2 - peak * SCALE2)
    add = jnp.sum(p, axis=1, keepdims=True)
    mixed = jnp.dot(p.astype(jnp.bfloat16), v, preferred_element_type=jnp.float32)
    if state is None:
        return mixed, peak, add
    alpha = jnp.exp2((top - peak) * SCALE2)
    return acc * alpha + mixed, peak, total * alpha + add


def over_parts(q, parts, state, most=1024):
    for part in parts:
        pieces, tokens = part.shape[0], part.shape[3]
        step = max(1, most // tokens)
        for i in range(0, pieces, step):
            n = min(step, pieces - i)
            k = part[i : i + n, 0, 0].reshape(n * tokens, HD)
            v = part[i : i + n, 1, 0].reshape(n * tokens, HD)
            state = softmax_step(q, k, v, state)
    return state


def keep(state, acc_ref, stat_ref):
    acc, top, total = state
    acc_ref[0] = acc
    lane = lax.broadcasted_iota(jnp.int32, acc.shape, 1)
    stat_ref[0] = jnp.where(lane < 64, top, total)


def kept(acc_ref, stat_ref):
    stat = stat_ref[0]
    return acc_ref[0], stat[:, :1], stat[:, 64:65]


def first_body(count_ref, m0, m1, m2, m3, mine, theirs, *refs):
    core, z, za, zp, zb = place()
    parts, (q_out, acc_out, stat_out) = refs[:-3], refs[-3:]
    for i, m in enumerate((m0, m1, m2, m3)):
        q_out[0, i * 64 : (i + 1) * 64] = m[0, 0]
    here = core == zp
    text = jnp.where(here, mine[0].astype(jnp.float32), theirs[0, OTHER:].astype(jnp.float32)).astype(jnp.bfloat16)
    q_out[0, OWN:HALF] = text[256:]
    q_out[0, HALF:] = theirs[0, :OTHER]
    q = q_out[0]
    state = over_parts(q, parts, None)
    left = count_ref[0] - core * 128
    live = lambda shape: lax.broadcasted_iota(jnp.int32, shape, 1) < left
    state = softmax_step(q, text[:128], text[128:256], state, live)
    keep(state, acc_out, stat_out)


def next_body(q_ref, acc_ref, stat_ref, *refs):
    parts, (acc_out, stat_out) = refs[:-2], refs[-2:]
    keep(over_parts(q_ref[0], parts, kept(acc_ref, stat_ref)), acc_out, stat_out)


def last_body(q_ref, acc_ref, stat_ref, *refs):
    parts, (acc_out, stat_out, send_out) = refs[:-3], refs[-3:]
    acc, top, total = over_parts(q_ref[0], parts, kept(acc_ref, stat_ref))
    lane = lax.broadcasted_iota(jnp.int32, (HALF, HD), 1)
    acc_out[0] = acc[:HALF]
    stat_out[0] = jnp.where(lane < 64, top[:HALF] * SCALE2, total[:HALF])
    send_out[0, :, :HD] = (acc[OWN:] / total[OWN:]).astype(jnp.bfloat16)
    level = top[OWN:] * SCALE2 + jnp.log2(total[OWN:])
    high = level.astype(jnp.bfloat16).astype(jnp.float32)
    mid = (level - high).astype(jnp.bfloat16).astype(jnp.float32)
    low = level - high - mid
    send_out[0, :, HD:] = jnp.where(lane < 32, high, jnp.where(lane < 64, mid, low)).astype(jnp.bfloat16)


def part_spec(part):
    return pl.BlockSpec((part.shape[0], 2, 1) + part.shape[3:], lambda h, *_: (0, 0, h, 0, 0))


def head_spec(*shape):
    return pl.BlockSpec((1,) + shape, lambda h, *_: (h,) + (0,) * len(shape))


def attend(body, name, parts, extra, extra_specs, outs, prefetch=()):
    keys = sum(p.shape[0] * p.shape[3] for p in parts)
    return pl.pallas_call(
        body,
        out_shape=[jax.ShapeDtypeStruct((3,) + s, t) for s, t in outs],
        grid_spec=pltpu.PrefetchScalarGridSpec(
            num_scalar_prefetch=len(prefetch),
            grid=(3,),
            in_specs=list(extra_specs) + [part_spec(p) for p in parts],
            out_specs=[head_spec(*s) for s, _ in outs],
        ),
        compiler_params=pltpu.CompilerParams(vmem_limit_bytes=40 * 1024 * 1024),
        cost_estimate=pl.CostEstimate(
            flops=12 * QROWS * keys * HD, bytes_accessed=keys * 1536 + 3000000, transcendentals=3 * QROWS * keys
        ),
        name=name,
    )(*prefetch, *extra, *parts)


F32, BF16 = jnp.float32, jnp.bfloat16
STATE = [((QROWS, HD), F32), ((QROWS, HD), F32)]


def merge_body(acc_ref, stat_ref, theirs, *outs):
    def weigh(rows, sent_rows):
        stat = stat_ref[0, rows]
        total = stat[:, 64:65]
        level = stat[:, :1] + jnp.log2(total)
        sent = theirs[0, sent_rows, HD:].astype(F32)
        level2 = sent[:, :1] + sent[:, 32:33] + sent[:, 64:65]
        peak = jnp.maximum(level, level2)
        w1, w2 = jnp.exp2(level - peak), jnp.exp2(level2 - peak)
        inv = 1.0 / (w1 + w2)
        return (acc_ref[0, rows] * (w1 * inv / total) + theirs[0, sent_rows, :HD].astype(F32) * (w2 * inv)).astype(BF16)

    video = weigh(slice(0, OWN), slice(TEXT, HALF))
    text = weigh(slice(OWN, HALF), slice(0, TEXT))
    for m in range(4):
        outs[m][0, :64] = video[m * 64 : (m + 1) * 64]
        outs[m][0, 64:] = text


def merge(acc, stat, theirs):
    return pl.pallas_call(
        merge_body,
        out_shape=[jax.ShapeDtypeStruct((3, 64 + TEXT, HD), BF16)] * 4,
        grid=(3,),
        in_specs=[head_spec(HALF, HD), head_spec(HALF, HD), head_spec(HALF, 2 * HD)],
        out_specs=[head_spec(64 + TEXT, HD)] * 4,
        name="merge",
    )(acc, stat, theirs)


def finish_body(*refs):
    messages, (video, text) = refs[:4], refs[4:]
    core, z, za, zp, zb = place()
    for m in range(4):
        group = group_of(m, core, z, zp)
        video[pl.ds(group * 3, 3)] = messages[m][:, :64]

        @pl.when(group // 2 == zb)
        def _():
            for h in range(3):
                rows = messages[m][h, 64:].astype(F32)
                own = jnp.zeros((4, HD), F32)
                for i in range(4):
                    own = jnp.where(za * 2 + zp == i, rows[4 * i : 4 * i + 4], own)
                text[lax.rem(group, 2) * 3 + h] = own.astype(BF16)


def finish(messages):
    return pl.pallas_call(
        finish_body,
        out_shape=[jax.ShapeDtypeStruct((12, 64, HD), BF16), jax.ShapeDtypeStruct((6, 4, HD), BF16)],
        name="finish",
    )(*messages)


def ring(block, axis):
    right, left = shift(block, axis, 1), shift(block, axis, -1)
    return right, left


def local(video_q, video_k, video_v, positions, text_q, text_k, text_v, text_count):
    flat = lambda a: jnp.transpose(a, (1, 0, 2))
    *out, own_text, send_text = prepare(
        flat(video_q), flat(video_k), flat(video_v), positions, flat(text_q), flat(text_k), flat(text_v)
    )
    m = [z_send(out[i], i) for i in range(4)]

    block_a = jnp.concatenate([m[0][:2], m[1][:2]], axis=2)
    right_a, left_a = ring(block_a, "x")
    block_b = jnp.concatenate([m[2][:2], m[3][:2]], axis=2)
    right_b, left_b = ring(block_b, "y")
    theirs = other_core(jnp.concatenate([m[0][2], m[1][2], m[2][2], m[3][2], send_text], axis=1))
    far_a = [shift(right_a[0], "x", 1), shift(left_a[1], "x", -1)]
    far_b = [shift(right_b[0], "y", 1), shift(left_b[1], "y", -1)]
    line_a = jnp.stack([block_a, right_a, left_a, jnp.stack(far_a)])
    line_b = jnp.stack([block_b, right_b, left_b, jnp.stack(far_b)])
    line_a, line_b, theirs = lax.optimization_barrier((line_a, line_b, theirs))

    right_a, left_a = ring(line_a, "y")
    right_b, left_b = ring(line_b, "x")
    q_specs = [pl.BlockSpec((1, 1, 64, HD), lambda h, *_: (2, h, 0, 0))] * 4
    q, acc, stat = attend(
        first_body,
        "attend_first",
        [line_a, line_b],
        [*m, own_text, theirs],
        q_specs + [head_spec(PACK, HD), head_spec(OTHER + PACK, HD)],
        [((QROWS, HD), BF16)] + STATE,
        prefetch=(text_count,),
    )
    right_a, left_a, right_b, left_b, acc, stat = lax.optimization_barrier(
        (right_a, left_a, right_b, left_b, acc, stat)
    )
    far = [shift(right_a[:2], "y", 1), shift(left_a[2:], "y", -1), shift(right_b[:2], "x", 1), shift(left_b[2:], "x", -1)]
    specs = [head_spec(QROWS, HD)] * 3
    acc, stat = attend(next_body, "attend_next", [right_a, left_a, right_b, left_b], [q, acc, stat], specs, STATE)
    acc, stat, send = attend(
        last_body,
        "attend_last",
        far,
        [q, acc, stat],
        specs,
        [((HALF, HD), F32), ((HALF, HD), F32), ((HALF, 2 * HD), BF16)],
    )
    done = merge(acc, stat, other_core(send))
    video, text = finish([z_return(done[i], i) for i in range(4)])
    return flat(video), flat(text)


def solution(mesh):
    fine = Mesh(mesh.devices.reshape(2, 4, 2, 2, 4, 2), ("grp", "x", "za", "zp", "y", "zb"))
    ctx = ("x", "za", "zp", "y")
    tokens = P(ctx + ("zb",), "grp", None)
    text = P(None, ("grp", "zb"), None)
    return jax.shard_map(
        local,
        mesh=fine,
        in_specs=(tokens, tokens, tokens, P(None, ctx + ("zb",)), text, text, text, P()),
        out_specs=(tokens, P(ctx, ("grp", "zb"), None)),
        check_vma=False,
    )
```

time: 812 us -> 130 us (0.16)
  waiting for transfers between devices: 699 us -> 27.7 us
  starting transfers between devices: 6.95 us -> 49 us
  Pallas kernels: 0 us -> 36.6 us
  matrix products: 32.3 us -> 0 us
  blocking collectives: 30.6 us -> 0 us
  other arithmetic: 16.4 us -> 0.35 us
  between operations: 14.8 us -> 1.59 us
    all_gather x2 -> x0, waiting for transfers between devices: 681 us -> none  [the longest x1 348 us: local(): lax.all_gather(values_video, 'ctx', axis=0, tiled=True)]
    ppermute x0 -> x26, starting transfers between devices: none -> 49 us  [the longest x16 27 us: shift(): return lax.ppermute(v, axis, [(i, (i + step) % 4) for i in range(4)])]
    pallas_call x0 -> x6, Pallas kernels: none -> 36.6 us  [the longest x3 30.9 us: attend(): pl.pallas_call(body, out_shape=[jax.ShapeDtypeStruct((3,) + s, t) for s,...]
    dot_general x4 -> x0, matrix products: 32.3 us -> none  [the longest x1 16.2 us: local(): jnp.einsum('qhd,khd->qhk', queries, keys_all, preferred_element_type=jnp....]
    all_to_all x2 -> x0, blocking collectives: 30.6 us -> none  [the longest x1 17.4 us: local(): lax.all_to_all(rotated_k, 'hd', split_axis=1, concat_axis=0, tiled=True)]
    ppermute x0 -> x26, waiting for transfers between devices: none -> 27.7 us  [the longest x16 13.2 us: shift(): return lax.ppermute(v, axis, [(i, (i + step) % 4) for i in range(4)])]
    all_to_all x2 -> x0, waiting for transfers between devices: 18 us -> none  [the longest x1 9.55 us: local(): lax.all_to_all(rotated_q, 'hd', split_axis=1, concat_axis=0, tiled=True)]
    reduce_sum x2 -> x0, other arithmetic: 11.9 us -> none  [the longest x1 11.4 us: local(): new_total = total * factor + jnp.sum(piece_probs, axis=2)]
  transfers between devices with their start and end apart: 4 -> 26, of which waited for: 4 -> 8; matrix products, arithmetic and copies ran while one was open for 4% -> 0% of each run, Pallas kernels for 0% -> 17%
where the time goes in v2:
time: 130 us; the launch traced here: 129 us
  starting transfers between devices  49 us (38%)
  Pallas kernels  36.6 us (28%)
  waiting for transfers between devices  27.7 us (21%)
  local copies, waits for them, and re-layouts  13.4 us (10%)
  between operations  1.59 us (1%)
    pallas_call x3, Pallas kernels, attend(): pl.pallas_call(body, out_shape=[jax.ShapeDtypeStruct((3,) + s, t) for s,...  30.9 us
    ppermute x16, starting transfers between devices, shift(): return lax.ppermute(v, axis, [(i, (i + step) % 4) for i in range(4)])  27 us
    ppermute x16, waiting for transfers between devices, shift(): return lax.ppermute(v, axis, [(i, (i + step) % 4) for i in range(4)])  13.2 us
    unnamed x44, local copies, waits for them, and re-layouts  11.5 us
    ppermute x4, starting transfers between devices, z_send(): return lax.ppermute(v, ZAXES, z_perm(m, False))  9.17 us
    ppermute x4, starting transfers between devices, z_return(): return lax.ppermute(v, ZAXES, z_perm(m, True))  8.48 us
    ppermute x4, waiting for transfers between devices, z_return(): return lax.ppermute(v, ZAXES, z_perm(m, True))  7.81 us
    ppermute x4, waiting for transfers between devices, z_send(): return lax.ppermute(v, ZAXES, z_perm(m, False))  4.93 us
  transfers between devices with their start and end apart: 26, of which 8 were waited for; matrix products, arithmetic and copies ran while one was open for 0% of the time, Pallas kernels for 17%

profile of v2, /device:TPU:32, one launch (start us, length us, event | category | flops | bytes accessed | tf_op | source)
XLA Modules:
  0.0 128.6 jit_solution(17508012956047537449)
XLA Ops:
  0.7 0.7 copy-done.14
  1.3 1.0 copy-done.2
  2.3 1.0 copy-done.3
  3.3 1.0 copy-done.4
  4.3 0.9 copy-done.5
  5.3 0.9 copy-done.6
  6.2 0.9 copy-done.7
  7.1 0.8 copy-done.12
  8.4 5.4 %collective-permute-start.2 = (bf16[3,3,64,128]{3,2,1,0:T(8,128)(2,1)S(1)}, bf16[3,3,64,128]{3,2,1,0:T(8,128)(2,1)S(1)}, u32[]{:S(2)}, u32[]{:S(2)}) collective-permute-start(bf16[3,3,64,128]{3,2,1,0:T(8,128)(2,1)S(1)} %get-tuple-element.33), channel_id=1, source_target_pairs={{0,17},{8,129},{16,0},{24,145},{1,16},{9,128},{17,1},{25,144},{128... | collective-permute-start | bytes 442376 | tf_op jit(solution)/shard_map/ppermute | solution.py:73
  13.8 3.2 %collective-permute-start = (bf16[3,3,64,128]{3,2,1,0:T(8,128)(2,1)S(1)}, bf16[3,3,64,128]{3,2,1,0:T(8,128)(2,1)S(1)}, u32[]{:S(2)}, u32[]{:S(2)}) collective-permute-start(bf16[3,3,64,128]{3,2,1,0:T(8,128)(2,1)S(1)} %get-tuple-element.31), channel_id=1, source_target_pairs={{0,0},{8,144},{16,16},{24,129},{1,1},{9,145},{17,17},{25,128},{128... | collective-permute-start | bytes 442376 | tf_op jit(solution)/shard_map/ppermute | solution.py:73
  17.0 0.5 collective-permute-start.1
  17.5 3.5 %collective-permute-done.2.m2 = bf16[3,3,64,128]{3,2,1,0:T(8,128)(2,1)S(1)} collective-permute-done((bf16[3,3,64,128]{3,2,1,0:T(8,128)(2,1)S(1)}, bf16[3,3,64,128]{3,2,1,0:T(8,128)(2,1)S(1)}, u32[]{:S(2)}, u32[]{:S(2)}) %collective-permute-start.2) | collective-permute-done | bytes 147488 | tf_op jit(solution)/shard_map/ppermute | solution.py:73
  21.0 0.7 copy-done.8
  21.7 1.4 %collective-permute-done.3.m3 = bf16[3,3,64,128]{3,2,1,0:T(8,128)(2,1)S(1)} collective-permute-done((bf16[3,3,64,128]{3,2,1,0:T(8,128)(2,1)S(1)}, bf16[3,3,64,128]{3,2,1,0:T(8,128)(2,1)S(1)}, u32[]{:S(2)}, u32[]{:S(2)}) %collective-permute-start.3) | collective-permute-done | bytes 147488 | tf_op jit(solution)/shard_map/ppermute | solution.py:73
  23.1 0.9 slice-done
  24.1 1.5 %collective-permute-start.8 = (bf16[2,3,128,128]{3,2,1,0:T(8,128)(2,1)S(1)}, bf16[2,3,128,128]{3,2,1,0:T(8,128)(2,1)S(1)}, u32[]{:S(2)}, u32[]{:S(2)}) collective-permute-start(bf16[2,3,128,128]{3,2,1,0:T(8,128)(2,1)S(1)} %get-tuple-element.61), channel_id=1, source_target_pairs={{0,2},{2,4},{4,6},{6,0},{1,3},{3,5},{5,7},{7,1},{8,10},{10,12},{12... | collective-permute-start | bytes 589832 | tf_op jit(solution)/shard_map/ppermute | solution.py:65
  25.6 1.8 %collective-permute-start.9 = (bf16[2,3,128,128]{3,2,1,0:T(8,128)(2,1)S(1)}, bf16[2,3,128,128]{3,2,1,0:T(8,128)(2,1)S(1)}, u32[]{:S(2)}, u32[]{:S(2)}) collective-permute-start(bf16[2,3,128,128]{3,2,1,0:T(8,128)(2,1)S(1)} %get-tuple-element.61), channel_id=1, source_target_pairs={{0,6},{2,0},{4,2},{6,4},{1,7},{3,1},{5,3},{7,5},{8,14},{10,8},{12,... | collective-permute-start | bytes 589832 | tf_op jit(solution)/shard_map/ppermute | solution.py:65
  27.4 0.7 copy-done.10
  28.1 0.9 slice-done.1
  29.0 1.4 %collective-permute-start.4 = (bf16[2,3,128,128]{3,2,1,0:T(8,128)(2,1)S(1)}, bf16[2,3,128,128]{3,2,1,0:T(8,128)(2,1)S(1)}, u32[]{:S(2)}, u32[]{:S(2)}) collective-permute-start(bf16[2,3,128,128]{3,2,1,0:T(8,128)(2,1)S(1)} %get-tuple-element.63), channel_id=1, source_target_pairs={{0,32},{32,64},{64,96},{96,0},{1,33},{33,65},{65,97},{97,1},{2,34}... | collective-permute-start | bytes 589832 | tf_op jit(solution)/shard_map/ppermute | solution.py:65
  30.4 1.9 %collective-permute-start.5 = (bf16[2,3,128,128]{3,2,1,0:T(8,128)(2,1)S(1)}, bf16[2,3,128,128]{3,2,1,0:T(8,128)(2,1)S(1)}, u32[]{:S(2)}, u32[]{:S(2)}) collective-permute-start(bf16[2,3,128,128]{3,2,1,0:T(8,128)(2,1)S(1)} %get-tuple-element.63), channel_id=1, source_target_pairs={{0,96},{32,0},{64,32},{96,64},{1,97},{33,1},{65,33},{97,65},{2,98}... | collective-permute-start | bytes 589832 | tf_op jit(solution)/shard_map/ppermute | solution.py:65
  32.4 4.3 %collective-permute-start.12 = (bf16[3,528,128]{2,1,0:T(8,128)(2,1)S(1)}, bf16[3,528,128]{2,1,0:T(8,128)(2,1)S(1)}, u32[]{:S(2)}, u32[]{:S(2)}) collective-permute-start(bf16[3,528,128]{2,1,0:T(8,128)(2,1)S(1)} %constant_dynamic-update-slice_fusion), channel_id=1, source_target_pairs={{0,128},{128,0},{1,129},{129,1},{2,130},{130,2},{3,131},{131,3},{4... | collective-permute-start | bytes 1216520 | tf_op jit(solution)/shard_map/ppermute | solution.py:69
  37.1 3.1 %collective-permute-start.11 = (bf16[3,128,128]{2,1,0:T(8,128)(2,1)S(1)}, bf16[3,128,128]{2,1,0:T(8,128)(2,1)S(1)}, u32[]{:S(2)}, u32[]{:S(2)}) collective-permute-start(bf16[3,128,128]{2,1,0:T(8,128)(2,1)S(1)} %slice_bitcast_fusion), channel_id=1, source_target_pairs={{0,6},{2,0},{4,2},{6,4},{1,7},{3,1},{5,3},{7,5},{8,14},{10,8},{12,... | collective-permute-start | bytes 294920 | tf_op jit(solution)/shard_map/ppermute | solution.py:65
  40.6 3.0 %collective-permute-start.7 = (bf16[3,128,128]{2,1,0:T(8,128)(2,1)S(1)}, bf16[3,128,128]{2,1,0:T(8,128)(2,1)S(1)}, u32[]{:S(2)}, u32[]{:S(2)}) collective-permute-start(bf16[3,128,128]{2,1,0:T(8,128)(2,1)S(1)} %slice_bitcast_fusion.2), channel_id=1, source_target_pairs={{0,96},{32,0},{64,32},{96,64},{1,97},{33,1},{65,33},{97,65},{2,98}... | collective-permute-start | bytes 294920 | tf_op jit(solution)/shard_map/ppermute | solution.py:65
  43.6 2.5 %collective-permute-done.6 = bf16[3,128,128]{2,1,0:T(8,128)(2,1)S(1)} collective-permute-done((bf16[3,128,128]{2,1,0:T(8,128)(2,1)S(1)}, bf16[3,128,128]{2,1,0:T(8,128)(2,1)S(1)}, u32[]{:S(2)}, u32[]{:S(2)}) %collective-permute-start.6) | collective-permute-done | bytes 98336 | tf_op jit(solution)/shard_map/ppermute | solution.py:65
  46.4 3.2 %collective-permute-start.14 = (bf16[4,2,3,128,128]{4,3,2,1,0:T(8,128)(2,1)S(1)}, bf16[4,2,3,128,128]{4,3,2,1,0:T(8,128)(2,1)S(1)}, u32[]{:S(2)}, u32[]{:S(2)}) collective-permute-start(bf16[4,2,3,128,128]{4,3,2,1,0:T(8,128)(2,1)S(1)} %pad_maximum_fusion.refs_0_), channel_id=1, source_target_pairs={{0,6},{2,0},{4,2},{6,4},{1,7},{3,1},{5,3},{7,5},{8,14},{10,8},{12,... | collective-permute-start | bytes 2359304 | tf_op jit(solution)/shard_map/ppermute | solution.py:65
  49.7 0.6 collective-permute-start.15
  50.3 2.7 %collective-permute-start.16 = (bf16[4,2,3,128,128]{4,3,2,1,0:T(8,128)(2,1)S(1)}, bf16[4,2,3,128,128]{4,3,2,1,0:T(8,128)(2,1)S(1)}, u32[]{:S(2)}, u32[]{:S(2)}) collective-permute-start(bf16[4,2,3,128,128]{4,3,2,1,0:T(8,128)(2,1)S(1)} %pad_maximum_fusion.1.refs_1_), channel_id=1, source_target_pairs={{0,96},{32,0},{64,32},{96,64},{1,97},{33,1},{65,33},{97,65},{2,98}... | collective-permute-start | bytes 2359304 | tf_op jit(solution)/shard_map/ppermute | solution.py:65
  53.6 3.9 %attend_first.1 = (bf16[3,528,128]{2,1,0:T(8,128)(2,1)S(1)}, f32[3,528,128]{2,1,0:T(8,128)S(1)}, f32[3,528,128]{2,1,0:T(8,128)S(1)}) custom-call(s32[1]{0:T(128)S(6)} %copy.16.count_ref, bf16[3,3,64,128]{3,2,1,0:T(8,128)(2,1)S(1)} %copy-done.11, bf16[3,3,64,128]{3,2,1,0:T(8,128)(2,1)S(1)} %collective-permute-done.1.m1, ...), custom_call_target="tpu_custom_call" | custom-call | flops 830472192 | bytes 4572864 | tf_op jit(solution)/shard_map/attend_first/pallas_call | solution.py:228
  57.5 7.9 %collective-permute-done.13.refs_0_ = bf16[4,2,3,128,128]{4,3,2,1,0:T(8,128)(2,1)S(1)} collective-permute-done((bf16[4,2,3,128,128]{4,3,2,1,0:T(8,128)(2,1)S(1)}, bf16[4,2,3,128,128]{4,3,2,1,0:T(8,128)(2,1)S(1)}, u32[]{:S(2)}, u32[]{:S(2)}) %collective-permute-start.13) | collective-permute-done | bytes 786464 | tf_op jit(solution)/shard_map/ppermute | solution.py:65
  65.4 2.8 %collective-permute-done.15.refs_2_ = bf16[4,2,3,128,128]{4,3,2,1,0:T(8,128)(2,1)S(1)} collective-permute-done((bf16[4,2,3,128,128]{4,3,2,1,0:T(8,128)(2,1)S(1)}, bf16[4,2,3,128,128]{4,3,2,1,0:T(8,128)(2,1)S(1)}, u32[]{:S(2)}, u32[]{:S(2)}) %collective-permute-start.15) | collective-permute-done | bytes 786464 | tf_op jit(solution)/shard_map/ppermute | solution.py:65
  68.3 3.3 %collective-permute-start.18 = (bf16[2,2,3,128,128]{4,3,2,1,0:T(8,128)(2,1)S(1)}, bf16[2,2,3,128,128]{4,3,2,1,0:T(8,128)(2,1)S(1)}, u32[]{:S(2)}, u32[]{:S(2)}) collective-permute-start(bf16[2,2,3,128,128]{4,3,2,1,0:T(8,128)(2,1)S(1)} %slice.61), channel_id=1, source_target_pairs={{0,6},{2,0},{4,2},{6,4},{1,7},{3,1},{5,3},{7,5},{8,14},{10,8},{12,... | collective-permute-start | bytes 1179656 | tf_op jit(solution)/shard_map/ppermute | solution.py:65
  71.7 1.2 collective-permute-start.19
  72.9 2.4 %collective-permute-start.20 = (bf16[2,2,3,128,128]{4,3,2,1,0:T(8,128)(2,1)S(1)}, bf16[2,2,3,128,128]{4,3,2,1,0:T(8,128)(2,1)S(1)}, u32[]{:S(2)}, u32[]{:S(2)}) collective-permute-start(bf16[2,2,3,128,128]{4,3,2,1,0:T(8,128)(2,1)S(1)} %slice.63), channel_id=1, source_target_pairs={{0,96},{32,0},{64,32},{96,64},{1,97},{33,1},{65,33},{97,65},{2,98}... | collective-permute-start | bytes 1179656 | tf_op jit(solution)/shard_map/ppermute | solution.py:65
  75.3 17.4 %attend_next.1 = (f32[3,528,128]{2,1,0:T(8,128)S(1)}, f32[3,528,128]{2,1,0:T(8,128)S(1)}) custom-call(bf16[3,528,128]{2,1,0:T(8,128)(2,1)S(1)} %get-tuple-element.40.q_ref, f32[3,528,128]{2,1,0:T(8,128)S(1)} %get-tuple-element.43.acc_ref, f32[3,528,128]{2,1,0:T(8,128)S(1)} %get-tuple-element.44.stat_ref, ...), custom_call_target="tpu_custom_call" | custom-call | flops 1660944384 | bytes 6145728 | tf_op jit(solution)/shard_map/attend_next/pallas_call | solution.py:228
  92.7 9.7 %attend_last.1 = (f32[3,272,128]{2,1,0:T(8,128)S(1)}, f32[3,272,128]{2,1,0:T(8,128)S(1)}, bf16[3,272,256]{2,1,0:T(8,128)(2,1)S(1)}) custom-call(bf16[3,528,128]{2,1,0:T(8,128)(2,1)S(1)} %get-tuple-element.40.q_ref, f32[3,528,128]{2,1,0:T(8,128)S(1)} %get-tuple-element.49.acc_ref, f32[3,528,128]{2,1,0:T(8,128)S(1)} %get-tuple-element.50.stat_ref, ...), custom_call_target="tpu_custom_call" | custom-call | flops 830472192 | bytes 4572864 | tf_op jit(solution)/shard_map/attend_last/pallas_call | solution.py:228
  102.4 0.8 copy-done
  103.2 0.7 copy-done.1
  103.9 1.8 %collective-permute-done.21.theirs = bf16[3,272,256]{2,1,0:T(8,128)(2,1)S(1)} collective-permute-done((bf16[3,272,256]{2,1,0:T(8,128)(2,1)S(1)}, bf16[3,272,256]{2,1,0:T(8,128)(2,1)S(1)}, u32[]{:S(2)}, u32[]{:S(2)}) %collective-permute-start.21) | collective-permute-done | bytes 417824 | tf_op jit(solution)/shard_map/ppermute | solution.py:69
  105.7 0.8 copy-done.15
  106.5 3.5 %merge.1 = (bf16[3,80,128]{2,1,0:T(8,128)(2,1)}, bf16[3,80,128]{2,1,0:T(8,128)(2,1)}, bf16[3,80,128]{2,1,0:T(8,128)(2,1)}, bf16[3,80,128]{2,1,0:T(8,128)(2,1)}) custom-call(f32[3,272,128]{2,1,0:T(8,128)} %copy-done, f32[3,272,128]{2,1,0:T(8,128)} %copy-done.1, bf16[3,272,256]{2,1,0:T(8,128)(2,1)} %copy-done.15), custom_call_target="tpu_custom_call" | custom-call | tf_op jit(solution)/shard_map/merge/pallas_call | solution.py:269
  110.0 2.9 %collective-permute-start.22 = (bf16[3,80,128]{2,1,0:T(8,128)(2,1)}, bf16[3,80,128]{2,1,0:T(8,128)(2,1)S(1)}, u32[]{:S(2)}, u32[]{:S(2)}) collective-permute-start(bf16[3,80,128]{2,1,0:T(8,128)(2,1)} %get-tuple-element.54), channel_id=1, source_target_pairs={{0,0},{144,8},{16,16},{129,24},{1,1},{145,9},{17,17},{128,25},{8,1... | collective-permute-start | bytes 184328 | tf_op jit(solution)/shard_map/ppermute | solution.py:77
  112.9 0.8 collective-permute-start.23
  113.7 4.5 %collective-permute-start.24 = (bf16[3,80,128]{2,1,0:T(8,128)(2,1)}, bf16[3,80,128]{2,1,0:T(8,128)(2,1)S(1)}, u32[]{:S(2)}, u32[]{:S(2)}) collective-permute-start(bf16[3,80,128]{2,1,0:T(8,128)(2,1)} %get-tuple-element.56), channel_id=1, source_target_pairs={{17,0},{129,8},{0,16},{145,24},{16,1},{128,9},{1,17},{144,25},{24,... | collective-permute-start | bytes 184328 | tf_op jit(solution)/shard_map/ppermute | solution.py:77
  118.5 3.2 %collective-permute-done.24.refs_2_ = bf16[3,80,128]{2,1,0:T(8,128)(2,1)S(1)} collective-permute-done((bf16[3,80,128]{2,1,0:T(8,128)(2,1)}, bf16[3,80,128]{2,1,0:T(8,128)(2,1)S(1)}, u32[]{:S(2)}, u32[]{:S(2)}) %collective-permute-start.24) | collective-permute-done | bytes 61472 | tf_op jit(solution)/shard_map/ppermute | solution.py:77
  121.7 4.6 %collective-permute-done.25.refs_3_ = bf16[3,80,128]{2,1,0:T(8,128)(2,1)S(1)} collective-permute-done((bf16[3,80,128]{2,1,0:T(8,128)(2,1)}, bf16[3,80,128]{2,1,0:T(8,128)(2,1)S(1)}, u32[]{:S(2)}, u32[]{:S(2)}) %collective-permute-start.25) | collective-permute-done | bytes 61472 | tf_op jit(solution)/shard_map/ppermute | solution.py:77
  126.3 0.6 copy-done.19
  126.9 1.7 %finish.1 = (bf16[12,64,128]{2,1,0:T(8,128)(2,1)}, bf16[6,4,128]{2,1,0:T(4,128)(2,1)}) custom-call(bf16[3,80,128]{2,1,0:T(8,128)(2,1)} %copy-done.16, bf16[3,80,128]{2,1,0:T(8,128)(2,1)} %copy-done.17, bf16[3,80,128]{2,1,0:T(8,128)(2,1)} %copy-done.18, bf16[3,80,128]{2,1,0:T(8,128)(2,1)} %copy-done.19), custom_call_target="tpu_custom_call" | custom-call | tf_op jit(solution)/shard_map/finish/pallas_call | solution.py:297
  (75 shorter events, 2.4 us)
Async XLA Ops:
  0.6 0.7 copy-start.14
  0.6 0.7 copy-start.13
  1.3 1.0 copy-start.2
  2.3 1.0 copy-start.3
  3.3 1.0 copy-start.4
  4.3 0.9 copy-start.5
  5.2 0.9 copy-start.6
  6.2 0.9 copy-start.7
  7.1 0.8 copy-start.12
  8.4 12.7 %collective-permute-start.2 = (bf16[3,3,64,128]{3,2,1,0:T(8,128)(2,1)S(1)}, bf16[3,3,64,128]{3,2,1,0:T(8,128)(2,1)S(1)}, u32[]{:S(2)}, u32[]{:S(2)}) collective-permute-start(bf16[3,3,64,128]{3,2,1,0:T(8,128)(2,1)S(1)} %get-tuple-element.33), channel_id=1, source_target_pairs={{0,17},{8,129},{16,0},{24,145},{1,16},{9,128},{17,1},{25,144},{128... | collective-permute-start | bytes 442376 | tf_op jit(solution)/shard_map/ppermute | solution.py:73
  13.7 9.4 %collective-permute-start.3 = (bf16[3,3,64,128]{3,2,1,0:T(8,128)(2,1)S(1)}, bf16[3,3,64,128]{3,2,1,0:T(8,128)(2,1)S(1)}, u32[]{:S(2)}, u32[]{:S(2)}) collective-permute-start(bf16[3,3,64,128]{3,2,1,0:T(8,128)(2,1)S(1)} %get-tuple-element.34), channel_id=1, source_target_pairs={{0,1},{8,145},{16,17},{24,128},{1,0},{9,144},{17,16},{25,129},{128... | collective-permute-start | bytes 442376 | tf_op jit(solution)/shard_map/ppermute | solution.py:73
  13.8 13.6 %collective-permute-start = (bf16[3,3,64,128]{3,2,1,0:T(8,128)(2,1)S(1)}, bf16[3,3,64,128]{3,2,1,0:T(8,128)(2,1)S(1)}, u32[]{:S(2)}, u32[]{:S(2)}) collective-permute-start(bf16[3,3,64,128]{3,2,1,0:T(8,128)(2,1)S(1)} %get-tuple-element.31), channel_id=1, source_target_pairs={{0,0},{8,144},{16,16},{24,129},{1,1},{9,145},{17,17},{25,128},{128... | collective-permute-start | bytes 442376 | tf_op jit(solution)/shard_map/ppermute | solution.py:73
  17.0 11.0 %collective-permute-start.1 = (bf16[3,3,64,128]{3,2,1,0:T(8,128)(2,1)S(1)}, bf16[3,3,64,128]{3,2,1,0:T(8,128)(2,1)S(1)}, u32[]{:S(2)}, u32[]{:S(2)}) collective-permute-start(bf16[3,3,64,128]{3,2,1,0:T(8,128)(2,1)S(1)} %get-tuple-element.32), channel_id=1, source_target_pairs={{0,16},{8,128},{16,1},{24,144},{1,17},{9,129},{17,0},{25,145},{128... | collective-permute-start | bytes 442376 | tf_op jit(solution)/shard_map/ppermute | solution.py:73
  21.0 0.7 copy-start.8
  23.1 0.9 slice-start
  24.1 12.7 %collective-permute-start.8 = (bf16[2,3,128,128]{3,2,1,0:T(8,128)(2,1)S(1)}, bf16[2,3,128,128]{3,2,1,0:T(8,128)(2,1)S(1)}, u32[]{:S(2)}, u32[]{:S(2)}) collective-permute-start(bf16[2,3,128,128]{3,2,1,0:T(8,128)(2,1)S(1)} %get-tuple-element.61), channel_id=1, source_target_pairs={{0,2},{2,4},{4,6},{6,0},{1,3},{3,5},{5,7},{7,1},{8,10},{10,12},{12... | collective-permute-start | bytes 589832 | tf_op jit(solution)/shard_map/ppermute | solution.py:65
  25.6 11.5 %collective-permute-start.9 = (bf16[2,3,128,128]{3,2,1,0:T(8,128)(2,1)S(1)}, bf16[2,3,128,128]{3,2,1,0:T(8,128)(2,1)S(1)}, u32[]{:S(2)}, u32[]{:S(2)}) collective-permute-start(bf16[2,3,128,128]{3,2,1,0:T(8,128)(2,1)S(1)} %get-tuple-element.61), channel_id=1, source_target_pairs={{0,6},{2,0},{4,2},{6,4},{1,7},{3,1},{5,3},{7,5},{8,14},{10,8},{12,... | collective-permute-start | bytes 589832 | tf_op jit(solution)/shard_map/ppermute | solution.py:65
  27.4 0.7 copy-start.10
  28.1 0.9 slice-start.1
  28.9 3.4 %copy-start.11 = (bf16[3,3,64,128]{3,2,1,0:T(8,128)(2,1)S(1)}, bf16[3,3,64,128]{3,2,1,0:T(8,128)(2,1)}, u32[]{:S(2)}) copy-start(bf16[3,3,64,128]{3,2,1,0:T(8,128)(2,1)} %copy-done.10) | copy-start | bytes 442372
  29.0 3.3 %copy-start.9 = (bf16[3,3,64,128]{3,2,1,0:T(8,128)(2,1)S(1)}, bf16[3,3,64,128]{3,2,1,0:T(8,128)(2,1)}, u32[]{:S(2)}) copy-start(bf16[3,3,64,128]{3,2,1,0:T(8,128)(2,1)} %copy-done.8) | copy-start | bytes 442372
  29.0 11.2 %collective-permute-start.4 = (bf16[2,3,128,128]{3,2,1,0:T(8,128)(2,1)S(1)}, bf16[2,3,128,128]{3,2,1,0:T(8,128)(2,1)S(1)}, u32[]{:S(2)}, u32[]{:S(2)}) collective-permute-start(bf16[2,3,128,128]{3,2,1,0:T(8,128)(2,1)S(1)} %get-tuple-element.63), channel_id=1, source_target_pairs={{0,32},{32,64},{64,96},{96,0},{1,33},{33,65},{65,97},{97,1},{2,34}... | collective-permute-start | bytes 589832 | tf_op jit(solution)/shard_map/ppermute | solution.py:65
  30.4 10.1 %collective-permute-start.5 = (bf16[2,3,128,128]{3,2,1,0:T(8,128)(2,1)S(1)}, bf16[2,3,128,128]{3,2,1,0:T(8,128)(2,1)S(1)}, u32[]{:S(2)}, u32[]{:S(2)}) collective-permute-start(bf16[2,3,128,128]{3,2,1,0:T(8,128)(2,1)S(1)} %get-tuple-element.63), channel_id=1, source_target_pairs={{0,96},{32,0},{64,32},{96,64},{1,97},{33,1},{65,33},{97,65},{2,98}... | collective-permute-start | bytes 589832 | tf_op jit(solution)/shard_map/ppermute | solution.py:65
  32.4 13.9 %collective-permute-start.12 = (bf16[3,528,128]{2,1,0:T(8,128)(2,1)S(1)}, bf16[3,528,128]{2,1,0:T(8,128)(2,1)S(1)}, u32[]{:S(2)}, u32[]{:S(2)}) collective-permute-start(bf16[3,528,128]{2,1,0:T(8,128)(2,1)S(1)} %constant_dynamic-update-slice_fusion), channel_id=1, source_target_pairs={{0,128},{128,0},{1,129},{129,1},{2,130},{130,2},{3,131},{131,3},{4... | collective-permute-start | bytes 1216520 | tf_op jit(solution)/shard_map/ppermute | solution.py:69
  36.8 6.8 %collective-permute-start.10 = (bf16[3,128,128]{2,1,0:T(8,128)(2,1)S(1)}, bf16[3,128,128]{2,1,0:T(8,128)(2,1)S(1)}, u32[]{:S(2)}, u32[]{:S(2)}) collective-permute-start(bf16[3,128,128]{2,1,0:T(8,128)(2,1)S(1)} %slice_bitcast_fusion.1), channel_id=1, source_target_pairs={{0,2},{2,4},{4,6},{6,0},{1,3},{3,5},{5,7},{7,1},{8,10},{10,12},{12... | collective-permute-start | bytes 294920 | tf_op jit(solution)/shard_map/ppermute | solution.py:65
  37.1 6.5 %collective-permute-start.11 = (bf16[3,128,128]{2,1,0:T(8,128)(2,1)S(1)}, bf16[3,128,128]{2,1,0:T(8,128)(2,1)S(1)}, u32[]{:S(2)}, u32[]{:S(2)}) collective-permute-start(bf16[3,128,128]{2,1,0:T(8,128)(2,1)S(1)} %slice_bitcast_fusion), channel_id=1, source_target_pairs={{0,6},{2,0},{4,2},{6,4},{1,7},{3,1},{5,3},{7,5},{8,14},{10,8},{12,... | collective-permute-start | bytes 294920 | tf_op jit(solution)/shard_map/ppermute | solution.py:65
  40.2 5.9 %collective-permute-start.6 = (bf16[3,128,128]{2,1,0:T(8,128)(2,1)S(1)}, bf16[3,128,128]{2,1,0:T(8,128)(2,1)S(1)}, u32[]{:S(2)}, u32[]{:S(2)}) collective-permute-start(bf16[3,128,128]{2,1,0:T(8,128)(2,1)S(1)} %slice_bitcast_fusion.3), channel_id=1, source_target_pairs={{0,32},{32,64},{64,96},{96,0},{1,33},{33,65},{65,97},{97,1},{2,34}... | collective-permute-start | bytes 294920 | tf_op jit(solution)/shard_map/ppermute | solution.py:65
  40.6 5.5 %collective-permute-start.7 = (bf16[3,128,128]{2,1,0:T(8,128)(2,1)S(1)}, bf16[3,128,128]{2,1,0:T(8,128)(2,1)S(1)}, u32[]{:S(2)}, u32[]{:S(2)}) collective-permute-start(bf16[3,128,128]{2,1,0:T(8,128)(2,1)S(1)} %slice_bitcast_fusion.2), channel_id=1, source_target_pairs={{0,96},{32,0},{64,32},{96,64},{1,97},{33,1},{65,33},{97,65},{2,98}... | collective-permute-start | bytes 294920 | tf_op jit(solution)/shard_map/ppermute | solution.py:65
  46.3 19.1 %collective-permute-start.13 = (bf16[4,2,3,128,128]{4,3,2,1,0:T(8,128)(2,1)S(1)}, bf16[4,2,3,128,128]{4,3,2,1,0:T(8,128)(2,1)S(1)}, u32[]{:S(2)}, u32[]{:S(2)}) collective-permute-start(bf16[4,2,3,128,128]{4,3,2,1,0:T(8,128)(2,1)S(1)} %pad_maximum_fusion.refs_0_), channel_id=1, source_target_pairs={{0,2},{2,4},{4,6},{6,0},{1,3},{3,5},{5,7},{7,1},{8,10},{10,12},{12... | collective-permute-start | bytes 2359304 | tf_op jit(solution)/shard_map/ppermute | solution.py:65
  46.4 19.0 %collective-permute-start.14 = (bf16[4,2,3,128,128]{4,3,2,1,0:T(8,128)(2,1)S(1)}, bf16[4,2,3,128,128]{4,3,2,1,0:T(8,128)(2,1)S(1)}, u32[]{:S(2)}, u32[]{:S(2)}) collective-permute-start(bf16[4,2,3,128,128]{4,3,2,1,0:T(8,128)(2,1)S(1)} %pad_maximum_fusion.refs_0_), channel_id=1, source_target_pairs={{0,6},{2,0},{4,2},{6,4},{1,7},{3,1},{5,3},{7,5},{8,14},{10,8},{12,... | collective-permute-start | bytes 2359304 | tf_op jit(solution)/shard_map/ppermute | solution.py:65
  49.7 18.5 %collective-permute-start.15 = (bf16[4,2,3,128,128]{4,3,2,1,0:T(8,128)(2,1)S(1)}, bf16[4,2,3,128,128]{4,3,2,1,0:T(8,128)(2,1)S(1)}, u32[]{:S(2)}, u32[]{:S(2)}) collective-permute-start(bf16[4,2,3,128,128]{4,3,2,1,0:T(8,128)(2,1)S(1)} %pad_maximum_fusion.1.refs_1_), channel_id=1, source_target_pairs={{0,32},{32,64},{64,96},{96,0},{1,33},{33,65},{65,97},{97,1},{2,34}... | collective-permute-start | bytes 2359304 | tf_op jit(solution)/shard_map/ppermute | solution.py:65
  50.3 17.9 %collective-permute-start.16 = (bf16[4,2,3,128,128]{4,3,2,1,0:T(8,128)(2,1)S(1)}, bf16[4,2,3,128,128]{4,3,2,1,0:T(8,128)(2,1)S(1)}, u32[]{:S(2)}, u32[]{:S(2)}) collective-permute-start(bf16[4,2,3,128,128]{4,3,2,1,0:T(8,128)(2,1)S(1)} %pad_maximum_fusion.1.refs_1_), channel_id=1, source_target_pairs={{0,96},{32,0},{64,32},{96,64},{1,97},{33,1},{65,33},{97,65},{2,98}... | collective-permute-start | bytes 2359304 | tf_op jit(solution)/shard_map/ppermute | solution.py:65
  68.2 24.5 %collective-permute-start.17 = (bf16[2,2,3,128,128]{4,3,2,1,0:T(8,128)(2,1)S(1)}, bf16[2,2,3,128,128]{4,3,2,1,0:T(8,128)(2,1)S(1)}, u32[]{:S(2)}, u32[]{:S(2)}) collective-permute-start(bf16[2,2,3,128,128]{4,3,2,1,0:T(8,128)(2,1)S(1)} %slice.60), channel_id=1, source_target_pairs={{0,2},{2,4},{4,6},{6,0},{1,3},{3,5},{5,7},{7,1},{8,10},{10,12},{12... | collective-permute-start | bytes 1179656 | tf_op jit(solution)/shard_map/ppermute | solution.py:65
  68.3 24.4 %collective-permute-start.18 = (bf16[2,2,3,128,128]{4,3,2,1,0:T(8,128)(2,1)S(1)}, bf16[2,2,3,128,128]{4,3,2,1,0:T(8,128)(2,1)S(1)}, u32[]{:S(2)}, u32[]{:S(2)}) collective-permute-start(bf16[2,2,3,128,128]{4,3,2,1,0:T(8,128)(2,1)S(1)} %slice.61), channel_id=1, source_target_pairs={{0,6},{2,0},{4,2},{6,4},{1,7},{3,1},{5,3},{7,5},{8,14},{10,8},{12,... | collective-permute-start | bytes 1179656 | tf_op jit(solution)/shard_map/ppermute | solution.py:65
  71.7 21.1 %collective-permute-start.19 = (bf16[2,2,3,128,128]{4,3,2,1,0:T(8,128)(2,1)S(1)}, bf16[2,2,3,128,128]{4,3,2,1,0:T(8,128)(2,1)S(1)}, u32[]{:S(2)}, u32[]{:S(2)}) collective-permute-start(bf16[2,2,3,128,128]{4,3,2,1,0:T(8,128)(2,1)S(1)} %slice.62), channel_id=1, source_target_pairs={{0,32},{32,64},{64,96},{96,0},{1,33},{33,65},{65,97},{97,1},{2,34}... | collective-permute-start | bytes 1179656 | tf_op jit(solution)/shard_map/ppermute | solution.py:65
  72.9 19.8 %collective-permute-start.20 = (bf16[2,2,3,128,128]{4,3,2,1,0:T(8,128)(2,1)S(1)}, bf16[2,2,3,128,128]{4,3,2,1,0:T(8,128)(2,1)S(1)}, u32[]{:S(2)}, u32[]{:S(2)}) collective-permute-start(bf16[2,2,3,128,128]{4,3,2,1,0:T(8,128)(2,1)S(1)} %slice.63), channel_id=1, source_target_pairs={{0,96},{32,0},{64,32},{96,64},{1,97},{33,1},{65,33},{97,65},{2,98}... | collective-permute-start | bytes 1179656 | tf_op jit(solution)/shard_map/ppermute | solution.py:65
  102.4 0.8 copy-start
  103.2 0.7 copy-start.1
  103.9 1.8 %collective-permute-start.21 = (bf16[3,272,256]{2,1,0:T(8,128)(2,1)S(1)}, bf16[3,272,256]{2,1,0:T(8,128)(2,1)S(1)}, u32[]{:S(2)}, u32[]{:S(2)}) collective-permute-start(bf16[3,272,256]{2,1,0:T(8,128)(2,1)S(1)} %get-tuple-element.53), channel_id=1, source_target_pairs={{0,128},{128,0},{1,129},{129,1},{2,130},{130,2},{3,131},{131,3},{4... | collective-permute-start | bytes 1253384 | tf_op jit(solution)/shard_map/ppermute | solution.py:69
  105.7 0.8 copy-start.15
  110.0 8.5 %collective-permute-start.22 = (bf16[3,80,128]{2,1,0:T(8,128)(2,1)}, bf16[3,80,128]{2,1,0:T(8,128)(2,1)S(1)}, u32[]{:S(2)}, u32[]{:S(2)}) collective-permute-start(bf16[3,80,128]{2,1,0:T(8,128)(2,1)} %get-tuple-element.54), channel_id=1, source_target_pairs={{0,0},{144,8},{16,16},{129,24},{1,1},{145,9},{17,17},{128,25},{8,1... | collective-permute-start | bytes 184328 | tf_op jit(solution)/shard_map/ppermute | solution.py:77
  112.9 5.6 %collective-permute-start.23 = (bf16[3,80,128]{2,1,0:T(8,128)(2,1)}, bf16[3,80,128]{2,1,0:T(8,128)(2,1)S(1)}, u32[]{:S(2)}, u32[]{:S(2)}) collective-permute-start(bf16[3,80,128]{2,1,0:T(8,128)(2,1)} %get-tuple-element.55), channel_id=1, source_target_pairs={{16,0},{128,8},{1,16},{144,24},{17,1},{129,9},{0,17},{145,25},{25,... | collective-permute-start | bytes 184328 | tf_op jit(solution)/shard_map/ppermute | solution.py:77
  113.7 7.9 %collective-permute-start.24 = (bf16[3,80,128]{2,1,0:T(8,128)(2,1)}, bf16[3,80,128]{2,1,0:T(8,128)(2,1)S(1)}, u32[]{:S(2)}, u32[]{:S(2)}) collective-permute-start(bf16[3,80,128]{2,1,0:T(8,128)(2,1)} %get-tuple-element.56), channel_id=1, source_target_pairs={{17,0},{129,8},{0,16},{145,24},{16,1},{128,9},{1,17},{144,25},{24,... | collective-permute-start | bytes 184328 | tf_op jit(solution)/shard_map/ppermute | solution.py:77
  118.2 8.1 %collective-permute-start.25 = (bf16[3,80,128]{2,1,0:T(8,128)(2,1)}, bf16[3,80,128]{2,1,0:T(8,128)(2,1)S(1)}, u32[]{:S(2)}, u32[]{:S(2)}) collective-permute-start(bf16[3,80,128]{2,1,0:T(8,128)(2,1)} %get-tuple-element.57), channel_id=1, source_target_pairs={{1,0},{145,8},{17,16},{128,24},{0,1},{144,9},{16,17},{129,25},{9,1... | collective-permute-start | bytes 184328 | tf_op jit(solution)/shard_map/ppermute | solution.py:77
  118.5 7.8 %copy-start.16 = (bf16[3,80,128]{2,1,0:T(8,128)(2,1)}, bf16[3,80,128]{2,1,0:T(8,128)(2,1)S(1)}, u32[]{:S(2)}) copy-start(bf16[3,80,128]{2,1,0:T(8,128)(2,1)S(1)} %collective-permute-done.22.refs_0_) | copy-start | bytes 184324
  118.5 7.8 %copy-start.17 = (bf16[3,80,128]{2,1,0:T(8,128)(2,1)}, bf16[3,80,128]{2,1,0:T(8,128)(2,1)S(1)}, u32[]{:S(2)}) copy-start(bf16[3,80,128]{2,1,0:T(8,128)(2,1)S(1)} %collective-permute-done.23.refs_1_) | copy-start | bytes 184324
  121.7 4.6 %copy-start.18 = (bf16[3,80,128]{2,1,0:T(8,128)(2,1)}, bf16[3,80,128]{2,1,0:T(8,128)(2,1)S(1)}, u32[]{:S(2)}) copy-start(bf16[3,80,128]{2,1,0:T(8,128)(2,1)S(1)} %collective-permute-done.24.refs_2_) | copy-start | bytes 184324
  126.3 0.6 copy-start.19

commit v3 on v2

v3 whole, which is shorter than its diff:
```python
import functools
import math

import jax
import jax.numpy as jnp
import numpy as np
from jax import lax
from jax.experimental import pallas as pl
from jax.experimental.pallas import tpu as pltpu
from jax.sharding import Mesh
from jax.sharding import PartitionSpec as P

THETA = 256.0
HD = 128
SCALE2 = math.log2(math.e) / math.sqrt(HD)
NT = (((1,), (1,)), ((), ()))
TN = (((0,), (0,)), ((), ()))

MOVES = (0, 1, -1, 2)
ZAXES = ("za", "zp", "zb")
VIDEO, TEXT, STATS = 256, 16, 16
SITE = VIDEO + TEXT
SHARE = 64
TILE = 2 * SITE
VMEM = 60 * 1024 * 1024
F32, BF16 = jnp.float32, jnp.bfloat16


def rotary_constants():
    freq = np.zeros((3, HD), np.float32)
    swap = np.zeros((HD, HD), np.float32)
    band_t = HD // 8
    band_h = (HD - band_t) // 2
    offset = 0
    for axis, band in enumerate((band_t, band_h, HD - band_t - band_h)):
        half = band // 2
        f = THETA ** (-2.0 * np.arange(half) / band)
        freq[axis, offset : offset + half] = f
        freq[axis, offset + half : offset + band] = f
        for i in range(half):
            swap[offset + half + i, offset + i] = -1.0
            swap[offset + i, offset + half + i] = 1.0
        offset += band
    return freq, swap


FREQ, SWAP = rotary_constants()


def shift(v, axis, step):
    return lax.ppermute(v, axis, [(i, (i + step) % 4) for i in range(4)])


def z_shift(v, step):
    line = lambda z: (z % 4) * 2 + z // 4
    return lax.ppermute(v, ZAXES, [(line(z), line((z + step) % 8)) for z in range(8)])


def to_far_half(v):
    return lax.ppermute(v, ("y", "zb"), [(y * 2 + y // 2, y * 2 + 1 - y // 2) for y in range(4)])


def group_of(m):
    return lax.rem(lax.axis_index("y") + (MOVES[m] + 4), 4)


def whole(*shape):
    return pl.BlockSpec(shape, lambda i: (0,) * len(shape))


def prepare_body(q_ref, k_ref, v_ref, pos_ref, tq_ref, tk_ref, tv_ref, freq_ref, swap_ref, *outs):
    x, y = lax.axis_index("x"), lax.axis_index("y")
    low = lax.axis_index("za") * 2 + lax.axis_index("zp")
    kv_out, q_out, text_out, text_q_out = outs[:4], outs[4:8], outs[8], outs[9]
    angles = lax.dot_general(
        pos_ref[...].astype(F32), freq_ref[...], TN, precision=lax.Precision.HIGHEST, preferred_element_type=F32
    )
    cos, sin = jnp.cos(angles), jnp.sin(angles)
    swap = swap_ref[...]

    def rotate(block):
        swapped = jnp.dot(block.reshape(3 * 64, HD), swap, preferred_element_type=F32)
        return (block.astype(F32) * cos + swapped.reshape(3, 64, HD) * sin).astype(BF16)

    for m in range(4):
        heads = pl.ds(group_of(m) * 3, 3)
        kv_out[m][0] = rotate(k_ref[heads])
        kv_out[m][1] = v_ref[heads]
        q_out[m][...] = rotate(q_ref[heads])

    heads = pl.ds(lax.rem(y, 2) * 3, 3)
    share = pl.ds(pl.multiple_of(x * SHARE, SHARE), SHARE)
    text_out[:, :SHARE] = tk_ref[heads, share]
    text_out[:, SHARE:] = tv_ref[heads, share]
    text_q_out[...] = tq_ref[heads, pl.ds(pl.multiple_of(x * 64 + low * TEXT, TEXT), TEXT)]


def prepare(q, k, v, positions, tq, tk, tv):
    outs = [(2, 3, 64, HD)] * 4 + [(3, 64, HD)] * 4 + [(3, 2 * SHARE, HD), (3, TEXT, HD)]
    args = (q, k, v, positions, tq, tk, tv, jnp.asarray(FREQ), jnp.asarray(SWAP, BF16))
    return pl.pallas_call(
        prepare_body,
        out_shape=[jax.ShapeDtypeStruct(o, BF16) for o in outs],
        grid=(1,),
        in_specs=[whole(*a.shape) for a in args],
        out_specs=[whole(*o) for o in outs],
        cost_estimate=pl.CostEstimate(flops=50000000, bytes_accessed=3000000, transcendentals=20000),
        compiler_params=pltpu.CompilerParams(vmem_limit_bytes=VMEM),
        name="prepare",
    )(*args)


def softmax_step(q, k, v, state, live=None):
    s = lax.dot_general(q, k, NT, preferred_element_type=F32)
    if live is not None:
        s = jnp.where(live(s.shape), s, -jnp.inf)
    peak = jnp.max(s, axis=1, keepdims=True)
    if state is not None:
        acc, top, total = state
        peak = jnp.maximum(top, peak)
    p = jnp.exp2(s * SCALE2 - peak * SCALE2)
    add = jnp.sum(p, axis=1, keepdims=True)
    mixed = jnp.dot(p.astype(BF16), v, preferred_element_type=F32)
    if state is None:
        return mixed, peak, add
    alpha = jnp.exp2((top - peak) * SCALE2)
    return acc * alpha + mixed, peak, total * alpha + add


def over_parts(q, refs, state):
    keys = jnp.concatenate([r[...].reshape(-1, HD) for r in refs[0::2]], axis=0)
    values = jnp.concatenate([r[...].reshape(-1, HD) for r in refs[1::2]], axis=0)
    return softmax_step(q, keys, values, state)


def keep(state, acc_ref, stat_ref):
    acc, top, total = state
    acc_ref[0] = acc
    lane = lax.broadcasted_iota(jnp.int32, acc.shape, 1)
    stat_ref[0] = jnp.where(lane < 64, top, total)


def kept(acc_ref, stat_ref):
    stat = stat_ref[0]
    first = lax.broadcasted_iota(jnp.int32, stat.shape, 1) < 64
    top = jnp.max(jnp.where(first, stat, -jnp.inf), axis=1, keepdims=True)
    return acc_ref[0], top, jnp.max(jnp.where(first, 0.0, stat), axis=1, keepdims=True)


def first_body(count_ref, q_ref, mine, sent, *refs):
    parts, (acc_out, stat_out) = refs[:-2], refs[-2:]
    q = q_ref[0]
    state = over_parts(q, parts, None)
    here = lax.axis_index("y") // 2 == lax.axis_index("zb")
    text = jnp.where(here, mine[0].astype(F32), sent[0].astype(F32)).astype(BF16)
    left = count_ref[0] - lax.axis_index("x") * SHARE
    live = lambda shape: lax.broadcasted_iota(jnp.int32, shape, 1) < left
    keep(softmax_step(q, text[:SHARE], text[SHARE:], state, live), acc_out, stat_out)


def next_body(q_ref, acc_ref, stat_ref, *refs):
    parts, (acc_out, stat_out) = refs[:-2], refs[-2:]
    keep(over_parts(q_ref[0], parts, kept(acc_ref, stat_ref)), acc_out, stat_out)


def diagonal(n):
    return lax.broadcasted_iota(jnp.int32, (n, HD), 0) == lax.broadcasted_iota(jnp.int32, (n, HD), 1)


def pack_level(level):
    place = lax.broadcasted_iota(jnp.int32, (STATS, HD), 0)
    block = jnp.zeros((STATS, HD), F32)
    for t in range(0, SITE, HD):
        n = min(HD, SITE - t)
        row = jnp.sum(jnp.where(diagonal(n), level[t : t + n], 0.0), axis=0, keepdims=True)
        for i in range(3):
            part = row.astype(BF16).astype(F32)
            block = jnp.where(place == t // HD * 3 + i, part, block)
            row = row - part
    return block.astype(BF16)


def unpack_level(block, t, n):
    i = t // HD * 3
    rows = block.astype(F32)
    row = rows[i : i + 1] + rows[i + 1 : i + 2] + rows[i + 2 : i + 3]
    return jnp.sum(jnp.where(diagonal(n), row, 0.0), axis=1, keepdims=True)


def last_body(q_ref, acc_ref, stat_ref, *refs):
    parts, outs = refs[:-4], refs[-4:]
    acc, top, total = over_parts(q_ref[0], parts, kept(acc_ref, stat_ref))
    mean = (acc / total).astype(BF16)
    level = top * SCALE2 + jnp.log2(total)
    for tile in range(2):

        @pl.when(pl.program_id(1) == tile)
        def _():
            for i in range(2):
                out = outs[tile * 2 + i]
                out[0, :SITE] = mean[i * SITE : (i + 1) * SITE]
                out[0, SITE:] = pack_level(level[i * SITE : (i + 1) * SITE])


def head_spec(*shape):
    return pl.BlockSpec((1,) + shape, lambda h, t, *_: (h,) + (0,) * len(shape))


TILE_SPEC = pl.BlockSpec((1, TILE, HD), lambda h, t, *_: (h, t, 0))


def key_specs(part):
    if part.ndim == 3:
        return [head_spec(*part.shape[1:])]
    return [pl.BlockSpec((1, 1) + part.shape[2:], lambda h, t, *_, i=i: (i, h, 0, 0)) for i in range(2)]


def attend(body, name, parts, extra, extra_specs, outs, out_specs, prefetch=()):
    keys = sum(p.shape[-2] for p in parts)
    specs, args = list(extra_specs), list(extra)
    for p in parts:
        new = key_specs(p)
        specs += new
        args += [p] * len(new)
    return pl.pallas_call(
        body,
        out_shape=[jax.ShapeDtypeStruct((3,) + s, t) for s, t in outs],
        grid_spec=pltpu.PrefetchScalarGridSpec(
            num_scalar_prefetch=len(prefetch), grid=(3, 2), in_specs=specs, out_specs=out_specs
        ),
        compiler_params=pltpu.CompilerParams(vmem_limit_bytes=VMEM),
        cost_estimate=pl.CostEstimate(
            flops=24 * TILE * keys * HD, bytes_accessed=keys * 1536 + 6000000, transcendentals=6 * TILE * keys
        ),
        name=name,
    )(*prefetch, *args)


STATE = [((2 * TILE, HD), F32)] * 2


def merge_body(*refs):
    sites, outs = refs[:4], refs[4:]
    for t in range(0, SITE, HD):
        n = min(HD, SITE - t)
        levels = [unpack_level(s[0, SITE:], t, n) for s in sites]
        peak = functools.reduce(jnp.maximum, levels)
        weights = [jnp.exp2(level - peak) for level in levels]
        mixed = sum(w * s[0, t : t + n].astype(F32) for w, s in zip(weights, sites))
        mixed = (mixed / sum(weights)).astype(BF16)
        if t < VIDEO:
            for i in range(0, n, 64):
                outs[(t + i) // 64][0, :64] = mixed[i : i + 64]
        else:
            for out in outs:
                out[0, 64:] = mixed


def merge(sites):
    spec = lambda rows: pl.BlockSpec((1, rows, HD), lambda h: (h, 0, 0))
    return pl.pallas_call(
        merge_body,
        out_shape=[jax.ShapeDtypeStruct((3, 64 + TEXT, HD), BF16)] * 4,
        grid=(3,),
        in_specs=[spec(SITE + STATS)] * 4,
        out_specs=[spec(64 + TEXT)] * 4,
        compiler_params=pltpu.CompilerParams(vmem_limit_bytes=VMEM),
        name="merge",
    )(*sites)


def finish_body(*refs):
    messages, (video, text) = refs[:4], refs[4:]
    y, zb = lax.axis_index("y"), lax.axis_index("zb")
    for m in range(4):
        group = group_of(m)
        video[pl.ds(group * 3, 3)] = messages[m][:, :64]

        @pl.when(group // 2 == zb)
        def _():
            for h in range(3):
                rows = messages[m][h, 64:].astype(F32)
                own = jnp.zeros((4, HD), F32)
                for i in range(4):
                    own = jnp.where(y == i, rows[4 * i : 4 * i + 4], own)
                text[lax.rem(group, 2) * 3 + h] = own.astype(BF16)


def finish(messages):
    return pl.pallas_call(
        finish_body,
        out_shape=[jax.ShapeDtypeStruct((12, 64, HD), BF16), jax.ShapeDtypeStruct((6, 4, HD), BF16)],
        grid=(1,),
        in_specs=[whole(3, 64 + TEXT, HD)] * 4,
        out_specs=[whole(12, 64, HD), whole(6, 4, HD)],
        compiler_params=pltpu.CompilerParams(vmem_limit_bytes=VMEM),
        name="finish",
    )(*messages)


def local(video_q, video_k, video_v, positions, text_q, text_k, text_v, text_count):
    flat = lambda a: jnp.transpose(a, (1, 0, 2))
    out = prepare(flat(video_q), flat(video_k), flat(video_v), positions, flat(text_q), flat(text_k), flat(text_v))
    kv, q, text, text_rows = out[:4], out[4:8], out[8], out[9]
    along_y = lambda v, m: shift(v, "y", MOVES[m])
    block = jnp.concatenate([kv[0]] + [along_y(kv[m], m) for m in range(1, 4)], axis=2)
    right, left = z_shift(block, 1), z_shift(block, -1)
    text_sent = to_far_half(text)
    site = jnp.concatenate([q[0]] + [along_y(q[m], m) for m in range(1, 4)] + [text_rows], axis=1)
    queries = jnp.concatenate([site] + [shift(site, "x", -d) for d in MOVES[1:]], axis=1)

    right2, left2 = z_shift(right, 1), z_shift(left, -1)
    pack = head_spec(2 * SHARE, HD)
    acc, stat = attend(
        first_body,
        "attend_first",
        [block, right, left],
        [queries, text, text_sent],
        [TILE_SPEC, pack, pack],
        STATE,
        [TILE_SPEC] * 2,
        prefetch=(text_count,),
    )
    right3, left3 = z_shift(right2, 1), z_shift(left2, -1)
    specs = [TILE_SPEC] * 3
    acc, stat = attend(next_body, "attend_2", [right2, left2], [queries, acc, stat], specs, STATE, [TILE_SPEC] * 2)
    far_k, far_v = z_shift(right3[0], 1), z_shift(left3[1], -1)
    acc, stat = attend(next_body, "attend_3", [right3, left3], [queries, acc, stat], specs, STATE, [TILE_SPEC] * 2)
    sites = attend(
        last_body,
        "attend_last",
        [far_k, far_v],
        [queries, acc, stat],
        specs,
        [((SITE + STATS, HD), BF16)] * 4,
        [head_spec(SITE + STATS, HD)] * 4,
    )
    done = merge([sites[0]] + [shift(sites[i], "x", MOVES[i]) for i in range(1, 4)])
    video, text = finish([done[0]] + [shift(done[m], "y", -MOVES[m]) for m in range(1, 4)])
    return flat(video), flat(text)


def solution(mesh):
    fine = Mesh(mesh.devices.reshape(2, 4, 2, 2, 4, 2), ("grp", "x", "za", "zp", "y", "zb"))
    ctx = ("x", "za", "zp", "y")
    tokens = P(ctx + ("zb",), "grp", None)
    text = P(None, ("grp", "zb"), None)
    return jax.shard_map(
        local,
        mesh=fine,
        in_specs=(tokens, tokens, tokens, P(None, ctx + ("zb",)), text, text, text, P()),
        out_specs=(tokens, P(ctx, ("grp", "zb"), None)),
        check_vma=False,
    )
```

time: 130 us -> 118 us (0.908)
  the two profiles are of different devices: /device:TPU:32 before, /device:TPU:24 now
where the time goes in v3:
time: 118 us; the launch traced here: 117 us
  starting transfers between devices  41.8 us (35%)
  Pallas kernels  37.9 us (32%)
  waiting for transfers between devices  30.5 us (26%)
  local copies, waits for them, and re-layouts  5.39 us (5%)
  between operations  1.54 us (1%)
    pallas_call x4, Pallas kernels, attend(): pl.pallas_call(body, out_shape=[jax.ShapeDtypeStruct((3,) + s, t) for s,...  30.3 us
    ppermute x8, starting transfers between devices, z_shift(): lax.ppermute(v, ZAXES, [(line(z), line((z + step) % 8)) for z in range(8)])  20.6 us
    ppermute x15, starting transfers between devices, shift(): return lax.ppermute(v, axis, [(i, (i + step) % 4) for i in range(4)])  19.9 us
    ppermute x15, waiting for transfers between devices, shift(): return lax.ppermute(v, axis, [(i, (i + step) % 4) for i in range(4)])  18.5 us
    ppermute x8, waiting for transfers between devices, z_shift(): lax.ppermute(v, ZAXES, [(line(z), line((z + step) % 8)) for z in range(8)])  12 us
    unnamed x43, local copies, waits for them, and re-layouts  4.6 us
    pallas_call x1, Pallas kernels, merge(): pl.pallas_call(merge_body, out_shape=[jax.ShapeDtypeStruct((3, 64 + TEXT,...  3.19 us
    pallas_call x1, Pallas kernels, prepare(): pl.pallas_call(prepare_body, out_shape=[jax.ShapeDtypeStruct(o, BF16) for...  2.72 us
  transfers between devices with their start and end apart: 24, of which 14 were waited for; matrix products, arithmetic and copies ran while one was open for 2% of the time, Pallas kernels for 20%

profile of v3, /device:TPU:24, one launch (start us, length us, event | category | flops | bytes accessed | tf_op | source)
XLA Modules:
  0.0 117.1 jit_solution(17632201818376405805)
XLA Ops:
  0.6 2.7 %prepare.1 = (bf16[2,3,64,128]{3,2,1,0:T(8,128)(2,1)}, bf16[2,3,64,128]{3,2,1,0:T(8,128)(2,1)}, bf16[2,3,64,128]{3,2,1,0:T(8,128)(2,1)}, bf16[2,3,64,128]{3,2,1,...) custom-call(bf16[12,64,128]{2,1,0:T(8,128)(2,1)} %bitcast.15, ...), custom_call_target="tpu_custom_call" | custom-call | flops 50000000 | bytes 3000000 | tf_op jit(solution)/shard_map/prepare/pallas_call | solution.py:101
  3.4 2.0 %collective-permute-start.7 = (bf16[2,3,64,128]{3,2,1,0:T(8,128)(2,1)}, bf16[2,3,64,128]{3,2,1,0:T(8,128)(2,1)S(1)}, u32[]{:S(2)}, u32[]{:S(2)}) collective-permute-start(bf16[2,3,64,128]{3,2,1,0:T(8,128)(2,1)} %get-tuple-element.35), channel_id=1, source_target_pairs={{0,2},{2,4},{4,6},{6,0},{1,3},{3,5},{5,7},{7,1},{8,10},{10,12},{12... | collective-permute-start | bytes 294920 | tf_op jit(solution)/shard_map/ppermute | solution.py:51
  5.5 1.5 %collective-permute-start.9 = (bf16[2,3,64,128]{3,2,1,0:T(8,128)(2,1)}, bf16[2,3,64,128]{3,2,1,0:T(8,128)(2,1)S(1)}, u32[]{:S(2)}, u32[]{:S(2)}) collective-permute-start(bf16[2,3,64,128]{3,2,1,0:T(8,128)(2,1)} %get-tuple-element.37), channel_id=1, source_target_pairs={{0,4},{2,6},{4,0},{6,2},{1,5},{3,7},{5,1},{7,3},{8,12},{10,14},{12... | collective-permute-start | bytes 294920 | tf_op jit(solution)/shard_map/ppermute | solution.py:51
  6.9 0.9 constant_dynamic-update-slice_fusion.16
  7.8 1.1 collective-permute-done.7
  8.9 3.9 %collective-permute-done.8 = bf16[2,3,64,128]{3,2,1,0:T(8,128)(2,1)S(1)} collective-permute-done((bf16[2,3,64,128]{3,2,1,0:T(8,128)(2,1)}, bf16[2,3,64,128]{3,2,1,0:T(8,128)(2,1)S(1)}, u32[]{:S(2)}, u32[]{:S(2)}) %collective-permute-start.8) | collective-permute-done | bytes 98336 | tf_op jit(solution)/shard_map/ppermute | solution.py:51
  12.9 0.9 collective-permute-start.10
  13.8 1.4 %collective-permute-start = (bf16[3,64,128]{2,1,0:T(8,128)(2,1)}, bf16[3,64,128]{2,1,0:T(8,128)(2,1)S(1)}, u32[]{:S(2)}, u32[]{:S(2)}) collective-permute-start(bf16[3,64,128]{2,1,0:T(8,128)(2,1)} %get-tuple-element.29), channel_id=1, source_target_pairs={{0,2},{2,4},{4,6},{6,0},{1,3},{3,5},{5,7},{7,1},{8,10},{10,12},{12... | collective-permute-start | bytes 147464 | tf_op jit(solution)/shard_map/ppermute | solution.py:51
  15.2 0.6 collective-permute-start.1
  15.8 1.7 %collective-permute-start.2 = (bf16[3,64,128]{2,1,0:T(8,128)(2,1)}, bf16[3,64,128]{2,1,0:T(8,128)(2,1)S(1)}, u32[]{:S(2)}, u32[]{:S(2)}) collective-permute-start(bf16[3,64,128]{2,1,0:T(8,128)(2,1)} %get-tuple-element.31), channel_id=1, source_target_pairs={{0,4},{2,6},{4,0},{6,2},{1,5},{3,7},{5,1},{7,3},{8,12},{10,14},{12... | collective-permute-start | bytes 147464 | tf_op jit(solution)/shard_map/ppermute | solution.py:51
  17.6 4.0 %collective-permute-start.11 = (bf16[2,3,256,128]{3,2,1,0:T(8,128)(2,1)S(1)}, bf16[2,3,256,128]{3,2,1,0:T(8,128)(2,1)S(1)}, u32[]{:S(2)}, u32[]{:S(2)}) collective-permute-start(bf16[2,3,256,128]{3,2,1,0:T(8,128)(2,1)S(1)} %constant_dynamic-update-slice_fusion.13.refs_0_.refs_1_), channel_id=1, source_target_pairs={{0,25},{8,0},{16,8},{24,16},{1,24},{9,1},{17,9},{25,17},{2,27},{10... | collective-permute-start | bytes 1179656 | tf_op jit(solution)/shard_map/ppermute | solution.py:56
  21.6 0.8 constant_dynamic-update-slice_fusion.4
  22.5 3.2 %collective-permute-done.10.refs_2_.refs_3_ = bf16[2,3,256,128]{3,2,1,0:T(8,128)(2,1)S(1)} collective-permute-done((bf16[2,3,256,128]{3,2,1,0:T(8,128)(2,1)S(1)}, bf16[2,3,256,128]{3,2,1,0:T(8,128)(2,1)S(1)}, u32[]{:S(2)}, u32[]{:S(2)}) %collective-permute-start.10) | collective-permute-done | bytes 393248 | tf_op jit(solution)/shard_map/ppermute | solution.py:56
  25.7 2.0 %collective-permute-done.11.refs_4_.refs_5_ = bf16[2,3,256,128]{3,2,1,0:T(8,128)(2,1)S(1)} collective-permute-done((bf16[2,3,256,128]{3,2,1,0:T(8,128)(2,1)S(1)}, bf16[2,3,256,128]{3,2,1,0:T(8,128)(2,1)S(1)}, u32[]{:S(2)}, u32[]{:S(2)}) %collective-permute-start.11) | collective-permute-done | bytes 393248 | tf_op jit(solution)/shard_map/ppermute | solution.py:56
  27.7 3.7 %collective-permute-start.13 = (bf16[2,3,256,128]{3,2,1,0:T(8,128)(2,1)S(1)}, bf16[2,3,256,128]{3,2,1,0:T(8,128)(2,1)S(1)}, u32[]{:S(2)}, u32[]{:S(2)}) collective-permute-start(bf16[2,3,256,128]{3,2,1,0:T(8,128)(2,1)S(1)} %collective-permute-done.11.refs_4_.refs_5_), channel_id=1, source_target_pairs={{0,25},{8,0},{16,8},{24,16},{1,24},{9,1},{17,9},{25,17},{2,27},{10... | collective-permute-start | bytes 1179656 | tf_op jit(solution)/shard_map/ppermute | solution.py:56
  31.4 0.7 constant_dynamic-update-slice_fusion
  32.1 2.8 %collective-permute-start.3 = (bf16[3,272,128]{2,1,0:T(8,128)(2,1)S(1)}, bf16[3,272,128]{2,1,0:T(8,128)(2,1)S(1)}, u32[]{:S(2)}, u32[]{:S(2)}) collective-permute-start(bf16[3,272,128]{2,1,0:T(8,128)(2,1)S(1)} %get-tuple-element.62), channel_id=1, source_target_pairs={{0,96},{32,0},{64,32},{96,64},{1,97},{33,1},{65,33},{97,65},{2,98}... | collective-permute-start | bytes 626696 | tf_op jit(solution)/shard_map/ppermute | solution.py:51
  34.8 1.0 collective-permute-done.12.refs_0_.refs_1_
  35.9 1.3 %collective-permute-start.6 = (bf16[3,128,128]{2,1,0:T(8,128)(2,1)}, bf16[3,128,128]{2,1,0:T(8,128)(2,1)S(1)}, u32[]{:S(2)}, u32[]{:S(2)}) collective-permute-start(bf16[3,128,128]{2,1,0:T(8,128)(2,1)} %get-tuple-element.33.mine), channel_id=1, source_target_pairs={{0,1},{2,3},{5,4},{7,6},{8,9},{10,11},{13,12},{15,14},{16,17},{18,... | collective-permute-start | bytes 294920 | tf_op jit(solution)/shard_map/ppermute | solution.py:60
  37.8 0.3 collective-permute-done.3
  38.2 2.8 %collective-permute-start.5 = (bf16[3,272,128]{2,1,0:T(8,128)(2,1)S(1)}, bf16[3,272,128]{2,1,0:T(8,128)(2,1)S(1)}, u32[]{:S(2)}, u32[]{:S(2)}) collective-permute-start(bf16[3,272,128]{2,1,0:T(8,128)(2,1)S(1)} %get-tuple-element.62), channel_id=1, source_target_pairs={{0,64},{32,96},{64,0},{96,32},{1,65},{33,97},{65,1},{97,33},{2,66}... | collective-permute-start | bytes 626696 | tf_op jit(solution)/shard_map/ppermute | solution.py:51
  41.0 7.9 %collective-permute-start.15 = (bf16[2,3,256,128]{3,2,1,0:T(8,128)(2,1)S(1)}, bf16[2,3,256,128]{3,2,1,0:T(8,128)(2,1)S(1)}, u32[]{:S(2)}, u32[]{:S(2)}) collective-permute-start(bf16[2,3,256,128]{3,2,1,0:T(8,128)(2,1)S(1)} %collective-permute-done.13.refs_2_.refs_3_), channel_id=1, source_target_pairs={{0,25},{8,0},{16,8},{24,16},{1,24},{9,1},{17,9},{25,17},{2,27},{10... | collective-permute-start | bytes 1179656 | tf_op jit(solution)/shard_map/ppermute | solution.py:56
  49.0 0.4 collective-permute-done.14.refs_0_.refs_1_
  49.4 0.3 collective-permute-start.16
  49.7 5.5 %collective-permute-done.15.refs_2_.refs_3_ = bf16[2,3,256,128]{3,2,1,0:T(8,128)(2,1)S(1)} collective-permute-done((bf16[2,3,256,128]{3,2,1,0:T(8,128)(2,1)S(1)}, bf16[2,3,256,128]{3,2,1,0:T(8,128)(2,1)S(1)}, u32[]{:S(2)}, u32[]{:S(2)}) %collective-permute-start.15) | collective-permute-done | bytes 393248 | tf_op jit(solution)/shard_map/ppermute | solution.py:56
  55.2 3.8 %collective-permute-start.17 = (bf16[3,256,128]{2,1,0:T(8,128)(2,1)S(1)}, bf16[3,256,128]{2,1,0:T(8,128)(2,1)S(1)}, u32[]{:S(2)}, u32[]{:S(2)}) collective-permute-start(bf16[3,256,128]{2,1,0:T(8,128)(2,1)S(1)} %slice_bitcast_fusion), channel_id=1, source_target_pairs={{0,25},{8,0},{16,8},{24,16},{1,24},{9,1},{17,9},{25,17},{2,27},{10... | collective-permute-start | bytes 589832 | tf_op jit(solution)/shard_map/ppermute | solution.py:56
  59.0 0.6 copy-done.16
  59.6 9.0 %attend_first.1 = (f32[3,1088,128]{2,1,0:T(8,128)}, f32[3,1088,128]{2,1,0:T(8,128)}) custom-call(s32[1]{0:T(128)S(6)} %copy.26.count_ref, bf16[3,1088,128]{2,1,0:T(8,128)(2,1)} %copy-done, bf16[3,128,128]{2,1,0:T(8,128)(2,1)} %get-tuple-element.33.mine, bf16[3,128,128]{2,1,0:T(8,128)(2,1)} %copy-done.16, bf16[2,3,256,128]{3,2,1,0:T(8,128)(2,1)} %copy-done.13, ...), custom_call_target="tpu_custom_call" | custom-call | flops 1283457024 | bytes 7179648 | tf_op jit(solution)/shard_map/attend_first/pallas_call | solution.py:225
  68.7 7.3 %attend_2.1 = (f32[3,1088,128]{2,1,0:T(8,128)}, f32[3,1088,128]{2,1,0:T(8,128)}) custom-call(bf16[3,1088,128]{2,1,0:T(8,128)(2,1)} %copy-done, f32[3,1088,128]{2,1,0:T(8,128)} %get-tuple-element.38.acc_ref, f32[3,1088,128]{2,1,0:T(8,128)} %get-tuple-element.39.stat_ref, bf16[2,3,256,128]{3,2,1,0:T(8,128)(2,1)} %copy-done.3, ...), custom_call_target="tpu_custom_call" | custom-call | flops 855638016 | bytes 6786432 | tf_op jit(solution)/shard_map/attend_2/pallas_call | solution.py:225
  76.0 7.3 %attend_3.1 = (f32[3,1088,128]{2,1,0:T(8,128)}, f32[3,1088,128]{2,1,0:T(8,128)}) custom-call(bf16[3,1088,128]{2,1,0:T(8,128)(2,1)} %copy-done, f32[3,1088,128]{2,1,0:T(8,128)} %get-tuple-element.40.acc_ref, f32[3,1088,128]{2,1,0:T(8,128)} %get-tuple-element.41.stat_ref, bf16[2,3,256,128]{3,2,1,0:T(8,128)(2,1)} %copy-done.1, ...), custom_call_target="tpu_custom_call" | custom-call | flops 855638016 | bytes 6786432 | tf_op jit(solution)/shard_map/attend_3/pallas_call | solution.py:225
  83.3 0.6 copy-done.8
  84.0 0.1 copy-done.9
  84.1 6.7 %attend_last.1 = (bf16[3,288,128]{2,1,0:T(8,128)(2,1)}, bf16[3,288,128]{2,1,0:T(8,128)(2,1)}, bf16[3,288,128]{2,1,0:T(8,128)(2,1)}, bf16[3,288,128]{2,1,0:T(8,128)(2,1)}) custom-call(bf16[3,1088,128]{2,1,0:T(8,128)(2,1)} %copy-done, f32[3,1088,128]{2,1,0:T(8,128)} %get-tuple-element.42.acc_ref, f32[3,1088,128]{2,1,0:T(8,128)} %get-tuple-element.43.stat_ref, ...), custom_call_target="tpu_custom_call" | custom-call | flops 855638016 | bytes 6786432 | tf_op jit(solution)/shard_map/attend_last/pallas_call | solution.py:225
  90.8 0.8 collective-permute-start.18
  91.6 2.5 %collective-permute-start.19 = (bf16[3,288,128]{2,1,0:T(8,128)(2,1)}, bf16[3,288,128]{2,1,0:T(8,128)(2,1)S(1)}, u32[]{:S(2)}, u32[]{:S(2)}) collective-permute-start(bf16[3,288,128]{2,1,0:T(8,128)(2,1)} %get-tuple-element.46), channel_id=1, source_target_pairs={{0,96},{32,0},{64,32},{96,64},{1,97},{33,1},{65,33},{97,65},{2,98}... | collective-permute-start | bytes 663560 | tf_op jit(solution)/shard_map/ppermute | solution.py:51
  94.1 4.1 %collective-permute-done.18.refs_1_ = bf16[3,288,128]{2,1,0:T(8,128)(2,1)S(1)} collective-permute-done((bf16[3,288,128]{2,1,0:T(8,128)(2,1)}, bf16[3,288,128]{2,1,0:T(8,128)(2,1)S(1)}, u32[]{:S(2)}, u32[]{:S(2)}) %collective-permute-start.18) | collective-permute-done | bytes 221216 | tf_op jit(solution)/shard_map/ppermute | solution.py:51
  98.2 2.1 %collective-permute-done.19.refs_2_ = bf16[3,288,128]{2,1,0:T(8,128)(2,1)S(1)} collective-permute-done((bf16[3,288,128]{2,1,0:T(8,128)(2,1)}, bf16[3,288,128]{2,1,0:T(8,128)(2,1)S(1)}, u32[]{:S(2)}, u32[]{:S(2)}) %collective-permute-start.19) | collective-permute-done | bytes 221216 | tf_op jit(solution)/shard_map/ppermute | solution.py:51
  100.2 1.5 %collective-permute-done.20.refs_3_ = bf16[3,288,128]{2,1,0:T(8,128)(2,1)S(1)} collective-permute-done((bf16[3,288,128]{2,1,0:T(8,128)(2,1)}, bf16[3,288,128]{2,1,0:T(8,128)(2,1)S(1)}, u32[]{:S(2)}, u32[]{:S(2)}) %collective-permute-start.20) | collective-permute-done | bytes 221216 | tf_op jit(solution)/shard_map/ppermute | solution.py:51
  101.7 0.7 copy-done.7
  102.4 3.2 %merge.1 = (bf16[3,80,128]{2,1,0:T(8,128)(2,1)}, bf16[3,80,128]{2,1,0:T(8,128)(2,1)}, bf16[3,80,128]{2,1,0:T(8,128)(2,1)}, bf16[3,80,128]{2,1,0:T(8,128)(2,1)}) custom-call(bf16[3,288,128]{2,1,0:T(8,128)(2,1)} %get-tuple-element.44.refs_0_, bf16[3,288,128]{2,1,0:T(8,128)(2,1)} %copy-done.5, bf16[3,288,128]{2,1,0:T(8,128)(2,1)} %copy-done.6, ...), custom_call_target="tpu_custom_call" | custom-call | tf_op jit(solution)/shard_map/merge/pallas_call | solution.py:261
  105.6 1.5 %collective-permute-start.21 = (bf16[3,80,128]{2,1,0:T(8,128)(2,1)}, bf16[3,80,128]{2,1,0:T(8,128)(2,1)S(1)}, u32[]{:S(2)}, u32[]{:S(2)}) collective-permute-start(bf16[3,80,128]{2,1,0:T(8,128)(2,1)} %get-tuple-element.49), channel_id=1, source_target_pairs={{0,6},{2,0},{4,2},{6,4},{1,7},{3,1},{5,3},{7,5},{8,14},{10,8},{12,... | collective-permute-start | bytes 184328 | tf_op jit(solution)/shard_map/ppermute | solution.py:51
  107.1 1.7 %collective-permute-start.22 = (bf16[3,80,128]{2,1,0:T(8,128)(2,1)}, bf16[3,80,128]{2,1,0:T(8,128)(2,1)S(1)}, u32[]{:S(2)}, u32[]{:S(2)}) collective-permute-start(bf16[3,80,128]{2,1,0:T(8,128)(2,1)} %get-tuple-element.50), channel_id=1, source_target_pairs={{0,2},{2,4},{4,6},{6,0},{1,3},{3,5},{5,7},{7,1},{8,10},{10,12},{12... | collective-permute-start | bytes 184328 | tf_op jit(solution)/shard_map/ppermute | solution.py:51
  108.9 0.4 collective-permute-start.23
  109.3 2.0 %collective-permute-done.21.refs_1_ = bf16[3,80,128]{2,1,0:T(8,128)(2,1)S(1)} collective-permute-done((bf16[3,80,128]{2,1,0:T(8,128)(2,1)}, bf16[3,80,128]{2,1,0:T(8,128)(2,1)S(1)}, u32[]{:S(2)}, u32[]{:S(2)}) %collective-permute-start.21) | collective-permute-done | bytes 61472 | tf_op jit(solution)/shard_map/ppermute | solution.py:51
  111.3 0.3 collective-permute-done.22.refs_2_
  111.6 3.2 %collective-permute-done.23.refs_3_ = bf16[3,80,128]{2,1,0:T(8,128)(2,1)S(1)} collective-permute-done((bf16[3,80,128]{2,1,0:T(8,128)(2,1)}, bf16[3,80,128]{2,1,0:T(8,128)(2,1)S(1)}, u32[]{:S(2)}, u32[]{:S(2)}) %collective-permute-start.23) | collective-permute-done | bytes 61472 | tf_op jit(solution)/shard_map/ppermute | solution.py:51
  114.8 0.6 copy-done.12
  115.4 1.7 %finish.1 = (bf16[12,64,128]{2,1,0:T(8,128)(2,1)}, bf16[6,4,128]{2,1,0:T(4,128)(2,1)}) custom-call(bf16[3,80,128]{2,1,0:T(8,128)(2,1)} %get-tuple-element.48.refs_0_, bf16[3,80,128]{2,1,0:T(8,128)(2,1)} %copy-done.10, bf16[3,80,128]{2,1,0:T(8,128)(2,1)} %copy-done.11, bf16[3,80,128]{2,1,0:T(8,128)(2,1)} %copy-done.12), custom_call_target="tpu_custom_call" | custom-call | tf_op jit(solution)/shard_map/finish/pallas_call | solution.py:290
  (55 shorter events, 0.4 us)
Async XLA Ops:
  3.4 5.6 %collective-permute-start.7 = (bf16[2,3,64,128]{3,2,1,0:T(8,128)(2,1)}, bf16[2,3,64,128]{3,2,1,0:T(8,128)(2,1)S(1)}, u32[]{:S(2)}, u32[]{:S(2)}) collective-permute-start(bf16[2,3,64,128]{3,2,1,0:T(8,128)(2,1)} %get-tuple-element.35), channel_id=1, source_target_pairs={{0,2},{2,4},{4,6},{6,0},{1,3},{3,5},{5,7},{7,1},{8,10},{10,12},{12... | collective-permute-start | bytes 294920 | tf_op jit(solution)/shard_map/ppermute | solution.py:51
  5.4 7.4 %collective-permute-start.8 = (bf16[2,3,64,128]{3,2,1,0:T(8,128)(2,1)}, bf16[2,3,64,128]{3,2,1,0:T(8,128)(2,1)S(1)}, u32[]{:S(2)}, u32[]{:S(2)}) collective-permute-start(bf16[2,3,64,128]{3,2,1,0:T(8,128)(2,1)} %get-tuple-element.36), channel_id=1, source_target_pairs={{0,6},{2,0},{4,2},{6,4},{1,7},{3,1},{5,3},{7,5},{8,14},{10,8},{12,... | collective-permute-start | bytes 294920 | tf_op jit(solution)/shard_map/ppermute | solution.py:51
  5.5 7.4 %collective-permute-start.9 = (bf16[2,3,64,128]{3,2,1,0:T(8,128)(2,1)}, bf16[2,3,64,128]{3,2,1,0:T(8,128)(2,1)S(1)}, u32[]{:S(2)}, u32[]{:S(2)}) collective-permute-start(bf16[2,3,64,128]{3,2,1,0:T(8,128)(2,1)} %get-tuple-element.37), channel_id=1, source_target_pairs={{0,4},{2,6},{4,0},{6,2},{1,5},{3,7},{5,1},{7,3},{8,12},{10,14},{12... | collective-permute-start | bytes 294920 | tf_op jit(solution)/shard_map/ppermute | solution.py:51
  12.9 46.1 %copy-start.13 = (bf16[2,3,256,128]{3,2,1,0:T(8,128)(2,1)}, bf16[2,3,256,128]{3,2,1,0:T(8,128)(2,1)S(1)}, u32[]{:S(2)}) copy-start(bf16[2,3,256,128]{3,2,1,0:T(8,128)(2,1)S(1)} %constant_dynamic-update-slice_fusion.13.refs_0_.refs_1_) | copy-start | bytes 1179652
  12.9 12.8 %collective-permute-start.10 = (bf16[2,3,256,128]{3,2,1,0:T(8,128)(2,1)S(1)}, bf16[2,3,256,128]{3,2,1,0:T(8,128)(2,1)S(1)}, u32[]{:S(2)}, u32[]{:S(2)}) collective-permute-start(bf16[2,3,256,128]{3,2,1,0:T(8,128)(2,1)S(1)} %constant_dynamic-update-slice_fusion.13.refs_0_.refs_1_), channel_id=1, source_target_pairs={{0,8},{8,16},{16,24},{24,1},{1,9},{9,17},{17,25},{25,0},{2,10},{10... | collective-permute-start | bytes 1179656 | tf_op jit(solution)/shard_map/ppermute | solution.py:56
  13.8 8.6 %collective-permute-start = (bf16[3,64,128]{2,1,0:T(8,128)(2,1)}, bf16[3,64,128]{2,1,0:T(8,128)(2,1)S(1)}, u32[]{:S(2)}, u32[]{:S(2)}) collective-permute-start(bf16[3,64,128]{2,1,0:T(8,128)(2,1)} %get-tuple-element.29), channel_id=1, source_target_pairs={{0,2},{2,4},{4,6},{6,0},{1,3},{3,5},{5,7},{7,1},{8,10},{10,12},{12... | collective-permute-start | bytes 147464 | tf_op jit(solution)/shard_map/ppermute | solution.py:51
  15.2 7.2 %collective-permute-start.1 = (bf16[3,64,128]{2,1,0:T(8,128)(2,1)}, bf16[3,64,128]{2,1,0:T(8,128)(2,1)S(1)}, u32[]{:S(2)}, u32[]{:S(2)}) collective-permute-start(bf16[3,64,128]{2,1,0:T(8,128)(2,1)} %get-tuple-element.30), channel_id=1, source_target_pairs={{0,6},{2,0},{4,2},{6,4},{1,7},{3,1},{5,3},{7,5},{8,14},{10,8},{12,... | collective-permute-start | bytes 147464 | tf_op jit(solution)/shard_map/ppermute | solution.py:51
  15.8 9.8 %collective-permute-start.2 = (bf16[3,64,128]{2,1,0:T(8,128)(2,1)}, bf16[3,64,128]{2,1,0:T(8,128)(2,1)S(1)}, u32[]{:S(2)}, u32[]{:S(2)}) collective-permute-start(bf16[3,64,128]{2,1,0:T(8,128)(2,1)} %get-tuple-element.31), channel_id=1, source_target_pairs={{0,4},{2,6},{4,0},{6,2},{1,5},{3,7},{5,1},{7,3},{8,12},{10,14},{12... | collective-permute-start | bytes 147464 | tf_op jit(solution)/shard_map/ppermute | solution.py:51
  17.6 10.1 %collective-permute-start.11 = (bf16[2,3,256,128]{3,2,1,0:T(8,128)(2,1)S(1)}, bf16[2,3,256,128]{3,2,1,0:T(8,128)(2,1)S(1)}, u32[]{:S(2)}, u32[]{:S(2)}) collective-permute-start(bf16[2,3,256,128]{3,2,1,0:T(8,128)(2,1)S(1)} %constant_dynamic-update-slice_fusion.13.refs_0_.refs_1_), channel_id=1, source_target_pairs={{0,25},{8,0},{16,8},{24,16},{1,24},{9,1},{17,9},{25,17},{2,27},{10... | collective-permute-start | bytes 1179656 | tf_op jit(solution)/shard_map/ppermute | solution.py:56
  25.7 33.3 %copy-start.14 = (bf16[2,3,256,128]{3,2,1,0:T(8,128)(2,1)}, bf16[2,3,256,128]{3,2,1,0:T(8,128)(2,1)S(1)}, u32[]{:S(2)}) copy-start(bf16[2,3,256,128]{3,2,1,0:T(8,128)(2,1)S(1)} %collective-permute-done.10.refs_2_.refs_3_) | copy-start | bytes 1179652
  25.7 10.2 %collective-permute-start.12 = (bf16[2,3,256,128]{3,2,1,0:T(8,128)(2,1)S(1)}, bf16[2,3,256,128]{3,2,1,0:T(8,128)(2,1)S(1)}, u32[]{:S(2)}, u32[]{:S(2)}) collective-permute-start(bf16[2,3,256,128]{3,2,1,0:T(8,128)(2,1)S(1)} %collective-permute-done.10.refs_2_.refs_3_), channel_id=1, source_target_pairs={{0,8},{8,16},{16,24},{24,1},{1,9},{9,17},{17,25},{25,0},{2,10},{10... | collective-permute-start | bytes 1179656 | tf_op jit(solution)/shard_map/ppermute | solution.py:56
  27.7 21.3 %copy-start.15 = (bf16[2,3,256,128]{3,2,1,0:T(8,128)(2,1)}, bf16[2,3,256,128]{3,2,1,0:T(8,128)(2,1)S(1)}, u32[]{:S(2)}) copy-start(bf16[2,3,256,128]{3,2,1,0:T(8,128)(2,1)S(1)} %collective-permute-done.11.refs_4_.refs_5_) | copy-start | bytes 1179652
  27.7 13.3 %collective-permute-start.13 = (bf16[2,3,256,128]{3,2,1,0:T(8,128)(2,1)S(1)}, bf16[2,3,256,128]{3,2,1,0:T(8,128)(2,1)S(1)}, u32[]{:S(2)}, u32[]{:S(2)}) collective-permute-start(bf16[2,3,256,128]{3,2,1,0:T(8,128)(2,1)S(1)} %collective-permute-done.11.refs_4_.refs_5_), channel_id=1, source_target_pairs={{0,25},{8,0},{16,8},{24,16},{1,24},{9,1},{17,9},{25,17},{2,27},{10... | collective-permute-start | bytes 1179656 | tf_op jit(solution)/shard_map/ppermute | solution.py:56
  32.1 6.1 %collective-permute-start.3 = (bf16[3,272,128]{2,1,0:T(8,128)(2,1)S(1)}, bf16[3,272,128]{2,1,0:T(8,128)(2,1)S(1)}, u32[]{:S(2)}, u32[]{:S(2)}) collective-permute-start(bf16[3,272,128]{2,1,0:T(8,128)(2,1)S(1)} %get-tuple-element.62), channel_id=1, source_target_pairs={{0,96},{32,0},{64,32},{96,64},{1,97},{33,1},{65,33},{97,65},{2,98}... | collective-permute-start | bytes 626696 | tf_op jit(solution)/shard_map/ppermute | solution.py:51
  34.8 14.1 %collective-permute-start.4 = (bf16[3,272,128]{2,1,0:T(8,128)(2,1)S(1)}, bf16[3,272,128]{2,1,0:T(8,128)(2,1)S(1)}, u32[]{:S(2)}, u32[]{:S(2)}) collective-permute-start(bf16[3,272,128]{2,1,0:T(8,128)(2,1)S(1)} %get-tuple-element.62), channel_id=1, source_target_pairs={{0,32},{32,64},{64,96},{96,0},{1,33},{33,65},{65,97},{97,1},{2,34}... | collective-permute-start | bytes 626696 | tf_op jit(solution)/shard_map/ppermute | solution.py:51
  35.9 32.8 %copy-start.3 = (bf16[2,3,256,128]{3,2,1,0:T(8,128)(2,1)}, bf16[2,3,256,128]{3,2,1,0:T(8,128)(2,1)S(1)}, u32[]{:S(2)}) copy-start(bf16[2,3,256,128]{3,2,1,0:T(8,128)(2,1)S(1)} %collective-permute-done.12.refs_0_.refs_1_) | copy-start | bytes 1179652
  35.9 13.5 %collective-permute-start.14 = (bf16[2,3,256,128]{3,2,1,0:T(8,128)(2,1)S(1)}, bf16[2,3,256,128]{3,2,1,0:T(8,128)(2,1)S(1)}, u32[]{:S(2)}, u32[]{:S(2)}) collective-permute-start(bf16[2,3,256,128]{3,2,1,0:T(8,128)(2,1)S(1)} %collective-permute-done.12.refs_0_.refs_1_), channel_id=1, source_target_pairs={{0,8},{8,16},{16,24},{24,1},{1,9},{9,17},{17,25},{25,0},{2,10},{10... | collective-permute-start | bytes 1179656 | tf_op jit(solution)/shard_map/ppermute | solution.py:56
  35.9 23.1 %collective-permute-start.6 = (bf16[3,128,128]{2,1,0:T(8,128)(2,1)}, bf16[3,128,128]{2,1,0:T(8,128)(2,1)S(1)}, u32[]{:S(2)}, u32[]{:S(2)}) collective-permute-start(bf16[3,128,128]{2,1,0:T(8,128)(2,1)} %get-tuple-element.33.mine), channel_id=1, source_target_pairs={{0,1},{2,3},{5,4},{7,6},{8,9},{10,11},{13,12},{15,14},{16,17},{18,... | collective-permute-start | bytes 294920 | tf_op jit(solution)/shard_map/ppermute | solution.py:60
  38.2 10.8 %collective-permute-start.5 = (bf16[3,272,128]{2,1,0:T(8,128)(2,1)S(1)}, bf16[3,272,128]{2,1,0:T(8,128)(2,1)S(1)}, u32[]{:S(2)}, u32[]{:S(2)}) collective-permute-start(bf16[3,272,128]{2,1,0:T(8,128)(2,1)S(1)} %get-tuple-element.62), channel_id=1, source_target_pairs={{0,64},{32,96},{64,0},{96,32},{1,65},{33,97},{65,1},{97,33},{2,66}... | collective-permute-start | bytes 626696 | tf_op jit(solution)/shard_map/ppermute | solution.py:51
  41.0 27.7 %copy-start.4 = (bf16[2,3,256,128]{3,2,1,0:T(8,128)(2,1)}, bf16[2,3,256,128]{3,2,1,0:T(8,128)(2,1)S(1)}, u32[]{:S(2)}) copy-start(bf16[2,3,256,128]{3,2,1,0:T(8,128)(2,1)S(1)} %collective-permute-done.13.refs_2_.refs_3_) | copy-start | bytes 1179652
  41.0 14.2 %collective-permute-start.15 = (bf16[2,3,256,128]{3,2,1,0:T(8,128)(2,1)S(1)}, bf16[2,3,256,128]{3,2,1,0:T(8,128)(2,1)S(1)}, u32[]{:S(2)}, u32[]{:S(2)}) collective-permute-start(bf16[2,3,256,128]{3,2,1,0:T(8,128)(2,1)S(1)} %collective-permute-done.13.refs_2_.refs_3_), channel_id=1, source_target_pairs={{0,25},{8,0},{16,8},{24,16},{1,24},{9,1},{17,9},{25,17},{2,27},{10... | collective-permute-start | bytes 1179656 | tf_op jit(solution)/shard_map/ppermute | solution.py:56
  49.0 9.9 %copy-start = (bf16[3,1088,128]{2,1,0:T(8,128)(2,1)}, bf16[3,1088,128]{2,1,0:T(8,128)(2,1)S(1)}, u32[]{:S(2)}) copy-start(bf16[3,1088,128]{2,1,0:T(8,128)(2,1)S(1)} %constant_dynamic-update-slice_fusion.5.q_ref) | copy-start | bytes 2506756
  49.4 19.3 %copy-start.1 = (bf16[2,3,256,128]{3,2,1,0:T(8,128)(2,1)}, bf16[2,3,256,128]{3,2,1,0:T(8,128)(2,1)S(1)}, u32[]{:S(2)}) copy-start(bf16[2,3,256,128]{3,2,1,0:T(8,128)(2,1)S(1)} %collective-permute-done.14.refs_0_.refs_1_) | copy-start | bytes 1179652
  49.4 33.9 %collective-permute-start.16 = (bf16[3,256,128]{2,1,0:T(8,128)(2,1)S(1)}, bf16[3,256,128]{2,1,0:T(8,128)(2,1)S(1)}, u32[]{:S(2)}, u32[]{:S(2)}) collective-permute-start(bf16[3,256,128]{2,1,0:T(8,128)(2,1)S(1)} %slice_bitcast_fusion.1), channel_id=1, source_target_pairs={{0,8},{8,16},{16,24},{24,1},{1,9},{9,17},{17,25},{25,0},{2,10},{10... | collective-permute-start | bytes 589832 | tf_op jit(solution)/shard_map/ppermute | solution.py:56
  55.2 13.5 %copy-start.2 = (bf16[2,3,256,128]{3,2,1,0:T(8,128)(2,1)}, bf16[2,3,256,128]{3,2,1,0:T(8,128)(2,1)S(1)}, u32[]{:S(2)}) copy-start(bf16[2,3,256,128]{3,2,1,0:T(8,128)(2,1)S(1)} %collective-permute-done.15.refs_2_.refs_3_) | copy-start | bytes 1179652
  55.2 28.1 %collective-permute-start.17 = (bf16[3,256,128]{2,1,0:T(8,128)(2,1)S(1)}, bf16[3,256,128]{2,1,0:T(8,128)(2,1)S(1)}, u32[]{:S(2)}, u32[]{:S(2)}) collective-permute-start(bf16[3,256,128]{2,1,0:T(8,128)(2,1)S(1)} %slice_bitcast_fusion), channel_id=1, source_target_pairs={{0,25},{8,0},{16,8},{24,16},{1,24},{9,1},{17,9},{25,17},{2,27},{10... | collective-permute-start | bytes 589832 | tf_op jit(solution)/shard_map/ppermute | solution.py:56
  59.0 0.6 copy-start.16
  83.3 0.7 copy-start.8
  83.3 0.7 copy-start.9
  90.8 7.4 %collective-permute-start.18 = (bf16[3,288,128]{2,1,0:T(8,128)(2,1)}, bf16[3,288,128]{2,1,0:T(8,128)(2,1)S(1)}, u32[]{:S(2)}, u32[]{:S(2)}) collective-permute-start(bf16[3,288,128]{2,1,0:T(8,128)(2,1)} %get-tuple-element.45), channel_id=1, source_target_pairs={{0,32},{32,64},{64,96},{96,0},{1,33},{33,65},{65,97},{97,1},{2,34}... | collective-permute-start | bytes 663560 | tf_op jit(solution)/shard_map/ppermute | solution.py:51
  91.6 8.6 %collective-permute-start.19 = (bf16[3,288,128]{2,1,0:T(8,128)(2,1)}, bf16[3,288,128]{2,1,0:T(8,128)(2,1)S(1)}, u32[]{:S(2)}, u32[]{:S(2)}) collective-permute-start(bf16[3,288,128]{2,1,0:T(8,128)(2,1)} %get-tuple-element.46), channel_id=1, source_target_pairs={{0,96},{32,0},{64,32},{96,64},{1,97},{33,1},{65,33},{97,65},{2,98}... | collective-permute-start | bytes 663560 | tf_op jit(solution)/shard_map/ppermute | solution.py:51
  94.1 7.6 %collective-permute-start.20 = (bf16[3,288,128]{2,1,0:T(8,128)(2,1)}, bf16[3,288,128]{2,1,0:T(8,128)(2,1)S(1)}, u32[]{:S(2)}, u32[]{:S(2)}) collective-permute-start(bf16[3,288,128]{2,1,0:T(8,128)(2,1)} %get-tuple-element.47), channel_id=1, source_target_pairs={{0,64},{32,96},{64,0},{96,32},{1,65},{33,97},{65,1},{97,33},{2,66}... | collective-permute-start | bytes 663560 | tf_op jit(solution)/shard_map/ppermute | solution.py:51
  98.2 3.5 %copy-start.5 = (bf16[3,288,128]{2,1,0:T(8,128)(2,1)}, bf16[3,288,128]{2,1,0:T(8,128)(2,1)S(1)}, u32[]{:S(2)}) copy-start(bf16[3,288,128]{2,1,0:T(8,128)(2,1)S(1)} %collective-permute-done.18.refs_1_) | copy-start | bytes 663556
  100.2 1.5 %copy-start.6 = (bf16[3,288,128]{2,1,0:T(8,128)(2,1)}, bf16[3,288,128]{2,1,0:T(8,128)(2,1)S(1)}, u32[]{:S(2)}) copy-start(bf16[3,288,128]{2,1,0:T(8,128)(2,1)S(1)} %collective-permute-done.19.refs_2_) | copy-start | bytes 663556
  101.7 0.7 copy-start.7
  105.6 5.7 %collective-permute-start.21 = (bf16[3,80,128]{2,1,0:T(8,128)(2,1)}, bf16[3,80,128]{2,1,0:T(8,128)(2,1)S(1)}, u32[]{:S(2)}, u32[]{:S(2)}) collective-permute-start(bf16[3,80,128]{2,1,0:T(8,128)(2,1)} %get-tuple-element.49), channel_id=1, source_target_pairs={{0,6},{2,0},{4,2},{6,4},{1,7},{3,1},{5,3},{7,5},{8,14},{10,8},{12,... | collective-permute-start | bytes 184328 | tf_op jit(solution)/shard_map/ppermute | solution.py:51
  107.1 4.5 %collective-permute-start.22 = (bf16[3,80,128]{2,1,0:T(8,128)(2,1)}, bf16[3,80,128]{2,1,0:T(8,128)(2,1)S(1)}, u32[]{:S(2)}, u32[]{:S(2)}) collective-permute-start(bf16[3,80,128]{2,1,0:T(8,128)(2,1)} %get-tuple-element.50), channel_id=1, source_target_pairs={{0,2},{2,4},{4,6},{6,0},{1,3},{3,5},{5,7},{7,1},{8,10},{10,12},{12... | collective-permute-start | bytes 184328 | tf_op jit(solution)/shard_map/ppermute | solution.py:51
  108.9 5.9 %collective-permute-start.23 = (bf16[3,80,128]{2,1,0:T(8,128)(2,1)}, bf16[3,80,128]{2,1,0:T(8,128)(2,1)S(1)}, u32[]{:S(2)}, u32[]{:S(2)}) collective-permute-start(bf16[3,80,128]{2,1,0:T(8,128)(2,1)} %get-tuple-element.51), channel_id=1, source_target_pairs={{0,4},{2,6},{4,0},{6,2},{1,5},{3,7},{5,1},{7,3},{8,12},{10,14},{12... | collective-permute-start | bytes 184328 | tf_op jit(solution)/shard_map/ppermute | solution.py:51
  111.3 3.5 %copy-start.10 = (bf16[3,80,128]{2,1,0:T(8,128)(2,1)}, bf16[3,80,128]{2,1,0:T(8,128)(2,1)S(1)}, u32[]{:S(2)}) copy-start(bf16[3,80,128]{2,1,0:T(8,128)(2,1)S(1)} %collective-permute-done.21.refs_1_) | copy-start | bytes 184324
  111.6 3.2 %copy-start.11 = (bf16[3,80,128]{2,1,0:T(8,128)(2,1)}, bf16[3,80,128]{2,1,0:T(8,128)(2,1)S(1)}, u32[]{:S(2)}) copy-start(bf16[3,80,128]{2,1,0:T(8,128)(2,1)S(1)} %collective-permute-done.22.refs_2_) | copy-start | bytes 184324
  114.8 0.6 copy-start.12

commit v4 on v3

--- a/solution.py
+++ b/solution.py
@@ -71,7 +71,7 @@
 def prepare_body(q_ref, k_ref, v_ref, pos_ref, tq_ref, tk_ref, tv_ref, freq_ref, swap_ref, *outs):
     x, y = lax.axis_index("x"), lax.axis_index("y")
     low = lax.axis_index("za") * 2 + lax.axis_index("zp")
-    kv_out, q_out, text_out, text_q_out = outs[:4], outs[4:8], outs[8], outs[9]
+    messages, text_out, text_q_out = outs[:4], outs[4], outs[5]
     angles = lax.dot_general(
         pos_ref[...].astype(F32), freq_ref[...], TN, precision=lax.Precision.HIGHEST, preferred_element_type=F32
     )
@@ -84,9 +84,9 @@
 
     for m in range(4):
         heads = pl.ds(group_of(m) * 3, 3)
-        kv_out[m][0] = rotate(k_ref[heads])
-        kv_out[m][1] = v_ref[heads]
-        q_out[m][...] = rotate(q_ref[heads])
+        messages[m][0] = rotate(k_ref[heads])
+        messages[m][1] = v_ref[heads]
+        messages[m][2] = rotate(q_ref[heads])
 
     heads = pl.ds(lax.rem(y, 2) * 3, 3)
     share = pl.ds(pl.multiple_of(x * SHARE, SHARE), SHARE)
@@ -96,7 +96,7 @@
 
 
 def prepare(q, k, v, positions, tq, tk, tv):
-    outs = [(2, 3, 64, HD)] * 4 + [(3, 64, HD)] * 4 + [(3, 2 * SHARE, HD), (3, TEXT, HD)]
+    outs = [(3, 3, 64, HD)] * 4 + [(3, 2 * SHARE, HD), (3, TEXT, HD)]
     args = (q, k, v, positions, tq, tk, tv, jnp.asarray(FREQ), jnp.asarray(SWAP, BF16))
     return pl.pallas_call(
         prepare_body,
@@ -110,20 +110,25 @@
     )(*args)
 
 
+def widen(v, n):
+    return jnp.concatenate([v] * (n // HD), axis=1) if n >= HD else v[:, :n]
+
+
 def softmax_step(q, k, v, state, live=None):
     s = lax.dot_general(q, k, NT, preferred_element_type=F32)
     if live is not None:
         s = jnp.where(live(s.shape), s, -jnp.inf)
-    peak = jnp.max(s, axis=1, keepdims=True)
+    lanes = (s.shape[0], HD)
+    peak = jnp.broadcast_to(jnp.max(s, axis=1, keepdims=True) * SCALE2, lanes)
     if state is not None:
         acc, top, total = state
         peak = jnp.maximum(top, peak)
-    p = jnp.exp2(s * SCALE2 - peak * SCALE2)
-    add = jnp.sum(p, axis=1, keepdims=True)
+    p = jnp.exp2(s * SCALE2 - widen(peak, s.shape[1]))
+    add = jnp.broadcast_to(jnp.sum(p, axis=1, keepdims=True), lanes)
     mixed = jnp.dot(p.astype(BF16), v, preferred_element_type=F32)
     if state is None:
         return mixed, peak, add
-    alpha = jnp.exp2((top - peak) * SCALE2)
+    alpha = jnp.exp2(top - peak)
     return acc * alpha + mixed, peak, total * alpha + add
 
 
@@ -133,65 +138,62 @@
     return softmax_step(q, keys, values, state)
 
 
-def keep(state, acc_ref, stat_ref):
-    acc, top, total = state
-    acc_ref[0] = acc
-    lane = lax.broadcasted_iota(jnp.int32, acc.shape, 1)
-    stat_ref[0] = jnp.where(lane < 64, top, total)
-
-
-def kept(acc_ref, stat_ref):
-    stat = stat_ref[0]
-    first = lax.broadcasted_iota(jnp.int32, stat.shape, 1) < 64
-    top = jnp.max(jnp.where(first, stat, -jnp.inf), axis=1, keepdims=True)
-    return acc_ref[0], top, jnp.max(jnp.where(first, 0.0, stat), axis=1, keepdims=True)
+def rows_here():
+    return pl.program_id(0), pl.ds(pl.multiple_of(pl.program_id(1) * TILE, 16), TILE)
+
+
+def keep(state, refs):
+    for value, ref in zip(state, refs):
+        ref[rows_here()] = value
+
+
+def kept(refs):
+    return tuple(ref[rows_here()] for ref in refs)
 
 
 def first_body(count_ref, q_ref, mine, sent, *refs):
-    parts, (acc_out, stat_out) = refs[:-2], refs[-2:]
+    parts, outs = refs[:-3], refs[-3:]
     q = q_ref[0]
     state = over_parts(q, parts, None)
     here = lax.axis_index("y") // 2 == lax.axis_index("zb")
     text = jnp.where(here, mine[0].astype(F32), sent[0].astype(F32)).astype(BF16)
     left = count_ref[0] - lax.axis_index("x") * SHARE
     live = lambda shape: lax.broadcasted_iota(jnp.int32, shape, 1) < left
-    keep(softmax_step(q, text[:SHARE], text[SHARE:], state, live), acc_out, stat_out)
-
-
-def next_body(q_ref, acc_ref, stat_ref, *refs):
-    parts, (acc_out, stat_out) = refs[:-2], refs[-2:]
-    keep(over_parts(q_ref[0], parts, kept(acc_ref, stat_ref)), acc_out, stat_out)
-
-
-def diagonal(n):
-    return lax.broadcasted_iota(jnp.int32, (n, HD), 0) == lax.broadcasted_iota(jnp.int32, (n, HD), 1)
+    keep(softmax_step(q, text[:SHARE], text[SHARE:], state, live), outs)
+
+
+def next_body(q_ref, acc_ref, top_ref, total_ref, *refs):
+    parts, outs = refs[:-3], refs[-3:]
+    keep(over_parts(q_ref[0], parts, kept((acc_ref, top_ref, total_ref))), outs)
 
 
 def pack_level(level):
-    place = lax.broadcasted_iota(jnp.int32, (STATS, HD), 0)
-    block = jnp.zeros((STATS, HD), F32)
+    blocks = []
     for t in range(0, SITE, HD):
         n = min(HD, SITE - t)
-        row = jnp.sum(jnp.where(diagonal(n), level[t : t + n], 0.0), axis=0, keepdims=True)
+        lane = lax.broadcasted_iota(jnp.int32, (n, HD), 1)
+        rest, parts = level[t : t + n], jnp.zeros((n, HD), F32)
         for i in range(3):
-            part = row.astype(BF16).astype(F32)
-            block = jnp.where(place == t // HD * 3 + i, part, block)
-            row = row - part
-    return block.astype(BF16)
+            part = rest.astype(BF16).astype(F32)
+            parts = jnp.where(lane == t // HD * 3 + i, part, parts)
+            rest = rest - part
+        unit = (lane == lax.broadcasted_iota(jnp.int32, (n, HD), 0)).astype(F32).astype(BF16)
+        blocks.append(lax.dot_general(parts.astype(BF16), unit, TN, preferred_element_type=F32))
+    return sum(blocks)[:STATS].astype(BF16)
 
 
 def unpack_level(block, t, n):
-    i = t // HD * 3
-    rows = block.astype(F32)
-    row = rows[i : i + 1] + rows[i + 1 : i + 2] + rows[i + 2 : i + 3]
-    return jnp.sum(jnp.where(diagonal(n), row, 0.0), axis=1, keepdims=True)
-
-
-def last_body(q_ref, acc_ref, stat_ref, *refs):
+    first = t // HD * 3
+    place = lax.broadcasted_iota(jnp.int32, (STATS, HD), 0)
+    pick = ((place >= first) & (place < first + 3)).astype(F32).astype(BF16)
+    return lax.dot_general(block, pick, TN, preferred_element_type=F32)[:n]
+
+
+def last_body(q_ref, acc_ref, top_ref, total_ref, *refs):
     parts, outs = refs[:-4], refs[-4:]
-    acc, top, total = over_parts(q_ref[0], parts, kept(acc_ref, stat_ref))
+    acc, top, total = over_parts(q_ref[0], parts, kept((acc_ref, top_ref, total_ref)))
     mean = (acc / total).astype(BF16)
-    level = top * SCALE2 + jnp.log2(total)
+    level = top + jnp.log2(total)
     for tile in range(2):
 
         @pl.when(pl.program_id(1) == tile)
@@ -228,7 +230,7 @@
         grid_spec=pltpu.PrefetchScalarGridSpec(
             num_scalar_prefetch=len(prefetch), grid=(3, 2), in_specs=specs, out_specs=out_specs
         ),
-        compiler_params=pltpu.CompilerParams(vmem_limit_bytes=VMEM),
+        compiler_params=pltpu.CompilerParams(vmem_limit_bytes=VMEM // 2),
         cost_estimate=pl.CostEstimate(
             flops=24 * TILE * keys * HD, bytes_accessed=keys * 1536 + 6000000, transcendentals=6 * TILE * keys
         ),
@@ -236,7 +238,8 @@
     )(*prefetch, *args)
 
 
-STATE = [((2 * TILE, HD), F32)] * 2
+STATE = [((2 * TILE, HD), F32)] * 3
+STATE_SPECS = [pl.BlockSpec(memory_space=pltpu.VMEM)] * 3
 
 
 def merge_body(*refs):
@@ -301,36 +304,39 @@
 def local(video_q, video_k, video_v, positions, text_q, text_k, text_v, text_count):
     flat = lambda a: jnp.transpose(a, (1, 0, 2))
     out = prepare(flat(video_q), flat(video_k), flat(video_v), positions, flat(text_q), flat(text_k), flat(text_v))
-    kv, q, text, text_rows = out[:4], out[4:8], out[8], out[9]
-    along_y = lambda v, m: shift(v, "y", MOVES[m])
-    block = jnp.concatenate([kv[0]] + [along_y(kv[m], m) for m in range(1, 4)], axis=2)
+    own, text, text_rows = out[:4], out[4], out[5]
+    text_sent = to_far_half(text)
+    m = [own[0]] + [shift(own[i], "y", MOVES[i]) for i in range(1, 4)]
+    block = jnp.concatenate([v[:2] for v in m], axis=2)
+    block, text_sent = lax.optimization_barrier((block, text_sent))
     right, left = z_shift(block, 1), z_shift(block, -1)
-    text_sent = to_far_half(text)
-    site = jnp.concatenate([q[0]] + [along_y(q[m], m) for m in range(1, 4)] + [text_rows], axis=1)
+    site = jnp.concatenate([v[2] for v in m] + [text_rows], axis=1)
     queries = jnp.concatenate([site] + [shift(site, "x", -d) for d in MOVES[1:]], axis=1)
 
     right2, left2 = z_shift(right, 1), z_shift(left, -1)
     pack = head_spec(2 * SHARE, HD)
-    acc, stat = attend(
+    state = attend(
         first_body,
         "attend_first",
         [block, right, left],
         [queries, text, text_sent],
         [TILE_SPEC, pack, pack],
         STATE,
-        [TILE_SPEC] * 2,
+        STATE_SPECS,
         prefetch=(text_count,),
     )
+    right2, left2, *state = lax.optimization_barrier((right2, left2, *state))
     right3, left3 = z_shift(right2, 1), z_shift(left2, -1)
-    specs = [TILE_SPEC] * 3
-    acc, stat = attend(next_body, "attend_2", [right2, left2], [queries, acc, stat], specs, STATE, [TILE_SPEC] * 2)
+    specs = [TILE_SPEC] + STATE_SPECS
+    state = attend(next_body, "attend_2", [right2, left2], [queries, *state], specs, STATE, STATE_SPECS)
+    right3, left3, *state = lax.optimization_barrier((right3, left3, *state))
     far_k, far_v = z_shift(right3[0], 1), z_shift(left3[1], -1)
-    acc, stat = attend(next_body, "attend_3", [right3, left3], [queries, acc, stat], specs, STATE, [TILE_SPEC] * 2)
+    state = attend(next_body, "attend_3", [right3, left3], [queries, *state], specs, STATE, STATE_SPECS)
     sites = attend(
         last_body,
         "attend_last",
         [far_k, far_v],
-        [queries, acc, stat],
+        [queries, *state],
         specs,
         [((SITE + STATS, HD), BF16)] * 4,
         [head_spec(SITE + STATS, HD)] * 4,

time: 118 us -> 94.2 us (0.80)
  the two profiles are of different devices: /device:TPU:24 before, /device:TPU:32 now
where the time goes in v4:
time: 94.2 us; the launch traced here: 93.8 us
  starting transfers between devices  34.2 us (36%)
  waiting for transfers between devices  27.2 us (29%)
  Pallas kernels  26.9 us (29%)
  local copies, waits for them, and re-layouts  3.97 us (4%)
  between operations  1.49 us (2%)
    ppermute x12, waiting for transfers between devices, shift(): return lax.ppermute(v, axis, [(i, (i + step) % 4) for i in range(4)])  20 us
    pallas_call x4, Pallas kernels, attend(): pl.pallas_call(body, out_shape=[jax.ShapeDtypeStruct((3,) + s, t) for s,...  19.2 us
    ppermute x12, starting transfers between devices, shift(): return lax.ppermute(v, axis, [(i, (i + step) % 4) for i in range(4)])  16.8 us
    ppermute x8, starting transfers between devices, z_shift(): lax.ppermute(v, ZAXES, [(line(z), line((z + step) % 8)) for z in range(8)])  9.08 us
    ppermute x1, starting transfers between devices, to_far_half(): lax.ppermute(v, ('y', 'zb'), [(y * 2 + y // 2, y * 2 + 1 - y // 2) for y...  8.32 us
    ppermute x8, waiting for transfers between devices, z_shift(): lax.ppermute(v, ZAXES, [(line(z), line((z + step) % 8)) for z in range(8)])  7.16 us
    pallas_call x1, Pallas kernels, merge(): pl.pallas_call(merge_body, out_shape=[jax.ShapeDtypeStruct((3, 64 + TEXT,...  3.37 us
    unnamed x24, local copies, waits for them, and re-layouts  2.97 us
  transfers between devices with their start and end apart: 21, of which 13 were waited for; matrix products, arithmetic and copies ran while one was open for 2% of the time, Pallas kernels for 15%

profile of v4, /device:TPU:32, one launch (start us, length us, event | category | flops | bytes accessed | tf_op | source)
XLA Modules:
  0.0 93.8 jit_solution(17477857078237890447)
XLA Ops:
  0.6 2.7 %prepare.1 = (bf16[3,3,64,128]{3,2,1,0:T(8,128)(2,1)}, bf16[3,3,64,128]{3,2,1,0:T(8,128)(2,1)}, bf16[3,3,64,128]{3,2,1,0:T(8,128)(2,1)}, bf16[3,3,64,128]{3,2,1,...) custom-call(bf16[12,64,128]{2,1,0:T(8,128)(2,1)} %bitcast.36, bf16[12,64,128]{2,1,0:T(8,128)(2,1)} %bitcast.37, ...), custom_call_target="tpu_custom_call" | custom-call | flops 50000000 | bytes 3000000 | tf_op jit(solution)/shard_map/prepare/pallas_call | solution.py:101
  3.4 8.3 %collective-permute-start.6 = (bf16[3,128,128]{2,1,0:T(8,128)(2,1)}, bf16[3,128,128]{2,1,0:T(8,128)(2,1)S(1)}, u32[]{:S(2)}, u32[]{:S(2)}) collective-permute-start(bf16[3,128,128]{2,1,0:T(8,128)(2,1)} %get-tuple-element.44.mine), channel_id=1, source_target_pairs={{0,1},{2,3},{5,4},{7,6},{8,9},{10,11},{13,12},{15,14},{16,17},{18,... | collective-permute-start | bytes 294920 | tf_op jit(solution)/shard_map/ppermute | solution.py:60
  11.7 1.7 %collective-permute-start = (bf16[3,3,64,128]{3,2,1,0:T(8,128)(2,1)}, bf16[3,3,64,128]{3,2,1,0:T(8,128)(2,1)S(1)}, u32[]{:S(2)}, u32[]{:S(2)}) collective-permute-start(bf16[3,3,64,128]{3,2,1,0:T(8,128)(2,1)} %get-tuple-element.40), channel_id=1, source_target_pairs={{0,2},{2,4},{4,6},{6,0},{1,3},{3,5},{5,7},{7,1},{8,10},{10,12},{12... | collective-permute-start | bytes 442376 | tf_op jit(solution)/shard_map/ppermute | solution.py:51
  13.4 1.7 %collective-permute-start.1 = (bf16[3,3,64,128]{3,2,1,0:T(8,128)(2,1)}, bf16[3,3,64,128]{3,2,1,0:T(8,128)(2,1)S(1)}, u32[]{:S(2)}, u32[]{:S(2)}) collective-permute-start(bf16[3,3,64,128]{3,2,1,0:T(8,128)(2,1)} %get-tuple-element.41), channel_id=1, source_target_pairs={{0,6},{2,0},{4,2},{6,4},{1,7},{3,1},{5,3},{7,5},{8,14},{10,8},{12,... | collective-permute-start | bytes 442376 | tf_op jit(solution)/shard_map/ppermute | solution.py:51
  15.0 0.5 collective-permute-start.2
  15.5 0.9 slice.34
  16.4 0.8 bitcast_dynamic-update-slice_fusion.1
  17.3 2.8 %collective-permute-done = bf16[3,3,64,128]{3,2,1,0:T(8,128)(2,1)S(1)} collective-permute-done((bf16[3,3,64,128]{3,2,1,0:T(8,128)(2,1)}, bf16[3,3,64,128]{3,2,1,0:T(8,128)(2,1)S(1)}, u32[]{:S(2)}, u32[]{:S(2)}) %collective-permute-start) | collective-permute-done | bytes 147488 | tf_op jit(solution)/shard_map/ppermute | solution.py:51
  20.1 0.1 collective-permute-done.1
  20.2 1.7 %collective-permute-done.2 = bf16[3,3,64,128]{3,2,1,0:T(8,128)(2,1)S(1)} collective-permute-done((bf16[3,3,64,128]{3,2,1,0:T(8,128)(2,1)}, bf16[3,3,64,128]{3,2,1,0:T(8,128)(2,1)S(1)}, u32[]{:S(2)}, u32[]{:S(2)}) %collective-permute-start.2) | collective-permute-done | bytes 147488 | tf_op jit(solution)/shard_map/ppermute | solution.py:51
  21.9 0.0 collective-permute-done.6.sent
  21.9 1.1 %collective-permute-start.9 = (bf16[2,3,256,128]{3,2,1,0:T(8,128)(2,1)S(1)}, bf16[2,3,256,128]{3,2,1,0:T(8,128)(2,1)S(1)}, u32[]{:S(2)}, u32[]{:S(2)}) collective-permute-start(bf16[2,3,256,128]{3,2,1,0:T(8,128)(2,1)S(1)} %pad_maximum_fusion.refs_0_.refs_1_), channel_id=1, source_target_pairs={{0,25},{8,0},{16,8},{24,16},{1,24},{9,1},{17,9},{25,17},{2,27},{10... | collective-permute-start | bytes 1179656 | tf_op jit(solution)/shard_map/ppermute | solution.py:56
  23.0 1.0 %collective-permute-start.7 = (bf16[2,3,256,128]{3,2,1,0:T(8,128)(2,1)S(1)}, bf16[2,3,256,128]{3,2,1,0:T(8,128)(2,1)S(1)}, u32[]{:S(2)}, u32[]{:S(2)}) collective-permute-start(bf16[2,3,256,128]{3,2,1,0:T(8,128)(2,1)S(1)} %pad_maximum_fusion.refs_0_.refs_1_), channel_id=1, source_target_pairs={{0,8},{8,16},{16,24},{24,1},{1,9},{9,17},{17,25},{25,0},{2,10},{10... | collective-permute-start | bytes 1179656 | tf_op jit(solution)/shard_map/ppermute | solution.py:56
  24.1 2.8 %collective-permute-start.3 = (bf16[3,272,128]{2,1,0:T(8,128)(2,1)S(1)}, bf16[3,272,128]{2,1,0:T(8,128)(2,1)S(1)}, u32[]{:S(2)}, u32[]{:S(2)}) collective-permute-start(bf16[3,272,128]{2,1,0:T(8,128)(2,1)S(1)} %get-tuple-element.84), channel_id=1, source_target_pairs={{0,96},{32,0},{64,32},{96,64},{1,97},{33,1},{65,33},{97,65},{2,98}... | collective-permute-start | bytes 626696 | tf_op jit(solution)/shard_map/ppermute | solution.py:51
  27.0 0.0 collective-permute-start.4
  27.6 2.4 %collective-permute-start.5 = (bf16[3,272,128]{2,1,0:T(8,128)(2,1)S(1)}, bf16[3,272,128]{2,1,0:T(8,128)(2,1)S(1)}, u32[]{:S(2)}, u32[]{:S(2)}) collective-permute-start(bf16[3,272,128]{2,1,0:T(8,128)(2,1)S(1)} %get-tuple-element.84), channel_id=1, source_target_pairs={{0,64},{32,96},{64,0},{96,32},{1,65},{33,97},{65,1},{97,33},{2,66}... | collective-permute-start | bytes 626696 | tf_op jit(solution)/shard_map/ppermute | solution.py:51
  30.0 1.3 %collective-permute-done.9.refs_4_.refs_5_ = bf16[2,3,256,128]{3,2,1,0:T(8,128)(2,1)S(1)} collective-permute-done((bf16[2,3,256,128]{3,2,1,0:T(8,128)(2,1)S(1)}, bf16[2,3,256,128]{3,2,1,0:T(8,128)(2,1)S(1)}, u32[]{:S(2)}, u32[]{:S(2)}) %collective-permute-start.9) | collective-permute-done | bytes 393248 | tf_op jit(solution)/shard_map/ppermute | solution.py:56
  31.3 0.7 collective-permute-start.10
  32.0 0.0 collective-permute-done.7.refs_2_.refs_3_
  32.0 1.3 %collective-permute-start.8 = (bf16[2,3,256,128]{3,2,1,0:T(8,128)(2,1)S(1)}, bf16[2,3,256,128]{3,2,1,0:T(8,128)(2,1)S(1)}, u32[]{:S(2)}, u32[]{:S(2)}) collective-permute-start(bf16[2,3,256,128]{3,2,1,0:T(8,128)(2,1)S(1)} %collective-permute-done.7.refs_2_.refs_3_), channel_id=1, source_target_pairs={{0,8},{8,16},{16,24},{24,1},{1,9},{9,17},{17,25},{25,0},{2,10},{10... | collective-permute-start | bytes 1179656 | tf_op jit(solution)/shard_map/ppermute | solution.py:56
  33.4 3.5 %collective-permute-done.4 = bf16[3,272,128]{2,1,0:T(8,128)(2,1)S(1)} collective-permute-done((bf16[3,272,128]{2,1,0:T(8,128)(2,1)S(1)}, bf16[3,272,128]{2,1,0:T(8,128)(2,1)S(1)}, u32[]{:S(2)}, u32[]{:S(2)}) %collective-permute-start.4) | collective-permute-done | bytes 208928 | tf_op jit(solution)/shard_map/ppermute | solution.py:51
  36.9 0.0 collective-permute-done.5
  36.9 7.1 %attend_first.1 = (f32[3,1088,128]{2,1,0:T(8,128)S(1)}, f32[3,1088,128]{2,1,0:T(8,128)S(1)}, f32[3,1088,128]{2,1,0:T(8,128)S(1)}) custom-call(s32[1]{0:T(128)S(6)} %copy.23.count_ref, bf16[3,1088,128]{2,1,0:T(8,128)(2,1)S(1)} %constant_dynamic-update-slice_fusion.1.q_ref, bf16[3,128,128]{2,1,0:T(8,128)(2,1)S(1)} %copy-done.1, ...), custom_call_target="tpu_custom_call" | custom-call | flops 1283457024 | bytes 7179648 | tf_op jit(solution)/shard_map/attend_first/pallas_call | solution.py:227
  44.1 1.1 %collective-permute-start.11 = (bf16[2,3,256,128]{3,2,1,0:T(8,128)(2,1)S(1)}, bf16[2,3,256,128]{3,2,1,0:T(8,128)(2,1)S(1)}, u32[]{:S(2)}, u32[]{:S(2)}) collective-permute-start(bf16[2,3,256,128]{3,2,1,0:T(8,128)(2,1)S(1)} %collective-permute-done.8.refs_0_.refs_1_), channel_id=1, source_target_pairs={{0,8},{8,16},{16,24},{24,1},{1,9},{9,17},{17,25},{25,0},{2,10},{10... | collective-permute-start | bytes 1179656 | tf_op jit(solution)/shard_map/ppermute | solution.py:56
  45.2 1.0 %collective-permute-start.12 = (bf16[2,3,256,128]{3,2,1,0:T(8,128)(2,1)S(1)}, bf16[2,3,256,128]{3,2,1,0:T(8,128)(2,1)S(1)}, u32[]{:S(2)}, u32[]{:S(2)}) collective-permute-start(bf16[2,3,256,128]{3,2,1,0:T(8,128)(2,1)S(1)} %collective-permute-done.10.refs_2_.refs_3_), channel_id=1, source_target_pairs={{0,25},{8,0},{16,8},{24,16},{1,24},{9,1},{17,9},{25,17},{2,27},{10... | collective-permute-start | bytes 1179656 | tf_op jit(solution)/shard_map/ppermute | solution.py:56
  46.2 3.7 %attend_2.1 = (f32[3,1088,128]{2,1,0:T(8,128)S(1)}, f32[3,1088,128]{2,1,0:T(8,128)S(1)}, f32[3,1088,128]{2,1,0:T(8,128)S(1)}) custom-call(bf16[3,1088,128]{2,1,0:T(8,128)(2,1)S(1)} %constant_dynamic-update-slice_fusion.1.q_ref, f32[3,1088,128]{2,1,0:T(8,128)S(1)} %get-tuple-element.52.acc_ref, f32[3,1088,128]{2,1,0:T(8,128)S(1)} %get-tuple-element.53.top_ref, ...), custom_call_target="tpu_custom_call" | custom-call | flops 855638016 | bytes 6786432 | tf_op jit(solution)/shard_map/attend_2/pallas_call | solution.py:227
  49.8 2.9 %collective-permute-done.11.refs_0_.refs_1_ = bf16[2,3,256,128]{3,2,1,0:T(8,128)(2,1)S(1)} collective-permute-done((bf16[2,3,256,128]{3,2,1,0:T(8,128)(2,1)S(1)}, bf16[2,3,256,128]{3,2,1,0:T(8,128)(2,1)S(1)}, u32[]{:S(2)}, u32[]{:S(2)}) %collective-permute-start.11) | collective-permute-done | bytes 393248 | tf_op jit(solution)/shard_map/ppermute | solution.py:56
  52.7 1.0 %collective-permute-done.12.refs_2_.refs_3_ = bf16[2,3,256,128]{3,2,1,0:T(8,128)(2,1)S(1)} collective-permute-done((bf16[2,3,256,128]{3,2,1,0:T(8,128)(2,1)S(1)}, bf16[2,3,256,128]{3,2,1,0:T(8,128)(2,1)S(1)}, u32[]{:S(2)}, u32[]{:S(2)}) %collective-permute-start.12) | collective-permute-done | bytes 393248 | tf_op jit(solution)/shard_map/ppermute | solution.py:56
  53.7 2.8 %collective-permute-start.13 = (bf16[3,256,128]{2,1,0:T(8,128)(2,1)S(1)}, bf16[3,256,128]{2,1,0:T(8,128)(2,1)S(1)}, u32[]{:S(2)}, u32[]{:S(2)}) collective-permute-start(bf16[3,256,128]{2,1,0:T(8,128)(2,1)S(1)} %slice_bitcast_fusion.1), channel_id=1, source_target_pairs={{0,8},{8,16},{16,24},{24,1},{1,9},{9,17},{17,25},{25,0},{2,10},{10... | collective-permute-start | bytes 589832 | tf_op jit(solution)/shard_map/ppermute | solution.py:56
  56.6 0.0 collective-permute-start.14
  56.6 3.7 %attend_3.1 = (f32[3,1088,128]{2,1,0:T(8,128)S(1)}, f32[3,1088,128]{2,1,0:T(8,128)S(1)}, f32[3,1088,128]{2,1,0:T(8,128)S(1)}) custom-call(bf16[3,1088,128]{2,1,0:T(8,128)(2,1)S(1)} %constant_dynamic-update-slice_fusion.1.q_ref, f32[3,1088,128]{2,1,0:T(8,128)S(1)} %get-tuple-element.58.acc_ref, f32[3,1088,128]{2,1,0:T(8,128)S(1)} %get-tuple-element.59.top_ref, ...), custom_call_target="tpu_custom_call" | custom-call | flops 855638016 | bytes 6786432 | tf_op jit(solution)/shard_map/attend_3/pallas_call | solution.py:227
  60.3 2.0 %collective-permute-done.14.refs_1_ = bf16[3,256,128]{2,1,0:T(8,128)(2,1)S(1)} collective-permute-done((bf16[3,256,128]{2,1,0:T(8,128)(2,1)S(1)}, bf16[3,256,128]{2,1,0:T(8,128)(2,1)S(1)}, u32[]{:S(2)}, u32[]{:S(2)}) %collective-permute-start.14) | collective-permute-done | bytes 196640 | tf_op jit(solution)/shard_map/ppermute | solution.py:56
  62.3 4.8 %attend_last.1 = (bf16[3,288,128]{2,1,0:T(8,128)(2,1)S(1)}, bf16[3,288,128]{2,1,0:T(8,128)(2,1)S(1)}, bf16[3,288,128]{2,1,0:T(8,128)(2,1)S(1)}, bf16[3,288,128]{2,1,0:T(8,128)(2,1)S(1)}) custom-call(bf16[3,1088,128]{2,1,0:T(8,128)(2,1)S(1)} %constant_dynamic-update-slice_fusion.1.q_ref, f32[3,1088,128]{2,1,0:T(8,128)S(1)} %get-tuple-element.63.acc_ref, ...), custom_call_target="tpu_custom_call" | custom-call | flops 855638016 | bytes 6786432 | tf_op jit(solution)/shard_map/attend_last/pallas_call | solution.py:227
  67.0 0.7 copy-done
  67.7 3.2 %collective-permute-start.16 = (bf16[3,288,128]{2,1,0:T(8,128)(2,1)S(1)}, bf16[3,288,128]{2,1,0:T(8,128)(2,1)S(1)}, u32[]{:S(2)}, u32[]{:S(2)}) collective-permute-start(bf16[3,288,128]{2,1,0:T(8,128)(2,1)S(1)} %get-tuple-element.68), channel_id=1, source_target_pairs={{0,96},{32,0},{64,32},{96,64},{1,97},{33,1},{65,33},{97,65},{2,98}... | collective-permute-start | bytes 663560 | tf_op jit(solution)/shard_map/ppermute | solution.py:51
  71.0 0.1 collective-permute-start.17
  71.1 3.8 %collective-permute-done.15.refs_1_ = bf16[3,288,128]{2,1,0:T(8,128)(2,1)S(1)} collective-permute-done((bf16[3,288,128]{2,1,0:T(8,128)(2,1)S(1)}, bf16[3,288,128]{2,1,0:T(8,128)(2,1)S(1)}, u32[]{:S(2)}, u32[]{:S(2)}) %collective-permute-start.15) | collective-permute-done | bytes 221216 | tf_op jit(solution)/shard_map/ppermute | solution.py:51
  74.9 1.9 %collective-permute-done.16.refs_2_ = bf16[3,288,128]{2,1,0:T(8,128)(2,1)S(1)} collective-permute-done((bf16[3,288,128]{2,1,0:T(8,128)(2,1)S(1)}, bf16[3,288,128]{2,1,0:T(8,128)(2,1)S(1)}, u32[]{:S(2)}, u32[]{:S(2)}) %collective-permute-start.16) | collective-permute-done | bytes 221216 | tf_op jit(solution)/shard_map/ppermute | solution.py:51
  76.8 1.6 %collective-permute-done.17.refs_3_ = bf16[3,288,128]{2,1,0:T(8,128)(2,1)S(1)} collective-permute-done((bf16[3,288,128]{2,1,0:T(8,128)(2,1)S(1)}, bf16[3,288,128]{2,1,0:T(8,128)(2,1)S(1)}, u32[]{:S(2)}, u32[]{:S(2)}) %collective-permute-start.17) | collective-permute-done | bytes 221216 | tf_op jit(solution)/shard_map/ppermute | solution.py:51
  78.4 0.7 copy-done.4
  79.1 3.4 %merge.1 = (bf16[3,80,128]{2,1,0:T(8,128)(2,1)}, bf16[3,80,128]{2,1,0:T(8,128)(2,1)}, bf16[3,80,128]{2,1,0:T(8,128)(2,1)}, bf16[3,80,128]{2,1,0:T(8,128)(2,1)}) custom-call(bf16[3,288,128]{2,1,0:T(8,128)(2,1)} %copy-done, bf16[3,288,128]{2,1,0:T(8,128)(2,1)} %copy-done.2, bf16[3,288,128]{2,1,0:T(8,128)(2,1)} %copy-done.3, bf16[3,288,128]{2,1,0:T(8,128)(2,1)} %copy-done.4), custom_call_target="tpu_custom_call" | custom-call | tf_op jit(solution)/shard_map/merge/pallas_call | solution.py:264
  82.4 2.7 %collective-permute-start.18 = (bf16[3,80,128]{2,1,0:T(8,128)(2,1)}, bf16[3,80,128]{2,1,0:T(8,128)(2,1)S(1)}, u32[]{:S(2)}, u32[]{:S(2)}) collective-permute-start(bf16[3,80,128]{2,1,0:T(8,128)(2,1)} %get-tuple-element.71), channel_id=1, source_target_pairs={{0,6},{2,0},{4,2},{6,4},{1,7},{3,1},{5,3},{7,5},{8,14},{10,8},{12,... | collective-permute-start | bytes 184328 | tf_op jit(solution)/shard_map/ppermute | solution.py:51
  85.2 1.6 %collective-permute-start.20 = (bf16[3,80,128]{2,1,0:T(8,128)(2,1)}, bf16[3,80,128]{2,1,0:T(8,128)(2,1)S(1)}, u32[]{:S(2)}, u32[]{:S(2)}) collective-permute-start(bf16[3,80,128]{2,1,0:T(8,128)(2,1)} %get-tuple-element.73), channel_id=1, source_target_pairs={{0,4},{2,6},{4,0},{6,2},{1,5},{3,7},{5,1},{7,3},{8,12},{10,14},{12... | collective-permute-start | bytes 184328 | tf_op jit(solution)/shard_map/ppermute | solution.py:51
  86.8 0.5 collective-permute-done.18.refs_1_
  87.4 4.1 %collective-permute-done.19.refs_2_ = bf16[3,80,128]{2,1,0:T(8,128)(2,1)S(1)} collective-permute-done((bf16[3,80,128]{2,1,0:T(8,128)(2,1)}, bf16[3,80,128]{2,1,0:T(8,128)(2,1)S(1)}, u32[]{:S(2)}, u32[]{:S(2)}) %collective-permute-start.19) | collective-permute-done | bytes 61472 | tf_op jit(solution)/shard_map/ppermute | solution.py:51
  91.5 0.6 copy-done.6
  92.1 0.0 copy-done.7
  92.1 1.7 %finish.1 = (bf16[12,64,128]{2,1,0:T(8,128)(2,1)}, bf16[6,4,128]{2,1,0:T(4,128)(2,1)}) custom-call(bf16[3,80,128]{2,1,0:T(8,128)(2,1)} %get-tuple-element.70.refs_0_, bf16[3,80,128]{2,1,0:T(8,128)(2,1)} %copy-done.5, bf16[3,80,128]{2,1,0:T(8,128)(2,1)} %copy-done.6, bf16[3,80,128]{2,1,0:T(8,128)(2,1)} %copy-done.7), custom_call_target="tpu_custom_call" | custom-call | tf_op jit(solution)/shard_map/finish/pallas_call | solution.py:293
  (34 shorter events, 0.3 us)
Async XLA Ops:
  3.4 20.7 %copy-start.8 = (bf16[3,16,128]{2,1,0:T(8,128)(2,1)S(1)}, bf16[3,16,128]{2,1,0:T(8,128)(2,1)}, u32[]{:S(2)}) copy-start(bf16[3,16,128]{2,1,0:T(8,128)(2,1)} %get-tuple-element.43) | copy-start | bytes 36868
  3.4 18.5 %collective-permute-start.6 = (bf16[3,128,128]{2,1,0:T(8,128)(2,1)}, bf16[3,128,128]{2,1,0:T(8,128)(2,1)S(1)}, u32[]{:S(2)}, u32[]{:S(2)}) collective-permute-start(bf16[3,128,128]{2,1,0:T(8,128)(2,1)} %get-tuple-element.44.mine), channel_id=1, source_target_pairs={{0,1},{2,3},{5,4},{7,6},{8,9},{10,11},{13,12},{15,14},{16,17},{18,... | collective-permute-start | bytes 294920 | tf_op jit(solution)/shard_map/ppermute | solution.py:60
  11.7 8.4 %collective-permute-start = (bf16[3,3,64,128]{3,2,1,0:T(8,128)(2,1)}, bf16[3,3,64,128]{3,2,1,0:T(8,128)(2,1)S(1)}, u32[]{:S(2)}, u32[]{:S(2)}) collective-permute-start(bf16[3,3,64,128]{3,2,1,0:T(8,128)(2,1)} %get-tuple-element.40), channel_id=1, source_target_pairs={{0,2},{2,4},{4,6},{6,0},{1,3},{3,5},{5,7},{7,1},{8,10},{10,12},{12... | collective-permute-start | bytes 442376 | tf_op jit(solution)/shard_map/ppermute | solution.py:51
  13.4 6.8 %collective-permute-start.1 = (bf16[3,3,64,128]{3,2,1,0:T(8,128)(2,1)}, bf16[3,3,64,128]{3,2,1,0:T(8,128)(2,1)S(1)}, u32[]{:S(2)}, u32[]{:S(2)}) collective-permute-start(bf16[3,3,64,128]{3,2,1,0:T(8,128)(2,1)} %get-tuple-element.41), channel_id=1, source_target_pairs={{0,6},{2,0},{4,2},{6,4},{1,7},{3,1},{5,3},{7,5},{8,14},{10,8},{12,... | collective-permute-start | bytes 442376 | tf_op jit(solution)/shard_map/ppermute | solution.py:51
  15.0 6.9 %collective-permute-start.2 = (bf16[3,3,64,128]{3,2,1,0:T(8,128)(2,1)}, bf16[3,3,64,128]{3,2,1,0:T(8,128)(2,1)S(1)}, u32[]{:S(2)}, u32[]{:S(2)}) collective-permute-start(bf16[3,3,64,128]{3,2,1,0:T(8,128)(2,1)} %get-tuple-element.42), channel_id=1, source_target_pairs={{0,4},{2,6},{4,0},{6,2},{1,5},{3,7},{5,1},{7,3},{8,12},{10,14},{12... | collective-permute-start | bytes 442376 | tf_op jit(solution)/shard_map/ppermute | solution.py:51
  16.4 20.5 %copy-start.1 = (bf16[3,128,128]{2,1,0:T(8,128)(2,1)S(1)}, bf16[3,128,128]{2,1,0:T(8,128)(2,1)}, u32[]{:S(2)}) copy-start(bf16[3,128,128]{2,1,0:T(8,128)(2,1)} %get-tuple-element.44.mine) | copy-start | bytes 294916
  21.9 9.4 %collective-permute-start.9 = (bf16[2,3,256,128]{3,2,1,0:T(8,128)(2,1)S(1)}, bf16[2,3,256,128]{3,2,1,0:T(8,128)(2,1)S(1)}, u32[]{:S(2)}, u32[]{:S(2)}) collective-permute-start(bf16[2,3,256,128]{3,2,1,0:T(8,128)(2,1)S(1)} %pad_maximum_fusion.refs_0_.refs_1_), channel_id=1, source_target_pairs={{0,25},{8,0},{16,8},{24,16},{1,24},{9,1},{17,9},{25,17},{2,27},{10... | collective-permute-start | bytes 1179656 | tf_op jit(solution)/shard_map/ppermute | solution.py:56
  23.0 9.0 %collective-permute-start.7 = (bf16[2,3,256,128]{3,2,1,0:T(8,128)(2,1)S(1)}, bf16[2,3,256,128]{3,2,1,0:T(8,128)(2,1)S(1)}, u32[]{:S(2)}, u32[]{:S(2)}) collective-permute-start(bf16[2,3,256,128]{3,2,1,0:T(8,128)(2,1)S(1)} %pad_maximum_fusion.refs_0_.refs_1_), channel_id=1, source_target_pairs={{0,8},{8,16},{16,24},{24,1},{1,9},{9,17},{17,25},{25,0},{2,10},{10... | collective-permute-start | bytes 1179656 | tf_op jit(solution)/shard_map/ppermute | solution.py:56
  24.1 9.2 %collective-permute-start.3 = (bf16[3,272,128]{2,1,0:T(8,128)(2,1)S(1)}, bf16[3,272,128]{2,1,0:T(8,128)(2,1)S(1)}, u32[]{:S(2)}, u32[]{:S(2)}) collective-permute-start(bf16[3,272,128]{2,1,0:T(8,128)(2,1)S(1)} %get-tuple-element.84), channel_id=1, source_target_pairs={{0,96},{32,0},{64,32},{96,64},{1,97},{33,1},{65,33},{97,65},{2,98}... | collective-permute-start | bytes 626696 | tf_op jit(solution)/shard_map/ppermute | solution.py:51
  27.0 9.9 %collective-permute-start.4 = (bf16[3,272,128]{2,1,0:T(8,128)(2,1)S(1)}, bf16[3,272,128]{2,1,0:T(8,128)(2,1)S(1)}, u32[]{:S(2)}, u32[]{:S(2)}) collective-permute-start(bf16[3,272,128]{2,1,0:T(8,128)(2,1)S(1)} %get-tuple-element.84), channel_id=1, source_target_pairs={{0,32},{32,64},{64,96},{96,0},{1,33},{33,65},{65,97},{97,1},{2,34}... | collective-permute-start | bytes 626696 | tf_op jit(solution)/shard_map/ppermute | solution.py:51
  27.6 9.2 %collective-permute-start.5 = (bf16[3,272,128]{2,1,0:T(8,128)(2,1)S(1)}, bf16[3,272,128]{2,1,0:T(8,128)(2,1)S(1)}, u32[]{:S(2)}, u32[]{:S(2)}) collective-permute-start(bf16[3,272,128]{2,1,0:T(8,128)(2,1)S(1)} %get-tuple-element.84), channel_id=1, source_target_pairs={{0,64},{32,96},{64,0},{96,32},{1,65},{33,97},{65,1},{97,33},{2,66}... | collective-permute-start | bytes 626696 | tf_op jit(solution)/shard_map/ppermute | solution.py:51
  31.3 12.7 %collective-permute-start.10 = (bf16[2,3,256,128]{3,2,1,0:T(8,128)(2,1)S(1)}, bf16[2,3,256,128]{3,2,1,0:T(8,128)(2,1)S(1)}, u32[]{:S(2)}, u32[]{:S(2)}) collective-permute-start(bf16[2,3,256,128]{3,2,1,0:T(8,128)(2,1)S(1)} %collective-permute-done.9.refs_4_.refs_5_), channel_id=1, source_target_pairs={{0,25},{8,0},{16,8},{24,16},{1,24},{9,1},{17,9},{25,17},{2,27},{10... | collective-permute-start | bytes 1179656 | tf_op jit(solution)/shard_map/ppermute | solution.py:56
  32.0 12.1 %collective-permute-start.8 = (bf16[2,3,256,128]{3,2,1,0:T(8,128)(2,1)S(1)}, bf16[2,3,256,128]{3,2,1,0:T(8,128)(2,1)S(1)}, u32[]{:S(2)}, u32[]{:S(2)}) collective-permute-start(bf16[2,3,256,128]{3,2,1,0:T(8,128)(2,1)S(1)} %collective-permute-done.7.refs_2_.refs_3_), channel_id=1, source_target_pairs={{0,8},{8,16},{16,24},{24,1},{1,9},{9,17},{17,25},{25,0},{2,10},{10... | collective-permute-start | bytes 1179656 | tf_op jit(solution)/shard_map/ppermute | solution.py:56
  44.1 8.7 %collective-permute-start.11 = (bf16[2,3,256,128]{3,2,1,0:T(8,128)(2,1)S(1)}, bf16[2,3,256,128]{3,2,1,0:T(8,128)(2,1)S(1)}, u32[]{:S(2)}, u32[]{:S(2)}) collective-permute-start(bf16[2,3,256,128]{3,2,1,0:T(8,128)(2,1)S(1)} %collective-permute-done.8.refs_0_.refs_1_), channel_id=1, source_target_pairs={{0,8},{8,16},{16,24},{24,1},{1,9},{9,17},{17,25},{25,0},{2,10},{10... | collective-permute-start | bytes 1179656 | tf_op jit(solution)/shard_map/ppermute | solution.py:56
  45.2 8.6 %collective-permute-start.12 = (bf16[2,3,256,128]{3,2,1,0:T(8,128)(2,1)S(1)}, bf16[2,3,256,128]{3,2,1,0:T(8,128)(2,1)S(1)}, u32[]{:S(2)}, u32[]{:S(2)}) collective-permute-start(bf16[2,3,256,128]{3,2,1,0:T(8,128)(2,1)S(1)} %collective-permute-done.10.refs_2_.refs_3_), channel_id=1, source_target_pairs={{0,25},{8,0},{16,8},{24,16},{1,24},{9,1},{17,9},{25,17},{2,27},{10... | collective-permute-start | bytes 1179656 | tf_op jit(solution)/shard_map/ppermute | solution.py:56
  53.7 6.5 %collective-permute-start.13 = (bf16[3,256,128]{2,1,0:T(8,128)(2,1)S(1)}, bf16[3,256,128]{2,1,0:T(8,128)(2,1)S(1)}, u32[]{:S(2)}, u32[]{:S(2)}) collective-permute-start(bf16[3,256,128]{2,1,0:T(8,128)(2,1)S(1)} %slice_bitcast_fusion.1), channel_id=1, source_target_pairs={{0,8},{8,16},{16,24},{24,1},{1,9},{9,17},{17,25},{25,0},{2,10},{10... | collective-permute-start | bytes 589832 | tf_op jit(solution)/shard_map/ppermute | solution.py:56
  56.6 5.7 %collective-permute-start.14 = (bf16[3,256,128]{2,1,0:T(8,128)(2,1)S(1)}, bf16[3,256,128]{2,1,0:T(8,128)(2,1)S(1)}, u32[]{:S(2)}, u32[]{:S(2)}) collective-permute-start(bf16[3,256,128]{2,1,0:T(8,128)(2,1)S(1)} %slice_bitcast_fusion), channel_id=1, source_target_pairs={{0,25},{8,0},{16,8},{24,16},{1,24},{9,1},{17,9},{25,17},{2,27},{10... | collective-permute-start | bytes 589832 | tf_op jit(solution)/shard_map/ppermute | solution.py:56
  67.0 0.7 copy-start
  67.7 7.1 %collective-permute-start.15 = (bf16[3,288,128]{2,1,0:T(8,128)(2,1)S(1)}, bf16[3,288,128]{2,1,0:T(8,128)(2,1)S(1)}, u32[]{:S(2)}, u32[]{:S(2)}) collective-permute-start(bf16[3,288,128]{2,1,0:T(8,128)(2,1)S(1)} %get-tuple-element.67), channel_id=1, source_target_pairs={{0,32},{32,64},{64,96},{96,0},{1,33},{33,65},{65,97},{97,1},{2,34}... | collective-permute-start | bytes 663560 | tf_op jit(solution)/shard_map/ppermute | solution.py:51
  67.7 9.1 %collective-permute-start.16 = (bf16[3,288,128]{2,1,0:T(8,128)(2,1)S(1)}, bf16[3,288,128]{2,1,0:T(8,128)(2,1)S(1)}, u32[]{:S(2)}, u32[]{:S(2)}) collective-permute-start(bf16[3,288,128]{2,1,0:T(8,128)(2,1)S(1)} %get-tuple-element.68), channel_id=1, source_target_pairs={{0,96},{32,0},{64,32},{96,64},{1,97},{33,1},{65,33},{97,65},{2,98}... | collective-permute-start | bytes 663560 | tf_op jit(solution)/shard_map/ppermute | solution.py:51
  71.0 7.4 %collective-permute-start.17 = (bf16[3,288,128]{2,1,0:T(8,128)(2,1)S(1)}, bf16[3,288,128]{2,1,0:T(8,128)(2,1)S(1)}, u32[]{:S(2)}, u32[]{:S(2)}) collective-permute-start(bf16[3,288,128]{2,1,0:T(8,128)(2,1)S(1)} %get-tuple-element.69), channel_id=1, source_target_pairs={{0,64},{32,96},{64,0},{96,32},{1,65},{33,97},{65,1},{97,33},{2,66}... | collective-permute-start | bytes 663560 | tf_op jit(solution)/shard_map/ppermute | solution.py:51
  74.9 3.5 %copy-start.2 = (bf16[3,288,128]{2,1,0:T(8,128)(2,1)}, bf16[3,288,128]{2,1,0:T(8,128)(2,1)S(1)}, u32[]{:S(2)}) copy-start(bf16[3,288,128]{2,1,0:T(8,128)(2,1)S(1)} %collective-permute-done.15.refs_1_) | copy-start | bytes 663556
  76.8 1.6 %copy-start.3 = (bf16[3,288,128]{2,1,0:T(8,128)(2,1)}, bf16[3,288,128]{2,1,0:T(8,128)(2,1)S(1)}, u32[]{:S(2)}) copy-start(bf16[3,288,128]{2,1,0:T(8,128)(2,1)S(1)} %collective-permute-done.16.refs_2_) | copy-start | bytes 663556
  78.4 0.7 copy-start.4
  82.4 4.9 %collective-permute-start.18 = (bf16[3,80,128]{2,1,0:T(8,128)(2,1)}, bf16[3,80,128]{2,1,0:T(8,128)(2,1)S(1)}, u32[]{:S(2)}, u32[]{:S(2)}) collective-permute-start(bf16[3,80,128]{2,1,0:T(8,128)(2,1)} %get-tuple-element.71), channel_id=1, source_target_pairs={{0,6},{2,0},{4,2},{6,4},{1,7},{3,1},{5,3},{7,5},{8,14},{10,8},{12,... | collective-permute-start | bytes 184328 | tf_op jit(solution)/shard_map/ppermute | solution.py:51
  85.2 6.3 %collective-permute-start.19 = (bf16[3,80,128]{2,1,0:T(8,128)(2,1)}, bf16[3,80,128]{2,1,0:T(8,128)(2,1)S(1)}, u32[]{:S(2)}, u32[]{:S(2)}) collective-permute-start(bf16[3,80,128]{2,1,0:T(8,128)(2,1)} %get-tuple-element.72), channel_id=1, source_target_pairs={{0,2},{2,4},{4,6},{6,0},{1,3},{3,5},{5,7},{7,1},{8,10},{10,12},{12... | collective-permute-start | bytes 184328 | tf_op jit(solution)/shard_map/ppermute | solution.py:51
  85.2 6.3 %collective-permute-start.20 = (bf16[3,80,128]{2,1,0:T(8,128)(2,1)}, bf16[3,80,128]{2,1,0:T(8,128)(2,1)S(1)}, u32[]{:S(2)}, u32[]{:S(2)}) collective-permute-start(bf16[3,80,128]{2,1,0:T(8,128)(2,1)} %get-tuple-element.73), channel_id=1, source_target_pairs={{0,4},{2,6},{4,0},{6,2},{1,5},{3,7},{5,1},{7,3},{8,12},{10,14},{12... | collective-permute-start | bytes 184328 | tf_op jit(solution)/shard_map/ppermute | solution.py:51
  87.4 4.1 %copy-start.5 = (bf16[3,80,128]{2,1,0:T(8,128)(2,1)}, bf16[3,80,128]{2,1,0:T(8,128)(2,1)S(1)}, u32[]{:S(2)}) copy-start(bf16[3,80,128]{2,1,0:T(8,128)(2,1)S(1)} %collective-permute-done.18.refs_1_) | copy-start | bytes 184324
  91.5 0.6 copy-start.6
  91.5 0.6 copy-start.7

commit v5 on v4

--- a/solution.py
+++ b/solution.py
@@ -20,9 +20,9 @@
 ZAXES = ("za", "zp", "zb")
 VIDEO, TEXT, STATS = 256, 16, 16
 SITE = VIDEO + TEXT
-SHARE = 64
+OFFSETS = (0, -1, 1, -2, 2, -3, 3, 4)
 TILE = 2 * SITE
-VMEM = 60 * 1024 * 1024
+VMEM = 63 * 1024 * 1024
 F32, BF16 = jnp.float32, jnp.bfloat16
 
 
@@ -56,10 +56,6 @@
     return lax.ppermute(v, ZAXES, [(line(z), line((z + step) % 8)) for z in range(8)])
 
 
-def to_far_half(v):
-    return lax.ppermute(v, ("y", "zb"), [(y * 2 + y // 2, y * 2 + 1 - y // 2) for y in range(4)])
-
-
 def group_of(m):
     return lax.rem(lax.axis_index("y") + (MOVES[m] + 4), 4)
 
@@ -89,14 +85,14 @@
         messages[m][2] = rotate(q_ref[heads])
 
     heads = pl.ds(lax.rem(y, 2) * 3, 3)
-    share = pl.ds(pl.multiple_of(x * SHARE, SHARE), SHARE)
-    text_out[:, :SHARE] = tk_ref[heads, share]
-    text_out[:, SHARE:] = tv_ref[heads, share]
-    text_q_out[...] = tq_ref[heads, pl.ds(pl.multiple_of(x * 64 + low * TEXT, TEXT), TEXT)]
+    share = pl.ds(pl.multiple_of(x * 64 + low * TEXT, TEXT), TEXT)
+    text_out[0] = tk_ref[heads, share]
+    text_out[1] = tv_ref[heads, share]
+    text_q_out[...] = tq_ref[heads, share]
 
 
 def prepare(q, k, v, positions, tq, tk, tv):
-    outs = [(3, 3, 64, HD)] * 4 + [(3, 2 * SHARE, HD), (3, TEXT, HD)]
+    outs = [(3, 3, 64, HD)] * 4 + [(2, 3, TEXT, HD), (3, TEXT, HD)]
     args = (q, k, v, positions, tq, tk, tv, jnp.asarray(FREQ), jnp.asarray(SWAP, BF16))
     return pl.pallas_call(
         prepare_body,
@@ -132,39 +128,36 @@
     return acc * alpha + mixed, peak, total * alpha + add
 
 
-def over_parts(q, refs, state):
+def joined(refs):
     keys = jnp.concatenate([r[...].reshape(-1, HD) for r in refs[0::2]], axis=0)
-    values = jnp.concatenate([r[...].reshape(-1, HD) for r in refs[1::2]], axis=0)
-    return softmax_step(q, keys, values, state)
-
-
-def rows_here():
-    return pl.program_id(0), pl.ds(pl.multiple_of(pl.program_id(1) * TILE, 16), TILE)
-
-
-def keep(state, refs):
+    return keys, jnp.concatenate([r[...].reshape(-1, HD) for r in refs[1::2]], axis=0)
+
+
+TILES = [slice(0, TILE), slice(TILE, 2 * TILE)]
+
+
+def keep(state, refs, rows):
     for value, ref in zip(state, refs):
-        ref[rows_here()] = value
-
-
-def kept(refs):
-    return tuple(ref[rows_here()] for ref in refs)
-
-
-def first_body(count_ref, q_ref, mine, sent, *refs):
+        ref[pl.program_id(0), rows] = value
+
+
+def kept(refs, rows):
+    return tuple(ref[pl.program_id(0), rows] for ref in refs)
+
+
+def first_body(q_ref, *refs):
     parts, outs = refs[:-3], refs[-3:]
-    q = q_ref[0]
-    state = over_parts(q, parts, None)
-    here = lax.axis_index("y") // 2 == lax.axis_index("zb")
-    text = jnp.where(here, mine[0].astype(F32), sent[0].astype(F32)).astype(BF16)
-    left = count_ref[0] - lax.axis_index("x") * SHARE
-    live = lambda shape: lax.broadcasted_iota(jnp.int32, shape, 1) < left
-    keep(softmax_step(q, text[:SHARE], text[SHARE:], state, live), outs)
+    keys, values = joined(parts)
+    for rows in TILES:
+        keep(softmax_step(q_ref[0, rows], keys, values, None), outs, rows)
 
 
 def next_body(q_ref, acc_ref, top_ref, total_ref, *refs):
     parts, outs = refs[:-3], refs[-3:]
-    keep(over_parts(q_ref[0], parts, kept((acc_ref, top_ref, total_ref))), outs)
+    keys, values = joined(parts)
+    for rows in TILES:
+        state = kept((acc_ref, top_ref, total_ref), rows)
+        keep(softmax_step(q_ref[0, rows], keys, values, state), outs, rows)
 
 
 def pack_level(level):
@@ -189,46 +182,62 @@
     return lax.dot_general(block, pick, TN, preferred_element_type=F32)[:n]
 
 
-def last_body(q_ref, acc_ref, top_ref, total_ref, *refs):
-    parts, outs = refs[:-4], refs[-4:]
-    acc, top, total = over_parts(q_ref[0], parts, kept((acc_ref, top_ref, total_ref)))
-    mean = (acc / total).astype(BF16)
-    level = top + jnp.log2(total)
-    for tile in range(2):
-
-        @pl.when(pl.program_id(1) == tile)
-        def _():
-            for i in range(2):
-                out = outs[tile * 2 + i]
-                out[0, :SITE] = mean[i * SITE : (i + 1) * SITE]
-                out[0, SITE:] = pack_level(level[i * SITE : (i + 1) * SITE])
+def live_text(count, shape):
+    z = lax.axis_index("zb") * 4 + lax.axis_index("za") * 2 + lax.axis_index("zp")
+    lane = lax.broadcasted_iota(jnp.int32, shape, 1)
+    source = jnp.zeros(shape, jnp.int32)
+    for i, offset in enumerate(OFFSETS):
+        source = jnp.where(lane // TEXT == i, lax.rem(z + (offset + 8), 8), source)
+    index = lax.axis_index("x") * 64 + source % 4 * TEXT + lane % TEXT
+    return (source // 4 == lax.axis_index("y") // 2) & (index < count)
+
+
+def last_body(count_ref, q_ref, acc_ref, top_ref, total_ref, *refs):
+    parts, text, outs = refs[:2], refs[2:-4], refs[-4:]
+    keys, values = joined(parts)
+    text_keys, text_values = joined(text)
+    live = lambda shape: live_text(count_ref[0], shape)
+    for tile, rows in enumerate(TILES):
+        state = kept((acc_ref, top_ref, total_ref), rows)
+        state = softmax_step(q_ref[0, rows], text_keys, text_values, state, live)
+        acc, top, total = softmax_step(q_ref[0, rows], keys, values, state)
+        mean = (acc / total).astype(BF16)
+        level = top + jnp.log2(total)
+        for i in range(2):
+            out = outs[tile * 2 + i]
+            out[0, :SITE] = mean[i * SITE : (i + 1) * SITE]
+            out[0, SITE:] = pack_level(level[i * SITE : (i + 1) * SITE])
 
 
 def head_spec(*shape):
-    return pl.BlockSpec((1,) + shape, lambda h, t, *_: (h,) + (0,) * len(shape))
-
-
-TILE_SPEC = pl.BlockSpec((1, TILE, HD), lambda h, t, *_: (h, t, 0))
-
-
-def key_specs(part):
+    return pl.BlockSpec((1,) + shape, lambda h, *_: (h,) + (0,) * len(shape))
+
+
+TILE_SPEC = head_spec(2 * TILE, HD)
+
+
+def key_specs(part, rows=VIDEO, at=0):
     if part.ndim == 3:
-        return [head_spec(*part.shape[1:])]
-    return [pl.BlockSpec((1, 1) + part.shape[2:], lambda h, t, *_, i=i: (i, h, 0, 0)) for i in range(2)]
-
-
-def attend(body, name, parts, extra, extra_specs, outs, out_specs, prefetch=()):
-    keys = sum(p.shape[-2] for p in parts)
+        return [pl.BlockSpec((1, rows, HD), lambda h, *_: (h, at, 0))]
+    return [pl.BlockSpec((1, 1, rows, HD), lambda h, *_, i=i: (i, h, at, 0)) for i in range(2)]
+
+
+def attend(body, name, parts, extra, extra_specs, outs, out_specs, prefetch=(), texts=()):
+    keys = VIDEO * len(parts)
     specs, args = list(extra_specs), list(extra)
     for p in parts:
         new = key_specs(p)
+        specs += new
+        args += [p] * len(new)
+    for p in texts:
+        new = key_specs(p, TEXT, VIDEO // TEXT)
         specs += new
         args += [p] * len(new)
     return pl.pallas_call(
         body,
         out_shape=[jax.ShapeDtypeStruct((3,) + s, t) for s, t in outs],
         grid_spec=pltpu.PrefetchScalarGridSpec(
-            num_scalar_prefetch=len(prefetch), grid=(3, 2), in_specs=specs, out_specs=out_specs
+            num_scalar_prefetch=len(prefetch), grid=(3,), in_specs=specs, out_specs=out_specs
         ),
         compiler_params=pltpu.CompilerParams(vmem_limit_bytes=VMEM // 2),
         cost_estimate=pl.CostEstimate(
@@ -244,29 +253,29 @@
 
 def merge_body(*refs):
     sites, outs = refs[:4], refs[4:]
-    for t in range(0, SITE, HD):
-        n = min(HD, SITE - t)
-        levels = [unpack_level(s[0, SITE:], t, n) for s in sites]
-        peak = functools.reduce(jnp.maximum, levels)
-        weights = [jnp.exp2(level - peak) for level in levels]
-        mixed = sum(w * s[0, t : t + n].astype(F32) for w, s in zip(weights, sites))
-        mixed = (mixed / sum(weights)).astype(BF16)
-        if t < VIDEO:
-            for i in range(0, n, 64):
-                outs[(t + i) // 64][0, :64] = mixed[i : i + 64]
-        else:
-            for out in outs:
-                out[0, 64:] = mixed
+    for h in range(3):
+        for t in range(0, SITE, HD):
+            n = min(HD, SITE - t)
+            levels = [unpack_level(s[h, SITE:], t, n) for s in sites]
+            peak = functools.reduce(jnp.maximum, levels)
+            weights = [jnp.exp2(level - peak) for level in levels]
+            mixed = sum(w * s[h, t : t + n].astype(F32) for w, s in zip(weights, sites))
+            mixed = (mixed / sum(weights)).astype(BF16)
+            if t < VIDEO:
+                for i in range(0, n, 64):
+                    outs[(t + i) // 64][h, :64] = mixed[i : i + 64]
+            else:
+                for out in outs:
+                    out[h, 64:] = mixed
 
 
 def merge(sites):
-    spec = lambda rows: pl.BlockSpec((1, rows, HD), lambda h: (h, 0, 0))
     return pl.pallas_call(
         merge_body,
         out_shape=[jax.ShapeDtypeStruct((3, 64 + TEXT, HD), BF16)] * 4,
-        grid=(3,),
-        in_specs=[spec(SITE + STATS)] * 4,
-        out_specs=[spec(64 + TEXT)] * 4,
+        grid=(1,),
+        in_specs=[whole(3, SITE + STATS, HD)] * 4,
+        out_specs=[whole(3, 64 + TEXT, HD)] * 4,
         compiler_params=pltpu.CompilerParams(vmem_limit_bytes=VMEM),
         name="merge",
     )(*sites)
@@ -305,30 +314,26 @@
     flat = lambda a: jnp.transpose(a, (1, 0, 2))
     out = prepare(flat(video_q), flat(video_k), flat(video_v), positions, flat(text_q), flat(text_k), flat(text_v))
     own, text, text_rows = out[:4], out[4], out[5]
-    text_sent = to_far_half(text)
     m = [own[0]] + [shift(own[i], "y", MOVES[i]) for i in range(1, 4)]
-    block = jnp.concatenate([v[:2] for v in m], axis=2)
-    block, text_sent = lax.optimization_barrier((block, text_sent))
+    block = jnp.concatenate([v[:2] for v in m] + [text], axis=2)
     right, left = z_shift(block, 1), z_shift(block, -1)
     site = jnp.concatenate([v[2] for v in m] + [text_rows], axis=1)
     queries = jnp.concatenate([site] + [shift(site, "x", -d) for d in MOVES[1:]], axis=1)
 
     right2, left2 = z_shift(right, 1), z_shift(left, -1)
-    pack = head_spec(2 * SHARE, HD)
     state = attend(
         first_body,
         "attend_first",
-        [block, right, left],
-        [queries, text, text_sent],
-        [TILE_SPEC, pack, pack],
+        [block, right],
+        [queries],
+        [TILE_SPEC],
         STATE,
         STATE_SPECS,
-        prefetch=(text_count,),
     )
     right2, left2, *state = lax.optimization_barrier((right2, left2, *state))
     right3, left3 = z_shift(right2, 1), z_shift(left2, -1)
     specs = [TILE_SPEC] + STATE_SPECS
-    state = attend(next_body, "attend_2", [right2, left2], [queries, *state], specs, STATE, STATE_SPECS)
+    state = attend(next_body, "attend_2", [left, right2, left2], [queries, *state], specs, STATE, STATE_SPECS)
     right3, left3, *state = lax.optimization_barrier((right3, left3, *state))
     far_k, far_v = z_shift(right3[0], 1), z_shift(left3[1], -1)
     state = attend(next_body, "attend_3", [right3, left3], [queries, *state], specs, STATE, STATE_SPECS)
@@ -340,6 +345,8 @@
         specs,
         [((SITE + STATS, HD), BF16)] * 4,
         [head_spec(SITE + STATS, HD)] * 4,
+        prefetch=(text_count,),
+        texts=[block, right, left, right2, left2, right3, left3, far_k, far_v],
     )
     done = merge([sites[0]] + [shift(sites[i], "x", MOVES[i]) for i in range(1, 4)])
     video, text = finish([done[0]] + [shift(done[m], "y", -MOVES[m]) for m in range(1, 4)])

time: 94.2 us -> 89.8 us (0.953)
  starting transfers between devices: 34.2 us -> 29.8 us
  Pallas kernels: 26.9 us -> 24 us
  waiting for transfers between devices: 27.2 us -> 28.8 us
  local copies, waits for them, and re-layouts: 3.97 us -> 5.4 us
    ppermute x1 -> x0, starting transfers between devices: 8.32 us -> none  [to_far_half(): lax.ppermute(v, ('y', 'zb'), [(y * 2 + y // 2, y * 2 + 1 - y // 2) for y...]
    ppermute x8, waiting for transfers between devices: 7.16 us -> 11.9 us  [z_shift(): lax.ppermute(v, ZAXES, [(line(z), line((z + step) % 8)) for z in range(8)])]
    ppermute x12, waiting for transfers between devices: 20 us -> 16.9 us  [shift(): return lax.ppermute(v, axis, [(i, (i + step) % 4) for i in range(4)])]
    ppermute x8, starting transfers between devices: 9.08 us -> 11.6 us  [z_shift(): lax.ppermute(v, ZAXES, [(line(z), line((z + step) % 8)) for z in range(8)])]
    pallas_call x4, Pallas kernels: 19.2 us -> 17 us  [attend(): pl.pallas_call(body, out_shape=[jax.ShapeDtypeStruct((3,) + s, t) for s,...]
    ppermute x12, starting transfers between devices: 16.8 us -> 18.3 us  [shift(): return lax.ppermute(v, axis, [(i, (i + step) % 4) for i in range(4)])]
  transfers between devices with their start and end apart: 21 -> 20, of which waited for: 13 -> 16; matrix products, arithmetic and copies ran while one was open for 2% -> 3% of each run, Pallas kernels for 15% -> 13%
where the time goes in v5:
time: 89.8 us; the launch traced here: 89.5 us
  starting transfers between devices  29.8 us (33%)
  waiting for transfers between devices  28.8 us (32%)
  Pallas kernels  24 us (27%)
  local copies, waits for them, and re-layouts  5.4 us (6%)
  between operations  1.42 us (2%)
    ppermute x12, starting transfers between devices, shift(): return lax.ppermute(v, axis, [(i, (i + step) % 4) for i in range(4)])  18.3 us
    pallas_call x4, Pallas kernels, attend(): pl.pallas_call(body, out_shape=[jax.ShapeDtypeStruct((3,) + s, t) for s,...  17 us
    ppermute x12, waiting for transfers between devices, shift(): return lax.ppermute(v, axis, [(i, (i + step) % 4) for i in range(4)])  16.9 us
    ppermute x8, waiting for transfers between devices, z_shift(): lax.ppermute(v, ZAXES, [(line(z), line((z + step) % 8)) for z in range(8)])  11.9 us
    ppermute x8, starting transfers between devices, z_shift(): lax.ppermute(v, ZAXES, [(line(z), line((z + step) % 8)) for z in range(8)])  11.6 us
    unnamed x24, local copies, waits for them, and re-layouts  3.87 us
    pallas_call x1, Pallas kernels, prepare(): pl.pallas_call(prepare_body, out_shape=[jax.ShapeDtypeStruct(o, BF16) for...  2.72 us
    pallas_call x1, Pallas kernels, merge(): pl.pallas_call(merge_body, out_shape=[jax.ShapeDtypeStruct((3, 64 + TEXT,...  2.58 us
  transfers between devices with their start and end apart: 20, of which 16 were waited for; matrix products, arithmetic and copies ran while one was open for 3% of the time, Pallas kernels for 13%

profile of v5, /device:TPU:32, one launch (start us, length us, event | category | flops | bytes accessed | tf_op | source)
XLA Modules:
  0.0 89.5 jit_solution(3066195357811941055)
XLA Ops:
  0.6 2.7 %prepare.1 = (bf16[3,3,64,128]{3,2,1,0:T(8,128)(2,1)}, bf16[3,3,64,128]{3,2,1,0:T(8,128)(2,1)}, bf16[3,3,64,128]{3,2,1,0:T(8,128)(2,1)}, bf16[3,3,64,128]{3,2,1,...) custom-call(bf16[12,64,128]{2,1,0:T(8,128)(2,1)} %bitcast.36, ...), custom_call_target="tpu_custom_call" | custom-call | flops 50000000 | bytes 3000000 | tf_op jit(solution)/shard_map/prepare/pallas_call | solution.py:97
  3.4 1.6 %collective-permute-start = (bf16[3,3,64,128]{3,2,1,0:T(8,128)(2,1)}, bf16[3,3,64,128]{3,2,1,0:T(8,128)(2,1)S(1)}, u32[]{:S(2)}, u32[]{:S(2)}) collective-permute-start(bf16[3,3,64,128]{3,2,1,0:T(8,128)(2,1)} %get-tuple-element.38), channel_id=1, source_target_pairs={{0,2},{2,4},{4,6},{6,0},{1,3},{3,5},{5,7},{7,1},{8,10},{10,12},{12... | collective-permute-start | bytes 442376 | tf_op jit(solution)/shard_map/ppermute | solution.py:51
  4.9 1.7 %collective-permute-start.1 = (bf16[3,3,64,128]{3,2,1,0:T(8,128)(2,1)}, bf16[3,3,64,128]{3,2,1,0:T(8,128)(2,1)S(1)}, u32[]{:S(2)}, u32[]{:S(2)}) collective-permute-start(bf16[3,3,64,128]{3,2,1,0:T(8,128)(2,1)} %get-tuple-element.39), channel_id=1, source_target_pairs={{0,6},{2,0},{4,2},{6,4},{1,7},{3,1},{5,3},{7,5},{8,14},{10,8},{12,... | collective-permute-start | bytes 442376 | tf_op jit(solution)/shard_map/ppermute | solution.py:51
  6.6 2.0 %collective-permute-start.2 = (bf16[3,3,64,128]{3,2,1,0:T(8,128)(2,1)}, bf16[3,3,64,128]{3,2,1,0:T(8,128)(2,1)S(1)}, u32[]{:S(2)}, u32[]{:S(2)}) collective-permute-start(bf16[3,3,64,128]{3,2,1,0:T(8,128)(2,1)} %get-tuple-element.40), channel_id=1, source_target_pairs={{0,4},{2,6},{4,0},{6,2},{1,5},{3,7},{5,1},{7,3},{8,12},{10,14},{12... | collective-permute-start | bytes 442376 | tf_op jit(solution)/shard_map/ppermute | solution.py:51
  8.6 0.9 %slice_dynamic-update-slice_fusion.3 = bf16[2,3,272,128]{3,2,1,0:T(8,128)(2,1)S(1)} fusion(bf16[3,3,64,128]{3,2,1,0:T(8,128)(2,1)} %get-tuple-element.37), kind=kLoop, calls=%fused_computation.5 | loop fusion | bytes 196608
  9.5 0.8 bitcast_dynamic-update-slice_fusion.1
  10.3 0.1 collective-permute-done
  10.4 2.6 %collective-permute-done.1 = bf16[3,3,64,128]{3,2,1,0:T(8,128)(2,1)S(1)} collective-permute-done((bf16[3,3,64,128]{3,2,1,0:T(8,128)(2,1)}, bf16[3,3,64,128]{3,2,1,0:T(8,128)(2,1)S(1)}, u32[]{:S(2)}, u32[]{:S(2)}) %collective-permute-start.1) | collective-permute-done | bytes 147488 | tf_op jit(solution)/shard_map/ppermute | solution.py:51
  13.1 1.7 %collective-permute-done.2 = bf16[3,3,64,128]{3,2,1,0:T(8,128)(2,1)S(1)} collective-permute-done((bf16[3,3,64,128]{3,2,1,0:T(8,128)(2,1)}, bf16[3,3,64,128]{3,2,1,0:T(8,128)(2,1)S(1)}, u32[]{:S(2)}, u32[]{:S(2)}) %collective-permute-start.2) | collective-permute-done | bytes 147488 | tf_op jit(solution)/shard_map/ppermute | solution.py:51
  14.8 0.7 constant_dynamic-update-slice_fusion.5.refs_0_.refs_1_.refs_2_.refs_3_
  15.5 1.9 %collective-permute-start.6 = (bf16[2,3,272,128]{3,2,1,0:T(8,128)(2,1)S(1)}, bf16[2,3,272,128]{3,2,1,0:T(8,128)(2,1)S(1)}, u32[]{:S(2)}, u32[]{:S(2)}) collective-permute-start(bf16[2,3,272,128]{3,2,1,0:T(8,128)(2,1)S(1)} %constant_dynamic-update-slice_fusion.5.refs_0_.refs_1_.refs_2_.refs_3_), channel_id=1, source_target_pairs={{0,8},{8,16},{16,24},{24,1},{1,9},{9,17},{17,25},{25,0},{2,10},{10... | collective-permute-start | bytes 1253384 | tf_op jit(solution)/shard_map/ppermute | solution.py:56
  17.4 0.1 collective-permute-start.8
  17.6 0.7 constant_dynamic-update-slice_fusion
  18.4 2.8 %collective-permute-start.3 = (bf16[3,272,128]{2,1,0:T(8,128)(2,1)S(1)}, bf16[3,272,128]{2,1,0:T(8,128)(2,1)S(1)}, u32[]{:S(2)}, u32[]{:S(2)}) collective-permute-start(bf16[3,272,128]{2,1,0:T(8,128)(2,1)S(1)} %get-tuple-element.80), channel_id=1, source_target_pairs={{0,96},{32,0},{64,32},{96,64},{1,97},{33,1},{65,33},{97,65},{2,98}... | collective-permute-start | bytes 626696 | tf_op jit(solution)/shard_map/ppermute | solution.py:51
  21.1 2.3 %collective-permute-start.5 = (bf16[3,272,128]{2,1,0:T(8,128)(2,1)S(1)}, bf16[3,272,128]{2,1,0:T(8,128)(2,1)S(1)}, u32[]{:S(2)}, u32[]{:S(2)}) collective-permute-start(bf16[3,272,128]{2,1,0:T(8,128)(2,1)S(1)} %get-tuple-element.80), channel_id=1, source_target_pairs={{0,64},{32,96},{64,0},{96,32},{1,65},{33,97},{65,1},{97,33},{2,66}... | collective-permute-start | bytes 626696 | tf_op jit(solution)/shard_map/ppermute | solution.py:51
  23.4 2.6 %collective-permute-done.6.refs_2_.refs_3_.refs_4_.refs_5_ = bf16[2,3,272,128]{3,2,1,0:T(8,128)(2,1)S(1)} collective-permute-done((bf16[2,3,272,128]{3,2,1,0:T(8,128)(2,1)S(1)}, bf16[2,3,272,128]{3,2,1,0:T(8,128)(2,1)S(1)}, u32[]{:S(2)}, u32[]{:S(2)}) %collective-permute-start.6) | collective-permute-done | bytes 417824 | tf_op jit(solution)/shard_map/ppermute | solution.py:56
  26.0 1.9 %collective-permute-start.7 = (bf16[2,3,272,128]{3,2,1,0:T(8,128)(2,1)S(1)}, bf16[2,3,272,128]{3,2,1,0:T(8,128)(2,1)S(1)}, u32[]{:S(2)}, u32[]{:S(2)}) collective-permute-start(bf16[2,3,272,128]{3,2,1,0:T(8,128)(2,1)S(1)} %collective-permute-done.6.refs_2_.refs_3_.refs_4_.refs_5_), channel_id=1, source_target_pairs={{0,8},{8,16},{16,24},{24,1},{1,9},{9,17},{17,25},{25,0},{2,10},{10... | collective-permute-start | bytes 1253384 | tf_op jit(solution)/shard_map/ppermute | solution.py:56
  28.0 2.3 %collective-permute-start.9 = (bf16[2,3,272,128]{3,2,1,0:T(8,128)(2,1)S(1)}, bf16[2,3,272,128]{3,2,1,0:T(8,128)(2,1)S(1)}, u32[]{:S(2)}, u32[]{:S(2)}) collective-permute-start(bf16[2,3,272,128]{3,2,1,0:T(8,128)(2,1)S(1)} %collective-permute-done.8.refs_0_.refs_1_.refs_6_.refs_7_), channel_id=1, source_target_pairs={{0,25},{8,0},{16,8},{24,16},{1,24},{9,1},{17,9},{25,17},{2,27},{10... | collective-permute-start | bytes 1253384 | tf_op jit(solution)/shard_map/ppermute | solution.py:56
  30.3 1.9 %collective-permute-done.4 = bf16[3,272,128]{2,1,0:T(8,128)(2,1)S(1)} collective-permute-done((bf16[3,272,128]{2,1,0:T(8,128)(2,1)S(1)}, bf16[3,272,128]{2,1,0:T(8,128)(2,1)S(1)}, u32[]{:S(2)}, u32[]{:S(2)}) %collective-permute-start.4) | collective-permute-done | bytes 208928 | tf_op jit(solution)/shard_map/ppermute | solution.py:51
  32.3 3.5 %attend_first.1 = (f32[3,1088,128]{2,1,0:T(8,128)S(1)}, f32[3,1088,128]{2,1,0:T(8,128)S(1)}, f32[3,1088,128]{2,1,0:T(8,128)S(1)}) custom-call(bf16[3,1088,128]{2,1,0:T(8,128)(2,1)S(1)} %constant_dynamic-update-slice_fusion.1.q_ref, bf16[2,3,272,128]{3,2,1,0:T(8,128)(2,1)S(1)} %constant_dynamic-update-slice_fusion.5.refs_0_.refs_1_.refs_2_.refs_3_, ...), custom_call_target="tpu_custom_call" | custom-call | flops 855638016 | bytes 6786432 | tf_op jit(solution)/shard_map/attend_first/pallas_call | solution.py:236
  35.8 2.6 %collective-permute-done.7.refs_2_.refs_3_.refs_8_.refs_9_ = bf16[2,3,272,128]{3,2,1,0:T(8,128)(2,1)S(1)} collective-permute-done((bf16[2,3,272,128]{3,2,1,0:T(8,128)(2,1)S(1)}, bf16[2,3,272,128]{3,2,1,0:T(8,128)(2,1)S(1)}, u32[]{:S(2)}, u32[]{:S(2)}) %collective-permute-start.7) | collective-permute-done | bytes 417824 | tf_op jit(solution)/shard_map/ppermute | solution.py:56
  38.4 0.4 collective-permute-done.9.refs_4_.refs_5_.refs_10_.refs_11_
  38.8 3.0 %collective-permute-start.10 = (bf16[2,3,272,128]{3,2,1,0:T(8,128)(2,1)S(1)}, bf16[2,3,272,128]{3,2,1,0:T(8,128)(2,1)S(1)}, u32[]{:S(2)}, u32[]{:S(2)}) collective-permute-start(bf16[2,3,272,128]{3,2,1,0:T(8,128)(2,1)S(1)} %collective-permute-done.7.refs_2_.refs_3_.refs_8_.refs_9_), channel_id=1, source_target_pairs={{0,8},{8,16},{16,24},{24,1},{1,9},{9,17},{17,25},{25,0},{2,10},{10... | collective-permute-start | bytes 1253384 | tf_op jit(solution)/shard_map/ppermute | solution.py:56
  41.8 4.7 %attend_2.1 = (f32[3,1088,128]{2,1,0:T(8,128)S(1)}, f32[3,1088,128]{2,1,0:T(8,128)S(1)}, f32[3,1088,128]{2,1,0:T(8,128)S(1)}) custom-call(bf16[3,1088,128]{2,1,0:T(8,128)(2,1)S(1)} %constant_dynamic-update-slice_fusion.1.q_ref, f32[3,1088,128]{2,1,0:T(8,128)S(1)} %get-tuple-element.48.acc_ref, f32[3,1088,128]{2,1,0:T(8,128)S(1)} %get-tuple-element.49.top_ref, ...), custom_call_target="tpu_custom_call" | custom-call | flops 1283457024 | bytes 7179648 | tf_op jit(solution)/shard_map/attend_2/pallas_call | solution.py:236
  46.5 2.0 %collective-permute-done.10.refs_0_.refs_1_.refs_12_.refs_13_ = bf16[2,3,272,128]{3,2,1,0:T(8,128)(2,1)S(1)} collective-permute-done((bf16[2,3,272,128]{3,2,1,0:T(8,128)(2,1)S(1)}, bf16[2,3,272,128]{3,2,1,0:T(8,128)(2,1)S(1)}, u32[]{:S(2)}, u32[]{:S(2)}) %collective-permute-start.10) | collective-permute-done | bytes 417824 | tf_op jit(solution)/shard_map/ppermute | solution.py:56
  48.6 2.5 %collective-permute-done.11.refs_2_.refs_3_.refs_14_.refs_15_ = bf16[2,3,272,128]{3,2,1,0:T(8,128)(2,1)S(1)} collective-permute-done((bf16[2,3,272,128]{3,2,1,0:T(8,128)(2,1)S(1)}, bf16[2,3,272,128]{3,2,1,0:T(8,128)(2,1)S(1)}, u32[]{:S(2)}, u32[]{:S(2)}) %collective-permute-start.11) | collective-permute-done | bytes 417824 | tf_op jit(solution)/shard_map/ppermute | solution.py:56
  51.1 2.0 %collective-permute-start.12 = (bf16[3,272,128]{2,1,0:T(8,128)(2,1)S(1)}, bf16[3,272,128]{2,1,0:T(8,128)(2,1)S(1)}, u32[]{:S(2)}, u32[]{:S(2)}) collective-permute-start(bf16[3,272,128]{2,1,0:T(8,128)(2,1)S(1)} %slice_bitcast_fusion.1), channel_id=1, source_target_pairs={{0,8},{8,16},{16,24},{24,1},{1,9},{9,17},{17,25},{25,0},{2,10},{10... | collective-permute-start | bytes 626696 | tf_op jit(solution)/shard_map/ppermute | solution.py:56
  53.1 0.4 collective-permute-start.13
  54.2 3.3 %attend_3.1 = (f32[3,1088,128]{2,1,0:T(8,128)S(1)}, f32[3,1088,128]{2,1,0:T(8,128)S(1)}, f32[3,1088,128]{2,1,0:T(8,128)S(1)}) custom-call(bf16[3,1088,128]{2,1,0:T(8,128)(2,1)S(1)} %constant_dynamic-update-slice_fusion.1.q_ref, f32[3,1088,128]{2,1,0:T(8,128)S(1)} %get-tuple-element.54.acc_ref, f32[3,1088,128]{2,1,0:T(8,128)S(1)} %get-tuple-element.55.top_ref, ...), custom_call_target="tpu_custom_call" | custom-call | flops 855638016 | bytes 6786432 | tf_op jit(solution)/shard_map/attend_3/pallas_call | solution.py:236
  57.4 1.6 %collective-permute-done.13.refs_1_.refs_17_ = bf16[3,272,128]{2,1,0:T(8,128)(2,1)S(1)} collective-permute-done((bf16[3,272,128]{2,1,0:T(8,128)(2,1)S(1)}, bf16[3,272,128]{2,1,0:T(8,128)(2,1)S(1)}, u32[]{:S(2)}, u32[]{:S(2)}) %collective-permute-start.13) | collective-permute-done | bytes 208928 | tf_op jit(solution)/shard_map/ppermute | solution.py:56
  59.0 5.5 %attend_last.1 = (bf16[3,288,128]{2,1,0:T(8,128)(2,1)S(1)}, bf16[3,288,128]{2,1,0:T(8,128)(2,1)S(1)}, bf16[3,288,128]{2,1,0:T(8,128)(2,1)S(1)}, bf16[3,288,128]{2,1,0:T(8,128)(2,1)S(1)}) custom-call(s32[1]{0:T(128)S(6)} %copy.27.count_ref, bf16[3,1088,128]{2,1,0:T(8,128)(2,1)S(1)} %constant_dynamic-update-slice_fusion.1.q_ref, ...), custom_call_target="tpu_custom_call" | custom-call | flops 855638016 | bytes 6786432 | tf_op jit(solution)/shard_map/attend_last/pallas_call | solution.py:236
  64.6 0.7 copy-done
  65.3 1.5 %collective-permute-start.14 = (bf16[3,288,128]{2,1,0:T(8,128)(2,1)S(1)}, bf16[3,288,128]{2,1,0:T(8,128)(2,1)S(1)}, u32[]{:S(2)}, u32[]{:S(2)}) collective-permute-start(bf16[3,288,128]{2,1,0:T(8,128)(2,1)S(1)} %get-tuple-element.63), channel_id=1, source_target_pairs={{0,32},{32,64},{64,96},{96,0},{1,33},{33,65},{65,97},{97,1},{2,34}... | collective-permute-start | bytes 663560 | tf_op jit(solution)/shard_map/ppermute | solution.py:51
  66.7 1.7 %collective-permute-start.15 = (bf16[3,288,128]{2,1,0:T(8,128)(2,1)S(1)}, bf16[3,288,128]{2,1,0:T(8,128)(2,1)S(1)}, u32[]{:S(2)}, u32[]{:S(2)}) collective-permute-start(bf16[3,288,128]{2,1,0:T(8,128)(2,1)S(1)} %get-tuple-element.64), channel_id=1, source_target_pairs={{0,96},{32,0},{64,32},{96,64},{1,97},{33,1},{65,33},{97,65},{2,98}... | collective-permute-start | bytes 663560 | tf_op jit(solution)/shard_map/ppermute | solution.py:51
  68.5 1.8 %collective-permute-start.16 = (bf16[3,288,128]{2,1,0:T(8,128)(2,1)S(1)}, bf16[3,288,128]{2,1,0:T(8,128)(2,1)S(1)}, u32[]{:S(2)}, u32[]{:S(2)}) collective-permute-start(bf16[3,288,128]{2,1,0:T(8,128)(2,1)S(1)} %get-tuple-element.65), channel_id=1, source_target_pairs={{0,64},{32,96},{64,0},{96,32},{1,65},{33,97},{65,1},{97,33},{2,66}... | collective-permute-start | bytes 663560 | tf_op jit(solution)/shard_map/ppermute | solution.py:51
  70.3 2.1 %collective-permute-done.14.refs_1_ = bf16[3,288,128]{2,1,0:T(8,128)(2,1)S(1)} collective-permute-done((bf16[3,288,128]{2,1,0:T(8,128)(2,1)S(1)}, bf16[3,288,128]{2,1,0:T(8,128)(2,1)S(1)}, u32[]{:S(2)}, u32[]{:S(2)}) %collective-permute-start.14) | collective-permute-done | bytes 221216 | tf_op jit(solution)/shard_map/ppermute | solution.py:51
  72.4 1.9 %collective-permute-done.15.refs_2_ = bf16[3,288,128]{2,1,0:T(8,128)(2,1)S(1)} collective-permute-done((bf16[3,288,128]{2,1,0:T(8,128)(2,1)S(1)}, bf16[3,288,128]{2,1,0:T(8,128)(2,1)S(1)}, u32[]{:S(2)}, u32[]{:S(2)}) %collective-permute-start.15) | collective-permute-done | bytes 221216 | tf_op jit(solution)/shard_map/ppermute | solution.py:51
  74.3 1.6 %collective-permute-done.16.refs_3_ = bf16[3,288,128]{2,1,0:T(8,128)(2,1)S(1)} collective-permute-done((bf16[3,288,128]{2,1,0:T(8,128)(2,1)S(1)}, bf16[3,288,128]{2,1,0:T(8,128)(2,1)S(1)}, u32[]{:S(2)}, u32[]{:S(2)}) %collective-permute-start.16) | collective-permute-done | bytes 221216 | tf_op jit(solution)/shard_map/ppermute | solution.py:51
  75.9 0.7 copy-done.3
  76.6 2.6 %merge.1 = (bf16[3,80,128]{2,1,0:T(8,128)(2,1)}, bf16[3,80,128]{2,1,0:T(8,128)(2,1)}, bf16[3,80,128]{2,1,0:T(8,128)(2,1)}, bf16[3,80,128]{2,1,0:T(8,128)(2,1)}) custom-call(bf16[3,288,128]{2,1,0:T(8,128)(2,1)} %copy-done, bf16[3,288,128]{2,1,0:T(8,128)(2,1)} %copy-done.1, bf16[3,288,128]{2,1,0:T(8,128)(2,1)} %copy-done.2, bf16[3,288,128]{2,1,0:T(8,128)(2,1)} %copy-done.3), custom_call_target="tpu_custom_call" | custom-call | tf_op jit(solution)/shard_map/merge/pallas_call | solution.py:273
  79.2 1.5 %collective-permute-start.17 = (bf16[3,80,128]{2,1,0:T(8,128)(2,1)}, bf16[3,80,128]{2,1,0:T(8,128)(2,1)S(1)}, u32[]{:S(2)}, u32[]{:S(2)}) collective-permute-start(bf16[3,80,128]{2,1,0:T(8,128)(2,1)} %get-tuple-element.67), channel_id=1, source_target_pairs={{0,6},{2,0},{4,2},{6,4},{1,7},{3,1},{5,3},{7,5},{8,14},{10,8},{12,... | collective-permute-start | bytes 184328 | tf_op jit(solution)/shard_map/ppermute | solution.py:51
  80.7 0.6 collective-permute-start.18
  81.2 0.9 %collective-permute-start.19 = (bf16[3,80,128]{2,1,0:T(8,128)(2,1)}, bf16[3,80,128]{2,1,0:T(8,128)(2,1)S(1)}, u32[]{:S(2)}, u32[]{:S(2)}) collective-permute-start(bf16[3,80,128]{2,1,0:T(8,128)(2,1)} %get-tuple-element.69), channel_id=1, source_target_pairs={{0,4},{2,6},{4,0},{6,2},{1,5},{3,7},{5,1},{7,3},{8,12},{10,14},{12... | collective-permute-start | bytes 184328 | tf_op jit(solution)/shard_map/ppermute | solution.py:51
  82.2 1.5 %collective-permute-done.17.refs_1_ = bf16[3,80,128]{2,1,0:T(8,128)(2,1)S(1)} collective-permute-done((bf16[3,80,128]{2,1,0:T(8,128)(2,1)}, bf16[3,80,128]{2,1,0:T(8,128)(2,1)S(1)}, u32[]{:S(2)}, u32[]{:S(2)}) %collective-permute-start.17) | collective-permute-done | bytes 61472 | tf_op jit(solution)/shard_map/ppermute | solution.py:51
  83.6 2.7 %collective-permute-done.18.refs_2_ = bf16[3,80,128]{2,1,0:T(8,128)(2,1)S(1)} collective-permute-done((bf16[3,80,128]{2,1,0:T(8,128)(2,1)}, bf16[3,80,128]{2,1,0:T(8,128)(2,1)S(1)}, u32[]{:S(2)}, u32[]{:S(2)}) %collective-permute-start.18) | collective-permute-done | bytes 61472 | tf_op jit(solution)/shard_map/ppermute | solution.py:51
  86.3 0.9 collective-permute-done.19.refs_3_
  87.2 0.6 copy-done.6
  87.8 1.7 %finish.1 = (bf16[12,64,128]{2,1,0:T(8,128)(2,1)}, bf16[6,4,128]{2,1,0:T(4,128)(2,1)}) custom-call(bf16[3,80,128]{2,1,0:T(8,128)(2,1)} %get-tuple-element.66.refs_0_, bf16[3,80,128]{2,1,0:T(8,128)(2,1)} %copy-done.4, bf16[3,80,128]{2,1,0:T(8,128)(2,1)} %copy-done.5, bf16[3,80,128]{2,1,0:T(8,128)(2,1)} %copy-done.6), custom_call_target="tpu_custom_call" | custom-call | tf_op jit(solution)/shard_map/finish/pallas_call | solution.py:302
  (28 shorter events, 0.3 us)
Async XLA Ops:
  3.4 7.1 %collective-permute-start = (bf16[3,3,64,128]{3,2,1,0:T(8,128)(2,1)}, bf16[3,3,64,128]{3,2,1,0:T(8,128)(2,1)S(1)}, u32[]{:S(2)}, u32[]{:S(2)}) collective-permute-start(bf16[3,3,64,128]{3,2,1,0:T(8,128)(2,1)} %get-tuple-element.38), channel_id=1, source_target_pairs={{0,2},{2,4},{4,6},{6,0},{1,3},{3,5},{5,7},{7,1},{8,10},{10,12},{12... | collective-permute-start | bytes 442376 | tf_op jit(solution)/shard_map/ppermute | solution.py:51
  4.9 8.1 %collective-permute-start.1 = (bf16[3,3,64,128]{3,2,1,0:T(8,128)(2,1)}, bf16[3,3,64,128]{3,2,1,0:T(8,128)(2,1)S(1)}, u32[]{:S(2)}, u32[]{:S(2)}) collective-permute-start(bf16[3,3,64,128]{3,2,1,0:T(8,128)(2,1)} %get-tuple-element.39), channel_id=1, source_target_pairs={{0,6},{2,0},{4,2},{6,4},{1,7},{3,1},{5,3},{7,5},{8,14},{10,8},{12,... | collective-permute-start | bytes 442376 | tf_op jit(solution)/shard_map/ppermute | solution.py:51
  6.6 8.2 %collective-permute-start.2 = (bf16[3,3,64,128]{3,2,1,0:T(8,128)(2,1)}, bf16[3,3,64,128]{3,2,1,0:T(8,128)(2,1)S(1)}, u32[]{:S(2)}, u32[]{:S(2)}) collective-permute-start(bf16[3,3,64,128]{3,2,1,0:T(8,128)(2,1)} %get-tuple-element.40), channel_id=1, source_target_pairs={{0,4},{2,6},{4,0},{6,2},{1,5},{3,7},{5,1},{7,3},{8,12},{10,14},{12... | collective-permute-start | bytes 442376 | tf_op jit(solution)/shard_map/ppermute | solution.py:51
  15.5 10.5 %collective-permute-start.6 = (bf16[2,3,272,128]{3,2,1,0:T(8,128)(2,1)S(1)}, bf16[2,3,272,128]{3,2,1,0:T(8,128)(2,1)S(1)}, u32[]{:S(2)}, u32[]{:S(2)}) collective-permute-start(bf16[2,3,272,128]{3,2,1,0:T(8,128)(2,1)S(1)} %constant_dynamic-update-slice_fusion.5.refs_0_.refs_1_.refs_2_.refs_3_), channel_id=1, source_target_pairs={{0,8},{8,16},{16,24},{24,1},{1,9},{9,17},{17,25},{25,0},{2,10},{10... | collective-permute-start | bytes 1253384 | tf_op jit(solution)/shard_map/ppermute | solution.py:56
  17.4 10.5 %collective-permute-start.8 = (bf16[2,3,272,128]{3,2,1,0:T(8,128)(2,1)S(1)}, bf16[2,3,272,128]{3,2,1,0:T(8,128)(2,1)S(1)}, u32[]{:S(2)}, u32[]{:S(2)}) collective-permute-start(bf16[2,3,272,128]{3,2,1,0:T(8,128)(2,1)S(1)} %constant_dynamic-update-slice_fusion.5.refs_0_.refs_1_.refs_2_.refs_3_), channel_id=1, source_target_pairs={{0,25},{8,0},{16,8},{24,16},{1,24},{9,1},{17,9},{25,17},{2,27},{10... | collective-permute-start | bytes 1253384 | tf_op jit(solution)/shard_map/ppermute | solution.py:56
  18.4 11.9 %collective-permute-start.3 = (bf16[3,272,128]{2,1,0:T(8,128)(2,1)S(1)}, bf16[3,272,128]{2,1,0:T(8,128)(2,1)S(1)}, u32[]{:S(2)}, u32[]{:S(2)}) collective-permute-start(bf16[3,272,128]{2,1,0:T(8,128)(2,1)S(1)} %get-tuple-element.80), channel_id=1, source_target_pairs={{0,96},{32,0},{64,32},{96,64},{1,97},{33,1},{65,33},{97,65},{2,98}... | collective-permute-start | bytes 626696 | tf_op jit(solution)/shard_map/ppermute | solution.py:51
  21.1 11.1 %collective-permute-start.4 = (bf16[3,272,128]{2,1,0:T(8,128)(2,1)S(1)}, bf16[3,272,128]{2,1,0:T(8,128)(2,1)S(1)}, u32[]{:S(2)}, u32[]{:S(2)}) collective-permute-start(bf16[3,272,128]{2,1,0:T(8,128)(2,1)S(1)} %get-tuple-element.80), channel_id=1, source_target_pairs={{0,32},{32,64},{64,96},{96,0},{1,33},{33,65},{65,97},{97,1},{2,34}... | collective-permute-start | bytes 626696 | tf_op jit(solution)/shard_map/ppermute | solution.py:51
  21.1 11.1 %collective-permute-start.5 = (bf16[3,272,128]{2,1,0:T(8,128)(2,1)S(1)}, bf16[3,272,128]{2,1,0:T(8,128)(2,1)S(1)}, u32[]{:S(2)}, u32[]{:S(2)}) collective-permute-start(bf16[3,272,128]{2,1,0:T(8,128)(2,1)S(1)} %get-tuple-element.80), channel_id=1, source_target_pairs={{0,64},{32,96},{64,0},{96,32},{1,65},{33,97},{65,1},{97,33},{2,66}... | collective-permute-start | bytes 626696 | tf_op jit(solution)/shard_map/ppermute | solution.py:51
  26.0 12.3 %collective-permute-start.7 = (bf16[2,3,272,128]{3,2,1,0:T(8,128)(2,1)S(1)}, bf16[2,3,272,128]{3,2,1,0:T(8,128)(2,1)S(1)}, u32[]{:S(2)}, u32[]{:S(2)}) collective-permute-start(bf16[2,3,272,128]{3,2,1,0:T(8,128)(2,1)S(1)} %collective-permute-done.6.refs_2_.refs_3_.refs_4_.refs_5_), channel_id=1, source_target_pairs={{0,8},{8,16},{16,24},{24,1},{1,9},{9,17},{17,25},{25,0},{2,10},{10... | collective-permute-start | bytes 1253384 | tf_op jit(solution)/shard_map/ppermute | solution.py:56
  28.0 10.9 %collective-permute-start.9 = (bf16[2,3,272,128]{3,2,1,0:T(8,128)(2,1)S(1)}, bf16[2,3,272,128]{3,2,1,0:T(8,128)(2,1)S(1)}, u32[]{:S(2)}, u32[]{:S(2)}) collective-permute-start(bf16[2,3,272,128]{3,2,1,0:T(8,128)(2,1)S(1)} %collective-permute-done.8.refs_0_.refs_1_.refs_6_.refs_7_), channel_id=1, source_target_pairs={{0,25},{8,0},{16,8},{24,16},{1,24},{9,1},{17,9},{25,17},{2,27},{10... | collective-permute-start | bytes 1253384 | tf_op jit(solution)/shard_map/ppermute | solution.py:56
  38.8 9.7 %collective-permute-start.10 = (bf16[2,3,272,128]{3,2,1,0:T(8,128)(2,1)S(1)}, bf16[2,3,272,128]{3,2,1,0:T(8,128)(2,1)S(1)}, u32[]{:S(2)}, u32[]{:S(2)}) collective-permute-start(bf16[2,3,272,128]{3,2,1,0:T(8,128)(2,1)S(1)} %collective-permute-done.7.refs_2_.refs_3_.refs_8_.refs_9_), channel_id=1, source_target_pairs={{0,8},{8,16},{16,24},{24,1},{1,9},{9,17},{17,25},{25,0},{2,10},{10... | collective-permute-start | bytes 1253384 | tf_op jit(solution)/shard_map/ppermute | solution.py:56
  41.8 9.3 %collective-permute-start.11 = (bf16[2,3,272,128]{3,2,1,0:T(8,128)(2,1)S(1)}, bf16[2,3,272,128]{3,2,1,0:T(8,128)(2,1)S(1)}, u32[]{:S(2)}, u32[]{:S(2)}) collective-permute-start(bf16[2,3,272,128]{3,2,1,0:T(8,128)(2,1)S(1)} %collective-permute-done.9.refs_4_.refs_5_.refs_10_.refs_11_), channel_id=1, source_target_pairs={{0,25},{8,0},{16,8},{24,16},{1,24},{9,1},{17,9},{25,17},{2,27},{10... | collective-permute-start | bytes 1253384 | tf_op jit(solution)/shard_map/ppermute | solution.py:56
  51.1 6.3 %collective-permute-start.12 = (bf16[3,272,128]{2,1,0:T(8,128)(2,1)S(1)}, bf16[3,272,128]{2,1,0:T(8,128)(2,1)S(1)}, u32[]{:S(2)}, u32[]{:S(2)}) collective-permute-start(bf16[3,272,128]{2,1,0:T(8,128)(2,1)S(1)} %slice_bitcast_fusion.1), channel_id=1, source_target_pairs={{0,8},{8,16},{16,24},{24,1},{1,9},{9,17},{17,25},{25,0},{2,10},{10... | collective-permute-start | bytes 626696 | tf_op jit(solution)/shard_map/ppermute | solution.py:56
  53.1 5.9 %collective-permute-start.13 = (bf16[3,272,128]{2,1,0:T(8,128)(2,1)S(1)}, bf16[3,272,128]{2,1,0:T(8,128)(2,1)S(1)}, u32[]{:S(2)}, u32[]{:S(2)}) collective-permute-start(bf16[3,272,128]{2,1,0:T(8,128)(2,1)S(1)} %slice_bitcast_fusion), channel_id=1, source_target_pairs={{0,25},{8,0},{16,8},{24,16},{1,24},{9,1},{17,9},{25,17},{2,27},{10... | collective-permute-start | bytes 626696 | tf_op jit(solution)/shard_map/ppermute | solution.py:56
  64.6 0.7 copy-start
  65.3 7.1 %collective-permute-start.14 = (bf16[3,288,128]{2,1,0:T(8,128)(2,1)S(1)}, bf16[3,288,128]{2,1,0:T(8,128)(2,1)S(1)}, u32[]{:S(2)}, u32[]{:S(2)}) collective-permute-start(bf16[3,288,128]{2,1,0:T(8,128)(2,1)S(1)} %get-tuple-element.63), channel_id=1, source_target_pairs={{0,32},{32,64},{64,96},{96,0},{1,33},{33,65},{65,97},{97,1},{2,34}... | collective-permute-start | bytes 663560 | tf_op jit(solution)/shard_map/ppermute | solution.py:51
  66.7 7.6 %collective-permute-start.15 = (bf16[3,288,128]{2,1,0:T(8,128)(2,1)S(1)}, bf16[3,288,128]{2,1,0:T(8,128)(2,1)S(1)}, u32[]{:S(2)}, u32[]{:S(2)}) collective-permute-start(bf16[3,288,128]{2,1,0:T(8,128)(2,1)S(1)} %get-tuple-element.64), channel_id=1, source_target_pairs={{0,96},{32,0},{64,32},{96,64},{1,97},{33,1},{65,33},{97,65},{2,98}... | collective-permute-start | bytes 663560 | tf_op jit(solution)/shard_map/ppermute | solution.py:51
  68.5 7.4 %collective-permute-start.16 = (bf16[3,288,128]{2,1,0:T(8,128)(2,1)S(1)}, bf16[3,288,128]{2,1,0:T(8,128)(2,1)S(1)}, u32[]{:S(2)}, u32[]{:S(2)}) collective-permute-start(bf16[3,288,128]{2,1,0:T(8,128)(2,1)S(1)} %get-tuple-element.65), channel_id=1, source_target_pairs={{0,64},{32,96},{64,0},{96,32},{1,65},{33,97},{65,1},{97,33},{2,66}... | collective-permute-start | bytes 663560 | tf_op jit(solution)/shard_map/ppermute | solution.py:51
  72.4 3.5 %copy-start.1 = (bf16[3,288,128]{2,1,0:T(8,128)(2,1)}, bf16[3,288,128]{2,1,0:T(8,128)(2,1)S(1)}, u32[]{:S(2)}) copy-start(bf16[3,288,128]{2,1,0:T(8,128)(2,1)S(1)} %collective-permute-done.14.refs_1_) | copy-start | bytes 663556
  74.3 1.6 %copy-start.2 = (bf16[3,288,128]{2,1,0:T(8,128)(2,1)}, bf16[3,288,128]{2,1,0:T(8,128)(2,1)S(1)}, u32[]{:S(2)}) copy-start(bf16[3,288,128]{2,1,0:T(8,128)(2,1)S(1)} %collective-permute-done.15.refs_2_) | copy-start | bytes 663556
  75.9 0.7 copy-start.3
  79.2 4.4 %collective-permute-start.17 = (bf16[3,80,128]{2,1,0:T(8,128)(2,1)}, bf16[3,80,128]{2,1,0:T(8,128)(2,1)S(1)}, u32[]{:S(2)}, u32[]{:S(2)}) collective-permute-start(bf16[3,80,128]{2,1,0:T(8,128)(2,1)} %get-tuple-element.67), channel_id=1, source_target_pairs={{0,6},{2,0},{4,2},{6,4},{1,7},{3,1},{5,3},{7,5},{8,14},{10,8},{12,... | collective-permute-start | bytes 184328 | tf_op jit(solution)/shard_map/ppermute | solution.py:51
  80.7 5.6 %collective-permute-start.18 = (bf16[3,80,128]{2,1,0:T(8,128)(2,1)}, bf16[3,80,128]{2,1,0:T(8,128)(2,1)S(1)}, u32[]{:S(2)}, u32[]{:S(2)}) collective-permute-start(bf16[3,80,128]{2,1,0:T(8,128)(2,1)} %get-tuple-element.68), channel_id=1, source_target_pairs={{0,2},{2,4},{4,6},{6,0},{1,3},{3,5},{5,7},{7,1},{8,10},{10,12},{12... | collective-permute-start | bytes 184328 | tf_op jit(solution)/shard_map/ppermute | solution.py:51
  81.2 5.9 %collective-permute-start.19 = (bf16[3,80,128]{2,1,0:T(8,128)(2,1)}, bf16[3,80,128]{2,1,0:T(8,128)(2,1)S(1)}, u32[]{:S(2)}, u32[]{:S(2)}) collective-permute-start(bf16[3,80,128]{2,1,0:T(8,128)(2,1)} %get-tuple-element.69), channel_id=1, source_target_pairs={{0,4},{2,6},{4,0},{6,2},{1,5},{3,7},{5,1},{7,3},{8,12},{10,14},{12... | collective-permute-start | bytes 184328 | tf_op jit(solution)/shard_map/ppermute | solution.py:51
  83.6 3.5 %copy-start.4 = (bf16[3,80,128]{2,1,0:T(8,128)(2,1)}, bf16[3,80,128]{2,1,0:T(8,128)(2,1)S(1)}, u32[]{:S(2)}) copy-start(bf16[3,80,128]{2,1,0:T(8,128)(2,1)S(1)} %collective-permute-done.17.refs_1_) | copy-start | bytes 184324
  86.3 0.9 copy-start.5
  87.2 0.6 copy-start.6

commit v6 on v5

--- a/solution.py
+++ b/solution.py
@@ -62,6 +62,9 @@
 
 def whole(*shape):
     return pl.BlockSpec(shape, lambda i: (0,) * len(shape))
+
+
+IN_VMEM = pl.BlockSpec(memory_space=pltpu.VMEM)
 
 
 def prepare_body(q_ref, k_ref, v_ref, pos_ref, tq_ref, tk_ref, tv_ref, freq_ref, swap_ref, *outs):
@@ -248,7 +251,7 @@
 
 
 STATE = [((2 * TILE, HD), F32)] * 3
-STATE_SPECS = [pl.BlockSpec(memory_space=pltpu.VMEM)] * 3
+STATE_SPECS = [IN_VMEM] * 3
 
 
 def merge_body(*refs):
@@ -274,9 +277,9 @@
         merge_body,
         out_shape=[jax.ShapeDtypeStruct((3, 64 + TEXT, HD), BF16)] * 4,
         grid=(1,),
-        in_specs=[whole(3, SITE + STATS, HD)] * 4,
-        out_specs=[whole(3, 64 + TEXT, HD)] * 4,
-        compiler_params=pltpu.CompilerParams(vmem_limit_bytes=VMEM),
+        in_specs=[IN_VMEM] * 4,
+        out_specs=[IN_VMEM] * 4,
+        compiler_params=pltpu.CompilerParams(vmem_limit_bytes=VMEM // 2),
         name="merge",
     )(*sites)
 
@@ -303,9 +306,9 @@
         finish_body,
         out_shape=[jax.ShapeDtypeStruct((12, 64, HD), BF16), jax.ShapeDtypeStruct((6, 4, HD), BF16)],
         grid=(1,),
-        in_specs=[whole(3, 64 + TEXT, HD)] * 4,
+        in_specs=[IN_VMEM] * 4,
         out_specs=[whole(12, 64, HD), whole(6, 4, HD)],
-        compiler_params=pltpu.CompilerParams(vmem_limit_bytes=VMEM),
+        compiler_params=pltpu.CompilerParams(vmem_limit_bytes=VMEM // 2),
         name="finish",
     )(*messages)
 

time: 89.8 us -> 84.8 us (0.944)
  Pallas kernels: 24 us -> 21.1 us
  local copies, waits for them, and re-layouts: 5.4 us -> 3.4 us
    unnamed x24 -> x10, local copies, waits for them, and re-layouts: 3.87 us -> 1.88 us
    pallas_call x1, Pallas kernels: 2.58 us -> 0.63 us  [merge(): pl.pallas_call(merge_body, out_shape=[jax.ShapeDtypeStruct((3, 64 + TEXT,...]
    pallas_call x1, Pallas kernels: 1.66 us -> 0.75 us  [finish(): pl.pallas_call(finish_body, out_shape=[jax.ShapeDtypeStruct((12, 64, HD),...]
  transfers between devices with their start and end apart: 20 -> 20, of which waited for: 16 -> 16; matrix products, arithmetic and copies ran while one was open for 3% -> 3% of each run, Pallas kernels for 13% -> 14%
where the time goes in v6:
time: 84.8 us; the launch traced here: 84.5 us
  starting transfers between devices  30 us (35%)
  waiting for transfers between devices  28.6 us (34%)
  Pallas kernels  21.1 us (25%)
  local copies, waits for them, and re-layouts  3.4 us (4%)
  between operations  1.41 us (2%)
    ppermute x12, starting transfers between devices, shift(): return lax.ppermute(v, axis, [(i, (i + step) % 4) for i in range(4)])  18.5 us
    pallas_call x4, Pallas kernels, attend(): pl.pallas_call(body, out_shape=[jax.ShapeDtypeStruct((3,) + s, t) for s,...  17 us
    ppermute x12, waiting for transfers between devices, shift(): return lax.ppermute(v, axis, [(i, (i + step) % 4) for i in range(4)])  16.7 us
    ppermute x8, waiting for transfers between devices, z_shift(): lax.ppermute(v, ZAXES, [(line(z), line((z + step) % 8)) for z in range(8)])  11.9 us
    ppermute x8, starting transfers between devices, z_shift(): lax.ppermute(v, ZAXES, [(line(z), line((z + step) % 8)) for z in range(8)])  11.6 us
    pallas_call x1, Pallas kernels, prepare(): pl.pallas_call(prepare_body, out_shape=[jax.ShapeDtypeStruct(o, BF16) for...  2.72 us
    unnamed x10, local copies, waits for them, and re-layouts  1.88 us
  transfers between devices with their start and end apart: 20, of which 16 were waited for; matrix products, arithmetic and copies ran while one was open for 3% of the time, Pallas kernels for 14%

profile of v6, /device:TPU:32, one launch (start us, length us, event | category | flops | bytes accessed | tf_op | source)
XLA Modules:
  0.0 84.5 jit_solution(7545702349603703479)
XLA Ops:
  0.6 2.7 %prepare.1 = (bf16[3,3,64,128]{3,2,1,0:T(8,128)(2,1)}, bf16[3,3,64,128]{3,2,1,0:T(8,128)(2,1)}, bf16[3,3,64,128]{3,2,1,0:T(8,128)(2,1)}, bf16[3,3,64,128]{3,2,1,...) custom-call(bf16[12,64,128]{2,1,0:T(8,128)(2,1)} %bitcast.36, ...), custom_call_target="tpu_custom_call" | custom-call | flops 50000000 | bytes 3000000 | tf_op jit(solution)/shard_map/prepare/pallas_call | solution.py:100
  3.3 1.6 %collective-permute-start = (bf16[3,3,64,128]{3,2,1,0:T(8,128)(2,1)}, bf16[3,3,64,128]{3,2,1,0:T(8,128)(2,1)S(1)}, u32[]{:S(2)}, u32[]{:S(2)}) collective-permute-start(bf16[3,3,64,128]{3,2,1,0:T(8,128)(2,1)} %get-tuple-element.38), channel_id=1, source_target_pairs={{0,2},{2,4},{4,6},{6,0},{1,3},{3,5},{5,7},{7,1},{8,10},{10,12},{12... | collective-permute-start | bytes 442376 | tf_op jit(solution)/shard_map/ppermute | solution.py:51
  4.9 1.7 %collective-permute-start.1 = (bf16[3,3,64,128]{3,2,1,0:T(8,128)(2,1)}, bf16[3,3,64,128]{3,2,1,0:T(8,128)(2,1)S(1)}, u32[]{:S(2)}, u32[]{:S(2)}) collective-permute-start(bf16[3,3,64,128]{3,2,1,0:T(8,128)(2,1)} %get-tuple-element.39), channel_id=1, source_target_pairs={{0,6},{2,0},{4,2},{6,4},{1,7},{3,1},{5,3},{7,5},{8,14},{10,8},{12,... | collective-permute-start | bytes 442376 | tf_op jit(solution)/shard_map/ppermute | solution.py:51
  6.6 2.0 %collective-permute-start.2 = (bf16[3,3,64,128]{3,2,1,0:T(8,128)(2,1)}, bf16[3,3,64,128]{3,2,1,0:T(8,128)(2,1)S(1)}, u32[]{:S(2)}, u32[]{:S(2)}) collective-permute-start(bf16[3,3,64,128]{3,2,1,0:T(8,128)(2,1)} %get-tuple-element.40), channel_id=1, source_target_pairs={{0,4},{2,6},{4,0},{6,2},{1,5},{3,7},{5,1},{7,3},{8,12},{10,14},{12... | collective-permute-start | bytes 442376 | tf_op jit(solution)/shard_map/ppermute | solution.py:51
  8.6 0.9 %slice_dynamic-update-slice_fusion.3 = bf16[2,3,272,128]{3,2,1,0:T(8,128)(2,1)S(1)} fusion(bf16[3,3,64,128]{3,2,1,0:T(8,128)(2,1)} %get-tuple-element.37), kind=kLoop, calls=%fused_computation.5 | loop fusion | bytes 196608
  9.5 0.8 bitcast_dynamic-update-slice_fusion.1
  10.3 0.1 collective-permute-done
  10.4 2.6 %collective-permute-done.1 = bf16[3,3,64,128]{3,2,1,0:T(8,128)(2,1)S(1)} collective-permute-done((bf16[3,3,64,128]{3,2,1,0:T(8,128)(2,1)}, bf16[3,3,64,128]{3,2,1,0:T(8,128)(2,1)S(1)}, u32[]{:S(2)}, u32[]{:S(2)}) %collective-permute-start.1) | collective-permute-done | bytes 147488 | tf_op jit(solution)/shard_map/ppermute | solution.py:51
  13.1 1.7 %collective-permute-done.2 = bf16[3,3,64,128]{3,2,1,0:T(8,128)(2,1)S(1)} collective-permute-done((bf16[3,3,64,128]{3,2,1,0:T(8,128)(2,1)}, bf16[3,3,64,128]{3,2,1,0:T(8,128)(2,1)S(1)}, u32[]{:S(2)}, u32[]{:S(2)}) %collective-permute-start.2) | collective-permute-done | bytes 147488 | tf_op jit(solution)/shard_map/ppermute | solution.py:51
  14.8 0.7 constant_dynamic-update-slice_fusion.5.refs_0_.refs_1_.refs_2_.refs_3_
  15.5 1.9 %collective-permute-start.6 = (bf16[2,3,272,128]{3,2,1,0:T(8,128)(2,1)S(1)}, bf16[2,3,272,128]{3,2,1,0:T(8,128)(2,1)S(1)}, u32[]{:S(2)}, u32[]{:S(2)}) collective-permute-start(bf16[2,3,272,128]{3,2,1,0:T(8,128)(2,1)S(1)} %constant_dynamic-update-slice_fusion.5.refs_0_.refs_1_.refs_2_.refs_3_), channel_id=1, source_target_pairs={{0,8},{8,16},{16,24},{24,1},{1,9},{9,17},{17,25},{25,0},{2,10},{10... | collective-permute-start | bytes 1253384 | tf_op jit(solution)/shard_map/ppermute | solution.py:56
  17.4 0.1 collective-permute-start.8
  17.6 0.7 constant_dynamic-update-slice_fusion
  18.4 2.8 %collective-permute-start.3 = (bf16[3,272,128]{2,1,0:T(8,128)(2,1)S(1)}, bf16[3,272,128]{2,1,0:T(8,128)(2,1)S(1)}, u32[]{:S(2)}, u32[]{:S(2)}) collective-permute-start(bf16[3,272,128]{2,1,0:T(8,128)(2,1)S(1)} %get-tuple-element.80), channel_id=1, source_target_pairs={{0,96},{32,0},{64,32},{96,64},{1,97},{33,1},{65,33},{97,65},{2,98}... | collective-permute-start | bytes 626696 | tf_op jit(solution)/shard_map/ppermute | solution.py:51
  21.1 0.0 collective-permute-start.4
  21.1 2.3 %collective-permute-start.5 = (bf16[3,272,128]{2,1,0:T(8,128)(2,1)S(1)}, bf16[3,272,128]{2,1,0:T(8,128)(2,1)S(1)}, u32[]{:S(2)}, u32[]{:S(2)}) collective-permute-start(bf16[3,272,128]{2,1,0:T(8,128)(2,1)S(1)} %get-tuple-element.80), channel_id=1, source_target_pairs={{0,64},{32,96},{64,0},{96,32},{1,65},{33,97},{65,1},{97,33},{2,66}... | collective-permute-start | bytes 626696 | tf_op jit(solution)/shard_map/ppermute | solution.py:51
  23.4 2.6 %collective-permute-done.6.refs_2_.refs_3_.refs_4_.refs_5_ = bf16[2,3,272,128]{3,2,1,0:T(8,128)(2,1)S(1)} collective-permute-done((bf16[2,3,272,128]{3,2,1,0:T(8,128)(2,1)S(1)}, bf16[2,3,272,128]{3,2,1,0:T(8,128)(2,1)S(1)}, u32[]{:S(2)}, u32[]{:S(2)}) %collective-permute-start.6) | collective-permute-done | bytes 417824 | tf_op jit(solution)/shard_map/ppermute | solution.py:56
  26.0 1.9 %collective-permute-start.7 = (bf16[2,3,272,128]{3,2,1,0:T(8,128)(2,1)S(1)}, bf16[2,3,272,128]{3,2,1,0:T(8,128)(2,1)S(1)}, u32[]{:S(2)}, u32[]{:S(2)}) collective-permute-start(bf16[2,3,272,128]{3,2,1,0:T(8,128)(2,1)S(1)} %collective-permute-done.6.refs_2_.refs_3_.refs_4_.refs_5_), channel_id=1, source_target_pairs={{0,8},{8,16},{16,24},{24,1},{1,9},{9,17},{17,25},{25,0},{2,10},{10... | collective-permute-start | bytes 1253384 | tf_op jit(solution)/shard_map/ppermute | solution.py:56
  28.0 0.0 collective-permute-done.8.refs_0_.refs_1_.refs_6_.refs_7_
  28.0 2.3 %collective-permute-start.9 = (bf16[2,3,272,128]{3,2,1,0:T(8,128)(2,1)S(1)}, bf16[2,3,272,128]{3,2,1,0:T(8,128)(2,1)S(1)}, u32[]{:S(2)}, u32[]{:S(2)}) collective-permute-start(bf16[2,3,272,128]{3,2,1,0:T(8,128)(2,1)S(1)} %collective-permute-done.8.refs_0_.refs_1_.refs_6_.refs_7_), channel_id=1, source_target_pairs={{0,25},{8,0},{16,8},{24,16},{1,24},{9,1},{17,9},{25,17},{2,27},{10... | collective-permute-start | bytes 1253384 | tf_op jit(solution)/shard_map/ppermute | solution.py:56
  30.3 1.9 %collective-permute-done.4 = bf16[3,272,128]{2,1,0:T(8,128)(2,1)S(1)} collective-permute-done((bf16[3,272,128]{2,1,0:T(8,128)(2,1)S(1)}, bf16[3,272,128]{2,1,0:T(8,128)(2,1)S(1)}, u32[]{:S(2)}, u32[]{:S(2)}) %collective-permute-start.4) | collective-permute-done | bytes 208928 | tf_op jit(solution)/shard_map/ppermute | solution.py:51
  32.2 0.0 collective-permute-done.5
  32.2 3.5 %attend_first.1 = (f32[3,1088,128]{2,1,0:T(8,128)S(1)}, f32[3,1088,128]{2,1,0:T(8,128)S(1)}, f32[3,1088,128]{2,1,0:T(8,128)S(1)}) custom-call(bf16[3,1088,128]{2,1,0:T(8,128)(2,1)S(1)} %constant_dynamic-update-slice_fusion.1.q_ref, bf16[2,3,272,128]{3,2,1,0:T(8,128)(2,1)S(1)} %constant_dynamic-update-slice_fusion.5.refs_0_.refs_1_.refs_2_.refs_3_, ...), custom_call_target="tpu_custom_call" | custom-call | flops 855638016 | bytes 6786432 | tf_op jit(solution)/shard_map/attend_first/pallas_call | solution.py:239
  35.8 2.6 %collective-permute-done.7.refs_2_.refs_3_.refs_8_.refs_9_ = bf16[2,3,272,128]{3,2,1,0:T(8,128)(2,1)S(1)} collective-permute-done((bf16[2,3,272,128]{3,2,1,0:T(8,128)(2,1)S(1)}, bf16[2,3,272,128]{3,2,1,0:T(8,128)(2,1)S(1)}, u32[]{:S(2)}, u32[]{:S(2)}) %collective-permute-start.7) | collective-permute-done | bytes 417824 | tf_op jit(solution)/shard_map/ppermute | solution.py:56
  38.4 0.4 collective-permute-done.9.refs_4_.refs_5_.refs_10_.refs_11_
  38.8 3.0 %collective-permute-start.10 = (bf16[2,3,272,128]{3,2,1,0:T(8,128)(2,1)S(1)}, bf16[2,3,272,128]{3,2,1,0:T(8,128)(2,1)S(1)}, u32[]{:S(2)}, u32[]{:S(2)}) collective-permute-start(bf16[2,3,272,128]{3,2,1,0:T(8,128)(2,1)S(1)} %collective-permute-done.7.refs_2_.refs_3_.refs_8_.refs_9_), channel_id=1, source_target_pairs={{0,8},{8,16},{16,24},{24,1},{1,9},{9,17},{17,25},{25,0},{2,10},{10... | collective-permute-start | bytes 1253384 | tf_op jit(solution)/shard_map/ppermute | solution.py:56
  41.8 4.7 %attend_2.1 = (f32[3,1088,128]{2,1,0:T(8,128)S(1)}, f32[3,1088,128]{2,1,0:T(8,128)S(1)}, f32[3,1088,128]{2,1,0:T(8,128)S(1)}) custom-call(bf16[3,1088,128]{2,1,0:T(8,128)(2,1)S(1)} %constant_dynamic-update-slice_fusion.1.q_ref, f32[3,1088,128]{2,1,0:T(8,128)S(1)} %get-tuple-element.48.acc_ref, f32[3,1088,128]{2,1,0:T(8,128)S(1)} %get-tuple-element.49.top_ref, ...), custom_call_target="tpu_custom_call" | custom-call | flops 1283457024 | bytes 7179648 | tf_op jit(solution)/shard_map/attend_2/pallas_call | solution.py:239
  46.5 2.0 %collective-permute-done.10.refs_0_.refs_1_.refs_12_.refs_13_ = bf16[2,3,272,128]{3,2,1,0:T(8,128)(2,1)S(1)} collective-permute-done((bf16[2,3,272,128]{3,2,1,0:T(8,128)(2,1)S(1)}, bf16[2,3,272,128]{3,2,1,0:T(8,128)(2,1)S(1)}, u32[]{:S(2)}, u32[]{:S(2)}) %collective-permute-start.10) | collective-permute-done | bytes 417824 | tf_op jit(solution)/shard_map/ppermute | solution.py:56
  48.5 2.5 %collective-permute-done.11.refs_2_.refs_3_.refs_14_.refs_15_ = bf16[2,3,272,128]{3,2,1,0:T(8,128)(2,1)S(1)} collective-permute-done((bf16[2,3,272,128]{3,2,1,0:T(8,128)(2,1)S(1)}, bf16[2,3,272,128]{3,2,1,0:T(8,128)(2,1)S(1)}, u32[]{:S(2)}, u32[]{:S(2)}) %collective-permute-start.11) | collective-permute-done | bytes 417824 | tf_op jit(solution)/shard_map/ppermute | solution.py:56
  51.1 2.0 %collective-permute-start.12 = (bf16[3,272,128]{2,1,0:T(8,128)(2,1)S(1)}, bf16[3,272,128]{2,1,0:T(8,128)(2,1)S(1)}, u32[]{:S(2)}, u32[]{:S(2)}) collective-permute-start(bf16[3,272,128]{2,1,0:T(8,128)(2,1)S(1)} %slice_bitcast_fusion.1), channel_id=1, source_target_pairs={{0,8},{8,16},{16,24},{24,1},{1,9},{9,17},{17,25},{25,0},{2,10},{10... | collective-permute-start | bytes 626696 | tf_op jit(solution)/shard_map/ppermute | solution.py:56
  53.1 0.4 collective-permute-start.13
  54.1 3.3 %attend_3.1 = (f32[3,1088,128]{2,1,0:T(8,128)S(1)}, f32[3,1088,128]{2,1,0:T(8,128)S(1)}, f32[3,1088,128]{2,1,0:T(8,128)S(1)}) custom-call(bf16[3,1088,128]{2,1,0:T(8,128)(2,1)S(1)} %constant_dynamic-update-slice_fusion.1.q_ref, f32[3,1088,128]{2,1,0:T(8,128)S(1)} %get-tuple-element.54.acc_ref, f32[3,1088,128]{2,1,0:T(8,128)S(1)} %get-tuple-element.55.top_ref, ...), custom_call_target="tpu_custom_call" | custom-call | flops 855638016 | bytes 6786432 | tf_op jit(solution)/shard_map/attend_3/pallas_call | solution.py:239
  57.4 1.6 %collective-permute-done.13.refs_1_.refs_17_ = bf16[3,272,128]{2,1,0:T(8,128)(2,1)S(1)} collective-permute-done((bf16[3,272,128]{2,1,0:T(8,128)(2,1)S(1)}, bf16[3,272,128]{2,1,0:T(8,128)(2,1)S(1)}, u32[]{:S(2)}, u32[]{:S(2)}) %collective-permute-start.13) | collective-permute-done | bytes 208928 | tf_op jit(solution)/shard_map/ppermute | solution.py:56
  59.0 5.5 %attend_last.1 = (bf16[3,288,128]{2,1,0:T(8,128)(2,1)S(1)}, bf16[3,288,128]{2,1,0:T(8,128)(2,1)S(1)}, bf16[3,288,128]{2,1,0:T(8,128)(2,1)S(1)}, bf16[3,288,128]{2,1,0:T(8,128)(2,1)S(1)}) custom-call(s32[1]{0:T(128)S(6)} %copy.27.count_ref, bf16[3,1088,128]{2,1,0:T(8,128)(2,1)S(1)} %constant_dynamic-update-slice_fusion.1.q_ref, ...), custom_call_target="tpu_custom_call" | custom-call | flops 855638016 | bytes 6786432 | tf_op jit(solution)/shard_map/attend_last/pallas_call | solution.py:239
  64.5 1.6 %collective-permute-start.14 = (bf16[3,288,128]{2,1,0:T(8,128)(2,1)S(1)}, bf16[3,288,128]{2,1,0:T(8,128)(2,1)S(1)}, u32[]{:S(2)}, u32[]{:S(2)}) collective-permute-start(bf16[3,288,128]{2,1,0:T(8,128)(2,1)S(1)} %get-tuple-element.63), channel_id=1, source_target_pairs={{0,32},{32,64},{64,96},{96,0},{1,33},{33,65},{65,97},{97,1},{2,34}... | collective-permute-start | bytes 663560 | tf_op jit(solution)/shard_map/ppermute | solution.py:51
  66.1 1.7 %collective-permute-start.15 = (bf16[3,288,128]{2,1,0:T(8,128)(2,1)S(1)}, bf16[3,288,128]{2,1,0:T(8,128)(2,1)S(1)}, u32[]{:S(2)}, u32[]{:S(2)}) collective-permute-start(bf16[3,288,128]{2,1,0:T(8,128)(2,1)S(1)} %get-tuple-element.64), channel_id=1, source_target_pairs={{0,96},{32,0},{64,32},{96,64},{1,97},{33,1},{65,33},{97,65},{2,98}... | collective-permute-start | bytes 663560 | tf_op jit(solution)/shard_map/ppermute | solution.py:51
  67.9 1.8 %collective-permute-start.16 = (bf16[3,288,128]{2,1,0:T(8,128)(2,1)S(1)}, bf16[3,288,128]{2,1,0:T(8,128)(2,1)S(1)}, u32[]{:S(2)}, u32[]{:S(2)}) collective-permute-start(bf16[3,288,128]{2,1,0:T(8,128)(2,1)S(1)} %get-tuple-element.65), channel_id=1, source_target_pairs={{0,64},{32,96},{64,0},{96,32},{1,65},{33,97},{65,1},{97,33},{2,66}... | collective-permute-start | bytes 663560 | tf_op jit(solution)/shard_map/ppermute | solution.py:51
  69.7 2.1 %collective-permute-done.14.refs_1_ = bf16[3,288,128]{2,1,0:T(8,128)(2,1)S(1)} collective-permute-done((bf16[3,288,128]{2,1,0:T(8,128)(2,1)S(1)}, bf16[3,288,128]{2,1,0:T(8,128)(2,1)S(1)}, u32[]{:S(2)}, u32[]{:S(2)}) %collective-permute-start.14) | collective-permute-done | bytes 221216 | tf_op jit(solution)/shard_map/ppermute | solution.py:51
  71.8 1.9 %collective-permute-done.15.refs_2_ = bf16[3,288,128]{2,1,0:T(8,128)(2,1)S(1)} collective-permute-done((bf16[3,288,128]{2,1,0:T(8,128)(2,1)S(1)}, bf16[3,288,128]{2,1,0:T(8,128)(2,1)S(1)}, u32[]{:S(2)}, u32[]{:S(2)}) %collective-permute-start.15) | collective-permute-done | bytes 221216 | tf_op jit(solution)/shard_map/ppermute | solution.py:51
  73.7 1.6 %collective-permute-done.16.refs_3_ = bf16[3,288,128]{2,1,0:T(8,128)(2,1)S(1)} collective-permute-done((bf16[3,288,128]{2,1,0:T(8,128)(2,1)S(1)}, bf16[3,288,128]{2,1,0:T(8,128)(2,1)S(1)}, u32[]{:S(2)}, u32[]{:S(2)}) %collective-permute-start.16) | collective-permute-done | bytes 221216 | tf_op jit(solution)/shard_map/ppermute | solution.py:51
  75.3 0.6 merge.1
  75.9 1.5 %collective-permute-start.17 = (bf16[3,80,128]{2,1,0:T(8,128)(2,1)S(1)}, bf16[3,80,128]{2,1,0:T(8,128)(2,1)S(1)}, u32[]{:S(2)}, u32[]{:S(2)}) collective-permute-start(bf16[3,80,128]{2,1,0:T(8,128)(2,1)S(1)} %get-tuple-element.67), channel_id=1, source_target_pairs={{0,6},{2,0},{4,2},{6,4},{1,7},{3,1},{5,3},{7,5},{8,14},{10,8},{12,... | collective-permute-start | bytes 184328 | tf_op jit(solution)/shard_map/ppermute | solution.py:51
  77.5 0.6 collective-permute-start.18
  78.0 1.0 %collective-permute-start.19 = (bf16[3,80,128]{2,1,0:T(8,128)(2,1)S(1)}, bf16[3,80,128]{2,1,0:T(8,128)(2,1)S(1)}, u32[]{:S(2)}, u32[]{:S(2)}) collective-permute-start(bf16[3,80,128]{2,1,0:T(8,128)(2,1)S(1)} %get-tuple-element.69), channel_id=1, source_target_pairs={{0,4},{2,6},{4,0},{6,2},{1,5},{3,7},{5,1},{7,3},{8,12},{10,14},{12... | collective-permute-start | bytes 184328 | tf_op jit(solution)/shard_map/ppermute | solution.py:51
  79.0 1.2 %collective-permute-done.17.refs_1_ = bf16[3,80,128]{2,1,0:T(8,128)(2,1)S(1)} collective-permute-done((bf16[3,80,128]{2,1,0:T(8,128)(2,1)S(1)}, bf16[3,80,128]{2,1,0:T(8,128)(2,1)S(1)}, u32[]{:S(2)}, u32[]{:S(2)}) %collective-permute-start.17) | collective-permute-done | bytes 61472 | tf_op jit(solution)/shard_map/ppermute | solution.py:51
  80.2 2.7 %collective-permute-done.18.refs_2_ = bf16[3,80,128]{2,1,0:T(8,128)(2,1)S(1)} collective-permute-done((bf16[3,80,128]{2,1,0:T(8,128)(2,1)S(1)}, bf16[3,80,128]{2,1,0:T(8,128)(2,1)S(1)}, u32[]{:S(2)}, u32[]{:S(2)}) %collective-permute-start.18) | collective-permute-done | bytes 61472 | tf_op jit(solution)/shard_map/ppermute | solution.py:51
  82.9 0.9 %collective-permute-done.19.refs_3_ = bf16[3,80,128]{2,1,0:T(8,128)(2,1)S(1)} collective-permute-done((bf16[3,80,128]{2,1,0:T(8,128)(2,1)S(1)}, bf16[3,80,128]{2,1,0:T(8,128)(2,1)S(1)}, u32[]{:S(2)}, u32[]{:S(2)}) %collective-permute-start.19) | collective-permute-done | bytes 61472 | tf_op jit(solution)/shard_map/ppermute | solution.py:51
  83.8 0.7 finish.1
  (14 shorter events, 0.2 us)
Async XLA Ops:
  3.3 7.1 %collective-permute-start = (bf16[3,3,64,128]{3,2,1,0:T(8,128)(2,1)}, bf16[3,3,64,128]{3,2,1,0:T(8,128)(2,1)S(1)}, u32[]{:S(2)}, u32[]{:S(2)}) collective-permute-start(bf16[3,3,64,128]{3,2,1,0:T(8,128)(2,1)} %get-tuple-element.38), channel_id=1, source_target_pairs={{0,2},{2,4},{4,6},{6,0},{1,3},{3,5},{5,7},{7,1},{8,10},{10,12},{12... | collective-permute-start | bytes 442376 | tf_op jit(solution)/shard_map/ppermute | solution.py:51
  4.9 8.1 %collective-permute-start.1 = (bf16[3,3,64,128]{3,2,1,0:T(8,128)(2,1)}, bf16[3,3,64,128]{3,2,1,0:T(8,128)(2,1)S(1)}, u32[]{:S(2)}, u32[]{:S(2)}) collective-permute-start(bf16[3,3,64,128]{3,2,1,0:T(8,128)(2,1)} %get-tuple-element.39), channel_id=1, source_target_pairs={{0,6},{2,0},{4,2},{6,4},{1,7},{3,1},{5,3},{7,5},{8,14},{10,8},{12,... | collective-permute-start | bytes 442376 | tf_op jit(solution)/shard_map/ppermute | solution.py:51
  6.6 8.2 %collective-permute-start.2 = (bf16[3,3,64,128]{3,2,1,0:T(8,128)(2,1)}, bf16[3,3,64,128]{3,2,1,0:T(8,128)(2,1)S(1)}, u32[]{:S(2)}, u32[]{:S(2)}) collective-permute-start(bf16[3,3,64,128]{3,2,1,0:T(8,128)(2,1)} %get-tuple-element.40), channel_id=1, source_target_pairs={{0,4},{2,6},{4,0},{6,2},{1,5},{3,7},{5,1},{7,3},{8,12},{10,14},{12... | collective-permute-start | bytes 442376 | tf_op jit(solution)/shard_map/ppermute | solution.py:51
  15.5 10.5 %collective-permute-start.6 = (bf16[2,3,272,128]{3,2,1,0:T(8,128)(2,1)S(1)}, bf16[2,3,272,128]{3,2,1,0:T(8,128)(2,1)S(1)}, u32[]{:S(2)}, u32[]{:S(2)}) collective-permute-start(bf16[2,3,272,128]{3,2,1,0:T(8,128)(2,1)S(1)} %constant_dynamic-update-slice_fusion.5.refs_0_.refs_1_.refs_2_.refs_3_), channel_id=1, source_target_pairs={{0,8},{8,16},{16,24},{24,1},{1,9},{9,17},{17,25},{25,0},{2,10},{10... | collective-permute-start | bytes 1253384 | tf_op jit(solution)/shard_map/ppermute | solution.py:56
  17.4 10.5 %collective-permute-start.8 = (bf16[2,3,272,128]{3,2,1,0:T(8,128)(2,1)S(1)}, bf16[2,3,272,128]{3,2,1,0:T(8,128)(2,1)S(1)}, u32[]{:S(2)}, u32[]{:S(2)}) collective-permute-start(bf16[2,3,272,128]{3,2,1,0:T(8,128)(2,1)S(1)} %constant_dynamic-update-slice_fusion.5.refs_0_.refs_1_.refs_2_.refs_3_), channel_id=1, source_target_pairs={{0,25},{8,0},{16,8},{24,16},{1,24},{9,1},{17,9},{25,17},{2,27},{10... | collective-permute-start | bytes 1253384 | tf_op jit(solution)/shard_map/ppermute | solution.py:56
  18.4 11.9 %collective-permute-start.3 = (bf16[3,272,128]{2,1,0:T(8,128)(2,1)S(1)}, bf16[3,272,128]{2,1,0:T(8,128)(2,1)S(1)}, u32[]{:S(2)}, u32[]{:S(2)}) collective-permute-start(bf16[3,272,128]{2,1,0:T(8,128)(2,1)S(1)} %get-tuple-element.80), channel_id=1, source_target_pairs={{0,96},{32,0},{64,32},{96,64},{1,97},{33,1},{65,33},{97,65},{2,98}... | collective-permute-start | bytes 626696 | tf_op jit(solution)/shard_map/ppermute | solution.py:51
  21.1 11.1 %collective-permute-start.4 = (bf16[3,272,128]{2,1,0:T(8,128)(2,1)S(1)}, bf16[3,272,128]{2,1,0:T(8,128)(2,1)S(1)}, u32[]{:S(2)}, u32[]{:S(2)}) collective-permute-start(bf16[3,272,128]{2,1,0:T(8,128)(2,1)S(1)} %get-tuple-element.80), channel_id=1, source_target_pairs={{0,32},{32,64},{64,96},{96,0},{1,33},{33,65},{65,97},{97,1},{2,34}... | collective-permute-start | bytes 626696 | tf_op jit(solution)/shard_map/ppermute | solution.py:51
  21.1 11.1 %collective-permute-start.5 = (bf16[3,272,128]{2,1,0:T(8,128)(2,1)S(1)}, bf16[3,272,128]{2,1,0:T(8,128)(2,1)S(1)}, u32[]{:S(2)}, u32[]{:S(2)}) collective-permute-start(bf16[3,272,128]{2,1,0:T(8,128)(2,1)S(1)} %get-tuple-element.80), channel_id=1, source_target_pairs={{0,64},{32,96},{64,0},{96,32},{1,65},{33,97},{65,1},{97,33},{2,66}... | collective-permute-start | bytes 626696 | tf_op jit(solution)/shard_map/ppermute | solution.py:51
  26.0 12.3 %collective-permute-start.7 = (bf16[2,3,272,128]{3,2,1,0:T(8,128)(2,1)S(1)}, bf16[2,3,272,128]{3,2,1,0:T(8,128)(2,1)S(1)}, u32[]{:S(2)}, u32[]{:S(2)}) collective-permute-start(bf16[2,3,272,128]{3,2,1,0:T(8,128)(2,1)S(1)} %collective-permute-done.6.refs_2_.refs_3_.refs_4_.refs_5_), channel_id=1, source_target_pairs={{0,8},{8,16},{16,24},{24,1},{1,9},{9,17},{17,25},{25,0},{2,10},{10... | collective-permute-start | bytes 1253384 | tf_op jit(solution)/shard_map/ppermute | solution.py:56
  28.0 10.9 %collective-permute-start.9 = (bf16[2,3,272,128]{3,2,1,0:T(8,128)(2,1)S(1)}, bf16[2,3,272,128]{3,2,1,0:T(8,128)(2,1)S(1)}, u32[]{:S(2)}, u32[]{:S(2)}) collective-permute-start(bf16[2,3,272,128]{3,2,1,0:T(8,128)(2,1)S(1)} %collective-permute-done.8.refs_0_.refs_1_.refs_6_.refs_7_), channel_id=1, source_target_pairs={{0,25},{8,0},{16,8},{24,16},{1,24},{9,1},{17,9},{25,17},{2,27},{10... | collective-permute-start | bytes 1253384 | tf_op jit(solution)/shard_map/ppermute | solution.py:56
  38.8 9.7 %collective-permute-start.10 = (bf16[2,3,272,128]{3,2,1,0:T(8,128)(2,1)S(1)}, bf16[2,3,272,128]{3,2,1,0:T(8,128)(2,1)S(1)}, u32[]{:S(2)}, u32[]{:S(2)}) collective-permute-start(bf16[2,3,272,128]{3,2,1,0:T(8,128)(2,1)S(1)} %collective-permute-done.7.refs_2_.refs_3_.refs_8_.refs_9_), channel_id=1, source_target_pairs={{0,8},{8,16},{16,24},{24,1},{1,9},{9,17},{17,25},{25,0},{2,10},{10... | collective-permute-start | bytes 1253384 | tf_op jit(solution)/shard_map/ppermute | solution.py:56
  41.8 9.3 %collective-permute-start.11 = (bf16[2,3,272,128]{3,2,1,0:T(8,128)(2,1)S(1)}, bf16[2,3,272,128]{3,2,1,0:T(8,128)(2,1)S(1)}, u32[]{:S(2)}, u32[]{:S(2)}) collective-permute-start(bf16[2,3,272,128]{3,2,1,0:T(8,128)(2,1)S(1)} %collective-permute-done.9.refs_4_.refs_5_.refs_10_.refs_11_), channel_id=1, source_target_pairs={{0,25},{8,0},{16,8},{24,16},{1,24},{9,1},{17,9},{25,17},{2,27},{10... | collective-permute-start | bytes 1253384 | tf_op jit(solution)/shard_map/ppermute | solution.py:56
  51.1 6.3 %collective-permute-start.12 = (bf16[3,272,128]{2,1,0:T(8,128)(2,1)S(1)}, bf16[3,272,128]{2,1,0:T(8,128)(2,1)S(1)}, u32[]{:S(2)}, u32[]{:S(2)}) collective-permute-start(bf16[3,272,128]{2,1,0:T(8,128)(2,1)S(1)} %slice_bitcast_fusion.1), channel_id=1, source_target_pairs={{0,8},{8,16},{16,24},{24,1},{1,9},{9,17},{17,25},{25,0},{2,10},{10... | collective-permute-start | bytes 626696 | tf_op jit(solution)/shard_map/ppermute | solution.py:56
  53.1 5.9 %collective-permute-start.13 = (bf16[3,272,128]{2,1,0:T(8,128)(2,1)S(1)}, bf16[3,272,128]{2,1,0:T(8,128)(2,1)S(1)}, u32[]{:S(2)}, u32[]{:S(2)}) collective-permute-start(bf16[3,272,128]{2,1,0:T(8,128)(2,1)S(1)} %slice_bitcast_fusion), channel_id=1, source_target_pairs={{0,25},{8,0},{16,8},{24,16},{1,24},{9,1},{17,9},{25,17},{2,27},{10... | collective-permute-start | bytes 626696 | tf_op jit(solution)/shard_map/ppermute | solution.py:56
  64.5 7.2 %collective-permute-start.14 = (bf16[3,288,128]{2,1,0:T(8,128)(2,1)S(1)}, bf16[3,288,128]{2,1,0:T(8,128)(2,1)S(1)}, u32[]{:S(2)}, u32[]{:S(2)}) collective-permute-start(bf16[3,288,128]{2,1,0:T(8,128)(2,1)S(1)} %get-tuple-element.63), channel_id=1, source_target_pairs={{0,32},{32,64},{64,96},{96,0},{1,33},{33,65},{65,97},{97,1},{2,34}... | collective-permute-start | bytes 663560 | tf_op jit(solution)/shard_map/ppermute | solution.py:51
  66.1 7.6 %collective-permute-start.15 = (bf16[3,288,128]{2,1,0:T(8,128)(2,1)S(1)}, bf16[3,288,128]{2,1,0:T(8,128)(2,1)S(1)}, u32[]{:S(2)}, u32[]{:S(2)}) collective-permute-start(bf16[3,288,128]{2,1,0:T(8,128)(2,1)S(1)} %get-tuple-element.64), channel_id=1, source_target_pairs={{0,96},{32,0},{64,32},{96,64},{1,97},{33,1},{65,33},{97,65},{2,98}... | collective-permute-start | bytes 663560 | tf_op jit(solution)/shard_map/ppermute | solution.py:51
  67.9 7.4 %collective-permute-start.16 = (bf16[3,288,128]{2,1,0:T(8,128)(2,1)S(1)}, bf16[3,288,128]{2,1,0:T(8,128)(2,1)S(1)}, u32[]{:S(2)}, u32[]{:S(2)}) collective-permute-start(bf16[3,288,128]{2,1,0:T(8,128)(2,1)S(1)} %get-tuple-element.65), channel_id=1, source_target_pairs={{0,64},{32,96},{64,0},{96,32},{1,65},{33,97},{65,1},{97,33},{2,66}... | collective-permute-start | bytes 663560 | tf_op jit(solution)/shard_map/ppermute | solution.py:51
  75.9 4.3 %collective-permute-start.17 = (bf16[3,80,128]{2,1,0:T(8,128)(2,1)S(1)}, bf16[3,80,128]{2,1,0:T(8,128)(2,1)S(1)}, u32[]{:S(2)}, u32[]{:S(2)}) collective-permute-start(bf16[3,80,128]{2,1,0:T(8,128)(2,1)S(1)} %get-tuple-element.67), channel_id=1, source_target_pairs={{0,6},{2,0},{4,2},{6,4},{1,7},{3,1},{5,3},{7,5},{8,14},{10,8},{12,... | collective-permute-start | bytes 184328 | tf_op jit(solution)/shard_map/ppermute | solution.py:51
  77.5 5.4 %collective-permute-start.18 = (bf16[3,80,128]{2,1,0:T(8,128)(2,1)S(1)}, bf16[3,80,128]{2,1,0:T(8,128)(2,1)S(1)}, u32[]{:S(2)}, u32[]{:S(2)}) collective-permute-start(bf16[3,80,128]{2,1,0:T(8,128)(2,1)S(1)} %get-tuple-element.68), channel_id=1, source_target_pairs={{0,2},{2,4},{4,6},{6,0},{1,3},{3,5},{5,7},{7,1},{8,10},{10,12},{12... | collective-permute-start | bytes 184328 | tf_op jit(solution)/shard_map/ppermute | solution.py:51
  78.0 5.7 %collective-permute-start.19 = (bf16[3,80,128]{2,1,0:T(8,128)(2,1)S(1)}, bf16[3,80,128]{2,1,0:T(8,128)(2,1)S(1)}, u32[]{:S(2)}, u32[]{:S(2)}) collective-permute-start(bf16[3,80,128]{2,1,0:T(8,128)(2,1)S(1)} %get-tuple-element.69), channel_id=1, source_target_pairs={{0,4},{2,6},{4,0},{6,2},{1,5},{3,7},{5,1},{7,3},{8,12},{10,14},{12... | collective-permute-start | bytes 184328 | tf_op jit(solution)/shard_map/ppermute | solution.py:51

commit v7 on v6

--- a/solution.py
+++ b/solution.py
@@ -116,7 +116,7 @@
 def softmax_step(q, k, v, state, live=None):
     s = lax.dot_general(q, k, NT, preferred_element_type=F32)
     if live is not None:
-        s = jnp.where(live(s.shape), s, -jnp.inf)
+        s = s + live
     lanes = (s.shape[0], HD)
     peak = jnp.broadcast_to(jnp.max(s, axis=1, keepdims=True) * SCALE2, lanes)
     if state is not None:
@@ -185,25 +185,28 @@
     return lax.dot_general(block, pick, TN, preferred_element_type=F32)[:n]
 
 
-def live_text(count, shape):
+def live_text(count, first):
     z = lax.axis_index("zb") * 4 + lax.axis_index("za") * 2 + lax.axis_index("zp")
-    lane = lax.broadcasted_iota(jnp.int32, shape, 1)
-    source = jnp.zeros(shape, jnp.int32)
+    all_lanes = lax.broadcasted_iota(jnp.int32, (8, first + TEXT * len(OFFSETS)), 1)
+    lane = jnp.maximum(all_lanes - first, 0)
+    source = jnp.zeros(lane.shape, jnp.int32)
     for i, offset in enumerate(OFFSETS):
         source = jnp.where(lane // TEXT == i, lax.rem(z + (offset + 8), 8), source)
     index = lax.axis_index("x") * 64 + source % 4 * TEXT + lane % TEXT
-    return (source // 4 == lax.axis_index("y") // 2) & (index < count)
+    live = (all_lanes < first) | ((source // 4 == lax.axis_index("y") // 2) & (index < count))
+    return jnp.where(live, 0.0, -jnp.inf)[:1]
 
 
 def last_body(count_ref, q_ref, acc_ref, top_ref, total_ref, *refs):
     parts, text, outs = refs[:2], refs[2:-4], refs[-4:]
     keys, values = joined(parts)
     text_keys, text_values = joined(text)
-    live = lambda shape: live_text(count_ref[0], shape)
+    keys = jnp.concatenate([keys, text_keys], axis=0)
+    values = jnp.concatenate([values, text_values], axis=0)
+    live = live_text(count_ref[0], VIDEO)
     for tile, rows in enumerate(TILES):
         state = kept((acc_ref, top_ref, total_ref), rows)
-        state = softmax_step(q_ref[0, rows], text_keys, text_values, state, live)
-        acc, top, total = softmax_step(q_ref[0, rows], keys, values, state)
+        acc, top, total = softmax_step(q_ref[0, rows], keys, values, state, live)
         mean = (acc / total).astype(BF16)
         level = top + jnp.log2(total)
         for i in range(2):

time: 84.8 us -> 83.8 us (0.988)
  Pallas kernels: 21.1 us -> 20.1 us
    pallas_call x4, Pallas kernels: 17 us -> 16 us  [attend(): pl.pallas_call(body, out_shape=[jax.ShapeDtypeStruct((3,) + s, t) for s,...]
where the time goes in v7:
time: 83.8 us; the launch traced here: 83.5 us
  starting transfers between devices  30 us (36%)
  waiting for transfers between devices  28.6 us (34%)
  Pallas kernels  20.1 us (24%)
  local copies, waits for them, and re-layouts  3.4 us (4%)
  between operations  1.41 us (2%)
    ppermute x12, starting transfers between devices, shift(): return lax.ppermute(v, axis, [(i, (i + step) % 4) for i in range(4)])  18.5 us
    ppermute x12, waiting for transfers between devices, shift(): return lax.ppermute(v, axis, [(i, (i + step) % 4) for i in range(4)])  16.7 us
    pallas_call x4, Pallas kernels, attend(): pl.pallas_call(body, out_shape=[jax.ShapeDtypeStruct((3,) + s, t) for s,...  16 us
    ppermute x8, waiting for transfers between devices, z_shift(): lax.ppermute(v, ZAXES, [(line(z), line((z + step) % 8)) for z in range(8)])  11.9 us
    ppermute x8, starting transfers between devices, z_shift(): lax.ppermute(v, ZAXES, [(line(z), line((z + step) % 8)) for z in range(8)])  11.6 us
    pallas_call x1, Pallas kernels, prepare(): pl.pallas_call(prepare_body, out_shape=[jax.ShapeDtypeStruct(o, BF16) for...  2.72 us
    unnamed x10, local copies, waits for them, and re-layouts  1.88 us
  transfers between devices with their start and end apart: 20, of which 16 were waited for; matrix products, arithmetic and copies ran while one was open for 3% of the time, Pallas kernels for 14%

profile of v7, /device:TPU:32, one launch (start us, length us, event | category | flops | bytes accessed | tf_op | source)
XLA Modules:
  0.0 83.5 jit_solution(6633161435281453673)
XLA Ops:
  0.6 2.7 %prepare.1 = (bf16[3,3,64,128]{3,2,1,0:T(8,128)(2,1)}, bf16[3,3,64,128]{3,2,1,0:T(8,128)(2,1)}, bf16[3,3,64,128]{3,2,1,0:T(8,128)(2,1)}, bf16[3,3,64,128]{3,2,1,...) custom-call(bf16[12,64,128]{2,1,0:T(8,128)(2,1)} %bitcast.36, ...), custom_call_target="tpu_custom_call" | custom-call | flops 50000000 | bytes 3000000 | tf_op jit(solution)/shard_map/prepare/pallas_call | solution.py:100
  3.3 1.6 %collective-permute-start = (bf16[3,3,64,128]{3,2,1,0:T(8,128)(2,1)}, bf16[3,3,64,128]{3,2,1,0:T(8,128)(2,1)S(1)}, u32[]{:S(2)}, u32[]{:S(2)}) collective-permute-start(bf16[3,3,64,128]{3,2,1,0:T(8,128)(2,1)} %get-tuple-element.38), channel_id=1, source_target_pairs={{0,2},{2,4},{4,6},{6,0},{1,3},{3,5},{5,7},{7,1},{8,10},{10,12},{12... | collective-permute-start | bytes 442376 | tf_op jit(solution)/shard_map/ppermute | solution.py:51
  4.9 1.7 %collective-permute-start.1 = (bf16[3,3,64,128]{3,2,1,0:T(8,128)(2,1)}, bf16[3,3,64,128]{3,2,1,0:T(8,128)(2,1)S(1)}, u32[]{:S(2)}, u32[]{:S(2)}) collective-permute-start(bf16[3,3,64,128]{3,2,1,0:T(8,128)(2,1)} %get-tuple-element.39), channel_id=1, source_target_pairs={{0,6},{2,0},{4,2},{6,4},{1,7},{3,1},{5,3},{7,5},{8,14},{10,8},{12,... | collective-permute-start | bytes 442376 | tf_op jit(solution)/shard_map/ppermute | solution.py:51
  6.6 2.0 %collective-permute-start.2 = (bf16[3,3,64,128]{3,2,1,0:T(8,128)(2,1)}, bf16[3,3,64,128]{3,2,1,0:T(8,128)(2,1)S(1)}, u32[]{:S(2)}, u32[]{:S(2)}) collective-permute-start(bf16[3,3,64,128]{3,2,1,0:T(8,128)(2,1)} %get-tuple-element.40), channel_id=1, source_target_pairs={{0,4},{2,6},{4,0},{6,2},{1,5},{3,7},{5,1},{7,3},{8,12},{10,14},{12... | collective-permute-start | bytes 442376 | tf_op jit(solution)/shard_map/ppermute | solution.py:51
  8.6 0.9 %slice_dynamic-update-slice_fusion.3 = bf16[2,3,272,128]{3,2,1,0:T(8,128)(2,1)S(1)} fusion(bf16[3,3,64,128]{3,2,1,0:T(8,128)(2,1)} %get-tuple-element.37), kind=kLoop, calls=%fused_computation.5 | loop fusion | bytes 196608
  9.5 0.8 bitcast_dynamic-update-slice_fusion.1
  10.3 0.1 collective-permute-done
  10.4 2.6 %collective-permute-done.1 = bf16[3,3,64,128]{3,2,1,0:T(8,128)(2,1)S(1)} collective-permute-done((bf16[3,3,64,128]{3,2,1,0:T(8,128)(2,1)}, bf16[3,3,64,128]{3,2,1,0:T(8,128)(2,1)S(1)}, u32[]{:S(2)}, u32[]{:S(2)}) %collective-permute-start.1) | collective-permute-done | bytes 147488 | tf_op jit(solution)/shard_map/ppermute | solution.py:51
  13.1 1.7 %collective-permute-done.2 = bf16[3,3,64,128]{3,2,1,0:T(8,128)(2,1)S(1)} collective-permute-done((bf16[3,3,64,128]{3,2,1,0:T(8,128)(2,1)}, bf16[3,3,64,128]{3,2,1,0:T(8,128)(2,1)S(1)}, u32[]{:S(2)}, u32[]{:S(2)}) %collective-permute-start.2) | collective-permute-done | bytes 147488 | tf_op jit(solution)/shard_map/ppermute | solution.py:51
  14.8 0.7 constant_dynamic-update-slice_fusion.5.refs_0_.refs_1_.refs_2_.refs_3_
  15.5 1.9 %collective-permute-start.6 = (bf16[2,3,272,128]{3,2,1,0:T(8,128)(2,1)S(1)}, bf16[2,3,272,128]{3,2,1,0:T(8,128)(2,1)S(1)}, u32[]{:S(2)}, u32[]{:S(2)}) collective-permute-start(bf16[2,3,272,128]{3,2,1,0:T(8,128)(2,1)S(1)} %constant_dynamic-update-slice_fusion.5.refs_0_.refs_1_.refs_2_.refs_3_), channel_id=1, source_target_pairs={{0,8},{8,16},{16,24},{24,1},{1,9},{9,17},{17,25},{25,0},{2,10},{10... | collective-permute-start | bytes 1253384 | tf_op jit(solution)/shard_map/ppermute | solution.py:56
  17.4 0.1 collective-permute-start.8
  17.6 0.7 constant_dynamic-update-slice_fusion
  18.4 2.8 %collective-permute-start.3 = (bf16[3,272,128]{2,1,0:T(8,128)(2,1)S(1)}, bf16[3,272,128]{2,1,0:T(8,128)(2,1)S(1)}, u32[]{:S(2)}, u32[]{:S(2)}) collective-permute-start(bf16[3,272,128]{2,1,0:T(8,128)(2,1)S(1)} %get-tuple-element.80), channel_id=1, source_target_pairs={{0,96},{32,0},{64,32},{96,64},{1,97},{33,1},{65,33},{97,65},{2,98}... | collective-permute-start | bytes 626696 | tf_op jit(solution)/shard_map/ppermute | solution.py:51
  21.1 0.0 collective-permute-start.4
  21.1 2.3 %collective-permute-start.5 = (bf16[3,272,128]{2,1,0:T(8,128)(2,1)S(1)}, bf16[3,272,128]{2,1,0:T(8,128)(2,1)S(1)}, u32[]{:S(2)}, u32[]{:S(2)}) collective-permute-start(bf16[3,272,128]{2,1,0:T(8,128)(2,1)S(1)} %get-tuple-element.80), channel_id=1, source_target_pairs={{0,64},{32,96},{64,0},{96,32},{1,65},{33,97},{65,1},{97,33},{2,66}... | collective-permute-start | bytes 626696 | tf_op jit(solution)/shard_map/ppermute | solution.py:51
  23.4 2.6 %collective-permute-done.6.refs_2_.refs_3_.refs_4_.refs_5_ = bf16[2,3,272,128]{3,2,1,0:T(8,128)(2,1)S(1)} collective-permute-done((bf16[2,3,272,128]{3,2,1,0:T(8,128)(2,1)S(1)}, bf16[2,3,272,128]{3,2,1,0:T(8,128)(2,1)S(1)}, u32[]{:S(2)}, u32[]{:S(2)}) %collective-permute-start.6) | collective-permute-done | bytes 417824 | tf_op jit(solution)/shard_map/ppermute | solution.py:56
  26.0 1.9 %collective-permute-start.7 = (bf16[2,3,272,128]{3,2,1,0:T(8,128)(2,1)S(1)}, bf16[2,3,272,128]{3,2,1,0:T(8,128)(2,1)S(1)}, u32[]{:S(2)}, u32[]{:S(2)}) collective-permute-start(bf16[2,3,272,128]{3,2,1,0:T(8,128)(2,1)S(1)} %collective-permute-done.6.refs_2_.refs_3_.refs_4_.refs_5_), channel_id=1, source_target_pairs={{0,8},{8,16},{16,24},{24,1},{1,9},{9,17},{17,25},{25,0},{2,10},{10... | collective-permute-start | bytes 1253384 | tf_op jit(solution)/shard_map/ppermute | solution.py:56
  28.0 0.0 collective-permute-done.8.refs_0_.refs_1_.refs_6_.refs_7_
  28.0 2.3 %collective-permute-start.9 = (bf16[2,3,272,128]{3,2,1,0:T(8,128)(2,1)S(1)}, bf16[2,3,272,128]{3,2,1,0:T(8,128)(2,1)S(1)}, u32[]{:S(2)}, u32[]{:S(2)}) collective-permute-start(bf16[2,3,272,128]{3,2,1,0:T(8,128)(2,1)S(1)} %collective-permute-done.8.refs_0_.refs_1_.refs_6_.refs_7_), channel_id=1, source_target_pairs={{0,25},{8,0},{16,8},{24,16},{1,24},{9,1},{17,9},{25,17},{2,27},{10... | collective-permute-start | bytes 1253384 | tf_op jit(solution)/shard_map/ppermute | solution.py:56
  30.3 0.0 collective-permute-done.3
  30.3 1.9 %collective-permute-done.4 = bf16[3,272,128]{2,1,0:T(8,128)(2,1)S(1)} collective-permute-done((bf16[3,272,128]{2,1,0:T(8,128)(2,1)S(1)}, bf16[3,272,128]{2,1,0:T(8,128)(2,1)S(1)}, u32[]{:S(2)}, u32[]{:S(2)}) %collective-permute-start.4) | collective-permute-done | bytes 208928 | tf_op jit(solution)/shard_map/ppermute | solution.py:51
  32.2 3.5 %attend_first.1 = (f32[3,1088,128]{2,1,0:T(8,128)S(1)}, f32[3,1088,128]{2,1,0:T(8,128)S(1)}, f32[3,1088,128]{2,1,0:T(8,128)S(1)}) custom-call(bf16[3,1088,128]{2,1,0:T(8,128)(2,1)S(1)} %constant_dynamic-update-slice_fusion.1.q_ref, bf16[2,3,272,128]{3,2,1,0:T(8,128)(2,1)S(1)} %constant_dynamic-update-slice_fusion.5.refs_0_.refs_1_.refs_2_.refs_3_, ...), custom_call_target="tpu_custom_call" | custom-call | flops 855638016 | bytes 6786432 | tf_op jit(solution)/shard_map/attend_first/pallas_call | solution.py:242
  35.8 2.6 %collective-permute-done.7.refs_2_.refs_3_.refs_8_.refs_9_ = bf16[2,3,272,128]{3,2,1,0:T(8,128)(2,1)S(1)} collective-permute-done((bf16[2,3,272,128]{3,2,1,0:T(8,128)(2,1)S(1)}, bf16[2,3,272,128]{3,2,1,0:T(8,128)(2,1)S(1)}, u32[]{:S(2)}, u32[]{:S(2)}) %collective-permute-start.7) | collective-permute-done | bytes 417824 | tf_op jit(solution)/shard_map/ppermute | solution.py:56
  38.4 0.4 collective-permute-done.9.refs_4_.refs_5_.refs_10_.refs_11_
  38.8 3.0 %collective-permute-start.10 = (bf16[2,3,272,128]{3,2,1,0:T(8,128)(2,1)S(1)}, bf16[2,3,272,128]{3,2,1,0:T(8,128)(2,1)S(1)}, u32[]{:S(2)}, u32[]{:S(2)}) collective-permute-start(bf16[2,3,272,128]{3,2,1,0:T(8,128)(2,1)S(1)} %collective-permute-done.7.refs_2_.refs_3_.refs_8_.refs_9_), channel_id=1, source_target_pairs={{0,8},{8,16},{16,24},{24,1},{1,9},{9,17},{17,25},{25,0},{2,10},{10... | collective-permute-start | bytes 1253384 | tf_op jit(solution)/shard_map/ppermute | solution.py:56
  41.8 4.7 %attend_2.1 = (f32[3,1088,128]{2,1,0:T(8,128)S(1)}, f32[3,1088,128]{2,1,0:T(8,128)S(1)}, f32[3,1088,128]{2,1,0:T(8,128)S(1)}) custom-call(bf16[3,1088,128]{2,1,0:T(8,128)(2,1)S(1)} %constant_dynamic-update-slice_fusion.1.q_ref, f32[3,1088,128]{2,1,0:T(8,128)S(1)} %get-tuple-element.48.acc_ref, f32[3,1088,128]{2,1,0:T(8,128)S(1)} %get-tuple-element.49.top_ref, ...), custom_call_target="tpu_custom_call" | custom-call | flops 1283457024 | bytes 7179648 | tf_op jit(solution)/shard_map/attend_2/pallas_call | solution.py:242
  46.5 2.0 %collective-permute-done.10.refs_0_.refs_1_.refs_12_.refs_13_ = bf16[2,3,272,128]{3,2,1,0:T(8,128)(2,1)S(1)} collective-permute-done((bf16[2,3,272,128]{3,2,1,0:T(8,128)(2,1)S(1)}, bf16[2,3,272,128]{3,2,1,0:T(8,128)(2,1)S(1)}, u32[]{:S(2)}, u32[]{:S(2)}) %collective-permute-start.10) | collective-permute-done | bytes 417824 | tf_op jit(solution)/shard_map/ppermute | solution.py:56
  48.5 2.5 %collective-permute-done.11.refs_2_.refs_3_.refs_14_.refs_15_ = bf16[2,3,272,128]{3,2,1,0:T(8,128)(2,1)S(1)} collective-permute-done((bf16[2,3,272,128]{3,2,1,0:T(8,128)(2,1)S(1)}, bf16[2,3,272,128]{3,2,1,0:T(8,128)(2,1)S(1)}, u32[]{:S(2)}, u32[]{:S(2)}) %collective-permute-start.11) | collective-permute-done | bytes 417824 | tf_op jit(solution)/shard_map/ppermute | solution.py:56
  51.1 2.0 %collective-permute-start.12 = (bf16[3,272,128]{2,1,0:T(8,128)(2,1)S(1)}, bf16[3,272,128]{2,1,0:T(8,128)(2,1)S(1)}, u32[]{:S(2)}, u32[]{:S(2)}) collective-permute-start(bf16[3,272,128]{2,1,0:T(8,128)(2,1)S(1)} %slice_bitcast_fusion.1), channel_id=1, source_target_pairs={{0,8},{8,16},{16,24},{24,1},{1,9},{9,17},{17,25},{25,0},{2,10},{10... | collective-permute-start | bytes 626696 | tf_op jit(solution)/shard_map/ppermute | solution.py:56
  53.1 0.4 collective-permute-start.13
  54.1 3.3 %attend_3.1 = (f32[3,1088,128]{2,1,0:T(8,128)S(1)}, f32[3,1088,128]{2,1,0:T(8,128)S(1)}, f32[3,1088,128]{2,1,0:T(8,128)S(1)}) custom-call(bf16[3,1088,128]{2,1,0:T(8,128)(2,1)S(1)} %constant_dynamic-update-slice_fusion.1.q_ref, f32[3,1088,128]{2,1,0:T(8,128)S(1)} %get-tuple-element.54.acc_ref, f32[3,1088,128]{2,1,0:T(8,128)S(1)} %get-tuple-element.55.top_ref, ...), custom_call_target="tpu_custom_call" | custom-call | flops 855638016 | bytes 6786432 | tf_op jit(solution)/shard_map/attend_3/pallas_call | solution.py:242
  57.4 1.6 %collective-permute-done.13.refs_1_.refs_17_ = bf16[3,272,128]{2,1,0:T(8,128)(2,1)S(1)} collective-permute-done((bf16[3,272,128]{2,1,0:T(8,128)(2,1)S(1)}, bf16[3,272,128]{2,1,0:T(8,128)(2,1)S(1)}, u32[]{:S(2)}, u32[]{:S(2)}) %collective-permute-start.13) | collective-permute-done | bytes 208928 | tf_op jit(solution)/shard_map/ppermute | solution.py:56
  59.0 4.5 %attend_last.1 = (bf16[3,288,128]{2,1,0:T(8,128)(2,1)S(1)}, bf16[3,288,128]{2,1,0:T(8,128)(2,1)S(1)}, bf16[3,288,128]{2,1,0:T(8,128)(2,1)S(1)}, bf16[3,288,128]{2,1,0:T(8,128)(2,1)S(1)}) custom-call(s32[1]{0:T(128)S(6)} %copy.27.count_ref, bf16[3,1088,128]{2,1,0:T(8,128)(2,1)S(1)} %constant_dynamic-update-slice_fusion.1.q_ref, ...), custom_call_target="tpu_custom_call" | custom-call | flops 855638016 | bytes 6786432 | tf_op jit(solution)/shard_map/attend_last/pallas_call | solution.py:242
  63.5 1.6 %collective-permute-start.14 = (bf16[3,288,128]{2,1,0:T(8,128)(2,1)S(1)}, bf16[3,288,128]{2,1,0:T(8,128)(2,1)S(1)}, u32[]{:S(2)}, u32[]{:S(2)}) collective-permute-start(bf16[3,288,128]{2,1,0:T(8,128)(2,1)S(1)} %get-tuple-element.63), channel_id=1, source_target_pairs={{0,32},{32,64},{64,96},{96,0},{1,33},{33,65},{65,97},{97,1},{2,34}... | collective-permute-start | bytes 663560 | tf_op jit(solution)/shard_map/ppermute | solution.py:51
  65.1 1.7 %collective-permute-start.15 = (bf16[3,288,128]{2,1,0:T(8,128)(2,1)S(1)}, bf16[3,288,128]{2,1,0:T(8,128)(2,1)S(1)}, u32[]{:S(2)}, u32[]{:S(2)}) collective-permute-start(bf16[3,288,128]{2,1,0:T(8,128)(2,1)S(1)} %get-tuple-element.64), channel_id=1, source_target_pairs={{0,96},{32,0},{64,32},{96,64},{1,97},{33,1},{65,33},{97,65},{2,98}... | collective-permute-start | bytes 663560 | tf_op jit(solution)/shard_map/ppermute | solution.py:51
  66.9 1.8 %collective-permute-start.16 = (bf16[3,288,128]{2,1,0:T(8,128)(2,1)S(1)}, bf16[3,288,128]{2,1,0:T(8,128)(2,1)S(1)}, u32[]{:S(2)}, u32[]{:S(2)}) collective-permute-start(bf16[3,288,128]{2,1,0:T(8,128)(2,1)S(1)} %get-tuple-element.65), channel_id=1, source_target_pairs={{0,64},{32,96},{64,0},{96,32},{1,65},{33,97},{65,1},{97,33},{2,66}... | collective-permute-start | bytes 663560 | tf_op jit(solution)/shard_map/ppermute | solution.py:51
  68.7 2.1 %collective-permute-done.14.refs_1_ = bf16[3,288,128]{2,1,0:T(8,128)(2,1)S(1)} collective-permute-done((bf16[3,288,128]{2,1,0:T(8,128)(2,1)S(1)}, bf16[3,288,128]{2,1,0:T(8,128)(2,1)S(1)}, u32[]{:S(2)}, u32[]{:S(2)}) %collective-permute-start.14) | collective-permute-done | bytes 221216 | tf_op jit(solution)/shard_map/ppermute | solution.py:51
  70.8 1.9 %collective-permute-done.15.refs_2_ = bf16[3,288,128]{2,1,0:T(8,128)(2,1)S(1)} collective-permute-done((bf16[3,288,128]{2,1,0:T(8,128)(2,1)S(1)}, bf16[3,288,128]{2,1,0:T(8,128)(2,1)S(1)}, u32[]{:S(2)}, u32[]{:S(2)}) %collective-permute-start.15) | collective-permute-done | bytes 221216 | tf_op jit(solution)/shard_map/ppermute | solution.py:51
  72.7 1.6 %collective-permute-done.16.refs_3_ = bf16[3,288,128]{2,1,0:T(8,128)(2,1)S(1)} collective-permute-done((bf16[3,288,128]{2,1,0:T(8,128)(2,1)S(1)}, bf16[3,288,128]{2,1,0:T(8,128)(2,1)S(1)}, u32[]{:S(2)}, u32[]{:S(2)}) %collective-permute-start.16) | collective-permute-done | bytes 221216 | tf_op jit(solution)/shard_map/ppermute | solution.py:51
  74.3 0.6 merge.1
  74.9 1.5 %collective-permute-start.17 = (bf16[3,80,128]{2,1,0:T(8,128)(2,1)S(1)}, bf16[3,80,128]{2,1,0:T(8,128)(2,1)S(1)}, u32[]{:S(2)}, u32[]{:S(2)}) collective-permute-start(bf16[3,80,128]{2,1,0:T(8,128)(2,1)S(1)} %get-tuple-element.67), channel_id=1, source_target_pairs={{0,6},{2,0},{4,2},{6,4},{1,7},{3,1},{5,3},{7,5},{8,14},{10,8},{12,... | collective-permute-start | bytes 184328 | tf_op jit(solution)/shard_map/ppermute | solution.py:51
  76.5 0.6 collective-permute-start.18
  77.0 1.0 %collective-permute-start.19 = (bf16[3,80,128]{2,1,0:T(8,128)(2,1)S(1)}, bf16[3,80,128]{2,1,0:T(8,128)(2,1)S(1)}, u32[]{:S(2)}, u32[]{:S(2)}) collective-permute-start(bf16[3,80,128]{2,1,0:T(8,128)(2,1)S(1)} %get-tuple-element.69), channel_id=1, source_target_pairs={{0,4},{2,6},{4,0},{6,2},{1,5},{3,7},{5,1},{7,3},{8,12},{10,14},{12... | collective-permute-start | bytes 184328 | tf_op jit(solution)/shard_map/ppermute | solution.py:51
  78.0 1.2 %collective-permute-done.17.refs_1_ = bf16[3,80,128]{2,1,0:T(8,128)(2,1)S(1)} collective-permute-done((bf16[3,80,128]{2,1,0:T(8,128)(2,1)S(1)}, bf16[3,80,128]{2,1,0:T(8,128)(2,1)S(1)}, u32[]{:S(2)}, u32[]{:S(2)}) %collective-permute-start.17) | collective-permute-done | bytes 61472 | tf_op jit(solution)/shard_map/ppermute | solution.py:51
  79.2 2.7 %collective-permute-done.18.refs_2_ = bf16[3,80,128]{2,1,0:T(8,128)(2,1)S(1)} collective-permute-done((bf16[3,80,128]{2,1,0:T(8,128)(2,1)S(1)}, bf16[3,80,128]{2,1,0:T(8,128)(2,1)S(1)}, u32[]{:S(2)}, u32[]{:S(2)}) %collective-permute-start.18) | collective-permute-done | bytes 61472 | tf_op jit(solution)/shard_map/ppermute | solution.py:51
  81.9 0.9 %collective-permute-done.19.refs_3_ = bf16[3,80,128]{2,1,0:T(8,128)(2,1)S(1)} collective-permute-done((bf16[3,80,128]{2,1,0:T(8,128)(2,1)S(1)}, bf16[3,80,128]{2,1,0:T(8,128)(2,1)S(1)}, u32[]{:S(2)}, u32[]{:S(2)}) %collective-permute-start.19) | collective-permute-done | bytes 61472 | tf_op jit(solution)/shard_map/ppermute | solution.py:51
  82.8 0.7 finish.1
  (14 shorter events, 0.2 us)
Async XLA Ops:
  3.3 7.1 %collective-permute-start = (bf16[3,3,64,128]{3,2,1,0:T(8,128)(2,1)}, bf16[3,3,64,128]{3,2,1,0:T(8,128)(2,1)S(1)}, u32[]{:S(2)}, u32[]{:S(2)}) collective-permute-start(bf16[3,3,64,128]{3,2,1,0:T(8,128)(2,1)} %get-tuple-element.38), channel_id=1, source_target_pairs={{0,2},{2,4},{4,6},{6,0},{1,3},{3,5},{5,7},{7,1},{8,10},{10,12},{12... | collective-permute-start | bytes 442376 | tf_op jit(solution)/shard_map/ppermute | solution.py:51
  4.9 8.1 %collective-permute-start.1 = (bf16[3,3,64,128]{3,2,1,0:T(8,128)(2,1)}, bf16[3,3,64,128]{3,2,1,0:T(8,128)(2,1)S(1)}, u32[]{:S(2)}, u32[]{:S(2)}) collective-permute-start(bf16[3,3,64,128]{3,2,1,0:T(8,128)(2,1)} %get-tuple-element.39), channel_id=1, source_target_pairs={{0,6},{2,0},{4,2},{6,4},{1,7},{3,1},{5,3},{7,5},{8,14},{10,8},{12,... | collective-permute-start | bytes 442376 | tf_op jit(solution)/shard_map/ppermute | solution.py:51
  6.6 8.2 %collective-permute-start.2 = (bf16[3,3,64,128]{3,2,1,0:T(8,128)(2,1)}, bf16[3,3,64,128]{3,2,1,0:T(8,128)(2,1)S(1)}, u32[]{:S(2)}, u32[]{:S(2)}) collective-permute-start(bf16[3,3,64,128]{3,2,1,0:T(8,128)(2,1)} %get-tuple-element.40), channel_id=1, source_target_pairs={{0,4},{2,6},{4,0},{6,2},{1,5},{3,7},{5,1},{7,3},{8,12},{10,14},{12... | collective-permute-start | bytes 442376 | tf_op jit(solution)/shard_map/ppermute | solution.py:51
  15.5 10.5 %collective-permute-start.6 = (bf16[2,3,272,128]{3,2,1,0:T(8,128)(2,1)S(1)}, bf16[2,3,272,128]{3,2,1,0:T(8,128)(2,1)S(1)}, u32[]{:S(2)}, u32[]{:S(2)}) collective-permute-start(bf16[2,3,272,128]{3,2,1,0:T(8,128)(2,1)S(1)} %constant_dynamic-update-slice_fusion.5.refs_0_.refs_1_.refs_2_.refs_3_), channel_id=1, source_target_pairs={{0,8},{8,16},{16,24},{24,1},{1,9},{9,17},{17,25},{25,0},{2,10},{10... | collective-permute-start | bytes 1253384 | tf_op jit(solution)/shard_map/ppermute | solution.py:56
  17.4 10.5 %collective-permute-start.8 = (bf16[2,3,272,128]{3,2,1,0:T(8,128)(2,1)S(1)}, bf16[2,3,272,128]{3,2,1,0:T(8,128)(2,1)S(1)}, u32[]{:S(2)}, u32[]{:S(2)}) collective-permute-start(bf16[2,3,272,128]{3,2,1,0:T(8,128)(2,1)S(1)} %constant_dynamic-update-slice_fusion.5.refs_0_.refs_1_.refs_2_.refs_3_), channel_id=1, source_target_pairs={{0,25},{8,0},{16,8},{24,16},{1,24},{9,1},{17,9},{25,17},{2,27},{10... | collective-permute-start | bytes 1253384 | tf_op jit(solution)/shard_map/ppermute | solution.py:56
  18.4 11.9 %collective-permute-start.3 = (bf16[3,272,128]{2,1,0:T(8,128)(2,1)S(1)}, bf16[3,272,128]{2,1,0:T(8,128)(2,1)S(1)}, u32[]{:S(2)}, u32[]{:S(2)}) collective-permute-start(bf16[3,272,128]{2,1,0:T(8,128)(2,1)S(1)} %get-tuple-element.80), channel_id=1, source_target_pairs={{0,96},{32,0},{64,32},{96,64},{1,97},{33,1},{65,33},{97,65},{2,98}... | collective-permute-start | bytes 626696 | tf_op jit(solution)/shard_map/ppermute | solution.py:51
  21.1 11.1 %collective-permute-start.4 = (bf16[3,272,128]{2,1,0:T(8,128)(2,1)S(1)}, bf16[3,272,128]{2,1,0:T(8,128)(2,1)S(1)}, u32[]{:S(2)}, u32[]{:S(2)}) collective-permute-start(bf16[3,272,128]{2,1,0:T(8,128)(2,1)S(1)} %get-tuple-element.80), channel_id=1, source_target_pairs={{0,32},{32,64},{64,96},{96,0},{1,33},{33,65},{65,97},{97,1},{2,34}... | collective-permute-start | bytes 626696 | tf_op jit(solution)/shard_map/ppermute | solution.py:51
  21.1 11.1 %collective-permute-start.5 = (bf16[3,272,128]{2,1,0:T(8,128)(2,1)S(1)}, bf16[3,272,128]{2,1,0:T(8,128)(2,1)S(1)}, u32[]{:S(2)}, u32[]{:S(2)}) collective-permute-start(bf16[3,272,128]{2,1,0:T(8,128)(2,1)S(1)} %get-tuple-element.80), channel_id=1, source_target_pairs={{0,64},{32,96},{64,0},{96,32},{1,65},{33,97},{65,1},{97,33},{2,66}... | collective-permute-start | bytes 626696 | tf_op jit(solution)/shard_map/ppermute | solution.py:51
  26.0 12.3 %collective-permute-start.7 = (bf16[2,3,272,128]{3,2,1,0:T(8,128)(2,1)S(1)}, bf16[2,3,272,128]{3,2,1,0:T(8,128)(2,1)S(1)}, u32[]{:S(2)}, u32[]{:S(2)}) collective-permute-start(bf16[2,3,272,128]{3,2,1,0:T(8,128)(2,1)S(1)} %collective-permute-done.6.refs_2_.refs_3_.refs_4_.refs_5_), channel_id=1, source_target_pairs={{0,8},{8,16},{16,24},{24,1},{1,9},{9,17},{17,25},{25,0},{2,10},{10... | collective-permute-start | bytes 1253384 | tf_op jit(solution)/shard_map/ppermute | solution.py:56
  28.0 10.9 %collective-permute-start.9 = (bf16[2,3,272,128]{3,2,1,0:T(8,128)(2,1)S(1)}, bf16[2,3,272,128]{3,2,1,0:T(8,128)(2,1)S(1)}, u32[]{:S(2)}, u32[]{:S(2)}) collective-permute-start(bf16[2,3,272,128]{3,2,1,0:T(8,128)(2,1)S(1)} %collective-permute-done.8.refs_0_.refs_1_.refs_6_.refs_7_), channel_id=1, source_target_pairs={{0,25},{8,0},{16,8},{24,16},{1,24},{9,1},{17,9},{25,17},{2,27},{10... | collective-permute-start | bytes 1253384 | tf_op jit(solution)/shard_map/ppermute | solution.py:56
  38.8 9.7 %collective-permute-start.10 = (bf16[2,3,272,128]{3,2,1,0:T(8,128)(2,1)S(1)}, bf16[2,3,272,128]{3,2,1,0:T(8,128)(2,1)S(1)}, u32[]{:S(2)}, u32[]{:S(2)}) collective-permute-start(bf16[2,3,272,128]{3,2,1,0:T(8,128)(2,1)S(1)} %collective-permute-done.7.refs_2_.refs_3_.refs_8_.refs_9_), channel_id=1, source_target_pairs={{0,8},{8,16},{16,24},{24,1},{1,9},{9,17},{17,25},{25,0},{2,10},{10... | collective-permute-start | bytes 1253384 | tf_op jit(solution)/shard_map/ppermute | solution.py:56
  41.8 9.3 %collective-permute-start.11 = (bf16[2,3,272,128]{3,2,1,0:T(8,128)(2,1)S(1)}, bf16[2,3,272,128]{3,2,1,0:T(8,128)(2,1)S(1)}, u32[]{:S(2)}, u32[]{:S(2)}) collective-permute-start(bf16[2,3,272,128]{3,2,1,0:T(8,128)(2,1)S(1)} %collective-permute-done.9.refs_4_.refs_5_.refs_10_.refs_11_), channel_id=1, source_target_pairs={{0,25},{8,0},{16,8},{24,16},{1,24},{9,1},{17,9},{25,17},{2,27},{10... | collective-permute-start | bytes 1253384 | tf_op jit(solution)/shard_map/ppermute | solution.py:56
  51.1 6.3 %collective-permute-start.12 = (bf16[3,272,128]{2,1,0:T(8,128)(2,1)S(1)}, bf16[3,272,128]{2,1,0:T(8,128)(2,1)S(1)}, u32[]{:S(2)}, u32[]{:S(2)}) collective-permute-start(bf16[3,272,128]{2,1,0:T(8,128)(2,1)S(1)} %slice_bitcast_fusion.1), channel_id=1, source_target_pairs={{0,8},{8,16},{16,24},{24,1},{1,9},{9,17},{17,25},{25,0},{2,10},{10... | collective-permute-start | bytes 626696 | tf_op jit(solution)/shard_map/ppermute | solution.py:56
  53.1 5.9 %collective-permute-start.13 = (bf16[3,272,128]{2,1,0:T(8,128)(2,1)S(1)}, bf16[3,272,128]{2,1,0:T(8,128)(2,1)S(1)}, u32[]{:S(2)}, u32[]{:S(2)}) collective-permute-start(bf16[3,272,128]{2,1,0:T(8,128)(2,1)S(1)} %slice_bitcast_fusion), channel_id=1, source_target_pairs={{0,25},{8,0},{16,8},{24,16},{1,24},{9,1},{17,9},{25,17},{2,27},{10... | collective-permute-start | bytes 626696 | tf_op jit(solution)/shard_map/ppermute | solution.py:56
  63.5 7.2 %collective-permute-start.14 = (bf16[3,288,128]{2,1,0:T(8,128)(2,1)S(1)}, bf16[3,288,128]{2,1,0:T(8,128)(2,1)S(1)}, u32[]{:S(2)}, u32[]{:S(2)}) collective-permute-start(bf16[3,288,128]{2,1,0:T(8,128)(2,1)S(1)} %get-tuple-element.63), channel_id=1, source_target_pairs={{0,32},{32,64},{64,96},{96,0},{1,33},{33,65},{65,97},{97,1},{2,34}... | collective-permute-start | bytes 663560 | tf_op jit(solution)/shard_map/ppermute | solution.py:51
  65.1 7.6 %collective-permute-start.15 = (bf16[3,288,128]{2,1,0:T(8,128)(2,1)S(1)}, bf16[3,288,128]{2,1,0:T(8,128)(2,1)S(1)}, u32[]{:S(2)}, u32[]{:S(2)}) collective-permute-start(bf16[3,288,128]{2,1,0:T(8,128)(2,1)S(1)} %get-tuple-element.64), channel_id=1, source_target_pairs={{0,96},{32,0},{64,32},{96,64},{1,97},{33,1},{65,33},{97,65},{2,98}... | collective-permute-start | bytes 663560 | tf_op jit(solution)/shard_map/ppermute | solution.py:51
  66.9 7.4 %collective-permute-start.16 = (bf16[3,288,128]{2,1,0:T(8,128)(2,1)S(1)}, bf16[3,288,128]{2,1,0:T(8,128)(2,1)S(1)}, u32[]{:S(2)}, u32[]{:S(2)}) collective-permute-start(bf16[3,288,128]{2,1,0:T(8,128)(2,1)S(1)} %get-tuple-element.65), channel_id=1, source_target_pairs={{0,64},{32,96},{64,0},{96,32},{1,65},{33,97},{65,1},{97,33},{2,66}... | collective-permute-start | bytes 663560 | tf_op jit(solution)/shard_map/ppermute | solution.py:51
  74.9 4.3 %collective-permute-start.17 = (bf16[3,80,128]{2,1,0:T(8,128)(2,1)S(1)}, bf16[3,80,128]{2,1,0:T(8,128)(2,1)S(1)}, u32[]{:S(2)}, u32[]{:S(2)}) collective-permute-start(bf16[3,80,128]{2,1,0:T(8,128)(2,1)S(1)} %get-tuple-element.67), channel_id=1, source_target_pairs={{0,6},{2,0},{4,2},{6,4},{1,7},{3,1},{5,3},{7,5},{8,14},{10,8},{12,... | collective-permute-start | bytes 184328 | tf_op jit(solution)/shard_map/ppermute | solution.py:51
  76.5 5.4 %collective-permute-start.18 = (bf16[3,80,128]{2,1,0:T(8,128)(2,1)S(1)}, bf16[3,80,128]{2,1,0:T(8,128)(2,1)S(1)}, u32[]{:S(2)}, u32[]{:S(2)}) collective-permute-start(bf16[3,80,128]{2,1,0:T(8,128)(2,1)S(1)} %get-tuple-element.68), channel_id=1, source_target_pairs={{0,2},{2,4},{4,6},{6,0},{1,3},{3,5},{5,7},{7,1},{8,10},{10,12},{12... | collective-permute-start | bytes 184328 | tf_op jit(solution)/shard_map/ppermute | solution.py:51
  77.0 5.7 %collective-permute-start.19 = (bf16[3,80,128]{2,1,0:T(8,128)(2,1)S(1)}, bf16[3,80,128]{2,1,0:T(8,128)(2,1)S(1)}, u32[]{:S(2)}, u32[]{:S(2)}) collective-permute-start(bf16[3,80,128]{2,1,0:T(8,128)(2,1)S(1)} %get-tuple-element.69), channel_id=1, source_target_pairs={{0,4},{2,6},{4,0},{6,2},{1,5},{3,7},{5,1},{7,3},{8,12},{10,14},{12... | collective-permute-start | bytes 184328 | tf_op jit(solution)/shard_map/ppermute | solution.py:51

commit v8 on v7

--- a/solution.py
+++ b/solution.py
@@ -131,9 +131,8 @@
     return acc * alpha + mixed, peak, total * alpha + add
 
 
-def joined(refs):
-    keys = jnp.concatenate([r[...].reshape(-1, HD) for r in refs[0::2]], axis=0)
-    return keys, jnp.concatenate([r[...].reshape(-1, HD) for r in refs[1::2]], axis=0)
+def joined(refs, skip=TEXT):
+    return tuple(jnp.concatenate([r[...].reshape(-1, HD)[skip:] for r in refs[i::2]], axis=0) for i in range(2))
 
 
 TILES = [slice(0, TILE), slice(TILE, 2 * TILE)]
@@ -200,7 +199,7 @@
 def last_body(count_ref, q_ref, acc_ref, top_ref, total_ref, *refs):
     parts, text, outs = refs[:2], refs[2:-4], refs[-4:]
     keys, values = joined(parts)
-    text_keys, text_values = joined(text)
+    text_keys, text_values = joined(text, 0)
     keys = jnp.concatenate([keys, text_keys], axis=0)
     values = jnp.concatenate([values, text_values], axis=0)
     live = live_text(count_ref[0], VIDEO)
@@ -222,21 +221,21 @@
 TILE_SPEC = head_spec(2 * TILE, HD)
 
 
-def key_specs(part, rows=VIDEO, at=0):
+def key_specs(part, rows):
     if part.ndim == 3:
-        return [pl.BlockSpec((1, rows, HD), lambda h, *_: (h, at, 0))]
-    return [pl.BlockSpec((1, 1, rows, HD), lambda h, *_, i=i: (i, h, at, 0)) for i in range(2)]
+        return [head_spec(rows, HD)]
+    return [pl.BlockSpec((1, 1, rows, HD), lambda h, *_, i=i: (i, h, 0, 0)) for i in range(2)]
 
 
 def attend(body, name, parts, extra, extra_specs, outs, out_specs, prefetch=(), texts=()):
     keys = VIDEO * len(parts)
     specs, args = list(extra_specs), list(extra)
     for p in parts:
-        new = key_specs(p)
+        new = key_specs(p, VIDEO + TEXT)
         specs += new
         args += [p] * len(new)
     for p in texts:
-        new = key_specs(p, TEXT, VIDEO // TEXT)
+        new = key_specs(p, TEXT)
         specs += new
         args += [p] * len(new)
     return pl.pallas_call(
@@ -321,7 +320,7 @@
     out = prepare(flat(video_q), flat(video_k), flat(video_v), positions, flat(text_q), flat(text_k), flat(text_v))
     own, text, text_rows = out[:4], out[4], out[5]
     m = [own[0]] + [shift(own[i], "y", MOVES[i]) for i in range(1, 4)]
-    block = jnp.concatenate([v[:2] for v in m] + [text], axis=2)
+    block = jnp.concatenate([text] + [v[:2] for v in m], axis=2)
     right, left = z_shift(block, 1), z_shift(block, -1)
     site = jnp.concatenate([v[2] for v in m] + [text_rows], axis=1)
     queries = jnp.concatenate([site] + [shift(site, "x", -d) for d in MOVES[1:]], axis=1)

time: 83.8 us -> 83.2 us (level)
  transfers between devices with their start and end apart: 20 -> 20, of which waited for: 16 -> 15; matrix products, arithmetic and copies ran while one was open for 3% -> 4% of each run, Pallas kernels for 14% -> 14%
where the time goes in v8:
time: 83.2 us; the launch traced here: 82.8 us
  starting transfers between devices  30.2 us (36%)
  waiting for transfers between devices  27.8 us (33%)
  Pallas kernels  20.1 us (24%)
  local copies, waits for them, and re-layouts  3.41 us (4%)
  between operations  1.42 us (2%)
    ppermute x12, starting transfers between devices, shift(): return lax.ppermute(v, axis, [(i, (i + step) % 4) for i in range(4)])  18.5 us
    pallas_call x4, Pallas kernels, attend(): pl.pallas_call(body, out_shape=[jax.ShapeDtypeStruct((3,) + s, t) for s,...  16 us
    ppermute x12, waiting for transfers between devices, shift(): return lax.ppermute(v, axis, [(i, (i + step) % 4) for i in range(4)])  15.9 us
    ppermute x8, waiting for transfers between devices, z_shift(): lax.ppermute(v, ZAXES, [(line(z), line((z + step) % 8)) for z in range(8)])  11.9 us
    ppermute x8, starting transfers between devices, z_shift(): lax.ppermute(v, ZAXES, [(line(z), line((z + step) % 8)) for z in range(8)])  11.7 us
    pallas_call x1, Pallas kernels, prepare(): pl.pallas_call(prepare_body, out_shape=[jax.ShapeDtypeStruct(o, BF16) for...  2.72 us
    unnamed x10, local copies, waits for them, and re-layouts  2.62 us
  transfers between devices with their start and end apart: 20, of which 15 were waited for; matrix products, arithmetic and copies ran while one was open for 4% of the time, Pallas kernels for 14%

profile of v8, /device:TPU:32, one launch (start us, length us, event | category | flops | bytes accessed | tf_op | source)
XLA Modules:
  0.0 82.8 jit_solution(8803528633861200924)
XLA Ops:
  0.6 2.7 %prepare.1 = (bf16[3,3,64,128]{3,2,1,0:T(8,128)(2,1)}, bf16[3,3,64,128]{3,2,1,0:T(8,128)(2,1)}, bf16[3,3,64,128]{3,2,1,0:T(8,128)(2,1)}, bf16[3,3,64,128]{3,2,1,...) custom-call(bf16[12,64,128]{2,1,0:T(8,128)(2,1)} %bitcast.36, ...), custom_call_target="tpu_custom_call" | custom-call | flops 50000000 | bytes 3000000 | tf_op jit(solution)/shard_map/prepare/pallas_call | solution.py:100
  3.3 1.6 %collective-permute-start = (bf16[3,3,64,128]{3,2,1,0:T(8,128)(2,1)}, bf16[3,3,64,128]{3,2,1,0:T(8,128)(2,1)S(1)}, u32[]{:S(2)}, u32[]{:S(2)}) collective-permute-start(bf16[3,3,64,128]{3,2,1,0:T(8,128)(2,1)} %get-tuple-element.38), channel_id=1, source_target_pairs={{0,2},{2,4},{4,6},{6,0},{1,3},{3,5},{5,7},{7,1},{8,10},{10,12},{12... | collective-permute-start | bytes 442376 | tf_op jit(solution)/shard_map/ppermute | solution.py:51
  4.9 1.7 %collective-permute-start.1 = (bf16[3,3,64,128]{3,2,1,0:T(8,128)(2,1)}, bf16[3,3,64,128]{3,2,1,0:T(8,128)(2,1)S(1)}, u32[]{:S(2)}, u32[]{:S(2)}) collective-permute-start(bf16[3,3,64,128]{3,2,1,0:T(8,128)(2,1)} %get-tuple-element.39), channel_id=1, source_target_pairs={{0,6},{2,0},{4,2},{6,4},{1,7},{3,1},{5,3},{7,5},{8,14},{10,8},{12,... | collective-permute-start | bytes 442376 | tf_op jit(solution)/shard_map/ppermute | solution.py:51
  6.6 2.0 %collective-permute-start.2 = (bf16[3,3,64,128]{3,2,1,0:T(8,128)(2,1)}, bf16[3,3,64,128]{3,2,1,0:T(8,128)(2,1)S(1)}, u32[]{:S(2)}, u32[]{:S(2)}) collective-permute-start(bf16[3,3,64,128]{3,2,1,0:T(8,128)(2,1)} %get-tuple-element.40), channel_id=1, source_target_pairs={{0,4},{2,6},{4,0},{6,2},{1,5},{3,7},{5,1},{7,3},{8,12},{10,14},{12... | collective-permute-start | bytes 442376 | tf_op jit(solution)/shard_map/ppermute | solution.py:51
  8.6 0.7 constant_dynamic-update-slice_fusion.5
  9.3 0.9 %slice_dynamic-update-slice_fusion.3 = bf16[2,3,272,128]{3,2,1,0:T(8,128)(2,1)S(1)} fusion(bf16[2,3,272,128]{3,2,1,0:T(8,128)(2,1)S(1)} %constant_dynamic-update-slice_fusion.5, bf16[3,3,64,128]{3,2,1,0:T(8,128)(2,1)} %get-tuple-element.37), kind=kLoop, calls=%fused_computation.5 | loop fusion | bytes 196608
  10.2 0.8 bitcast_dynamic-update-slice_fusion.1
  11.0 0.0 collective-permute-done
  11.1 2.0 %collective-permute-done.1 = bf16[3,3,64,128]{3,2,1,0:T(8,128)(2,1)S(1)} collective-permute-done((bf16[3,3,64,128]{3,2,1,0:T(8,128)(2,1)}, bf16[3,3,64,128]{3,2,1,0:T(8,128)(2,1)S(1)}, u32[]{:S(2)}, u32[]{:S(2)}) %collective-permute-start.1) | collective-permute-done | bytes 147488 | tf_op jit(solution)/shard_map/ppermute | solution.py:51
  13.1 1.7 %collective-permute-done.2 = bf16[3,3,64,128]{3,2,1,0:T(8,128)(2,1)S(1)} collective-permute-done((bf16[3,3,64,128]{3,2,1,0:T(8,128)(2,1)}, bf16[3,3,64,128]{3,2,1,0:T(8,128)(2,1)S(1)}, u32[]{:S(2)}, u32[]{:S(2)}) %collective-permute-start.2) | collective-permute-done | bytes 147488 | tf_op jit(solution)/shard_map/ppermute | solution.py:51
  14.8 2.0 %collective-permute-start.6 = (bf16[2,3,272,128]{3,2,1,0:T(8,128)(2,1)S(1)}, bf16[2,3,272,128]{3,2,1,0:T(8,128)(2,1)S(1)}, u32[]{:S(2)}, u32[]{:S(2)}) collective-permute-start(bf16[2,3,272,128]{3,2,1,0:T(8,128)(2,1)S(1)} %slice_dynamic-update-slice_fusion.refs_0_.refs_1_.refs_2_.refs_3_), channel_id=1, source_target_pairs={{0,8},{8,16},{16,24},{24,1},{1,9},{9,17},{17,25},{25,0},{2,10},{10... | collective-permute-start | bytes 1253384 | tf_op jit(solution)/shard_map/ppermute | solution.py:56
  16.8 0.1 collective-permute-start.8
  17.0 0.7 constant_dynamic-update-slice_fusion
  17.7 2.8 %collective-permute-start.3 = (bf16[3,272,128]{2,1,0:T(8,128)(2,1)S(1)}, bf16[3,272,128]{2,1,0:T(8,128)(2,1)S(1)}, u32[]{:S(2)}, u32[]{:S(2)}) collective-permute-start(bf16[3,272,128]{2,1,0:T(8,128)(2,1)S(1)} %get-tuple-element.80), channel_id=1, source_target_pairs={{0,96},{32,0},{64,32},{96,64},{1,97},{33,1},{65,33},{97,65},{2,98}... | collective-permute-start | bytes 626696 | tf_op jit(solution)/shard_map/ppermute | solution.py:51
  20.4 0.0 collective-permute-start.4
  20.4 2.3 %collective-permute-start.5 = (bf16[3,272,128]{2,1,0:T(8,128)(2,1)S(1)}, bf16[3,272,128]{2,1,0:T(8,128)(2,1)S(1)}, u32[]{:S(2)}, u32[]{:S(2)}) collective-permute-start(bf16[3,272,128]{2,1,0:T(8,128)(2,1)S(1)} %get-tuple-element.80), channel_id=1, source_target_pairs={{0,64},{32,96},{64,0},{96,32},{1,65},{33,97},{65,1},{97,33},{2,66}... | collective-permute-start | bytes 626696 | tf_op jit(solution)/shard_map/ppermute | solution.py:51
  22.7 2.6 %collective-permute-done.6.refs_2_.refs_3_.refs_4_.refs_5_ = bf16[2,3,272,128]{3,2,1,0:T(8,128)(2,1)S(1)} collective-permute-done((bf16[2,3,272,128]{3,2,1,0:T(8,128)(2,1)S(1)}, bf16[2,3,272,128]{3,2,1,0:T(8,128)(2,1)S(1)}, u32[]{:S(2)}, u32[]{:S(2)}) %collective-permute-start.6) | collective-permute-done | bytes 417824 | tf_op jit(solution)/shard_map/ppermute | solution.py:56
  25.4 1.9 %collective-permute-start.7 = (bf16[2,3,272,128]{3,2,1,0:T(8,128)(2,1)S(1)}, bf16[2,3,272,128]{3,2,1,0:T(8,128)(2,1)S(1)}, u32[]{:S(2)}, u32[]{:S(2)}) collective-permute-start(bf16[2,3,272,128]{3,2,1,0:T(8,128)(2,1)S(1)} %collective-permute-done.6.refs_2_.refs_3_.refs_4_.refs_5_), channel_id=1, source_target_pairs={{0,8},{8,16},{16,24},{24,1},{1,9},{9,17},{17,25},{25,0},{2,10},{10... | collective-permute-start | bytes 1253384 | tf_op jit(solution)/shard_map/ppermute | solution.py:56
  27.3 0.0 collective-permute-done.8.refs_0_.refs_1_.refs_6_.refs_7_
  27.3 2.3 %collective-permute-start.9 = (bf16[2,3,272,128]{3,2,1,0:T(8,128)(2,1)S(1)}, bf16[2,3,272,128]{3,2,1,0:T(8,128)(2,1)S(1)}, u32[]{:S(2)}, u32[]{:S(2)}) collective-permute-start(bf16[2,3,272,128]{3,2,1,0:T(8,128)(2,1)S(1)} %collective-permute-done.8.refs_0_.refs_1_.refs_6_.refs_7_), channel_id=1, source_target_pairs={{0,25},{8,0},{16,8},{24,16},{1,24},{9,1},{17,9},{25,17},{2,27},{10... | collective-permute-start | bytes 1253384 | tf_op jit(solution)/shard_map/ppermute | solution.py:56
  29.6 0.0 collective-permute-done.3
  29.6 1.9 %collective-permute-done.4 = bf16[3,272,128]{2,1,0:T(8,128)(2,1)S(1)} collective-permute-done((bf16[3,272,128]{2,1,0:T(8,128)(2,1)S(1)}, bf16[3,272,128]{2,1,0:T(8,128)(2,1)S(1)}, u32[]{:S(2)}, u32[]{:S(2)}) %collective-permute-start.4) | collective-permute-done | bytes 208928 | tf_op jit(solution)/shard_map/ppermute | solution.py:51
  31.6 3.5 %attend_first.1 = (f32[3,1088,128]{2,1,0:T(8,128)S(1)}, f32[3,1088,128]{2,1,0:T(8,128)S(1)}, f32[3,1088,128]{2,1,0:T(8,128)S(1)}) custom-call(bf16[3,1088,128]{2,1,0:T(8,128)(2,1)S(1)} %constant_dynamic-update-slice_fusion.1.q_ref, bf16[2,3,272,128]{3,2,1,0:T(8,128)(2,1)S(1)} %slice_dynamic-update-slice_fusion.refs_0_.refs_1_.refs_2_.refs_3_, ...), custom_call_target="tpu_custom_call" | custom-call | flops 855638016 | bytes 6786432 | tf_op jit(solution)/shard_map/attend_first/pallas_call | solution.py:241
  35.1 2.6 %collective-permute-done.7.refs_2_.refs_3_.refs_8_.refs_9_ = bf16[2,3,272,128]{3,2,1,0:T(8,128)(2,1)S(1)} collective-permute-done((bf16[2,3,272,128]{3,2,1,0:T(8,128)(2,1)S(1)}, bf16[2,3,272,128]{3,2,1,0:T(8,128)(2,1)S(1)}, u32[]{:S(2)}, u32[]{:S(2)}) %collective-permute-start.7) | collective-permute-done | bytes 417824 | tf_op jit(solution)/shard_map/ppermute | solution.py:56
  37.7 0.4 collective-permute-done.9.refs_4_.refs_5_.refs_10_.refs_11_
  38.2 3.0 %collective-permute-start.10 = (bf16[2,3,272,128]{3,2,1,0:T(8,128)(2,1)S(1)}, bf16[2,3,272,128]{3,2,1,0:T(8,128)(2,1)S(1)}, u32[]{:S(2)}, u32[]{:S(2)}) collective-permute-start(bf16[2,3,272,128]{3,2,1,0:T(8,128)(2,1)S(1)} %collective-permute-done.7.refs_2_.refs_3_.refs_8_.refs_9_), channel_id=1, source_target_pairs={{0,8},{8,16},{16,24},{24,1},{1,9},{9,17},{17,25},{25,0},{2,10},{10... | collective-permute-start | bytes 1253384 | tf_op jit(solution)/shard_map/ppermute | solution.py:56
  41.1 4.7 %attend_2.1 = (f32[3,1088,128]{2,1,0:T(8,128)S(1)}, f32[3,1088,128]{2,1,0:T(8,128)S(1)}, f32[3,1088,128]{2,1,0:T(8,128)S(1)}) custom-call(bf16[3,1088,128]{2,1,0:T(8,128)(2,1)S(1)} %constant_dynamic-update-slice_fusion.1.q_ref, f32[3,1088,128]{2,1,0:T(8,128)S(1)} %get-tuple-element.48.acc_ref, f32[3,1088,128]{2,1,0:T(8,128)S(1)} %get-tuple-element.49.top_ref, ...), custom_call_target="tpu_custom_call" | custom-call | flops 1283457024 | bytes 7179648 | tf_op jit(solution)/shard_map/attend_2/pallas_call | solution.py:241
  45.8 2.0 %collective-permute-done.10.refs_0_.refs_1_.refs_12_.refs_13_ = bf16[2,3,272,128]{3,2,1,0:T(8,128)(2,1)S(1)} collective-permute-done((bf16[2,3,272,128]{3,2,1,0:T(8,128)(2,1)S(1)}, bf16[2,3,272,128]{3,2,1,0:T(8,128)(2,1)S(1)}, u32[]{:S(2)}, u32[]{:S(2)}) %collective-permute-start.10) | collective-permute-done | bytes 417824 | tf_op jit(solution)/shard_map/ppermute | solution.py:56
  47.9 2.5 %collective-permute-done.11.refs_2_.refs_3_.refs_14_.refs_15_ = bf16[2,3,272,128]{3,2,1,0:T(8,128)(2,1)S(1)} collective-permute-done((bf16[2,3,272,128]{3,2,1,0:T(8,128)(2,1)S(1)}, bf16[2,3,272,128]{3,2,1,0:T(8,128)(2,1)S(1)}, u32[]{:S(2)}, u32[]{:S(2)}) %collective-permute-start.11) | collective-permute-done | bytes 417824 | tf_op jit(solution)/shard_map/ppermute | solution.py:56
  50.4 2.0 %collective-permute-start.12 = (bf16[3,272,128]{2,1,0:T(8,128)(2,1)S(1)}, bf16[3,272,128]{2,1,0:T(8,128)(2,1)S(1)}, u32[]{:S(2)}, u32[]{:S(2)}) collective-permute-start(bf16[3,272,128]{2,1,0:T(8,128)(2,1)S(1)} %slice_bitcast_fusion.1), channel_id=1, source_target_pairs={{0,8},{8,16},{16,24},{24,1},{1,9},{9,17},{17,25},{25,0},{2,10},{10... | collective-permute-start | bytes 626696 | tf_op jit(solution)/shard_map/ppermute | solution.py:56
  52.5 0.4 collective-permute-start.13
  53.5 3.3 %attend_3.1 = (f32[3,1088,128]{2,1,0:T(8,128)S(1)}, f32[3,1088,128]{2,1,0:T(8,128)S(1)}, f32[3,1088,128]{2,1,0:T(8,128)S(1)}) custom-call(bf16[3,1088,128]{2,1,0:T(8,128)(2,1)S(1)} %constant_dynamic-update-slice_fusion.1.q_ref, f32[3,1088,128]{2,1,0:T(8,128)S(1)} %get-tuple-element.54.acc_ref, f32[3,1088,128]{2,1,0:T(8,128)S(1)} %get-tuple-element.55.top_ref, ...), custom_call_target="tpu_custom_call" | custom-call | flops 855638016 | bytes 6786432 | tf_op jit(solution)/shard_map/attend_3/pallas_call | solution.py:241
  56.8 1.6 %collective-permute-done.13.refs_1_.refs_17_ = bf16[3,272,128]{2,1,0:T(8,128)(2,1)S(1)} collective-permute-done((bf16[3,272,128]{2,1,0:T(8,128)(2,1)S(1)}, bf16[3,272,128]{2,1,0:T(8,128)(2,1)S(1)}, u32[]{:S(2)}, u32[]{:S(2)}) %collective-permute-start.13) | collective-permute-done | bytes 208928 | tf_op jit(solution)/shard_map/ppermute | solution.py:56
  58.3 4.5 %attend_last.1 = (bf16[3,288,128]{2,1,0:T(8,128)(2,1)S(1)}, bf16[3,288,128]{2,1,0:T(8,128)(2,1)S(1)}, bf16[3,288,128]{2,1,0:T(8,128)(2,1)S(1)}, bf16[3,288,128]{2,1,0:T(8,128)(2,1)S(1)}) custom-call(s32[1]{0:T(128)S(6)} %copy.27.count_ref, bf16[3,1088,128]{2,1,0:T(8,128)(2,1)S(1)} %constant_dynamic-update-slice_fusion.1.q_ref, ...), custom_call_target="tpu_custom_call" | custom-call | flops 855638016 | bytes 6786432 | tf_op jit(solution)/shard_map/attend_last/pallas_call | solution.py:241
  62.9 1.6 %collective-permute-start.14 = (bf16[3,288,128]{2,1,0:T(8,128)(2,1)S(1)}, bf16[3,288,128]{2,1,0:T(8,128)(2,1)S(1)}, u32[]{:S(2)}, u32[]{:S(2)}) collective-permute-start(bf16[3,288,128]{2,1,0:T(8,128)(2,1)S(1)} %get-tuple-element.63), channel_id=1, source_target_pairs={{0,32},{32,64},{64,96},{96,0},{1,33},{33,65},{65,97},{97,1},{2,34}... | collective-permute-start | bytes 663560 | tf_op jit(solution)/shard_map/ppermute | solution.py:51
  64.5 1.7 %collective-permute-start.15 = (bf16[3,288,128]{2,1,0:T(8,128)(2,1)S(1)}, bf16[3,288,128]{2,1,0:T(8,128)(2,1)S(1)}, u32[]{:S(2)}, u32[]{:S(2)}) collective-permute-start(bf16[3,288,128]{2,1,0:T(8,128)(2,1)S(1)} %get-tuple-element.64), channel_id=1, source_target_pairs={{0,96},{32,0},{64,32},{96,64},{1,97},{33,1},{65,33},{97,65},{2,98}... | collective-permute-start | bytes 663560 | tf_op jit(solution)/shard_map/ppermute | solution.py:51
  66.2 1.8 %collective-permute-start.16 = (bf16[3,288,128]{2,1,0:T(8,128)(2,1)S(1)}, bf16[3,288,128]{2,1,0:T(8,128)(2,1)S(1)}, u32[]{:S(2)}, u32[]{:S(2)}) collective-permute-start(bf16[3,288,128]{2,1,0:T(8,128)(2,1)S(1)} %get-tuple-element.65), channel_id=1, source_target_pairs={{0,64},{32,96},{64,0},{96,32},{1,65},{33,97},{65,1},{97,33},{2,66}... | collective-permute-start | bytes 663560 | tf_op jit(solution)/shard_map/ppermute | solution.py:51
  68.0 2.1 %collective-permute-done.14.refs_1_ = bf16[3,288,128]{2,1,0:T(8,128)(2,1)S(1)} collective-permute-done((bf16[3,288,128]{2,1,0:T(8,128)(2,1)S(1)}, bf16[3,288,128]{2,1,0:T(8,128)(2,1)S(1)}, u32[]{:S(2)}, u32[]{:S(2)}) %collective-permute-start.14) | collective-permute-done | bytes 221216 | tf_op jit(solution)/shard_map/ppermute | solution.py:51
  70.1 0.3 collective-permute-done.15.refs_2_
  70.4 3.2 %collective-permute-done.16.refs_3_ = bf16[3,288,128]{2,1,0:T(8,128)(2,1)S(1)} collective-permute-done((bf16[3,288,128]{2,1,0:T(8,128)(2,1)S(1)}, bf16[3,288,128]{2,1,0:T(8,128)(2,1)S(1)}, u32[]{:S(2)}, u32[]{:S(2)}) %collective-permute-start.16) | collective-permute-done | bytes 221216 | tf_op jit(solution)/shard_map/ppermute | solution.py:51
  73.6 0.6 merge.1
  74.3 1.6 %collective-permute-start.17 = (bf16[3,80,128]{2,1,0:T(8,128)(2,1)S(1)}, bf16[3,80,128]{2,1,0:T(8,128)(2,1)S(1)}, u32[]{:S(2)}, u32[]{:S(2)}) collective-permute-start(bf16[3,80,128]{2,1,0:T(8,128)(2,1)S(1)} %get-tuple-element.67), channel_id=1, source_target_pairs={{0,6},{2,0},{4,2},{6,4},{1,7},{3,1},{5,3},{7,5},{8,14},{10,8},{12,... | collective-permute-start | bytes 184328 | tf_op jit(solution)/shard_map/ppermute | solution.py:51
  75.8 0.6 collective-permute-start.18
  76.4 1.0 %collective-permute-start.19 = (bf16[3,80,128]{2,1,0:T(8,128)(2,1)S(1)}, bf16[3,80,128]{2,1,0:T(8,128)(2,1)S(1)}, u32[]{:S(2)}, u32[]{:S(2)}) collective-permute-start(bf16[3,80,128]{2,1,0:T(8,128)(2,1)S(1)} %get-tuple-element.69), channel_id=1, source_target_pairs={{0,4},{2,6},{4,0},{6,2},{1,5},{3,7},{5,1},{7,3},{8,12},{10,14},{12... | collective-permute-start | bytes 184328 | tf_op jit(solution)/shard_map/ppermute | solution.py:51
  77.4 1.2 %collective-permute-done.17.refs_1_ = bf16[3,80,128]{2,1,0:T(8,128)(2,1)S(1)} collective-permute-done((bf16[3,80,128]{2,1,0:T(8,128)(2,1)S(1)}, bf16[3,80,128]{2,1,0:T(8,128)(2,1)S(1)}, u32[]{:S(2)}, u32[]{:S(2)}) %collective-permute-start.17) | collective-permute-done | bytes 61472 | tf_op jit(solution)/shard_map/ppermute | solution.py:51
  78.6 2.7 %collective-permute-done.18.refs_2_ = bf16[3,80,128]{2,1,0:T(8,128)(2,1)S(1)} collective-permute-done((bf16[3,80,128]{2,1,0:T(8,128)(2,1)S(1)}, bf16[3,80,128]{2,1,0:T(8,128)(2,1)S(1)}, u32[]{:S(2)}, u32[]{:S(2)}) %collective-permute-start.18) | collective-permute-done | bytes 61472 | tf_op jit(solution)/shard_map/ppermute | solution.py:51
  81.2 0.8 %collective-permute-done.19.refs_3_ = bf16[3,80,128]{2,1,0:T(8,128)(2,1)S(1)} collective-permute-done((bf16[3,80,128]{2,1,0:T(8,128)(2,1)S(1)}, bf16[3,80,128]{2,1,0:T(8,128)(2,1)S(1)}, u32[]{:S(2)}, u32[]{:S(2)}) %collective-permute-start.19) | collective-permute-done | bytes 61472 | tf_op jit(solution)/shard_map/ppermute | solution.py:51
  82.1 0.7 finish.1
  (14 shorter events, 0.2 us)
Async XLA Ops:
  3.3 7.7 %collective-permute-start = (bf16[3,3,64,128]{3,2,1,0:T(8,128)(2,1)}, bf16[3,3,64,128]{3,2,1,0:T(8,128)(2,1)S(1)}, u32[]{:S(2)}, u32[]{:S(2)}) collective-permute-start(bf16[3,3,64,128]{3,2,1,0:T(8,128)(2,1)} %get-tuple-element.38), channel_id=1, source_target_pairs={{0,2},{2,4},{4,6},{6,0},{1,3},{3,5},{5,7},{7,1},{8,10},{10,12},{12... | collective-permute-start | bytes 442376 | tf_op jit(solution)/shard_map/ppermute | solution.py:51
  4.9 8.1 %collective-permute-start.1 = (bf16[3,3,64,128]{3,2,1,0:T(8,128)(2,1)}, bf16[3,3,64,128]{3,2,1,0:T(8,128)(2,1)S(1)}, u32[]{:S(2)}, u32[]{:S(2)}) collective-permute-start(bf16[3,3,64,128]{3,2,1,0:T(8,128)(2,1)} %get-tuple-element.39), channel_id=1, source_target_pairs={{0,6},{2,0},{4,2},{6,4},{1,7},{3,1},{5,3},{7,5},{8,14},{10,8},{12,... | collective-permute-start | bytes 442376 | tf_op jit(solution)/shard_map/ppermute | solution.py:51
  6.6 8.2 %collective-permute-start.2 = (bf16[3,3,64,128]{3,2,1,0:T(8,128)(2,1)}, bf16[3,3,64,128]{3,2,1,0:T(8,128)(2,1)S(1)}, u32[]{:S(2)}, u32[]{:S(2)}) collective-permute-start(bf16[3,3,64,128]{3,2,1,0:T(8,128)(2,1)} %get-tuple-element.40), channel_id=1, source_target_pairs={{0,4},{2,6},{4,0},{6,2},{1,5},{3,7},{5,1},{7,3},{8,12},{10,14},{12... | collective-permute-start | bytes 442376 | tf_op jit(solution)/shard_map/ppermute | solution.py:51
  14.8 10.6 %collective-permute-start.6 = (bf16[2,3,272,128]{3,2,1,0:T(8,128)(2,1)S(1)}, bf16[2,3,272,128]{3,2,1,0:T(8,128)(2,1)S(1)}, u32[]{:S(2)}, u32[]{:S(2)}) collective-permute-start(bf16[2,3,272,128]{3,2,1,0:T(8,128)(2,1)S(1)} %slice_dynamic-update-slice_fusion.refs_0_.refs_1_.refs_2_.refs_3_), channel_id=1, source_target_pairs={{0,8},{8,16},{16,24},{24,1},{1,9},{9,17},{17,25},{25,0},{2,10},{10... | collective-permute-start | bytes 1253384 | tf_op jit(solution)/shard_map/ppermute | solution.py:56
  16.8 10.5 %collective-permute-start.8 = (bf16[2,3,272,128]{3,2,1,0:T(8,128)(2,1)S(1)}, bf16[2,3,272,128]{3,2,1,0:T(8,128)(2,1)S(1)}, u32[]{:S(2)}, u32[]{:S(2)}) collective-permute-start(bf16[2,3,272,128]{3,2,1,0:T(8,128)(2,1)S(1)} %slice_dynamic-update-slice_fusion.refs_0_.refs_1_.refs_2_.refs_3_), channel_id=1, source_target_pairs={{0,25},{8,0},{16,8},{24,16},{1,24},{9,1},{17,9},{25,17},{2,27},{10... | collective-permute-start | bytes 1253384 | tf_op jit(solution)/shard_map/ppermute | solution.py:56
  17.7 11.9 %collective-permute-start.3 = (bf16[3,272,128]{2,1,0:T(8,128)(2,1)S(1)}, bf16[3,272,128]{2,1,0:T(8,128)(2,1)S(1)}, u32[]{:S(2)}, u32[]{:S(2)}) collective-permute-start(bf16[3,272,128]{2,1,0:T(8,128)(2,1)S(1)} %get-tuple-element.80), channel_id=1, source_target_pairs={{0,96},{32,0},{64,32},{96,64},{1,97},{33,1},{65,33},{97,65},{2,98}... | collective-permute-start | bytes 626696 | tf_op jit(solution)/shard_map/ppermute | solution.py:51
  20.4 11.1 %collective-permute-start.4 = (bf16[3,272,128]{2,1,0:T(8,128)(2,1)S(1)}, bf16[3,272,128]{2,1,0:T(8,128)(2,1)S(1)}, u32[]{:S(2)}, u32[]{:S(2)}) collective-permute-start(bf16[3,272,128]{2,1,0:T(8,128)(2,1)S(1)} %get-tuple-element.80), channel_id=1, source_target_pairs={{0,32},{32,64},{64,96},{96,0},{1,33},{33,65},{65,97},{97,1},{2,34}... | collective-permute-start | bytes 626696 | tf_op jit(solution)/shard_map/ppermute | solution.py:51
  20.4 11.1 %collective-permute-start.5 = (bf16[3,272,128]{2,1,0:T(8,128)(2,1)S(1)}, bf16[3,272,128]{2,1,0:T(8,128)(2,1)S(1)}, u32[]{:S(2)}, u32[]{:S(2)}) collective-permute-start(bf16[3,272,128]{2,1,0:T(8,128)(2,1)S(1)} %get-tuple-element.80), channel_id=1, source_target_pairs={{0,64},{32,96},{64,0},{96,32},{1,65},{33,97},{65,1},{97,33},{2,66}... | collective-permute-start | bytes 626696 | tf_op jit(solution)/shard_map/ppermute | solution.py:51
  25.4 12.4 %collective-permute-start.7 = (bf16[2,3,272,128]{3,2,1,0:T(8,128)(2,1)S(1)}, bf16[2,3,272,128]{3,2,1,0:T(8,128)(2,1)S(1)}, u32[]{:S(2)}, u32[]{:S(2)}) collective-permute-start(bf16[2,3,272,128]{3,2,1,0:T(8,128)(2,1)S(1)} %collective-permute-done.6.refs_2_.refs_3_.refs_4_.refs_5_), channel_id=1, source_target_pairs={{0,8},{8,16},{16,24},{24,1},{1,9},{9,17},{17,25},{25,0},{2,10},{10... | collective-permute-start | bytes 1253384 | tf_op jit(solution)/shard_map/ppermute | solution.py:56
  27.3 10.9 %collective-permute-start.9 = (bf16[2,3,272,128]{3,2,1,0:T(8,128)(2,1)S(1)}, bf16[2,3,272,128]{3,2,1,0:T(8,128)(2,1)S(1)}, u32[]{:S(2)}, u32[]{:S(2)}) collective-permute-start(bf16[2,3,272,128]{3,2,1,0:T(8,128)(2,1)S(1)} %collective-permute-done.8.refs_0_.refs_1_.refs_6_.refs_7_), channel_id=1, source_target_pairs={{0,25},{8,0},{16,8},{24,16},{1,24},{9,1},{17,9},{25,17},{2,27},{10... | collective-permute-start | bytes 1253384 | tf_op jit(solution)/shard_map/ppermute | solution.py:56
  38.2 9.7 %collective-permute-start.10 = (bf16[2,3,272,128]{3,2,1,0:T(8,128)(2,1)S(1)}, bf16[2,3,272,128]{3,2,1,0:T(8,128)(2,1)S(1)}, u32[]{:S(2)}, u32[]{:S(2)}) collective-permute-start(bf16[2,3,272,128]{3,2,1,0:T(8,128)(2,1)S(1)} %collective-permute-done.7.refs_2_.refs_3_.refs_8_.refs_9_), channel_id=1, source_target_pairs={{0,8},{8,16},{16,24},{24,1},{1,9},{9,17},{17,25},{25,0},{2,10},{10... | collective-permute-start | bytes 1253384 | tf_op jit(solution)/shard_map/ppermute | solution.py:56
  41.1 9.3 %collective-permute-start.11 = (bf16[2,3,272,128]{3,2,1,0:T(8,128)(2,1)S(1)}, bf16[2,3,272,128]{3,2,1,0:T(8,128)(2,1)S(1)}, u32[]{:S(2)}, u32[]{:S(2)}) collective-permute-start(bf16[2,3,272,128]{3,2,1,0:T(8,128)(2,1)S(1)} %collective-permute-done.9.refs_4_.refs_5_.refs_10_.refs_11_), channel_id=1, source_target_pairs={{0,25},{8,0},{16,8},{24,16},{1,24},{9,1},{17,9},{25,17},{2,27},{10... | collective-permute-start | bytes 1253384 | tf_op jit(solution)/shard_map/ppermute | solution.py:56
  50.4 6.3 %collective-permute-start.12 = (bf16[3,272,128]{2,1,0:T(8,128)(2,1)S(1)}, bf16[3,272,128]{2,1,0:T(8,128)(2,1)S(1)}, u32[]{:S(2)}, u32[]{:S(2)}) collective-permute-start(bf16[3,272,128]{2,1,0:T(8,128)(2,1)S(1)} %slice_bitcast_fusion.1), channel_id=1, source_target_pairs={{0,8},{8,16},{16,24},{24,1},{1,9},{9,17},{17,25},{25,0},{2,10},{10... | collective-permute-start | bytes 626696 | tf_op jit(solution)/shard_map/ppermute | solution.py:56
  52.5 5.9 %collective-permute-start.13 = (bf16[3,272,128]{2,1,0:T(8,128)(2,1)S(1)}, bf16[3,272,128]{2,1,0:T(8,128)(2,1)S(1)}, u32[]{:S(2)}, u32[]{:S(2)}) collective-permute-start(bf16[3,272,128]{2,1,0:T(8,128)(2,1)S(1)} %slice_bitcast_fusion), channel_id=1, source_target_pairs={{0,25},{8,0},{16,8},{24,16},{1,24},{9,1},{17,9},{25,17},{2,27},{10... | collective-permute-start | bytes 626696 | tf_op jit(solution)/shard_map/ppermute | solution.py:56
  62.9 7.2 %collective-permute-start.14 = (bf16[3,288,128]{2,1,0:T(8,128)(2,1)S(1)}, bf16[3,288,128]{2,1,0:T(8,128)(2,1)S(1)}, u32[]{:S(2)}, u32[]{:S(2)}) collective-permute-start(bf16[3,288,128]{2,1,0:T(8,128)(2,1)S(1)} %get-tuple-element.63), channel_id=1, source_target_pairs={{0,32},{32,64},{64,96},{96,0},{1,33},{33,65},{65,97},{97,1},{2,34}... | collective-permute-start | bytes 663560 | tf_op jit(solution)/shard_map/ppermute | solution.py:51
  64.5 5.9 %collective-permute-start.15 = (bf16[3,288,128]{2,1,0:T(8,128)(2,1)S(1)}, bf16[3,288,128]{2,1,0:T(8,128)(2,1)S(1)}, u32[]{:S(2)}, u32[]{:S(2)}) collective-permute-start(bf16[3,288,128]{2,1,0:T(8,128)(2,1)S(1)} %get-tuple-element.64), channel_id=1, source_target_pairs={{0,96},{32,0},{64,32},{96,64},{1,97},{33,1},{65,33},{97,65},{2,98}... | collective-permute-start | bytes 663560 | tf_op jit(solution)/shard_map/ppermute | solution.py:51
  66.2 7.4 %collective-permute-start.16 = (bf16[3,288,128]{2,1,0:T(8,128)(2,1)S(1)}, bf16[3,288,128]{2,1,0:T(8,128)(2,1)S(1)}, u32[]{:S(2)}, u32[]{:S(2)}) collective-permute-start(bf16[3,288,128]{2,1,0:T(8,128)(2,1)S(1)} %get-tuple-element.65), channel_id=1, source_target_pairs={{0,64},{32,96},{64,0},{96,32},{1,65},{33,97},{65,1},{97,33},{2,66}... | collective-permute-start | bytes 663560 | tf_op jit(solution)/shard_map/ppermute | solution.py:51
  74.3 4.3 %collective-permute-start.17 = (bf16[3,80,128]{2,1,0:T(8,128)(2,1)S(1)}, bf16[3,80,128]{2,1,0:T(8,128)(2,1)S(1)}, u32[]{:S(2)}, u32[]{:S(2)}) collective-permute-start(bf16[3,80,128]{2,1,0:T(8,128)(2,1)S(1)} %get-tuple-element.67), channel_id=1, source_target_pairs={{0,6},{2,0},{4,2},{6,4},{1,7},{3,1},{5,3},{7,5},{8,14},{10,8},{12,... | collective-permute-start | bytes 184328 | tf_op jit(solution)/shard_map/ppermute | solution.py:51
  75.8 5.4 %collective-permute-start.18 = (bf16[3,80,128]{2,1,0:T(8,128)(2,1)S(1)}, bf16[3,80,128]{2,1,0:T(8,128)(2,1)S(1)}, u32[]{:S(2)}, u32[]{:S(2)}) collective-permute-start(bf16[3,80,128]{2,1,0:T(8,128)(2,1)S(1)} %get-tuple-element.68), channel_id=1, source_target_pairs={{0,2},{2,4},{4,6},{6,0},{1,3},{3,5},{5,7},{7,1},{8,10},{10,12},{12... | collective-permute-start | bytes 184328 | tf_op jit(solution)/shard_map/ppermute | solution.py:51
  76.4 5.7 %collective-permute-start.19 = (bf16[3,80,128]{2,1,0:T(8,128)(2,1)S(1)}, bf16[3,80,128]{2,1,0:T(8,128)(2,1)S(1)}, u32[]{:S(2)}, u32[]{:S(2)}) collective-permute-start(bf16[3,80,128]{2,1,0:T(8,128)(2,1)S(1)} %get-tuple-element.69), channel_id=1, source_target_pairs={{0,4},{2,6},{4,0},{6,2},{1,5},{3,7},{5,1},{7,3},{8,12},{10,14},{12... | collective-permute-start | bytes 184328 | tf_op jit(solution)/shard_map/ppermute | solution.py:51
